TPU v7x, 32 devices: a whole 2x2x4 slice. The times are simulated.
32 devices in a mesh: dp: 8 (over z, x), tensor: 4 (over y, core).
Axes of the slice: x: 2, y: 2, z: 4, core: 2. Of those that a mesh axis runs over, the one named last changes fastest.
Arguments:
- tokens_in: bfloat16 [96, 200, 768], P(('dp', 'tensor')), may hold values from -6 to 6
- key_mask: int32 [96, 200], P('dp'), may hold values from 0 to 1, as said below
- expert_ids: int32 [96, 200, 2], P('dp'), may hold values from 0 to 7, as said below
- expert_slots: int32 [96, 200, 2], P('dp'), may hold values from 0 to 127, as said below
- norm1_gain: float32 [768], P('dp'), may hold values from 0.5 to 1.5
- norm1_shift: float32 [768], P('dp'), may hold values from -1.5 to 1.5
- qkv_weight: float32 [3, 768, 768], P(None, 'dp', 'tensor'), may hold values from -0.21875 to 0.21875
- qv_bias: float32 [2, 768], P(None, 'dp'), may hold values from -1.5 to 1.5
- out_weight: float32 [768, 768], P('tensor', 'dp'), may hold values from -1.75 to 1.75
- out_bias: float32 [768], P('dp'), may hold values from -1.5 to 1.5
- norm2_gain: float32 [768], P('dp'), may hold values from 0.5 to 1.5
- norm2_shift: float32 [768], P('dp'), may hold values from -1.5 to 1.5
- router_weight: float32 [768, 8], P('dp'), may hold values from -0.15625 to 0.15625
- up_weight: float32 [8, 768, 3072], P(None, 'dp', 'tensor'), may hold values from -0.21875 to 0.21875
- up_bias: float32 [8, 3072], P(None, 'dp'), may hold values from -1.5 to 1.5
- down_weight: float32 [8, 3072, 768], P(None, 'tensor', 'dp'), may hold values from -0.875 to 0.875
- down_bias: float32 [8, 768], P(None, 'dp'), may hold values from -5 to 5
- out_grad: bfloat16 [96, 200, 768], P(('dp', 'tensor')), may hold values from -6 to 6
Outputs:
- output: bfloat16 [96, 200, 768], P(('dp', 'tensor'))
- input_grad: float32 [96, 200, 768], P(('dp', 'tensor'))
- norm1_gain_grad: float32 [768], P('dp')
- norm1_shift_grad: float32 [768], P('dp')
- qkv_weight_grad: float32 [3, 768, 768], P(None, 'dp', 'tensor')
- qv_bias_grad: float32 [2, 768], P(None, 'dp')
- out_weight_grad: float32 [768, 768], P('tensor', 'dp')
- out_bias_grad: float32 [768], P('dp')
- norm2_gain_grad: float32 [768], P('dp')
- norm2_shift_grad: float32 [768], P('dp')
- router_weight_grad: float32 [768, 8], P('dp')
- up_weight_grad: float32 [8, 768, 3072], P(None, 'dp', 'tensor')
- up_bias_grad: float32 [8, 3072], P(None, 'dp')
- down_weight_grad: float32 [8, 3072, 768], P(None, 'tensor', 'dp')
- down_bias_grad: float32 [8, 768], P(None, 'dp')
Inputs may be any that keep to these rules, and one draw needn't show every extreme that they name: `key_mask`: each image's keys with value 1 are its first 200 - p positions, with p from 1 to 3; some image has p = 3 and some has p = 1. `expert_ids`: A token's two ids differ. In each group of 2 consecutive images expert e is named by L_e of the 800 choices, L_e at most 128, and some expert of every group has exactly 128. Within a group the pairs (expert_ids, expert_slots) of all tokens and both choices are distinct, and the slots of expert e are exactly 0 to L_e - 1.
All inputs are finite; a program needn't handle non-finite values.
Results may differ from a plain program's by a relative error of at most 0.017.
Values may be sent and summed in bfloat16 or wider, within the bound.
No kernel may reach another device: no remote copies, remote signals or barrier semaphores. Data moves between devices by JAX's collectives and lax.ppermute only.
A program may use at most 320 MiB of HBM per device.

v0:
```python
import jax
import jax.numpy as jnp
from jax import lax
from jax.sharding import PartitionSpec as P

HD = 64
SEQ = 200
CAP = 128
GROUP_IMG = 2


EPSILON = 1e-06
NEGATIVE = -1e30
HIGHEST_PRECISION = lax.Precision.HIGHEST


def norm_forward(values, gains, shifts):
    middle = jnp.mean(values, -1, keepdims=True)
    centred = values - middle
    inverse = lax.rsqrt(jnp.mean(centred * centred, -1, keepdims=True) + EPSILON)
    unit_rows = centred * inverse
    return (unit_rows * gains + shifts, unit_rows, inverse)


def norm_backward(grad_rows, unit_rows, inverse, gains):
    scaled = grad_rows * gains
    return inverse * (
        scaled
        - jnp.mean(scaled, -1, keepdims=True)
        - unit_rows * jnp.mean(scaled * unit_rows, -1, keepdims=True)
    )


def gelu_exact(values):
    return jax.nn.gelu(values, approximate=False)


def gather_images(values):
    return lax.all_gather(values, "tensor", axis=0, tiled=True)


def scatter_images(values):
    return lax.psum_scatter(values, "tensor", scatter_dimension=0, tiled=True)


def attention_scores(queries, key_rows, key_mask):
    scores = jnp.einsum(
        "bihc,bjhc->bhij", queries, key_rows, preferred_element_type=jnp.float32
    ) * HD ** (-0.5)
    return jnp.where(key_mask[:, None, None, :] > 0, scores, NEGATIVE)


def fill_table(where, entries, length):
    return jnp.zeros((length,), entries.dtype).at[where].set(entries)


def shards(
    tokens_in,
    key_mask,
    expert_ids,
    expert_slots,
    norm1_gain,
    norm1_shift,
    qkv_weight,
    qv_bias,
    out_weight,
    out_bias,
    norm2_gain,
    norm2_shift,
    router_weight,
    up_weight,
    up_bias,
    down_weight,
    down_bias,
    out_grad,
):
    tensor_place = lax.axis_index("tensor")
    images = key_mask.shape[0]
    piece = tokens_in.shape[0]
    sequence = key_mask.shape[1]
    experts = up_weight.shape[0]
    local_start = tensor_place * piece
    (
        gain_one,
        shift_one,
        qkv_full,
        bias_pair,
        out_full,
        bias_out,
        gain_two,
        shift_two,
        router_full,
        bias_up,
        bias_down,
    ) = (
        lax.all_gather(norm1_gain.astype(jnp.bfloat16), "dp", axis=0, tiled=True),
        lax.all_gather(norm1_shift.astype(jnp.bfloat16), "dp", axis=0, tiled=True),
        lax.all_gather(qkv_weight.astype(jnp.bfloat16), "dp", axis=1, tiled=True),
        lax.all_gather(qv_bias.astype(jnp.bfloat16), "dp", axis=1, tiled=True),
        lax.all_gather(out_weight.astype(jnp.bfloat16), "dp", axis=1, tiled=True),
        lax.all_gather(out_bias.astype(jnp.bfloat16), "dp", axis=0, tiled=True),
        lax.all_gather(norm2_gain.astype(jnp.bfloat16), "dp", axis=0, tiled=True),
        lax.all_gather(norm2_shift.astype(jnp.bfloat16), "dp", axis=0, tiled=True),
        lax.all_gather(router_weight.astype(jnp.bfloat16), "dp", axis=0, tiled=True),
        lax.all_gather(up_bias.astype(jnp.bfloat16), "dp", axis=1, tiled=True),
        lax.all_gather(down_bias.astype(jnp.bfloat16), "dp", axis=1, tiled=True),
    )
    gain_one_f = gain_one.astype(jnp.float32)
    gain_two_f = gain_two.astype(jnp.float32)
    bias_down_f = bias_down.astype(jnp.float32)
    width = qkv_full.shape[2]
    model_width = qkv_full.shape[1]
    heads_here = width // HD
    shape_heads = (images, sequence, heads_here, HD)
    inputs = tokens_in.astype(jnp.float32)
    normed_one, unit_one, inverse_one = norm_forward(
        inputs, gain_one_f, shift_one.astype(jnp.float32)
    )
    full_one = gather_images(normed_one.astype(jnp.bfloat16))
    qkv_joined = qkv_full.transpose(1, 0, 2).reshape(model_width, 3 * width)
    bias_here = lax.dynamic_slice_in_dim(bias_pair, tensor_place * width, width, 1).astype(
        jnp.float32
    )
    projected = jnp.einsum("bsd,dk->bsk", full_one, qkv_joined, preferred_element_type=jnp.float32)
    queries = (projected[..., :width] + bias_here[0]).astype(jnp.bfloat16).reshape(shape_heads)
    key_rows = projected[..., width : 2 * width].astype(jnp.bfloat16).reshape(shape_heads)
    value_rows = (
        (projected[..., 2 * width :] + bias_here[1]).astype(jnp.bfloat16).reshape(shape_heads)
    )
    masked = attention_scores(queries, key_rows, key_mask)
    largest = jnp.max(masked, -1, keepdims=True)
    log_total = largest + jnp.log(jnp.sum(jnp.exp(masked - largest), -1, keepdims=True))
    weights_low = jnp.exp(masked - log_total).astype(jnp.bfloat16)
    attended = jnp.einsum(
        "bhij,bjhc->bihc", weights_low, value_rows, preferred_element_type=jnp.float32
    )
    attended = attended.astype(jnp.bfloat16).reshape(images, sequence, width)
    attention_local = scatter_images(
        jnp.einsum("bsk,kd->bsd", attended, out_full, preferred_element_type=jnp.float32)
    )
    residual = inputs + attention_local + bias_out.astype(jnp.float32)
    normed_two, unit_two, inverse_two = norm_forward(
        residual, gain_two_f, shift_two.astype(jnp.float32)
    )
    full_two = gather_images(normed_two.astype(jnp.bfloat16))
    logits = jnp.einsum("bsd,de->bse", full_two, router_full, preferred_element_type=jnp.float32)
    chances = jax.nn.softmax(logits, -1)
    route_hot = (expert_ids[..., None] == jnp.arange(experts, dtype=jnp.int32)).astype(jnp.float32)
    gates = jnp.sum(route_hot * chances[:, :, None, :], -1)
    hot_local = lax.dynamic_slice_in_dim(route_hot, local_start, piece, 0)
    gates_local = lax.dynamic_slice_in_dim(gates, local_start, piece, 0)
    share_local = jnp.sum(hot_local * gates_local[..., None], 2)
    group_tokens = GROUP_IMG * SEQ
    groups = images * sequence // group_tokens
    position = (expert_ids * CAP + expert_slots).reshape(groups, 2 * group_tokens)
    token_rows = (jnp.arange(images * sequence * 2, dtype=jnp.int32) // 2).reshape(
        groups, 2 * group_tokens
    )
    table_fill = jax.vmap(lambda where, entries: fill_table(where, entries, experts * CAP))
    row_table = table_fill(position, token_rows).reshape(groups, experts, CAP).transpose(1, 0, 2)
    row_table = row_table.reshape(experts, groups * CAP)
    gate_table = table_fill(position, gates.reshape(groups, 2 * group_tokens)).reshape(
        groups, experts, CAP
    )
    gate_table = gate_table.transpose(1, 0, 2).reshape(experts, groups * CAP)
    flat_two = full_two.reshape(images * sequence, model_width)
    up_ready = up_weight.astype(jnp.bfloat16)
    down_ready = down_weight.astype(jnp.bfloat16).transpose(0, 2, 1)
    units_here = up_weight.shape[2]
    bias_owned = lax.dynamic_slice_in_dim(bias_up, tensor_place * units_here, units_here, 1)
    bias_owned = bias_owned.astype(jnp.float32)
    up_all, down_all = (
        lax.all_gather(up_ready, "dp", axis=1, tiled=True),
        lax.all_gather(down_ready, "dp", axis=1, tiled=True),
    )

    def expert_forward(mixture, items):
        up_one, down_one, bias_one, rows_one, gates_one = items
        chosen = jnp.take(flat_two, rows_one, 0)
        hidden = jnp.dot(chosen, up_one, preferred_element_type=jnp.float32) + bias_one
        active = gelu_exact(hidden).astype(jnp.bfloat16)
        produced = jnp.einsum("rf,df->rd", active, down_one, preferred_element_type=jnp.float32)
        return (mixture.at[rows_one].add(produced * gates_one[:, None]), (hidden, active, produced))

    mixture, (hidden_kept, active_all, produced_kept) = lax.scan(
        expert_forward,
        jnp.zeros((images * sequence, model_width), jnp.float32),
        (up_all, down_all, bias_owned, row_table, gate_table),
    )
    mixture_local = scatter_images(mixture.reshape(images, sequence, model_width))
    bias_term = jnp.einsum("bse,ed->bsd", share_local, bias_down_f, precision=HIGHEST_PRECISION)
    output = (residual + mixture_local + bias_term).astype(jnp.bfloat16)
    grad_local = out_grad.astype(jnp.float32)
    grad_full = gather_images(out_grad)
    grad_flat = grad_full.reshape(images * sequence, model_width)
    up_again, down_again = (
        lax.all_gather(up_ready, "dp", axis=1, tiled=True),
        lax.all_gather(down_ready, "dp", axis=1, tiled=True),
    )

    def expert_backward(pulled, items):
        up_one, down_one, rows_one, gates_one, hidden, produced = items
        unused_values, pull_gelu = jax.vjp(gelu_exact, hidden)
        incoming = jnp.take(grad_flat, rows_one, 0).astype(jnp.float32)
        gate_part = jnp.sum(incoming * produced, -1)
        out_part = (incoming * gates_one[:, None]).astype(jnp.bfloat16)
        active_grad = jnp.dot(out_part, down_one, preferred_element_type=jnp.float32)
        hidden_grad = pull_gelu(active_grad)[0].astype(jnp.bfloat16)
        row_grad = jnp.einsum("rf,df->rd", hidden_grad, up_one, preferred_element_type=jnp.float32)
        bias_part = jnp.sum(hidden_grad.astype(jnp.float32), 0)
        return (pulled.at[rows_one].add(row_grad), (out_part, hidden_grad, gate_part, bias_part))

    pulled, (out_all, hidden_all, gate_parts, bias_parts) = lax.scan(
        expert_backward,
        jnp.zeros((images * sequence, model_width), jnp.float32),
        (up_again, down_again, row_table, gate_table, hidden_kept, produced_kept),
    )
    columns = flat_two
    picked = jnp.take(columns, row_table, 0)
    up_grad = lax.psum_scatter(
        jnp.einsum("nrc,nrf->cnf", picked, hidden_all, preferred_element_type=jnp.float32),
        "dp",
        scatter_dimension=0,
        tiled=True,
    ).transpose(1, 0, 2)
    columns = out_all
    down_grad = lax.psum_scatter(
        jnp.einsum("nrc,nrf->cnf", columns, active_all, preferred_element_type=jnp.float32),
        "dp",
        scatter_dimension=0,
        tiled=True,
    ).transpose(1, 0, 2)
    full_units = bias_up.shape[1]
    up_bias_grad = lax.dynamic_update_slice_in_dim(
        jnp.zeros((experts, full_units), jnp.float32), bias_parts, tensor_place * units_here, 1
    )
    slot_flat = (
        gate_parts.reshape(experts, groups, CAP).transpose(1, 0, 2).reshape(groups, experts * CAP)
    )
    gate_grad = jnp.take_along_axis(slot_flat, position, 1).reshape(images, sequence, 2)
    bias_dot = jnp.einsum("bsd,ed->bse", out_grad, bias_down, preferred_element_type=jnp.float32)
    gate_bias = jnp.sum(hot_local * bias_dot[:, :, None, :], -1)
    gate_grad = gate_grad + lax.dynamic_update_slice_in_dim(
        jnp.zeros_like(gate_grad), gate_bias, local_start, 0
    )
    gate_grad = lax.psum(gate_grad, "tensor")
    chance_grad = jnp.sum(route_hot * gate_grad[..., None], 2)
    logit_grad = chances * (chance_grad - jnp.sum(chances * chance_grad, -1, keepdims=True))
    logit_grad = logit_grad.astype(jnp.bfloat16)
    router_grad = jnp.einsum(
        "bsd,bse->de", full_two, logit_grad, preferred_element_type=jnp.float32
    )
    logit_local = lax.dynamic_slice_in_dim(logit_grad, local_start, piece, 0)
    norm_two_grad = scatter_images(pulled.reshape(images, sequence, model_width))
    norm_two_grad = norm_two_grad + jnp.einsum(
        "bse,de->bsd", logit_local, router_full, preferred_element_type=jnp.float32
    )
    down_bias_grad = jnp.einsum("bse,bsd->ed", share_local, grad_local, precision=HIGHEST_PRECISION)
    gain_two_grad = jnp.sum(norm_two_grad * unit_two, (0, 1))
    shift_two_grad = jnp.sum(norm_two_grad, (0, 1))
    residual_grad = grad_local + norm_backward(norm_two_grad, unit_two, inverse_two, gain_two_f)
    out_bias_grad = jnp.sum(residual_grad, (0, 1))
    residual_full = gather_images(residual_grad.astype(jnp.bfloat16))
    out_weight_grad = jnp.einsum(
        "bsk,bsd->kd", attended, residual_full, preferred_element_type=jnp.float32
    )
    attended_grad = jnp.einsum(
        "bsd,kd->bsk", residual_full, out_full, preferred_element_type=jnp.float32
    )
    attended_grad = attended_grad.astype(jnp.bfloat16).reshape(shape_heads)
    masked = attention_scores(queries, key_rows, key_mask)
    chances_again = jnp.exp(masked - log_total)
    weights_again = chances_again.astype(jnp.bfloat16)
    value_grad = jnp.einsum(
        "bhij,bihc->bjhc", weights_again, attended_grad, preferred_element_type=jnp.float32
    ).astype(jnp.bfloat16)
    weight_grad = jnp.einsum(
        "bihc,bjhc->bhij", attended_grad, value_rows, preferred_element_type=jnp.float32
    )
    score_grad = chances_again * (
        weight_grad - jnp.sum(chances_again * weight_grad, -1, keepdims=True)
    )
    score_grad = score_grad.astype(jnp.bfloat16)
    scale = HD ** (-0.5)
    query_grad = (
        jnp.einsum("bhij,bjhc->bihc", score_grad, key_rows, preferred_element_type=jnp.float32)
        * scale
    ).astype(jnp.bfloat16)
    key_grad = (
        jnp.einsum("bhij,bihc->bjhc", score_grad, queries, preferred_element_type=jnp.float32)
        * scale
    ).astype(jnp.bfloat16)
    joined_grad = jnp.concatenate(
        [
            query_grad.reshape(images, sequence, width),
            key_grad.reshape(images, sequence, width),
            value_grad.reshape(images, sequence, width),
        ],
        -1,
    )
    qkv_grad = jnp.einsum("bsd,bsk->dk", full_one, joined_grad, preferred_element_type=jnp.float32)
    qkv_grad = qkv_grad.reshape(model_width, 3, width).transpose(1, 0, 2)
    pair_here = jnp.stack(
        [
            jnp.sum(query_grad.astype(jnp.float32), (0, 1)).reshape(width),
            jnp.sum(value_grad.astype(jnp.float32), (0, 1)).reshape(width),
        ]
    )
    pair_grad = lax.dynamic_update_slice_in_dim(
        jnp.zeros((2, bias_pair.shape[1]), jnp.float32), pair_here, tensor_place * width, 1
    )
    norm_one_grad = scatter_images(
        jnp.einsum("bsk,dk->bsd", joined_grad, qkv_joined, preferred_element_type=jnp.float32)
    )
    gain_one_grad = jnp.sum(norm_one_grad * unit_one, (0, 1))
    shift_one_grad = jnp.sum(norm_one_grad, (0, 1))
    input_grad = residual_grad + norm_backward(norm_one_grad, unit_one, inverse_one, gain_one_f)
    (
        gain_one_grad,
        shift_one_grad,
        pair_grad,
        out_bias_grad,
        gain_two_grad,
        shift_two_grad,
        up_bias_grad,
        down_bias_grad,
    ) = (
        lax.psum(gain_one_grad.astype(jnp.bfloat16), "tensor").astype(jnp.float32),
        lax.psum(shift_one_grad.astype(jnp.bfloat16), "tensor").astype(jnp.float32),
        lax.psum(pair_grad.astype(jnp.bfloat16), "tensor").astype(jnp.float32),
        lax.psum(out_bias_grad.astype(jnp.bfloat16), "tensor").astype(jnp.float32),
        lax.psum(gain_two_grad.astype(jnp.bfloat16), "tensor").astype(jnp.float32),
        lax.psum(shift_two_grad.astype(jnp.bfloat16), "tensor").astype(jnp.float32),
        lax.psum(up_bias_grad.astype(jnp.bfloat16), "tensor").astype(jnp.float32),
        lax.psum(down_bias_grad.astype(jnp.bfloat16), "tensor").astype(jnp.float32),
    )
    (
        gain_one_grad,
        shift_one_grad,
        qkv_grad,
        pair_grad,
        out_weight_grad,
        out_bias_grad,
        gain_two_grad,
        shift_two_grad,
        router_grad,
        up_bias_grad,
        down_bias_grad,
    ) = (
        lax.psum_scatter(gain_one_grad, "dp", scatter_dimension=0, tiled=True),
        lax.psum_scatter(shift_one_grad, "dp", scatter_dimension=0, tiled=True),
        lax.psum_scatter(qkv_grad, "dp", scatter_dimension=1, tiled=True),
        lax.psum_scatter(pair_grad, "dp", scatter_dimension=1, tiled=True),
        lax.psum_scatter(out_weight_grad, "dp", scatter_dimension=1, tiled=True),
        lax.psum_scatter(out_bias_grad, "dp", scatter_dimension=0, tiled=True),
        lax.psum_scatter(gain_two_grad, "dp", scatter_dimension=0, tiled=True),
        lax.psum_scatter(shift_two_grad, "dp", scatter_dimension=0, tiled=True),
        lax.psum_scatter(router_grad, "dp", scatter_dimension=0, tiled=True),
        lax.psum_scatter(up_bias_grad, "dp", scatter_dimension=1, tiled=True),
        lax.psum_scatter(down_bias_grad, "dp", scatter_dimension=1, tiled=True),
    )
    return (
        output,
        input_grad,
        gain_one_grad,
        shift_one_grad,
        qkv_grad,
        pair_grad,
        out_weight_grad,
        out_bias_grad,
        gain_two_grad,
        shift_two_grad,
        router_grad,
        up_grad,
        up_bias_grad,
        down_grad.transpose(0, 2, 1),
        down_bias_grad,
    )


def solution(mesh):
    return jax.shard_map(
        shards,
        mesh=mesh,
        in_specs=(
            P(("dp", "tensor"), None, None),
            P("dp", None),
            P("dp", None, None),
            P("dp", None, None),
            P("dp"),
            P("dp"),
            P(None, "dp", "tensor"),
            P(None, "dp"),
            P("tensor", "dp"),
            P("dp"),
            P("dp"),
            P("dp"),
            P("dp", None),
            P(None, "dp", "tensor"),
            P(None, "dp"),
            P(None, "tensor", "dp"),
            P(None, "dp"),
            P(("dp", "tensor"), None, None),
        ),
        out_specs=(
            P(("dp", "tensor"), None, None),
            P(("dp", "tensor"), None, None),
            P("dp"),
            P("dp"),
            P(None, "dp", "tensor"),
            P(None, "dp"),
            P("tensor", "dp"),
            P("dp"),
            P("dp"),
            P("dp"),
            P("dp", None),
            P(None, "dp", "tensor"),
            P(None, "dp"),
            P(None, "tensor", "dp"),
            P(None, "dp"),
        ),
        check_vma=False,
    )
```

profile of v0, /device:TPU:0, one launch (start us, length us, event | category | flops | bytes accessed | tf_op | source)
XLA Modules:
  0.0 2504.9 jit_solution(16611879427394642080)
XLA Ops:
  13.6 38.8 %all-reduce.11 = (bf16[768]{0:T(1024)(128)(2,1)S(1)}, bf16[768]{0:T(1024)(128)(2,1)S(1)}, bf16[768]{0:T(1024)(128)(2,1)S(1)}, bf16[768]{0:T(1024)(128)(2,1)S(1)}, bf16[768]{0:T(1024)(128)(2,1)S(1)}) all-reduce(bf16[768]{0:T(1024)(128)(2,1)S(1)} %dynamic-update-slice.2, ...), channel_id=1, replica_groups=mesh['dp'=8,'tensor'=4] {'dp'}, use_global_device_ids=true, to_apply=%add.1 | all-reduce | flops 3840 | bytes 15360
  57.5 33.0 %all_gather.56 = bf16[3,768,192]{2,1,0:T(8,128)(2,1)S(1)} all-gather(bf16[3,96,192]{2,1,0:T(8,128)(2,1)S(1)} %convert_element_type.201), channel_id=1, replica_groups=mesh['dp'=8,'tensor'=4] {'dp'}, dimensions={1}, use_global_device_ids=true | all-gather | bytes 995328 | tf_op jit(solution)/shard_map/all_gather | solution.py:98
  91.3 16.2 all-gather
  107.7 33.2 %all_gather.58 = bf16[192,768]{0,1:T(8,128)(2,1)} all-gather(bf16[192,96]{0,1:T(8,128)(2,1)S(1)} %copy.146), channel_id=1, replica_groups=mesh['dp'=8,'tensor'=4] {'dp'}, dimensions={1}, use_global_device_ids=true | all-gather | bytes 331776 | tf_op jit(solution)/shard_map/all_gather | solution.py:100
  172.5 64.6 %reduce-scatter.21.cloned.1.call-done = f32[3,200,768]{2,1,0:T(8,128)} async-done(((f32[12,200,768]{2,1,0:T(8,128)}), f32[3,200,768]{2,1,0:T(8,128)}) %reduce-scatter.21.cloned.1.call-update) | async-done | bytes 1843216 | tf_op jit(solution)/shard_map/reduce_scatter | solution.py:43
  248.9 30.7 %all_gather.64 = bf16[8,3072]{1,0:T(8,128)(2,1)S(1)} all-gather(bf16[8,384]{1,0:T(8,128)(2,1)S(1)} %convert_element_type.218), channel_id=1, replica_groups=mesh['dp'=8,'tensor'=4] {'dp'}, dimensions={1}, use_global_device_ids=true | all-gather | bytes 55296 | tf_op jit(solution)/shard_map/all_gather | solution.py:105
  279.6 27.2 %all-gather.1 = bf16[8,96,8]{1,2,0:T(8,128)(2,1)S(1)} all-gather(bf16[1,96,8]{1,2,0:T(8,128)(2,1)S(1)} %convert_bitcast_fusion.3), channel_id=1, replica_groups=mesh['dp'=8,'tensor'=4] {'dp'}, dimensions={0}, use_global_device_ids=true | all-gather | bytes 13824 | tf_op jit(solution)/shard_map/all_gather | solution.py:104
  306.9 22.9 scatter_custom_fusion.2
  334.7 22.9 scatter_custom_fusion.3
  357.6 57.3 %all-gather.14.cloned.1.call-done = bf16[8,768,768]{2,1,0:T(8,128)(2,1)} async-done(((bf16[8,96,768]{2,1,0:T(8,128)(2,1)}), bf16[8,768,768]{2,1,0:T(8,128)(2,1)}) %all-gather.14.cloned.1.call-update) | async-done | bytes 9437200 | tf_op jit(solution)/shard_map/all_gather | solution.py:173
  414.9 139.1 %all-gather.16.cloned.1.call-done = bf16[8,768,768]{2,1,0:T(8,128)(2,1)} async-done(((bf16[8,96,768]{2,1,0:T(8,128)(2,1)}), bf16[8,768,768]{2,1,0:T(8,128)(2,1)}) %all-gather.16.cloned.1.call-update) | async-done | bytes 9437200 | tf_op jit(solution)/shard_map/all_gather | solution.py:174
  562.4 285.9 %while.34 = (s32[]{:T(128)}, f32[2400,768]{1,0:T(8,128)}, f32[8,768,768]{2,1,0:T(8,128)}, bf16[8,768,768]{2,1,0:T(8,128)(2,1)}, f32[8,768,768]{2,1,0:T(8,128)}, ...) while((s32[]{:T(128)}, f32[2400,768]{1,0:T(8,128)}, ...), condition=%wide.region_14.16_spmd, body=%wide.region_12.15_spmd.sunk | while | flops 1853237248 | bytes 31023756 | solution.py:185
  860.0 305.5 %while.35 = (s32[]{:T(128)}, f32[2400,768]{1,0:T(8,128)}, bf16[8,768,768]{2,1,0:T(8,128)(2,1)}, bf16[8,768,768]{2,1,0:T(8,128)(2,1)}, f32[8,768]{1,0:T(8,128)}, ...) while((s32[]{:T(128)}, f32[2400,768]{1,0:T(8,128)}, ...), condition=%wide.region_21.23_spmd, body=%wide.region_17.22_spmd.sunk | while | flops 1863262720 | bytes 38216540 | solution.py:213
  1166.8 26.0 %all-gather.2 = bf16[8,96,8]{1,2,0:T(8,128)(2,1)S(1)} all-gather(bf16[1,96,8]{1,2,0:T(8,128)(2,1)S(1)} %convert_bitcast_fusion.2), channel_id=1, replica_groups=mesh['dp'=8,'tensor'=4] {'dp'}, dimensions={0}, use_global_device_ids=true | all-gather | bytes 13824 | tf_op jit(solution)/shard_map/all_gather | solution.py:106
  1193.5 28.0 %gather_fusion.3 = f32[4800]{0:T(1024)S(1)} fusion(f32[6,1024]{1,0:T(8,128)S(1)} %bitcast.281, s32[4800]{0:T(1024)S(1)} %reshape.375), kind=kCustom, calls=%fused_computation.3 | custom fusion | bytes 76800 | tf_op jit(solution)/shard_map/jit(take_along_axis)/gather | solution.py:240
  1243.8 29.2 %all-gather.20.cloned.1.call-done = bf16[12,200,768]{2,1,0:T(8,128)(2,1)} async-done(((bf16[3,200,768]{2,1,0:T(8,128)(2,1)}), bf16[12,200,768]{2,1,0:T(8,128)(2,1)}) %all-gather.20.cloned.1.call-update) | async-done | bytes 3686416 | tf_op jit(solution)/shard_map/all_gather | solution.py:39
  1310.1 62.4 %reduce-scatter.27.cloned.1.call-done = f32[3,200,768]{2,1,0:T(8,128)} async-done(((f32[12,200,768]{2,1,0:T(8,128)}), f32[3,200,768]{2,1,0:T(8,128)}) %reduce-scatter.27.cloned.1.call-update) | async-done | bytes 1843216 | tf_op jit(solution)/shard_map/reduce_scatter | solution.py:43
  1386.4 20.3 all-reduce.15.cloned.1.call-done
  1408.4 30.6 %gather_fusion.2 = bf16[6144,768]{1,0:T(8,128)(2,1)} fusion(bf16[2400,768]{1,0:T(8,128)(2,1)} %get-tuple-element.621, s32[6144]{0:T(1024)S(1)} %broadcast_clamp_fusion), kind=kCustom, calls=%fused_computation.2 | custom fusion | bytes 18898944 | tf_op jit(solution)/shard_map/jit(_take)/gather | solution.py:219
  1440.0 15.7 fusion.70
  1455.7 19.2 copy.162
  1475.2 16.9 convolution_bitcast_fusion
  1492.1 19.3 copy.164
  1524.0 16.9 reduce-scatter.23.cloned.1.call-done
  1544.2 62.8 %reduce-scatter.39.cloned.1.call-done = f32[96,192]{1,0:T(8,128)} async-done(((f32[768,192]{1,0:T(8,128)}), f32[96,192]{1,0:T(8,128)}) %reduce-scatter.39.cloned.1.call-update) | async-done | bytes 73744
  1613.4 35.1 %all-reduce.10 = (f32[768]{0:T(1024)S(1)}, f32[768]{0:T(1024)S(1)}, f32[768]{0:T(1024)S(1)}, f32[768]{0:T(1024)S(1)}, f32[768]{0:T(1024)S(1)}) all-reduce(bf16[768]{0:T(1024)(128)(2,1)S(1)} %copy-done.68, bf16[768]{0:T(1024)(128)(2,1)S(1)} %copy-done.69, ...), channel_id=6, replica_groups=mesh['dp'=8,'tensor'=4] {'dp'}, use_global_device_ids=true, to_apply=%region_35.37.clone | all-reduce | flops 3840 | bytes 23040
  1651.4 19.2 reduce-scatter.37.cloned.1.call-done
  1672.0 62.1 %reduce-scatter.43.cloned.1.call-done = f32[96,8]{1,0:T(8,128)} async-done(((f32[768,8]{1,0:T(8,128)}), f32[96,8]{1,0:T(8,128)}) %reduce-scatter.43.cloned.1.call-update) | async-done | bytes 3088
  1735.6 314.1 %reduce-scatter.31.cloned.1.call-done = f32[96,8,768]{2,1,0:T(8,128)} async-done(((f32[768,8,768]{2,1,0:T(8,128)}), f32[96,8,768]{2,1,0:T(8,128)}) %reduce-scatter.31.cloned.1.call-update) | async-done | bytes 2359312 | tf_op jit(solution)/shard_map/reduce_scatter | solution.py:220
  2053.6 311.9 %reduce-scatter.35.cloned.1.call-done = f32[96,8,768]{2,1,0:T(8,128)} async-done(((f32[768,8,768]{2,1,0:T(8,128)}), f32[96,8,768]{2,1,0:T(8,128)}) %reduce-scatter.35.cloned.1.call-update) | async-done | bytes 2359312 | tf_op jit(solution)/shard_map/reduce_scatter | solution.py:227
  2369.3 68.4 %reduce-scatter.29.cloned.1.call-done = f32[3,96,192]{2,1,0:T(8,128)} async-done(((f32[3,768,192]{2,1,0:T(8,128)}), f32[3,96,192]{2,1,0:T(8,128)}) %reduce-scatter.29.cloned.1.call-update) | async-done | bytes 221200 | tf_op jit(solution)/shard_map/reduce_scatter | solution.py:352
  2437.7 60.6 %reduce-scatter.33.cloned.1.call-done = f32[8,384]{1,0:T(8,128)} async-done(((f32[8,3072]{1,0:T(8,128)}), f32[8,384]{1,0:T(8,128)}) %reduce-scatter.33.cloned.1.call-update) | async-done | bytes 12304 | tf_op jit(solution)/shard_map/reduce_scatter | solution.py:359
  (659 shorter events, 782.5 us)
Async XLA Ops:
  7.2 133.7 %all-gather.10.cloned.1.call-start = ((), (), s32[]{:S(2)}) async-start(), calls=%async_computation.12 | async-start | bytes 4608000 | tf_op jit(solution)/shard_map/all_gather | solution.py:39
  57.4 50.1 %copy-start.49 = (f32[192,96]{1,0:T(8,128)S(1)}, f32[192,96]{1,0:T(8,128)}, u32[]{:S(2)}) copy-start(f32[192,96]{1,0:T(8,128)} %param.32) | copy-start | bytes 221188
  57.4 83.4 %copy-start.61 = (s32[12,200]{1,0:T(8,128)S(1)}, s32[12,200]{1,0:T(8,128)}, u32[]{:S(2)}) copy-start(s32[12,200]{1,0:T(8,128)} %param.25) | copy-start | bytes 28804
  57.5 179.7 %reduce-scatter.21.cloned.1.call-start = ((), (), s32[]{:S(2)}) async-start(), calls=%async_computation.13 | async-start | bytes 9216000 | tf_op jit(solution)/shard_map/reduce_scatter | solution.py:43
  172.4 157.4 %all-gather.12.cloned.1.call-start = ((), (), s32[]{:S(2)}) async-start(), calls=%async_computation.14 | async-start | bytes 4608000 | tf_op jit(solution)/shard_map/all_gather | solution.py:39
  172.5 66.8 %copy-start.54 = (f32[768]{0:T(1024)}, f32[768]{0:T(1024)S(1)}, u32[]{:S(2)}) copy-start(f32[768]{0:T(1024)S(1)} %convert_element_type.213) | copy-start | bytes 9220
  242.1 172.8 %all-gather.14.cloned.1.call-start = ((), (), s32[]{:S(2)}) async-start(), calls=%async_computation.15 | async-start | bytes 10616832 | tf_op jit(solution)/shard_map/all_gather | solution.py:173
  243.3 310.7 %all-gather.16.cloned.1.call-start = ((), (), s32[]{:S(2)}) async-start(), calls=%async_computation.16 | async-start | bytes 10616832 | tf_op jit(solution)/shard_map/all_gather | solution.py:174
  246.2 602.0 %all-gather.18.cloned.1.call-start = ((), (), s32[]{:S(2)}) async-start(), calls=%async_computation.18 | async-start | bytes 4608000 | tf_op jit(solution)/shard_map/all_gather | solution.py:39
  246.8 990.2 %reduce-scatter.25.cloned.1.call-start = ((), (), s32[]{:S(2)}) async-start(), calls=%async_computation.19 | async-start | bytes 9216000 | tf_op jit(solution)/shard_map/reduce_scatter | solution.py:43
  246.9 86.0 %copy-start.34 = (s32[12,200,2]{1,2,0:T(2,128)}, s32[12,200,2]{1,2,0:T(2,128)S(1)}, u32[]{:S(2)}) copy-start(s32[12,200,2]{1,2,0:T(2,128)S(1)} %multiply_add_fusion.2) | copy-start | bytes 57604
  333.0 224.6 %copy-start.32 = (f32[12,200]{1,0:T(8,128)}, f32[12,200]{1,0:T(8,128)S(1)}, u32[]{:S(2)}) copy-start(f32[12,200]{1,0:T(8,128)S(1)} %get-tuple-element.330) | copy-start | bytes 28804
  333.7 223.9 %copy-start.39 = (f32[12,200,2]{1,2,0:T(2,128)}, f32[12,200,2]{1,2,0:T(2,128)S(1)}, u32[]{:S(2)}) copy-start(f32[12,200,2]{1,2,0:T(2,128)S(1)} %select_reduce_fusion.1) | copy-start | bytes 57604
  1166.2 106.8 %all-gather.20.cloned.1.call-start = ((), (), s32[]{:S(2)}) async-start(), calls=%async_computation.20 | async-start | bytes 4608000 | tf_op jit(solution)/shard_map/all_gather | solution.py:39
  1243.8 128.7 %reduce-scatter.27.cloned.1.call-start = ((), (), s32[]{:S(2)}) async-start(), calls=%async_computation.21 | async-start | bytes 9216000 | tf_op jit(solution)/shard_map/reduce_scatter | solution.py:43
  1306.6 65.9 %copy-start.4 = (bf16[3,200,768]{2,1,0:T(8,128)(2,1)S(1)}, bf16[3,200,768]{2,1,0:T(8,128)(2,1)}, u32[]{:S(2)}) copy-start(bf16[3,200,768]{2,1,0:T(8,128)(2,1)} %param.24) | copy-start | bytes 2764804
  1306.6 65.9 %copy-start.44 = (f32[3,200]{1,0:T(4,128)S(1)}, f32[3,200]{1,0:T(4,128)}, u32[]{:S(2)}) copy-start(f32[3,200]{1,0:T(4,128)} %copy-done.43) | copy-start | bytes 7204
  1306.6 65.9 %copy-start.51 = (f32[768]{0:T(1024)S(1)}, f32[768]{0:T(1024)}, u32[]{:S(2)}) copy-start(f32[768]{0:T(1024)} %copy-done.50) | copy-start | bytes 9220
  1306.6 65.9 %copy-start.53 = (f32[3,200]{1,0:T(4,128)S(1)}, f32[3,200]{1,0:T(4,128)}, u32[]{:S(2)}) copy-start(f32[3,200]{1,0:T(4,128)} %copy-done.52) | copy-start | bytes 7204
  1306.6 100.1 %all-reduce.15.cloned.1.call-start = ((), (), s32[]{:S(2)}) async-start(), calls=%async_computation.30 | async-start | bytes 149504 | tf_op jit(solution)/shard_map/psum | solution.py:328
  1307.3 68.2 %copy-start.36 = (bf16[8,3072]{1,0:T(8,128)(2,1)}, bf16[8,3072]{1,0:T(8,128)(2,1)S(1)}, u32[]{:S(2)}) copy-start(bf16[8,3072]{1,0:T(8,128)(2,1)S(1)} %constant_dynamic-update-slice_fusion) | copy-start | bytes 147460
  1310.0 65.4 %copy-start.63 = (bf16[2,768]{1,0:T(2,128)(2,1)}, bf16[2,768]{1,0:T(2,128)(2,1)S(1)}, u32[]{:S(2)}) copy-start(bf16[2,768]{1,0:T(2,128)(2,1)S(1)} %dynamic_update_slice.34) | copy-start | bytes 9220
  1375.5 147.0 %reduce-scatter.41.cloned.1.call-start = ((), (), s32[]{:S(2)}) async-start(), calls=%async_computation.28 | async-start | bytes 442368
  1379.9 161.0 %reduce-scatter.23.cloned.1.call-start = ((), (), s32[]{:S(2)}) async-start(), calls=%async_computation.17 | async-start | bytes 9216000 | tf_op jit(solution)/shard_map/reduce_scatter | solution.py:43
  1380.5 226.6 %reduce-scatter.39.cloned.1.call-start = ((), (), s32[]{:S(2)}) async-start(), calls=%async_computation.27 | async-start | bytes 884736
  1386.3 284.3 %reduce-scatter.37.cloned.1.call-start = ((), (), s32[]{:S(2)}) async-start(), calls=%async_computation.26 | async-start | bytes 442368
  1408.3 325.8 %reduce-scatter.43.cloned.1.call-start = ((), (), s32[]{:S(2)}) async-start(), calls=%async_computation.29 | async-start | bytes 442368
  1440.0 609.8 %reduce-scatter.31.cloned.1.call-start = ((), (), s32[]{:S(2)}) async-start(), calls=%async_computation.23 | async-start | bytes 21233664 | tf_op jit(solution)/shard_map/reduce_scatter | solution.py:220
  1474.9 890.5 %reduce-scatter.35.cloned.1.call-start = ((), (), s32[]{:S(2)}) async-start(), calls=%async_computation.25 | async-start | bytes 21233664 | tf_op jit(solution)/shard_map/reduce_scatter | solution.py:227
  1511.4 926.3 %reduce-scatter.29.cloned.1.call-start = ((), (), s32[]{:S(2)}) async-start(), calls=%async_computation.22 | async-start | bytes 2654208 | tf_op jit(solution)/shard_map/reduce_scatter | solution.py:352
  1521.8 976.5 %reduce-scatter.33.cloned.1.call-start = ((), (), s32[]{:S(2)}) async-start(), calls=%async_computation.24 | async-start | bytes 110592 | tf_op jit(solution)/shard_map/reduce_scatter | solution.py:359
  1524.0 84.8 %copy-start.58 = (bf16[8,3072]{1,0:T(8,128)(2,1)S(1)}, bf16[8,3072]{1,0:T(8,128)(2,1)}, u32[]{:S(2)}) copy-start(bf16[8,3072]{1,0:T(8,128)(2,1)} %get-tuple-element.306) | copy-start | bytes 147460
  (107 other events, 1009.0 us)
Sparse Core Ops, SparseCore 0:
  57.6 28.8 all-gather.9
  172.6 64.4 reduce-scatter.20
  242.2 31.5 all-gather.11
  276.7 138.1 all-gather.13
  417.7 136.2 all-gather.15
  555.5 29.7 all-gather.17
  1166.3 63.6 reduce-scatter.24
  1243.9 29.1 all-gather.19
  1306.7 65.6 reduce-scatter.26
  1376.5 30.1 all-reduce.14
  1410.6 63.0 reduce-scatter.40
  1476.1 64.7 reduce-scatter.22
  1544.5 62.5 reduce-scatter.38
  1610.2 60.3 reduce-scatter.36
  1673.7 60.3 reduce-scatter.42
  1737.9 311.8 reduce-scatter.30
  2053.5 311.9 reduce-scatter.34
  2369.4 68.2 reduce-scatter.28
  2441.5 56.6 reduce-scatter.32
where the time goes:
time: 2510 us; the launch traced here: 2500 us
  waiting for transfers between devices  1290 us (51%)
  local copies, waits for them, and re-layouts  345 us (14%)
  other arithmetic  310 us (12%)
  matrix products  291 us (12%)
  blocking collectives  251 us (10%)
    reduce_scatter x1, waiting for transfers between devices, shards(): lax.psum_scatter(jnp.einsum('nrc,nrf->cnf', picked, hidden_all, preferred...  314 us
    reduce_scatter x1, waiting for transfers between devices, shards(): lax.psum_scatter(jnp.einsum('nrc,nrf->cnf', columns, active_all, preferre...  312 us
    unnamed x23, waiting for transfers between devices  145 us
    reduce_scatter x4, waiting for transfers between devices, scatter_images(): return lax.psum_scatter(values, 'tensor', scatter_dimension=0, tiled=True)  144 us
    all_gather x1, waiting for transfers between devices, shards(): lax.all_gather(down_ready, 'dp', axis=1, tiled=True)  139 us
    scatter-add x8, other arithmetic, expert_forward(): mixture.at[rows_one].add(produced * gates_one[:, None])  113 us
    scatter-add x8, other arithmetic, expert_backward(): pulled.at[rows_one].add(row_grad)  105 us
    unnamed x178, local copies, waits for them, and re-layouts  81.1 us
  transfers between devices with their start and end apart: 19, of which 14 were waited for; matrix products, arithmetic and copies ran while one was open for 21% of the time, Pallas kernels for 0%

commit v1 on v0

v1 whole, which is shorter than its diff:
```python
import jax
import jax.numpy as jnp
from jax import lax
from jax.sharding import Mesh
from jax.sharding import PartitionSpec as P

HD = 64
CAP = 128
GROUP_IMG = 2
CHUNK = 128

EPSILON = 1e-06
NEGATIVE = -1e30
HIGHEST = lax.Precision.HIGHEST
F32 = jnp.float32
BF16 = jnp.bfloat16
PLANE = ("x", "t")
EVERY = ("t", "z", "x")


def norm_forward(values, gains, shifts):
    middle = jnp.mean(values, -1, keepdims=True)
    centred = values - middle
    inverse = lax.rsqrt(jnp.mean(centred * centred, -1, keepdims=True) + EPSILON)
    unit_rows = centred * inverse
    return (unit_rows * gains + shifts, unit_rows, inverse)


def norm_backward(grad_rows, unit_rows, inverse, gains):
    scaled = grad_rows * gains
    return inverse * (
        scaled
        - jnp.mean(scaled, -1, keepdims=True)
        - unit_rows * jnp.mean(scaled * unit_rows, -1, keepdims=True)
    )


def gelu_exact(values):
    return jax.nn.gelu(values, approximate=False)


def dot(left, right, left_dim=1, right_dim=0):
    return lax.dot_general(
        left, right, (((left_dim,), (right_dim,)), ((), ())), preferred_element_type=F32
    )


def gather_line(own, length):
    if length != 4:
        return lax.all_gather(own, "z", axis=1, tiled=True)
    rows = own.shape[1]
    place = lax.axis_index("z")
    inward = lax.ppermute(own, "z", [(0, 1), (3, 2)])
    middle = lax.ppermute(jnp.concatenate([own, inward], 1), "z", [(1, 2), (2, 1)])
    outward = lax.ppermute(jnp.concatenate([own, middle], 1), "z", [(1, 0), (2, 3)])
    inner = (place == 1) | (place == 2)
    near = jnp.where(inner, inward, outward[:, :rows])
    far = jnp.where(inner, middle, outward[:, rows:])
    far_one, far_two = far[:, :rows], far[:, rows:]
    low = jnp.concatenate(
        [
            jnp.where(place == 0, own, near),
            jnp.where(place == 0, near, own),
            far_one,
            far_two,
        ],
        1,
    )
    high = jnp.concatenate(
        [
            far_two,
            far_one,
            jnp.where(place == 2, own, near),
            jnp.where(place == 2, near, own),
        ],
        1,
    )
    return jnp.where(place < 2, low, high)


def scatter_line(full, length):
    if length != 4:
        return lax.psum_scatter(
            full.astype(BF16), "z", scatter_dimension=1, tiled=True
        ).astype(F32)
    rows = full.shape[1] // 4
    place = lax.axis_index("z")
    piece = [full[:, k * rows : (k + 1) * rows] for k in range(4)]
    low = place < 2
    own = jnp.where(
        low,
        jnp.where(place == 0, piece[0], piece[1]),
        jnp.where(place == 2, piece[2], piece[3]),
    )
    near = jnp.where(
        low,
        jnp.where(place == 0, piece[1], piece[0]),
        jnp.where(place == 2, piece[3], piece[2]),
    )
    far_one = jnp.where(low, piece[2], piece[1])
    far_two = jnp.where(low, piece[3], piece[0])
    far = jnp.concatenate([far_one, far_two], 1)
    inward = lax.ppermute(
        jnp.concatenate([near, far], 1).astype(BF16), "z", [(0, 1), (3, 2)]
    )
    middle = lax.ppermute(
        (far + inward[:, rows:].astype(F32)).astype(BF16), "z", [(1, 2), (2, 1)]
    )
    outward = lax.ppermute(
        (near + middle[:, rows:].astype(F32)).astype(BF16), "z", [(1, 0), (2, 3)]
    )
    return (
        own
        + inward[:, :rows].astype(F32)
        + middle[:, :rows].astype(F32)
        + outward.astype(F32)
    )


def shards(
    tokens_in,
    key_mask,
    expert_ids,
    expert_slots,
    norm1_gain,
    norm1_shift,
    qkv_weight,
    qv_bias,
    out_weight,
    out_bias,
    norm2_gain,
    norm2_shift,
    router_weight,
    up_weight,
    up_bias,
    down_weight,
    down_bias,
    out_grad,
):
    length = lax.axis_size("z")
    quarter = lax.axis_size("t")
    core = lax.axis_index("t") % 2
    chip_y = lax.axis_index("t") // 2
    expert = lax.axis_index("x") * quarter + lax.axis_index("t")
    piece, sequence, model = tokens_in.shape
    experts, part, units = up_weight.shape
    dp = model // part
    width = qkv_weight.shape[2]
    heads = width // HD
    tokens = piece * sequence
    chunks = units // CHUNK

    smalls = jnp.concatenate(
        [
            norm1_gain[None],
            norm1_shift[None],
            qv_bias,
            out_bias[None],
            norm2_gain[None],
            norm2_shift[None],
            down_bias,
            router_weight.T,
            up_bias.reshape(experts * quarter, part),
        ],
        0,
    ).astype(BF16)
    small_rows = smalls.shape[0]
    pad = -(small_rows * part) % (16 * model)
    small_block = jnp.pad(smalls.reshape(-1), (0, pad)).reshape(-1, model)
    pack = jnp.concatenate(
        [
            jnp.concatenate(
                [qkv_weight[0], qkv_weight[1], qkv_weight[2], out_weight.T], 1
            ).astype(BF16),
            small_block,
        ],
        0,
    )
    packs = lax.all_gather(pack, EVERY, axis=0, tiled=False)
    packs = packs.reshape(quarter, dp, pack.shape[0], model)
    block = packs[:, :, :part].reshape(quarter, model, model)
    vectors = packs[0, :, part:].reshape(dp, -1)[:, : small_rows * part]
    vectors = vectors.reshape(dp, small_rows, part).transpose(1, 0, 2)
    lines = vectors[: 7 + 2 * experts].reshape(-1, model).astype(F32)
    gain_one, shift_one, bias_q, bias_v, bias_out, gain_two, shift_two = [
        lines[k] for k in range(7)
    ]
    bias_down = lines[7 : 7 + experts]
    router = lines[7 + experts :].astype(BF16)
    bias_up = vectors[7 + 2 * experts :].reshape(experts, quarter, dp, part)
    bias_up = bias_up.transpose(0, 2, 1, 3).reshape(experts, quarter, chunks, CHUNK)
    bias_up = lax.dynamic_index_in_dim(bias_up, expert, 0, keepdims=False)
    bias_up = bias_up.transpose(1, 0, 2).reshape(chunks, quarter * CHUNK).astype(F32)

    weights = jnp.stack(
        [up_weight.astype(BF16), down_weight.astype(BF16).transpose(0, 2, 1)], 1
    )
    parts = []
    for first, last in ((0, 1), (1, 3), (3, 6)):
        if first >= chunks:
            continue
        last = min(last, chunks) if last < 6 else chunks
        some = lax.all_to_all(
            weights[:, :, :, first * CHUNK : last * CHUNK], PLANE, 0, 0, tiled=True
        )
        some = some.reshape(2, quarter, 2, part, last - first, CHUNK)
        some = some.transpose(4, 2, 0, 3, 1, 5)
        some = some.reshape(last - first, 2, 2 * part, quarter * CHUNK)
        parts += [some[k] for k in range(last - first)]

    first_group = chip_y * 3
    group_tokens = GROUP_IMG * sequence
    position = (expert_ids * CAP + expert_slots).reshape(-1, group_tokens, 2)
    position_full = lax.dynamic_index_in_dim(position, first_group + 2 * core, 0, keepdims=False)
    position_half = lax.dynamic_index_in_dim(position, first_group + 1, 0, keepdims=False)
    slots_full = jnp.arange(experts * CAP, dtype=jnp.int32)
    half = CAP // 2
    slots_half = (
        jnp.arange(experts, dtype=jnp.int32)[:, None] * CAP
        + core * half
        + jnp.arange(half, dtype=jnp.int32)
    ).reshape(-1)
    match_full = slots_full[:, None, None] == position_full.T[None]
    match_half = slots_half[:, None, None] == position_half.T[None]
    hot_full = (match_full[:, 0] | match_full[:, 1]).astype(BF16)
    hot_half = (match_half[:, 0] | match_half[:, 1]).astype(BF16)
    swap = [(k, k ^ 1) for k in range(quarter)]

    def both_groups(values):
        lent = jnp.where(core == 0, values[2], values[0])
        other = lax.ppermute(lent, "t", swap)
        full = jnp.where(core == 0, values[:2], values[1:])
        shared = jnp.where(
            core == 0, jnp.stack([lent, other]), jnp.stack([other, lent])
        )
        return (
            full.reshape(group_tokens, -1),
            shared.reshape(group_tokens, -1),
        )

    def join_rows(full, shared):
        full = full.reshape((experts, CAP) + full.shape[1:])
        shared = shared.reshape((experts, half) + shared.shape[1:])
        return jnp.concatenate([full, shared], 1)

    def dispatch(full, shared):
        rows = join_rows(dot(hot_full, full).astype(BF16), dot(hot_half, shared).astype(BF16))
        return lax.all_to_all(rows, PLANE, 0, 0, tiled=True).reshape(-1, model)

    def combine(rows):
        back = lax.all_to_all(
            rows.reshape(experts, CAP + half, model), PLANE, 0, 0, tiled=True
        )
        full = dot(hot_full, back[:, :CAP].reshape(-1, model), 0, 0)
        shared = dot(hot_half, back[:, CAP:].reshape(-1, model), 0, 0)
        full = full.reshape(GROUP_IMG, sequence, model)
        shared = shared.reshape(GROUP_IMG, sequence, model)
        mine = jnp.where(core == 0, shared[0], shared[1])
        theirs = jnp.where(core == 0, shared[1], shared[0])
        mine = mine + lax.ppermute(theirs, "t", swap)
        return jnp.where(
            core == 0,
            jnp.concatenate([full, mine[None]]),
            jnp.concatenate([mine[None], full]),
        ).reshape(tokens, model)

    grad_full, grad_shared = both_groups(out_grad)
    incoming = dispatch(grad_full, grad_shared)

    local_start = lax.axis_index("t") * piece
    mask_here = lax.dynamic_slice_in_dim(key_mask, local_start, piece, 0)
    inputs = tokens_in.reshape(tokens, model).astype(F32)
    normed_one, unit_one, inverse_one = norm_forward(inputs, gain_one, shift_one)
    normed_one = normed_one.astype(BF16)
    projected = jnp.einsum(
        "sd,tdk->tsk", normed_one, block[:, :, : 3 * width], preferred_element_type=F32
    )
    shape_heads = (quarter, piece, sequence, heads, HD)

    def to_heads(values):
        return values.astype(BF16).reshape(shape_heads)

    queries = to_heads(projected[..., :width] + bias_q.reshape(quarter, 1, width))
    key_rows = to_heads(projected[..., width : 2 * width])
    value_rows = to_heads(projected[..., 2 * width :] + bias_v.reshape(quarter, 1, width))

    def scores_of():
        scores = jnp.einsum(
            "tbihc,tbjhc->tbhij", queries, key_rows, preferred_element_type=F32
        ) * HD ** (-0.5)
        return jnp.where(mask_here[None, :, None, None, :] > 0, scores, NEGATIVE)

    masked = scores_of()
    largest = jnp.max(masked, -1, keepdims=True)
    log_total = largest + jnp.log(jnp.sum(jnp.exp(masked - largest), -1, keepdims=True))
    chances = jnp.exp(masked - log_total)
    chances_low = chances.astype(BF16)
    attended = jnp.einsum(
        "tbhij,tbjhc->tbihc", chances_low, value_rows, preferred_element_type=F32
    )
    attended = attended.astype(BF16).reshape(quarter, tokens, width)
    out_rows = block[:, :, 3 * width :]
    attention_out = jnp.einsum("tsk,tdk->sd", attended, out_rows, preferred_element_type=F32)
    residual = inputs + attention_out + bias_out
    normed_two, unit_two, inverse_two = norm_forward(residual, gain_two, shift_two)
    normed_two = normed_two.astype(BF16)

    normed_full, normed_shared = both_groups(normed_two.reshape(piece, sequence, model))

    def chances_of(rows):
        return jax.nn.softmax(dot(rows, router, 1, 1), -1)

    probabilities = chances_of(normed_two)
    hot_ids = expert_ids[..., None] == jnp.arange(experts, dtype=jnp.int32)
    hot_here = lax.dynamic_slice_in_dim(hot_ids, local_start, piece, 0).astype(F32)
    hot_here = hot_here.reshape(tokens, 2, experts)
    share_here = jnp.sum(hot_here, 1) * probabilities

    def slot_gates(match, rows, position_here):
        chance = chances_of(rows)
        hot = (position_here // CAP)[..., None] == jnp.arange(experts, dtype=jnp.int32)
        gates = jnp.sum(hot.astype(F32) * chance[:, None], -1)
        return jnp.sum(jnp.where(match, gates.T[None], 0.0), (1, 2))

    gates_sent = join_rows(
        slot_gates(match_full, normed_full, position_full),
        slot_gates(match_half, normed_shared, position_half),
    )
    chosen = dispatch(normed_full, normed_shared)
    slot_gate = lax.all_to_all(gates_sent, PLANE, 0, 0, tiled=True).reshape(-1, 1)

    incoming_f = incoming.astype(F32)
    out_part = (incoming_f * slot_gate).astype(BF16)
    produced = jnp.zeros((chosen.shape[0], model), F32)
    pulled = jnp.zeros((chosen.shape[0], model), F32)
    bias_parts = []
    reduced = []
    for k in range(chunks):
        both = gather_line(parts[k], length)
        up_one, down_one = both[0], both[1]
        hidden = dot(chosen, up_one) + bias_up[k]
        active, pull_gelu = jax.vjp(gelu_exact, hidden)
        active = active.astype(BF16)
        produced = produced + dot(active, down_one, 1, 1)
        hidden_grad = pull_gelu(dot(out_part, down_one))[0].astype(BF16)
        pulled = pulled + dot(hidden_grad, up_one, 1, 1)
        bias_parts.append(jnp.sum(hidden_grad.astype(F32), 0))
        weight_grads = jnp.stack([dot(chosen, hidden_grad, 0, 0), dot(out_part, active, 0, 0)])
        reduced.append(scatter_line(weight_grads, length).astype(BF16))

    gate_part = jnp.sum(incoming_f * produced, -1)
    gate_back = lax.all_to_all(
        gate_part.reshape(experts, CAP + half), PLANE, 0, 0, tiled=True
    )
    norm_two_grad = combine(pulled.astype(BF16))
    mixture = combine((produced * slot_gate).astype(BF16))

    def slots_to_tokens(match, parts_here):
        parts_here = parts_here.reshape(experts, -1)
        match = (match[:, 0] | match[:, 1]).reshape(experts, -1, group_tokens)
        return jnp.sum(jnp.where(match, parts_here[..., None], 0.0), 1).T

    prob_full = slots_to_tokens(match_full, gate_back[:, :CAP])
    prob_shared = slots_to_tokens(match_half, gate_back[:, CAP:])
    prob_full = prob_full.reshape(GROUP_IMG, sequence, experts)
    prob_shared = prob_shared.reshape(GROUP_IMG, sequence, experts)
    mine = jnp.where(core == 0, prob_shared[0], prob_shared[1])
    theirs = jnp.where(core == 0, prob_shared[1], prob_shared[0])
    mine = mine + lax.ppermute(theirs, "t", swap)
    chance_grad = jnp.where(
        core == 0,
        jnp.concatenate([prob_full, mine[None]]),
        jnp.concatenate([mine[None], prob_full]),
    ).reshape(tokens, experts)
    grad_rows = out_grad.reshape(tokens, model)
    bias_dot = dot(grad_rows, bias_down.astype(BF16), 1, 1)
    chance_grad = chance_grad + jnp.sum(hot_here, 1) * bias_dot
    logit_grad = probabilities * (
        chance_grad - jnp.sum(probabilities * chance_grad, -1, keepdims=True)
    )
    logit_grad = logit_grad.astype(BF16)
    router_grad = dot(logit_grad, normed_two, 0, 0)
    bias_term = jnp.dot(share_here, bias_down, precision=HIGHEST)
    output = (residual + mixture + bias_term).astype(BF16).reshape(tokens_in.shape)

    grad_f = grad_rows.astype(F32)
    norm_two_grad = norm_two_grad + dot(logit_grad, router)
    down_bias_grad = lax.dot_general(
        share_here, grad_f, (((0,), (0,)), ((), ())), precision=HIGHEST
    )
    gain_two_grad = jnp.sum(norm_two_grad * unit_two, 0)
    shift_two_grad = jnp.sum(norm_two_grad, 0)
    residual_grad = grad_f + norm_backward(norm_two_grad, unit_two, inverse_two, gain_two)
    out_bias_grad = jnp.sum(residual_grad, 0)
    residual_low = residual_grad.astype(BF16)
    out_rows_grad = jnp.einsum(
        "sd,tsk->tdk", residual_low, attended, preferred_element_type=F32
    )
    attended_grad = jnp.einsum(
        "sd,tdk->tsk", residual_low, out_rows, preferred_element_type=F32
    )
    attended_grad = to_heads(attended_grad)
    value_grad = jnp.einsum(
        "tbhij,tbihc->tbjhc", chances_low, attended_grad, preferred_element_type=F32
    ).astype(BF16)
    weight_grad = jnp.einsum(
        "tbihc,tbjhc->tbhij", attended_grad, value_rows, preferred_element_type=F32
    )
    score_grad = chances * (
        weight_grad - jnp.sum(chances * weight_grad, -1, keepdims=True)
    )
    score_grad = score_grad.astype(BF16)
    scale = HD ** (-0.5)
    query_grad = (
        jnp.einsum("tbhij,tbjhc->tbihc", score_grad, key_rows, preferred_element_type=F32)
        * scale
    ).astype(BF16)
    key_grad = (
        jnp.einsum("tbhij,tbihc->tbjhc", score_grad, queries, preferred_element_type=F32)
        * scale
    ).astype(BF16)
    joined_grad = jnp.concatenate(
        [v.reshape(quarter, tokens, width) for v in (query_grad, key_grad, value_grad)], -1
    )
    qkv_grad = jnp.einsum(
        "sd,tsk->tdk", normed_one, joined_grad, preferred_element_type=F32
    )
    query_bias_grad = jnp.sum(query_grad.astype(F32), (1, 2)).reshape(model)
    value_bias_grad = jnp.sum(value_grad.astype(F32), (1, 2)).reshape(model)
    norm_one_grad = jnp.einsum(
        "tsk,tdk->sd", joined_grad, block[:, :, : 3 * width], preferred_element_type=F32
    )
    gain_one_grad = jnp.sum(norm_one_grad * unit_one, 0)
    shift_one_grad = jnp.sum(norm_one_grad, 0)
    input_grad = residual_grad + norm_backward(
        norm_one_grad, unit_one, inverse_one, gain_one
    )

    bias_rows = jnp.stack(bias_parts).reshape(chunks, quarter, CHUNK)
    bias_rows = bias_rows.transpose(1, 0, 2).reshape(dp, quarter, part)
    bias_rows = jnp.where(
        jnp.arange(experts)[:, None, None, None] == expert, bias_rows[None], 0.0
    )
    bias_rows = bias_rows.transpose(0, 2, 1, 3).reshape(experts * quarter, dp, part)
    line_grads = jnp.concatenate(
        [
            jnp.stack(
                [
                    gain_one_grad,
                    shift_one_grad,
                    query_bias_grad,
                    value_bias_grad,
                    out_bias_grad,
                    gain_two_grad,
                    shift_two_grad,
                ]
            ),
            down_bias_grad,
            router_grad,
        ],
        0,
    ).reshape(-1, dp, part)
    vector_grads = jnp.concatenate([line_grads, bias_rows], 0).astype(BF16)
    vector_grads = vector_grads.transpose(1, 0, 2).reshape(dp, small_rows * part)
    vector_grads = jnp.pad(vector_grads, ((0, 0), (0, pad))).reshape(dp, -1, model)
    pack_grads = jnp.concatenate(
        [
            jnp.concatenate([qkv_grad, out_rows_grad], -1)
            .astype(BF16)
            .reshape(quarter, dp, part, model),
            jnp.broadcast_to(vector_grads[None], (quarter,) + vector_grads.shape),
        ],
        2,
    )
    pack_grads = pack_grads.reshape((quarter * dp,) + pack_grads.shape[2:])
    pack_grad = lax.psum_scatter(pack_grads, EVERY, scatter_dimension=0, tiled=False)
    pack_grad = pack_grad.astype(F32)
    qkv_out = pack_grad[:part, : 3 * width].reshape(part, 3, width).transpose(1, 0, 2)
    out_weight_grad = pack_grad[:part, 3 * width :].T
    small_grads = pack_grad[part:].reshape(-1)[: small_rows * part].reshape(small_rows, part)

    ups, downs = [], []
    for first, last in ((0, 2), (2, 4), (4, 6)):
        if first >= chunks:
            continue
        last = min(last, chunks) if last < 6 else chunks
        some = jnp.stack(reduced[first:last])
        some = some.reshape(last - first, 2, 2, part, quarter, CHUNK)
        some = some.transpose(2, 4, 1, 3, 0, 5).reshape(experts, 2, part, -1)
        some = lax.all_to_all(some, PLANE, 0, 0, tiled=True).astype(F32)
        ups.append(some[:, 0])
        downs.append(some[:, 1])
    up_grad = jnp.concatenate(ups, -1)
    down_grad = jnp.concatenate(downs, -1).transpose(0, 2, 1)
    return (
        output,
        input_grad.reshape(tokens_in.shape),
        small_grads[0],
        small_grads[1],
        qkv_out,
        small_grads[2:4],
        out_weight_grad,
        small_grads[4],
        small_grads[5],
        small_grads[6],
        small_grads[7 + experts : 7 + 2 * experts].T,
        up_grad,
        small_grads[7 + 2 * experts :].reshape(experts, -1),
        down_grad,
        small_grads[7 : 7 + experts],
    )


def solution(mesh):
    dp, tensor = mesh.devices.shape
    planes = Mesh(mesh.devices.reshape(dp // 2, 2, tensor), ("z", "x", "t"))
    rows = ("z", "x")
    images = P(("z", "x", "t"), None, None)
    return jax.shard_map(
        shards,
        mesh=planes,
        in_specs=(
            images,
            P(rows, None),
            P(rows, None, None),
            P(rows, None, None),
            P(rows),
            P(rows),
            P(None, rows, "t"),
            P(None, rows),
            P("t", rows),
            P(rows),
            P(rows),
            P(rows),
            P(rows, None),
            P(None, rows, "t"),
            P(None, rows),
            P(None, "t", rows),
            P(None, rows),
            images,
        ),
        out_specs=(
            images,
            images,
            P(rows),
            P(rows),
            P(None, rows, "t"),
            P(None, rows),
            P("t", rows),
            P(rows),
            P(rows),
            P(rows),
            P(rows, None),
            P(None, rows, "t"),
            P(None, rows),
            P(None, "t", rows),
            P(None, rows),
        ),
        check_vma=False,
    )
```

time: 2510 us -> 983 us (0.39)
  waiting for transfers between devices: 1290 us -> 263 us
  blocking collectives: 251 us -> 0 us
  local copies, waits for them, and re-layouts: 345 us -> 146 us
  other arithmetic: 310 us -> 188 us
  starting transfers between devices: 1.36 us -> 123 us
  matrix products: 291 us -> 231 us
    reduce_scatter x8 -> x1, waiting for transfers between devices: 899 us -> 22 us  [shards(): lax.psum_scatter(pack_grads, EVERY, scatter_dimension=0, tiled=False)]
    all_gather x6 -> x1, waiting for transfers between devices: 226 us -> 0.01 us  [shards(): packs = lax.all_gather(pack, EVERY, axis=0, tiled=False)]
    scatter-add x16 -> x0, other arithmetic: 218 us -> none  [the longest x8 113 us: expert_forward(): mixture.at[rows_one].add(produced * gates_one[:, None])]
    ppermute x0 -> x41, waiting for transfers between devices: none -> 203 us  [the longest x6 121 us: gather_line(): lax.ppermute(jnp.concatenate([own, middle], 1), 'z', [(1, 0), (2, 3)])]
    all_gather x6 -> x0, blocking collectives: 166 us -> none  [the longest x1 33.2 us: shards(): lax.all_gather(out_weight.astype(jnp.bfloat16), 'dp', axis=1, tiled=True)]
    gather x20 -> x0, local copies, waits for them, and re-layouts: 156 us -> none  [the longest x8 46.8 us: expert_forward(): chosen = jnp.take(flat_two, rows_one, 0)]
    unnamed x23 -> x2, waiting for transfers between devices: 145 us -> 0.03 us
    unnamed x2 -> x0, blocking collectives: 73.9 us -> none
  transfers between devices with their start and end apart: 19 -> 55, of which waited for: 14 -> 17; matrix products, arithmetic and copies ran while one was open for 21% -> 39% of each run, Pallas kernels for 0% -> 0%
where the time goes in v1:
time: 983 us; the launch traced here: 969 us
  waiting for transfers between devices  263 us (27%)
  matrix products  231 us (23%)
  other arithmetic  188 us (19%)
  local copies, waits for them, and re-layouts  146 us (15%)
  starting transfers between devices  123 us (13%)
  between operations  17.5 us (2%)
    dot_general x50, matrix products, dot(): lax.dot_general(left, right, (((left_dim,), (right_dim,)), ((), ())), pre...  177 us
    ppermute x6, waiting for transfers between devices, gather_line(): lax.ppermute(jnp.concatenate([own, middle], 1), 'z', [(1, 0), (2, 3)])  121 us
    ppermute x6, waiting for transfers between devices, scatter_line(): lax.ppermute(jnp.concatenate([near, far], 1).astype(BF16), 'z', [(0, 1),...  80.5 us
    another operation x17, other arithmetic  24.5 us
    reduce_scatter x1, waiting for transfers between devices, shards(): lax.psum_scatter(pack_grads, EVERY, scatter_dimension=0, tiled=False)  22 us
    unnamed x397, local copies, waits for them, and re-layouts  20.8 us
  transfers between devices with their start and end apart: 55, of which 17 were waited for; matrix products, arithmetic and copies ran while one was open for 39% of the time, Pallas kernels for 0%

profile of v1, /device:TPU:0, one launch (start us, length us, event | category | flops | bytes accessed | tf_op | source)
XLA Modules:
  0.0 968.9 jit_solution(6620073212696320179)
XLA Ops:
  20.7 4.8 all-to-all-start.1
  44.4 7.4 all-to-all-done.2
  85.7 5.8 fusion.178
  94.0 6.3 collective-permute-start.10
  155.7 9.7 collective-permute-done.3
  169.5 46.4 %collective-permute-done.6 = bf16[2,576,512]{2,1,0:T(8,128)(2,1)S(1)} collective-permute-done((bf16[2,576,512]{2,1,0:T(8,128)(2,1)S(1)}, bf16[2,576,512]{2,1,0:T(8,128)(2,1)S(1)}, u32[]{:S(2)}, u32[]{:S(2)}) %collective-permute-start.6) | collective-permute-done | bytes 1179680 | tf_op jit(solution)/shard_map/ppermute | solution.py:55
  221.0 20.1 %collective-permute-done.12 = bf16[2,576,512]{2,1,0:T(8,128)(2,1)S(1)} collective-permute-done((bf16[2,576,512]{2,1,0:T(8,128)(2,1)S(1)}, bf16[2,576,512]{2,1,0:T(8,128)(2,1)S(1)}, u32[]{:S(2)}, u32[]{:S(2)}) %collective-permute-start.12) | collective-permute-done | bytes 1179680 | tf_op jit(solution)/shard_map/ppermute | solution.py:55
  241.1 25.3 %collective-permute-done.15 = bf16[2,576,512]{2,1,0:T(8,128)(2,1)S(1)} collective-permute-done((bf16[2,576,512]{2,1,0:T(8,128)(2,1)S(1)}, bf16[2,576,512]{2,1,0:T(8,128)(2,1)S(1)}, u32[]{:S(2)}, u32[]{:S(2)}) %collective-permute-start.15) | collective-permute-done | bytes 1179680 | tf_op jit(solution)/shard_map/ppermute | solution.py:55
  267.6 20.0 %collective-permute-done.18 = bf16[2,576,512]{2,1,0:T(8,128)(2,1)S(1)} collective-permute-done((bf16[2,576,512]{2,1,0:T(8,128)(2,1)S(1)}, bf16[2,576,512]{2,1,0:T(8,128)(2,1)S(1)}, u32[]{:S(2)}, u32[]{:S(2)}) %collective-permute-start.18) | collective-permute-done | bytes 1179680 | tf_op jit(solution)/shard_map/ppermute | solution.py:55
  294.2 5.0 slice.740
  317.2 5.4 fusion.45
  386.8 13.5 %all-to-all-done = bf16[8,192,768]{2,1,0:T(8,128)(2,1)} async-done(((bf16[8,192,768]{2,1,0:T(8,128)(2,1)}), bf16[8,192,768]{2,1,0:T(8,128)(2,1)}, u32[]{:S(2)}, u32[]{:S(2)}) %all-to-all-start) | async-done | bytes 2359328 | tf_op jit(solution)/shard_map/all_to_all | solution.py:248
  400.3 10.2 %multiply_convert_fusion.3 = (bf16[1536,512]{1,0:T(8,128)(2,1)}, f32[1536,512]{1,0:T(8,128)S(1)}, f32[1536,512]{1,0:T(8,128)S(1)}) fusion(f32[512]{0:T(512)S(1)} %bitcast.575, bf16[1536,768]{1,0:T(8,128)(2,1)} %bitcast.29, bf16[2,768,512]{2,1,0:T(8,128)(2,1)S(1)} %copy-done.49), kind=kOutput, calls=%fused_computation.103 | convolution fusion | flops 1259864064 | bytes 11012096 | tf_op jit(solution)/shard_map/dot_general | solution.py:43
  421.5 10.4 %multiply_convert_fusion.4 = (bf16[1536,512]{1,0:T(8,128)(2,1)}, f32[1536,512]{1,0:T(8,128)S(1)}, f32[1536,512]{1,0:T(8,128)S(1)}) fusion(f32[512]{0:T(512)S(1)} %bitcast.574, bf16[1536,768]{1,0:T(8,128)(2,1)} %bitcast.29, bf16[2,768,512]{2,1,0:T(8,128)(2,1)S(1)} %copy-done.51), kind=kOutput, calls=%fused_computation.116 | convolution fusion | flops 1259864064 | bytes 11012096 | tf_op jit(solution)/shard_map/dot_general | solution.py:43
  442.9 9.4 multiply_convert_fusion.5
  463.3 9.4 multiply_convert_fusion.6
  483.1 9.6 multiply_convert_fusion.7
  515.3 11.3 %multiply_convert_fusion.2 = (bf16[1536,512]{1,0:T(8,128)(2,1)}, f32[1536,512]{1,0:T(8,128)}, f32[1536,512]{1,0:T(8,128)}) fusion(f32[512]{0:T(512)S(1)} %bitcast.567, bf16[1536,768]{1,0:T(8,128)(2,1)} %bitcast.29, bf16[2,768,512]{2,1,0:T(8,128)(2,1)S(1)} %copy-done.45), kind=kOutput, calls=%fused_computation.90 | convolution fusion | flops 1259864064 | bytes 11012096 | tf_op jit(solution)/shard_map/dot_general | solution.py:43
  526.6 9.7 %fusion.2 = (f32[1536]{0:T(1024)S(1)}, bf16[1536,768]{1,0:T(8,128)(2,1)}, bf16[1536,768]{1,0:T(8,128)(2,1)}) fusion(bf16[8,192,768]{2,1,0:T(8,128)(2,1)} %all-to-all-done.6, f32[1536]{0:T(1024)S(1)} %copy-done.159, bf16[1536,512]{1,0:T(8,128)(2,1)} %get-tuple-element.136, bf16[2,768,512]{2,1,0:T(8,128)(2,1)} %maximum_select_fusion.7, ...), kind=kOutput, calls=%fused_computation.17 | convolution fusion | flops 1222113792 | bytes 33042432 | tf_op jit(solution)/shard_map/dot_general | solution.py:43
  574.5 5.6 collective-permute-start.38
  609.6 6.3 add_convert_fusion
  640.1 16.2 %collective-permute-done.32 = bf16[2,576,512]{2,1,0:T(8,128)(2,1)} collective-permute-done((bf16[2,576,512]{2,1,0:T(8,128)(2,1)}, bf16[2,576,512]{2,1,0:T(8,128)(2,1)}, u32[]{:S(2)}, u32[]{:S(2)}) %collective-permute-start.32) | collective-permute-done | bytes 1179680 | tf_op jit(solution)/shard_map/ppermute | solution.py:103
  659.4 22.1 %collective-permute-done.29 = bf16[2,576,512]{2,1,0:T(8,128)(2,1)} collective-permute-done((bf16[2,576,512]{2,1,0:T(8,128)(2,1)}, bf16[2,576,512]{2,1,0:T(8,128)(2,1)}, u32[]{:S(2)}, u32[]{:S(2)}) %collective-permute-start.29) | collective-permute-done | bytes 1179680 | tf_op jit(solution)/shard_map/ppermute | solution.py:103
  685.5 21.3 %collective-permute-done.26 = bf16[2,576,512]{2,1,0:T(8,128)(2,1)} collective-permute-done((bf16[2,576,512]{2,1,0:T(8,128)(2,1)}, bf16[2,576,512]{2,1,0:T(8,128)(2,1)}, u32[]{:S(2)}, u32[]{:S(2)}) %collective-permute-start.26) | collective-permute-done | bytes 1179680 | tf_op jit(solution)/shard_map/ppermute | solution.py:103
  710.7 20.9 %collective-permute-done.23 = bf16[2,576,512]{2,1,0:T(8,128)(2,1)S(1)} collective-permute-done((bf16[2,576,512]{2,1,0:T(8,128)(2,1)}, bf16[2,576,512]{2,1,0:T(8,128)(2,1)S(1)}, u32[]{:S(2)}, u32[]{:S(2)}) %collective-permute-start.23) | collective-permute-done | bytes 1179680 | tf_op jit(solution)/shard_map/ppermute | solution.py:103
  762.5 5.2 fusion.194
  767.7 5.2 multiply_reduce_fusion
  794.9 7.2 bitcast_reduce_fusion
  812.6 6.0 copy.258
  818.6 7.2 pad_maximum_fusion
  918.2 10.6 %all-to-all-done.10 = bf16[8,2,96,256]{3,2,1,0:T(8,128)(2,1)} async-done(((bf16[8,2,96,256]{3,2,1,0:T(8,128)(2,1)}), bf16[8,2,96,256]{3,2,1,0:T(8,128)(2,1)}, u32[]{:S(2)}, u32[]{:S(2)}) %all-to-all-start.10) | async-done | bytes 786464 | tf_op jit(solution)/shard_map/all_to_all | solution.py:490
  933.5 22.0 %reduce-scatter.2.cloned.1.call-done = bf16[1,112,768]{2,1,0:T(8,128)(2,1)} async-done(((bf16[32,112,768]{2,1,0:T(8,128)(2,1)}), bf16[1,112,768]{2,1,0:T(8,128)(2,1)}) %reduce-scatter.2.cloned.1.call-update) | async-done | bytes 172048 | tf_op jit(solution)/shard_map/reduce_scatter | solution.py:476
  (838 shorter events, 556.1 us)
Async XLA Ops:
  7.2 286.1 %all-gather.3.cloned.1.call-start = ((), (), s32[]{:S(2)}) async-start(), calls=%async_computation.14 | async-start | bytes 5677056 | tf_op jit(solution)/shard_map/all_gather | solution.py:179
  17.4 95.5 %collective-permute-start.20 = (bf16[200,768]{1,0:T(8,128)(2,1)}, bf16[200,768]{1,0:T(8,128)(2,1)}, u32[]{:S(2)}, u32[]{:S(2)}) collective-permute-start(bf16[200,768]{1,0:T(8,128)(2,1)} %fusion.275), channel_id=1, source_target_pairs={{0,1},{1,0},{2,3},{3,2},{4,5},{5,4},{6,7},{7,6},{8,9},{9,8},{10,11... | collective-permute-start | bytes 921608 | tf_op jit(solution)/shard_map/ppermute | solution.py:231
  73.1 35.7 %collective-permute-start.7 = (bf16[2,192,512]{2,1,0:T(8,128)(2,1)S(1)}, bf16[2,192,512]{2,1,0:T(8,128)(2,1)}, u32[]{:S(2)}, u32[]{:S(2)}) collective-permute-start(bf16[2,192,512]{2,1,0:T(8,128)(2,1)S(1)} %squeeze.129), channel_id=1, source_target_pairs={{0,8},{24,16},{1,9},{25,17},{2,10},{26,18},{3,11},{27,19},{4,12},{... | collective-permute-start | bytes 1179656 | tf_op jit(solution)/shard_map/ppermute | solution.py:53
  75.2 44.0 %collective-permute-start.4 = (bf16[2,192,512]{2,1,0:T(8,128)(2,1)S(1)}, bf16[2,192,512]{2,1,0:T(8,128)(2,1)}, u32[]{:S(2)}, u32[]{:S(2)}) collective-permute-start(bf16[2,192,512]{2,1,0:T(8,128)(2,1)S(1)} %squeeze.126), channel_id=1, source_target_pairs={{0,8},{24,16},{1,9},{25,17},{2,10},{26,18},{3,11},{27,19},{4,12},{... | collective-permute-start | bytes 1179656 | tf_op jit(solution)/shard_map/ppermute | solution.py:53
  80.0 50.0 %collective-permute-start.2 = (bf16[2,384,512]{2,1,0:T(8,128)(2,1)}, bf16[2,384,512]{2,1,0:T(8,128)(2,1)}, u32[]{:S(2)}, u32[]{:S(2)}) collective-permute-start(bf16[2,384,512]{2,1,0:T(8,128)(2,1)} %pad_maximum_fusion.24), channel_id=1, source_target_pairs={{8,16},{16,8},{9,17},{17,9},{10,18},{18,10},{11,19},{19,11},{12,20... | collective-permute-start | bytes 2359304 | tf_op jit(solution)/shard_map/ppermute | solution.py:54
  140.0 218.8 %all-to-all-start.6 = ((bf16[8,192,768]{2,1,0:T(8,128)(2,1)}), bf16[8,192,768]{2,1,0:T(8,128)(2,1)}, u32[]{:S(2)}, u32[]{:S(2)}) async-start(bf16[8,192,768]{2,1,0:T(8,128)(2,1)} %pad_maximum_fusion.2), calls=%async_computation.6 | async-start | bytes 4718592 | tf_op jit(solution)/shard_map/all_to_all | solution.py:248
  145.6 70.5 %collective-permute-start.9 = (bf16[2,576,512]{2,1,0:T(8,128)(2,1)S(1)}, bf16[2,576,512]{2,1,0:T(8,128)(2,1)S(1)}, u32[]{:S(2)}, u32[]{:S(2)}) collective-permute-start(bf16[2,576,512]{2,1,0:T(8,128)(2,1)S(1)} %pad_maximum_fusion.7), channel_id=1, source_target_pairs={{8,0},{16,24},{9,1},{17,25},{10,2},{18,26},{11,3},{19,27},{12,4},{... | collective-permute-start | bytes 3538952 | tf_op jit(solution)/shard_map/ppermute | solution.py:55
  148.2 67.7 %collective-permute-start.6 = (bf16[2,576,512]{2,1,0:T(8,128)(2,1)S(1)}, bf16[2,576,512]{2,1,0:T(8,128)(2,1)S(1)}, u32[]{:S(2)}, u32[]{:S(2)}) collective-permute-start(bf16[2,576,512]{2,1,0:T(8,128)(2,1)S(1)} %pad_maximum_fusion.6), channel_id=1, source_target_pairs={{8,0},{16,24},{9,1},{17,25},{10,2},{18,26},{11,3},{19,27},{12,4},{... | collective-permute-start | bytes 3538952 | tf_op jit(solution)/shard_map/ppermute | solution.py:55
  150.7 90.4 %collective-permute-start.12 = (bf16[2,576,512]{2,1,0:T(8,128)(2,1)S(1)}, bf16[2,576,512]{2,1,0:T(8,128)(2,1)S(1)}, u32[]{:S(2)}, u32[]{:S(2)}) collective-permute-start(bf16[2,576,512]{2,1,0:T(8,128)(2,1)S(1)} %pad_maximum_fusion.8), channel_id=1, source_target_pairs={{8,0},{16,24},{9,1},{17,25},{10,2},{18,26},{11,3},{19,27},{12,4},{... | collective-permute-start | bytes 3538952 | tf_op jit(solution)/shard_map/ppermute | solution.py:55
  153.2 113.2 %collective-permute-start.15 = (bf16[2,576,512]{2,1,0:T(8,128)(2,1)S(1)}, bf16[2,576,512]{2,1,0:T(8,128)(2,1)S(1)}, u32[]{:S(2)}, u32[]{:S(2)}) collective-permute-start(bf16[2,576,512]{2,1,0:T(8,128)(2,1)S(1)} %pad_maximum_fusion.9), channel_id=1, source_target_pairs={{8,0},{16,24},{9,1},{17,25},{10,2},{18,26},{11,3},{19,27},{12,4},{... | collective-permute-start | bytes 3538952 | tf_op jit(solution)/shard_map/ppermute | solution.py:55
  165.4 122.2 %collective-permute-start.18 = (bf16[2,576,512]{2,1,0:T(8,128)(2,1)S(1)}, bf16[2,576,512]{2,1,0:T(8,128)(2,1)S(1)}, u32[]{:S(2)}, u32[]{:S(2)}) collective-permute-start(bf16[2,576,512]{2,1,0:T(8,128)(2,1)S(1)} %pad_maximum_fusion.10), channel_id=1, source_target_pairs={{8,0},{16,24},{9,1},{17,25},{10,2},{18,26},{11,3},{19,27},{12,4},{... | collective-permute-start | bytes 3538952 | tf_op jit(solution)/shard_map/ppermute | solution.py:55
  563.5 54.7 %all-to-all-start.8 = ((f32[8,1,192]{2,1,0:T(1,128)}), f32[8,1,192]{2,1,0:T(1,128)S(1)}, u32[]{:S(2)}, u32[]{:S(2)}) async-start(f32[8,1,192]{2,1,0:T(1,128)} %all_to_all.53), calls=%async_computation.8 | async-start | bytes 16384 | tf_op jit(solution)/shard_map/all_to_all | solution.py:352
  574.5 57.7 %collective-permute-start.38 = (bf16[2,576,512]{2,1,0:T(8,128)(2,1)}, bf16[2,576,512]{2,1,0:T(8,128)(2,1)}, u32[]{:S(2)}, u32[]{:S(2)}) collective-permute-start(bf16[2,576,512]{2,1,0:T(8,128)(2,1)} %pad_maximum_fusion.16), channel_id=1, source_target_pairs={{0,8},{24,16},{1,9},{25,17},{2,10},{26,18},{3,11},{27,19},{4,12},{... | collective-permute-start | bytes 3538952 | tf_op jit(solution)/shard_map/ppermute | solution.py:103
  584.2 51.9 %collective-permute-start.35 = (bf16[2,576,512]{2,1,0:T(8,128)(2,1)}, bf16[2,576,512]{2,1,0:T(8,128)(2,1)}, u32[]{:S(2)}, u32[]{:S(2)}) collective-permute-start(bf16[2,576,512]{2,1,0:T(8,128)(2,1)} %pad_maximum_fusion.15), channel_id=1, source_target_pairs={{0,8},{24,16},{1,9},{25,17},{2,10},{26,18},{3,11},{27,19},{4,12},{... | collective-permute-start | bytes 3538952 | tf_op jit(solution)/shard_map/ppermute | solution.py:103
  590.5 65.8 %collective-permute-start.32 = (bf16[2,576,512]{2,1,0:T(8,128)(2,1)}, bf16[2,576,512]{2,1,0:T(8,128)(2,1)}, u32[]{:S(2)}, u32[]{:S(2)}) collective-permute-start(bf16[2,576,512]{2,1,0:T(8,128)(2,1)} %pad_maximum_fusion.14), channel_id=1, source_target_pairs={{0,8},{24,16},{1,9},{25,17},{2,10},{26,18},{3,11},{27,19},{4,12},{... | collective-permute-start | bytes 3538952 | tf_op jit(solution)/shard_map/ppermute | solution.py:103
  596.9 84.6 %collective-permute-start.29 = (bf16[2,576,512]{2,1,0:T(8,128)(2,1)}, bf16[2,576,512]{2,1,0:T(8,128)(2,1)}, u32[]{:S(2)}, u32[]{:S(2)}) collective-permute-start(bf16[2,576,512]{2,1,0:T(8,128)(2,1)} %pad_maximum_fusion.13), channel_id=1, source_target_pairs={{0,8},{24,16},{1,9},{25,17},{2,10},{26,18},{3,11},{27,19},{4,12},{... | collective-permute-start | bytes 3538952 | tf_op jit(solution)/shard_map/ppermute | solution.py:103
  618.8 116.0 %all-to-all-start.7 = ((bf16[8,192,768]{2,1,0:T(8,128)(2,1)}), bf16[8,192,768]{2,1,0:T(8,128)(2,1)}, u32[]{:S(2)}, u32[]{:S(2)}) async-start(bf16[8,192,768]{2,1,0:T(8,128)(2,1)} %bitcast.505), calls=%async_computation.7 | async-start | bytes 4718592 | tf_op jit(solution)/shard_map/all_to_all | solution.py:251
  628.2 78.6 %collective-permute-start.26 = (bf16[2,576,512]{2,1,0:T(8,128)(2,1)}, bf16[2,576,512]{2,1,0:T(8,128)(2,1)}, u32[]{:S(2)}, u32[]{:S(2)}) collective-permute-start(bf16[2,576,512]{2,1,0:T(8,128)(2,1)} %pad_maximum_fusion.12), channel_id=1, source_target_pairs={{0,8},{24,16},{1,9},{25,17},{2,10},{26,18},{3,11},{27,19},{4,12},{... | collective-permute-start | bytes 3538952 | tf_op jit(solution)/shard_map/ppermute | solution.py:103
  632.2 99.4 %collective-permute-start.23 = (bf16[2,576,512]{2,1,0:T(8,128)(2,1)}, bf16[2,576,512]{2,1,0:T(8,128)(2,1)S(1)}, u32[]{:S(2)}, u32[]{:S(2)}) collective-permute-start(bf16[2,576,512]{2,1,0:T(8,128)(2,1)} %pad_maximum_fusion.11), channel_id=1, source_target_pairs={{0,8},{24,16},{1,9},{25,17},{2,10},{26,18},{3,11},{27,19},{4,12},{... | collective-permute-start | bytes 3538952 | tf_op jit(solution)/shard_map/ppermute | solution.py:103
  636.1 105.2 %collective-permute-start.39 = (bf16[2,384,512]{2,1,0:T(8,128)(2,1)}, bf16[2,384,512]{2,1,0:T(8,128)(2,1)}, u32[]{:S(2)}, u32[]{:S(2)}) collective-permute-start(bf16[2,384,512]{2,1,0:T(8,128)(2,1)} %fusion.65), channel_id=1, source_target_pairs={{8,16},{16,8},{9,17},{17,9},{10,18},{18,10},{11,19},{19,11},{12,20... | collective-permute-start | bytes 2359304 | tf_op jit(solution)/shard_map/ppermute | solution.py:106
  656.2 87.3 %collective-permute-start.36 = (bf16[2,384,512]{2,1,0:T(8,128)(2,1)}, bf16[2,384,512]{2,1,0:T(8,128)(2,1)S(1)}, u32[]{:S(2)}, u32[]{:S(2)}) collective-permute-start(bf16[2,384,512]{2,1,0:T(8,128)(2,1)} %fusion.64), channel_id=1, source_target_pairs={{8,16},{16,8},{9,17},{17,9},{10,18},{18,10},{11,19},{19,11},{12,20... | collective-permute-start | bytes 2359304 | tf_op jit(solution)/shard_map/ppermute | solution.py:106
  681.5 144.3 %collective-permute-start.33 = (bf16[2,384,512]{2,1,0:T(8,128)(2,1)}, bf16[2,384,512]{2,1,0:T(8,128)(2,1)}, u32[]{:S(2)}, u32[]{:S(2)}) collective-permute-start(bf16[2,384,512]{2,1,0:T(8,128)(2,1)} %fusion.63), channel_id=1, source_target_pairs={{8,16},{16,8},{9,17},{17,9},{10,18},{18,10},{11,19},{19,11},{12,20... | collective-permute-start | bytes 2359304 | tf_op jit(solution)/shard_map/ppermute | solution.py:106
  706.8 122.3 %collective-permute-start.30 = (bf16[2,384,512]{2,1,0:T(8,128)(2,1)}, bf16[2,384,512]{2,1,0:T(8,128)(2,1)}, u32[]{:S(2)}, u32[]{:S(2)}) collective-permute-start(bf16[2,384,512]{2,1,0:T(8,128)(2,1)} %fusion.62), channel_id=1, source_target_pairs={{8,16},{16,8},{9,17},{17,9},{10,18},{18,10},{11,19},{19,11},{12,20... | collective-permute-start | bytes 2359304 | tf_op jit(solution)/shard_map/ppermute | solution.py:106
  731.6 100.9 %collective-permute-start.27 = (bf16[2,384,512]{2,1,0:T(8,128)(2,1)}, bf16[2,384,512]{2,1,0:T(8,128)(2,1)}, u32[]{:S(2)}, u32[]{:S(2)}) collective-permute-start(bf16[2,384,512]{2,1,0:T(8,128)(2,1)} %fusion.61), channel_id=1, source_target_pairs={{8,16},{16,8},{9,17},{17,9},{10,18},{18,10},{11,19},{19,11},{12,20... | collective-permute-start | bytes 2359304 | tf_op jit(solution)/shard_map/ppermute | solution.py:106
  734.8 104.2 %all-to-all-start.5 = ((bf16[8,192,768]{2,1,0:T(8,128)(2,1)}), bf16[8,192,768]{2,1,0:T(8,128)(2,1)}, u32[]{:S(2)}, u32[]{:S(2)}) async-start(bf16[8,192,768]{2,1,0:T(8,128)(2,1)} %bitcast.504), calls=%async_computation.5 | async-start | bytes 4718592 | tf_op jit(solution)/shard_map/all_to_all | solution.py:251
  739.3 216.2 %reduce-scatter.2.cloned.1.call-start = ((), (), s32[]{:S(2)}) async-start(), calls=%async_computation.13 | async-start | bytes 5677056 | tf_op jit(solution)/shard_map/reduce_scatter | solution.py:476
  743.6 92.2 %collective-permute-start.24 = (bf16[2,384,512]{2,1,0:T(8,128)(2,1)}, bf16[2,384,512]{2,1,0:T(8,128)(2,1)}, u32[]{:S(2)}, u32[]{:S(2)}) collective-permute-start(bf16[2,384,512]{2,1,0:T(8,128)(2,1)} %fusion.60), channel_id=1, source_target_pairs={{8,16},{16,8},{9,17},{17,9},{10,18},{18,10},{11,19},{19,11},{12,20... | collective-permute-start | bytes 2359304 | tf_op jit(solution)/shard_map/ppermute | solution.py:106
  748.4 97.7 %collective-permute-start.40 = (bf16[2,192,512]{2,1,0:T(8,128)(2,1)}, bf16[2,192,512]{2,1,0:T(8,128)(2,1)}, u32[]{:S(2)}, u32[]{:S(2)}) collective-permute-start(bf16[2,192,512]{2,1,0:T(8,128)(2,1)} %add_convert_fusion.10), channel_id=1, source_target_pairs={{8,0},{16,24},{9,1},{17,25},{10,2},{18,26},{11,3},{19,27},{12,4},{... | collective-permute-start | bytes 1179656 | tf_op jit(solution)/shard_map/ppermute | solution.py:109
  829.1 39.2 %collective-permute-start.34 = (bf16[2,192,512]{2,1,0:T(8,128)(2,1)}, bf16[2,192,512]{2,1,0:T(8,128)(2,1)}, u32[]{:S(2)}, u32[]{:S(2)}) collective-permute-start(bf16[2,192,512]{2,1,0:T(8,128)(2,1)} %add_convert_fusion.14), channel_id=1, source_target_pairs={{8,0},{16,24},{9,1},{17,25},{10,2},{18,26},{11,3},{19,27},{12,4},{... | collective-permute-start | bytes 1179656 | tf_op jit(solution)/shard_map/ppermute | solution.py:109
  832.6 39.2 %collective-permute-start.31 = (bf16[2,192,512]{2,1,0:T(8,128)(2,1)}, bf16[2,192,512]{2,1,0:T(8,128)(2,1)}, u32[]{:S(2)}, u32[]{:S(2)}) collective-permute-start(bf16[2,192,512]{2,1,0:T(8,128)(2,1)} %add_convert_fusion.16), channel_id=1, source_target_pairs={{8,0},{16,24},{9,1},{17,25},{10,2},{18,26},{11,3},{19,27},{12,4},{... | collective-permute-start | bytes 1179656 | tf_op jit(solution)/shard_map/ppermute | solution.py:109
  835.7 38.0 %collective-permute-start.28 = (bf16[2,192,512]{2,1,0:T(8,128)(2,1)}, bf16[2,192,512]{2,1,0:T(8,128)(2,1)}, u32[]{:S(2)}, u32[]{:S(2)}) collective-permute-start(bf16[2,192,512]{2,1,0:T(8,128)(2,1)} %add_convert_fusion.18), channel_id=1, source_target_pairs={{8,0},{16,24},{9,1},{17,25},{10,2},{18,26},{11,3},{19,27},{12,4},{... | collective-permute-start | bytes 1179656 | tf_op jit(solution)/shard_map/ppermute | solution.py:109
  852.1 38.4 %collective-permute-start.19 = (f32[200,768]{1,0:T(8,128)}, f32[200,768]{1,0:T(8,128)}, u32[]{:S(2)}, u32[]{:S(2)}) collective-permute-start(f32[200,768]{1,0:T(8,128)} %slice_select_fusion.9), channel_id=1, source_target_pairs={{0,1},{1,0},{2,3},{3,2},{4,5},{5,4},{6,7},{7,6},{8,9},{9,8},{10,11... | collective-permute-start | bytes 1843208 | tf_op jit(solution)/shard_map/ppermute | solution.py:260
  (216 other events, 2028.1 us)
Sparse Core Ops, SparseCore 0:
  15.5 81.2 all-gather.2
  825.9 129.5 reduce-scatter.1

commit v2 on v1

v2 whole, which is shorter than its diff:
```python
import functools
import jax
import jax.numpy as jnp
from jax import lax
from jax.experimental import pallas as pl
from jax.experimental.pallas import tpu as pltpu
from jax.sharding import PartitionSpec as P

HD = 64
EPSILON = 1e-06
NEGATIVE = -1e30
F32 = jnp.float32
BF16 = jnp.bfloat16


def dot(left, right, left_dim=1, right_dim=0):
    return lax.dot_general(
        left, right, (((left_dim,), (right_dim,)), ((), ())), preferred_element_type=F32
    )


def norm_forward(values, gains, shifts):
    middle = jnp.mean(values, -1, keepdims=True)
    centred = values - middle
    inverse = lax.rsqrt(jnp.mean(centred * centred, -1, keepdims=True) + EPSILON)
    unit_rows = centred * inverse
    return (unit_rows * gains + shifts, unit_rows, inverse)


def norm_backward(grad_rows, unit_rows, inverse, gains):
    scaled = grad_rows * gains
    return inverse * (
        scaled
        - jnp.mean(scaled, -1, keepdims=True)
        - unit_rows * jnp.mean(scaled * unit_rows, -1, keepdims=True)
    )


def head_masks(width):
    lane = lax.broadcasted_iota(jnp.int32, (1, width), 1)
    return [(lane // HD == k) for k in range(width // HD)]


def attend_forward_kernel(
    tokens_ref, mask_ref, wq_ref, wk_ref, wv_ref, wo_ref, lines_ref, bias_ref,
    n1_ref, n2_ref, h_ref, q_ref, k_ref, v_ref, o_ref, lse_ref,
):
    x = tokens_ref[0].astype(F32)
    n1, _, _ = norm_forward(x, lines_ref[0:1, :], lines_ref[1:2, :])
    n1 = n1.astype(BF16)
    n1_ref[0] = n1
    width = wq_ref.shape[2]
    masks = head_masks(width)
    keys = mask_ref[0] > 0
    total = x + lines_ref[4:5, :]
    for t in range(wq_ref.shape[0]):
        q = (dot(n1, wq_ref[t]) + bias_ref[t, 0:1, :]).astype(BF16)
        k = dot(n1, wk_ref[t]).astype(BF16)
        v = (dot(n1, wv_ref[t]) + bias_ref[t, 1:2, :]).astype(BF16)
        q_ref[0, t] = q
        k_ref[0, t] = k
        v_ref[0, t] = v
        scaled = q * jnp.asarray(HD ** (-0.5), BF16)
        o = jnp.zeros(q.shape, F32)
        for h, here in enumerate(masks):
            s = dot(jnp.where(here, scaled, jnp.zeros_like(scaled)), k, 1, 1)
            s = jnp.where(keys, s, NEGATIVE)
            largest = jnp.max(s, -1, keepdims=True)
            e = jnp.exp(s - largest)
            total_e = jnp.sum(e, -1, keepdims=True)
            p = (e / total_e).astype(BF16)
            o = jnp.where(here, dot(p, v), o)
            index = t * len(masks) + h
            lse_ref[0, :, index : index + 1] = largest + jnp.log(total_e)
        o = o.astype(BF16)
        o_ref[0, t] = o
        total = total + dot(o, wo_ref[t], 1, 1)
    h_ref[0] = total
    n2, _, _ = norm_forward(total, lines_ref[5:6, :], lines_ref[6:7, :])
    n2_ref[0] = n2.astype(BF16)


def whole(shape):
    return pl.BlockSpec(shape, lambda b: (0,) * len(shape))


def by_image(shape):
    return pl.BlockSpec((1,) + shape[1:], lambda b: (b,) + (0,) * (len(shape) - 1))


def attend_forward(tokens_in, mask, wq, wk, wv, wo, lines, bias_pairs):
    images, sequence, model = tokens_in.shape
    quarter, _, width = wq.shape
    rows = (images, sequence, model)
    heads = (images, quarter, sequence, width)
    outs = [
        (rows, BF16), (rows, BF16), (rows, F32), (heads, BF16), (heads, BF16),
        (heads, BF16), (heads, BF16), ((images, sequence, 128), F32),
    ]
    return pl.pallas_call(
        attend_forward_kernel,
        grid=(images,),
        in_specs=[
            by_image(tokens_in.shape),
            by_image(mask.shape),
            whole(wq.shape), whole(wk.shape), whole(wv.shape), whole(wo.shape),
            whole(lines.shape), whole(bias_pairs.shape),
        ],
        out_specs=[by_image(s) for s, _ in outs],
        out_shape=[jax.ShapeDtypeStruct(s, d) for s, d in outs],
        compiler_params=pltpu.CompilerParams(vmem_limit_bytes=56 * 2**20),
        cost_estimate=pl.CostEstimate(flops=3 * 10**9, bytes_accessed=2 * 10**7, transcendentals=2 * 10**6),
        name="attend_forward",
    )(tokens_in, mask, wq, wk, wv, wo, lines, bias_pairs)


def attend_backward_kernel(
    n2_grad_ref, grad_ref, tokens_ref, h_ref, mask_ref, wq_ref, wk_ref, wv_ref, wo_ref, lines_ref,
    n1_ref, q_ref, k_ref, v_ref, o_ref, lse_ref,
    input_grad_ref, dwq_ref, dwk_ref, dwv_ref, dwo_ref, vec_ref, pair_ref,
):
    first = pl.program_id(0) == 0

    @pl.when(first)
    def _():
        for ref in (dwq_ref, dwk_ref, dwv_ref, dwo_ref, vec_ref, pair_ref):
            ref[...] = jnp.zeros_like(ref)

    grad = grad_ref[0].astype(F32)
    n2_grad = n2_grad_ref[0]
    _, unit_two, inverse_two = norm_forward(h_ref[0], lines_ref[5:6, :], lines_ref[6:7, :])
    vec_ref[5:6, :] += jnp.sum(n2_grad * unit_two, 0, keepdims=True)
    vec_ref[6:7, :] += jnp.sum(n2_grad, 0, keepdims=True)
    h_grad = grad + norm_backward(n2_grad, unit_two, inverse_two, lines_ref[5:6, :])
    vec_ref[4:5, :] += jnp.sum(h_grad, 0, keepdims=True)
    hb = h_grad.astype(BF16)
    n1 = n1_ref[0]
    width = wq_ref.shape[2]
    masks = head_masks(width)
    keys = mask_ref[0] > 0
    scale = HD ** (-0.5)
    n1_grad = jnp.zeros(grad.shape, F32)
    for t in range(wq_ref.shape[0]):
        o = o_ref[0, t]
        dwo_ref[t] += dot(hb, o, 0, 0)
        do = dot(hb, wo_ref[t]).astype(BF16)
        q, k, v = q_ref[0, t], k_ref[0, t], v_ref[0, t]
        zero = jnp.zeros_like(q)
        scaled = q * jnp.asarray(scale, BF16)
        dq = jnp.zeros(q.shape, F32)
        dk = jnp.zeros(q.shape, F32)
        dv = jnp.zeros(q.shape, F32)
        for h, here in enumerate(masks):
            index = t * len(masks) + h
            s = dot(jnp.where(here, scaled, zero), k, 1, 1)
            s = jnp.where(keys, s, NEGATIVE)
            p = jnp.exp(s - lse_ref[0, :, index : index + 1])
            dp = dot(jnp.where(here, do, zero), v, 1, 1)
            ds = p * (dp - jnp.sum(p * dp, -1, keepdims=True))
            ds = ds.astype(BF16)
            dv = jnp.where(here, dot(p.astype(BF16), do, 0, 0), dv)
            dq = jnp.where(here, dot(ds, k), dq)
            dk = jnp.where(here, dot(ds, q, 0, 0), dk)
        dq = (dq * scale).astype(BF16)
        dk = (dk * scale).astype(BF16)
        dv = dv.astype(BF16)
        pair_ref[t, 0:1, :] += jnp.sum(dq.astype(F32), 0, keepdims=True)
        pair_ref[t, 1:2, :] += jnp.sum(dv.astype(F32), 0, keepdims=True)
        dwq_ref[t] += dot(n1, dq, 0, 0)
        dwk_ref[t] += dot(n1, dk, 0, 0)
        dwv_ref[t] += dot(n1, dv, 0, 0)
        n1_grad += dot(dq, wq_ref[t], 1, 1) + dot(dk, wk_ref[t], 1, 1) + dot(dv, wv_ref[t], 1, 1)
    _, unit_one, inverse_one = norm_forward(
        tokens_ref[0].astype(F32), lines_ref[0:1, :], lines_ref[1:2, :]
    )
    vec_ref[0:1, :] += jnp.sum(n1_grad * unit_one, 0, keepdims=True)
    vec_ref[1:2, :] += jnp.sum(n1_grad, 0, keepdims=True)
    input_grad_ref[0] = h_grad + norm_backward(n1_grad, unit_one, inverse_one, lines_ref[0:1, :])


def attend_backward(n2_grad, out_grad, tokens_in, h, mask, wq, wk, wv, wo, lines, n1, q, k, v, o, lse):
    ins = (n2_grad, out_grad, tokens_in, h, mask, wq, wk, wv, wo, lines, n1, q, k, v, o, lse)
    shared = {5, 6, 7, 8, 9}
    outs = [
        (n2_grad.shape, F32), (wq.shape, F32), (wq.shape, F32), (wq.shape, F32), (wq.shape, F32),
        ((8, n2_grad.shape[2]), F32), ((wq.shape[0], 8, wq.shape[2]), F32),
    ]
    return pl.pallas_call(
        attend_backward_kernel,
        grid=(n2_grad.shape[0],),
        in_specs=[whole(a.shape) if i in shared else by_image(a.shape) for i, a in enumerate(ins)],
        out_specs=[by_image(outs[0][0])] + [whole(s) for s, _ in outs[1:]],
        out_shape=[jax.ShapeDtypeStruct(s, d) for s, d in outs],
        compiler_params=pltpu.CompilerParams(vmem_limit_bytes=56 * 2**20),
        cost_estimate=pl.CostEstimate(flops=8 * 10**9, bytes_accessed=4 * 10**7, transcendentals=2 * 10**6),
        name="attend_backward",
    )(*ins)


def expert_kernel(first, order_ref, x_ref, g_ref, w_ref, b_ref, *refs):
    if first:
        y_out, p_out, bias_ref, *grads, acc_ref = refs
    else:
        y_in, p_in, y_out, p_out, bias_ref, *grads, acc_ref = refs
    step = pl.program_id(0)

    @pl.when(step == 0)
    def _():
        acc_ref[...] = jnp.zeros_like(acc_ref)
        bias_ref[...] = jnp.zeros_like(bias_ref)

    x = x_ref[...]
    g = g_ref[...]
    hidden = dot(x, w_ref[0]) + b_ref[...]
    cdf = 0.5 * (1.0 + lax.erf(hidden * (0.5 ** 0.5)))
    active = (hidden * cdf).astype(BF16)
    slope = cdf + hidden * (jnp.exp(-0.5 * hidden * hidden) * 0.3989422804014327)
    hidden_grad = (dot(g, w_ref[1]) * slope).astype(BF16)
    y = dot(active, w_ref[1], 1, 1)
    p = dot(hidden_grad, w_ref[0], 1, 1)
    if first:
        y_out[...] = y
        p_out[...] = p
    else:
        y_out[...] = y_in[...] + y
        p_out[...] = p_in[...] + p
    bias_ref[...] += jnp.sum(hidden_grad.astype(F32), 0, keepdims=True)
    acc_ref[0] += dot(x, hidden_grad, 0, 0)
    acc_ref[1] += dot(g, active, 0, 0)

    @pl.when(step == pl.num_programs(0) - 1)
    def _():
        for k, ref in enumerate(grads):
            rows = ref.shape[1]
            start = pl.multiple_of(order_ref[k] * rows, 16)
            for side in range(2):
                ref[side] = acc_ref[side, pl.ds(start, rows), :].astype(ref.dtype)


def expert_chunk(order, x, g, w, b, sums, pieces, piece_type):
    count, model = x.shape
    block = 256
    units = w.shape[2]
    row = lambda: pl.BlockSpec((block, model), lambda i, o: (i, 0))
    full = lambda shape: pl.BlockSpec(shape, lambda i, o: (0,) * len(shape))
    first = sums is None
    ins = [x, g, w, b] + ([] if first else list(sums))
    in_specs = [row(), row(), full(w.shape), full(b.shape)] + ([] if first else [row(), row()])
    piece = (2, model // pieces, units)
    outs = [((count, model), F32), ((count, model), F32), (b.shape, F32)] + [(piece, piece_type)] * pieces
    return pl.pallas_call(
        functools.partial(expert_kernel, first),
        grid_spec=pltpu.PrefetchScalarGridSpec(
            num_scalar_prefetch=1,
            grid=(count // block,),
            in_specs=in_specs,
            out_specs=[row(), row(), full(b.shape)] + [full(piece)] * pieces,
            scratch_shapes=[pltpu.VMEM((2, model, units), F32)],
        ),
        out_shape=[jax.ShapeDtypeStruct(s, d) for s, d in outs],
        input_output_aliases={} if first else {5: 0, 6: 1},
        compiler_params=pltpu.CompilerParams(vmem_limit_bytes=56 * 2**20),
        cost_estimate=pl.CostEstimate(flops=12 * count * model * units, bytes_accessed=3 * 10**7, transcendentals=2 * count * units),
        name="expert_chunk",
    )(order, *ins)


CAP = 128
GROUP_IMG = 2
CHUNK = 128
HIGHEST = lax.Precision.HIGHEST
PLANE = ("x", "t")
EVERY = ("t", "z", "x")
INWARD = [(0, 1), (3, 2)]
MIDDLE = [(1, 2), (2, 1)]
OUTWARD = [(1, 0), (2, 3)]
ORDER = ((0, 1, 2, 3), (1, 0, 2, 3), (2, 3, 1, 0), (3, 2, 1, 0))


def tie(values, *events):
    events = [e for e in events if e is not None]
    if not events:
        return values
    return lax.optimization_barrier((values, *events))[0]


def gather_lines(owns, length):
    if length != 4:
        return [lax.all_gather(own, "z", axis=1, tiled=True) for own in owns]
    place = lax.axis_index("z")
    inner = (place == 1) | (place == 2)
    result = []
    last_in = last_mid = last_out = None
    for own in owns:
        inward = lax.ppermute(tie(own, last_in), "z", INWARD)
        middle_one = lax.ppermute(tie(own, last_mid), "z", MIDDLE)
        outward_one = lax.ppermute(tie(own, last_out), "z", OUTWARD)
        middle_two = lax.ppermute(inward, "z", MIDDLE)
        outward_two = lax.ppermute(middle_one, "z", OUTWARD)
        outward_three = lax.ppermute(middle_two, "z", OUTWARD)
        last_in, last_mid, last_out = inward, middle_one, outward_two
        near = jnp.where(inner, inward, outward_one)
        far_one = jnp.where(inner, middle_one, outward_two)
        far_two = jnp.where(inner, middle_two, outward_three)
        low = place < 2
        end = (place == 0) | (place == 3)
        first = jnp.where(end, own, near)
        second = jnp.where(end, near, own)
        result.append(
            jnp.concatenate(
                [
                    jnp.where(low, first, far_two),
                    jnp.where(low, second, far_one),
                    jnp.where(low, far_one, second),
                    jnp.where(low, far_two, first),
                ],
                1,
            )
        )
    return result


def scatter_line(pieces):
    if len(pieces) == 1:
        return lax.psum_scatter(pieces[0], "z", scatter_dimension=1, tiled=True)
    own, near, far_one, far_two = pieces

    def add(*terms):
        return sum(term.astype(F32) for term in terms).astype(BF16)

    inward_three = lax.ppermute(far_two, "z", INWARD)
    inward_two = lax.ppermute(far_one, "z", INWARD)
    inward_one = lax.ppermute(near, "z", INWARD)
    middle_two = lax.ppermute(add(far_two, inward_three), "z", MIDDLE)
    middle_one = lax.ppermute(add(far_one, inward_two), "z", MIDDLE)
    outward = lax.ppermute(add(near, middle_two), "z", OUTWARD)
    return add(own, inward_one, middle_one, outward)


def shards(
    tokens_in,
    key_mask,
    expert_ids,
    expert_slots,
    norm1_gain,
    norm1_shift,
    qkv_weight,
    qv_bias,
    out_weight,
    out_bias,
    norm2_gain,
    norm2_shift,
    router_weight,
    up_weight,
    up_bias,
    down_weight,
    down_bias,
    out_grad,
):
    length = lax.axis_size("z")
    quarter = lax.axis_size("t")
    core = lax.axis_index("t") % 2
    chip_y = lax.axis_index("t") // 2
    expert = lax.axis_index("x") * quarter + lax.axis_index("t")
    piece, sequence, model = tokens_in.shape
    experts, part, units = up_weight.shape
    dp = model // part
    width = qkv_weight.shape[2]
    tokens = piece * sequence
    blocks = units // CHUNK
    spans = [(0, 1), (1, 3), (3, 5), (5, 6)] if blocks == 6 else [(0, blocks)]

    smalls = jnp.concatenate(
        [
            norm1_gain[None],
            norm1_shift[None],
            qv_bias,
            out_bias[None],
            norm2_gain[None],
            norm2_shift[None],
            down_bias,
            router_weight.T,
            up_bias.reshape(experts * quarter, part),
        ],
        0,
    ).astype(BF16)
    small_rows = smalls.shape[0]
    pad = -(small_rows * part) % (16 * model)
    small_block = jnp.pad(smalls.reshape(-1), (0, pad)).reshape(-1, model)
    pack = jnp.concatenate(
        [
            jnp.concatenate(
                [qkv_weight[0], qkv_weight[1], qkv_weight[2], out_weight.T], 1
            ).astype(BF16),
            small_block,
        ],
        0,
    )
    packs = lax.all_gather(pack, EVERY, axis=0, tiled=False)
    packs = packs.reshape(quarter, dp, pack.shape[0], model)
    wq, wk, wv, wo = [
        packs[:, :, :part, k * width : (k + 1) * width].reshape(quarter, model, width)
        for k in range(4)
    ]
    vectors = packs[0, :, part:].reshape(dp, -1)[:, : small_rows * part]
    vectors = vectors.reshape(dp, small_rows, part).transpose(1, 0, 2)
    lines = vectors[: 7 + 2 * experts].reshape(-1, model).astype(F32)
    bias_pairs = lines[2:4].reshape(2, quarter, width).transpose(1, 0, 2)
    bias_down = lines[7 : 7 + experts]
    router = lines[7 + experts :].astype(BF16)
    bias_up = vectors[7 + 2 * experts :].reshape(experts, quarter, dp, part)
    bias_up = bias_up.transpose(0, 2, 1, 3).reshape(experts, quarter, units)
    bias_up = lax.dynamic_index_in_dim(bias_up, expert, 0, keepdims=False).astype(F32)

    parts = []
    event = None
    for first, last in spans:
        some = jnp.stack(
            [
                up_weight[:, :, first * CHUNK : last * CHUNK].astype(BF16),
                down_weight[:, first * CHUNK : last * CHUNK].astype(BF16).transpose(0, 2, 1),
            ],
            1,
        )
        some = lax.all_to_all(tie(some, event), PLANE, 0, 0, tiled=True)
        event = some
        some = some.reshape(2, quarter, 2, part, (last - first) * CHUNK)
        some = some.transpose(2, 0, 3, 1, 4)
        parts.append(some.reshape(2, 2 * part, quarter * (last - first) * CHUNK))

    first_group = chip_y * 3
    group_tokens = GROUP_IMG * sequence
    position = (expert_ids * CAP + expert_slots).reshape(-1, group_tokens, 2)
    position_full = lax.dynamic_index_in_dim(position, first_group + 2 * core, 0, keepdims=False)
    position_half = lax.dynamic_index_in_dim(position, first_group + 1, 0, keepdims=False)
    slots_full = jnp.arange(experts * CAP, dtype=jnp.int32)
    half = CAP // 2
    slots_half = (
        jnp.arange(experts, dtype=jnp.int32)[:, None] * CAP
        + core * half
        + jnp.arange(half, dtype=jnp.int32)
    ).reshape(-1)
    match_full = slots_full[:, None, None] == position_full.T[None]
    match_half = slots_half[:, None, None] == position_half.T[None]
    hot_full = (match_full[:, 0] | match_full[:, 1]).astype(BF16)
    hot_half = (match_half[:, 0] | match_half[:, 1]).astype(BF16)
    swap = [(k, k ^ 1) for k in range(quarter)]

    def both_groups(values):
        lent = jnp.where(core == 0, values[2], values[0])
        other = lax.ppermute(lent, "t", swap)
        full = jnp.where(core == 0, values[:2], values[1:])
        shared = jnp.where(core == 0, jnp.stack([lent, other]), jnp.stack([other, lent]))
        return (
            full.reshape(group_tokens, -1),
            shared.reshape(group_tokens, -1),
        )

    def join_rows(full, shared):
        full = full.reshape((experts, CAP) + full.shape[1:])
        shared = shared.reshape((experts, half) + shared.shape[1:])
        return jnp.concatenate([full, shared], 1)

    def dispatch(full, shared, after=None):
        rows = join_rows(dot(hot_full, full).astype(BF16), dot(hot_half, shared).astype(BF16))
        rows = tie(rows, after)
        return lax.all_to_all(rows, PLANE, 0, 0, tiled=True).reshape(-1, model)

    def combine(rows):
        back = lax.all_to_all(
            rows.reshape(experts, CAP + half, model), PLANE, 0, 0, tiled=True
        )
        full = dot(hot_full, back[:, :CAP].reshape(-1, model), 0, 0)
        shared = dot(hot_half, back[:, CAP:].reshape(-1, model), 0, 0)
        full = full.reshape(GROUP_IMG, sequence, model)
        shared = shared.reshape(GROUP_IMG, sequence, model)
        mine = jnp.where(core == 0, shared[0], shared[1])
        theirs = jnp.where(core == 0, shared[1], shared[0])
        mine = mine + lax.ppermute(theirs, "t", swap)
        return jnp.where(
            core == 0,
            jnp.concatenate([full, mine[None]]),
            jnp.concatenate([mine[None], full]),
        )

    grad_full, grad_shared = both_groups(out_grad)
    incoming = dispatch(grad_full, grad_shared, event)

    local_start = lax.axis_index("t") * piece
    mask_here = lax.dynamic_slice_in_dim(key_mask, local_start, piece, 0)[:, None]
    n1, n2, residual, q, k, v, attended, lse = attend_forward(
        tokens_in, mask_here, wq, wk, wv, wo, lines, bias_pairs
    )
    normed_two = n2.reshape(tokens, model)

    normed_full, normed_shared = both_groups(n2)

    def chances_of(rows):
        return jax.nn.softmax(dot(rows, router, 1, 1), -1)

    probabilities = chances_of(normed_two)
    hot_ids = expert_ids[..., None] == jnp.arange(experts, dtype=jnp.int32)
    hot_here = lax.dynamic_slice_in_dim(hot_ids, local_start, piece, 0).astype(F32)
    hot_here = jnp.sum(hot_here.reshape(tokens, 2, experts), 1)
    share_here = hot_here * probabilities

    def slot_gates(match, rows, position_here):
        chance = chances_of(rows)
        hot = (position_here // CAP)[..., None] == jnp.arange(experts, dtype=jnp.int32)
        gates = jnp.sum(hot.astype(F32) * chance[:, None], -1)
        return jnp.sum(jnp.where(match, gates.T[None], 0.0), (1, 2))

    gates_sent = join_rows(
        slot_gates(match_full, normed_full, position_full),
        slot_gates(match_half, normed_shared, position_half),
    )
    chosen = dispatch(normed_full, normed_shared, incoming)
    slot_gate = lax.all_to_all(gates_sent, PLANE, 0, 0, tiled=True).reshape(-1, 1)

    incoming_f = incoming.astype(F32)
    out_part = (incoming_f * slot_gate).astype(BF16)
    place = lax.axis_index("z")
    pieces, piece_type = (4, BF16) if length == 4 else (1, F32)
    order = jnp.asarray(ORDER if length == 4 else [[0]] * length, jnp.int32)
    order = lax.dynamic_index_in_dim(order, place, 0, keepdims=False)
    sums = None
    bias_parts = []
    reduced = []
    for (first, last), both in zip(spans, gather_lines(parts, length)):
        bias_one = bias_up[:, first * CHUNK : last * CHUNK].reshape(1, -1)
        produced, pulled, bias_part, *grads = expert_chunk(
            order, chosen, out_part, both, bias_one, sums, pieces, piece_type
        )
        sums = (produced, pulled)
        bias_parts.append(bias_part.reshape(quarter, -1))
        reduced.append(scatter_line(grads).astype(BF16))

    gate_part = jnp.sum(incoming_f * produced, -1)
    gate_back = lax.all_to_all(
        gate_part.reshape(experts, CAP + half), PLANE, 0, 0, tiled=True
    )
    norm_two_grad = combine(pulled.astype(BF16))

    def slots_to_tokens(match, parts_here):
        parts_here = parts_here.reshape(experts, -1)
        match = (match[:, 0] | match[:, 1]).reshape(experts, -1, group_tokens)
        return jnp.sum(jnp.where(match, parts_here[..., None], 0.0), 1).T

    prob_full = slots_to_tokens(match_full, gate_back[:, :CAP])
    prob_shared = slots_to_tokens(match_half, gate_back[:, CAP:])
    prob_full = prob_full.reshape(GROUP_IMG, sequence, experts)
    prob_shared = prob_shared.reshape(GROUP_IMG, sequence, experts)
    mine = jnp.where(core == 0, prob_shared[0], prob_shared[1])
    theirs = jnp.where(core == 0, prob_shared[1], prob_shared[0])
    mine = mine + lax.ppermute(theirs, "t", swap)
    chance_grad = jnp.where(
        core == 0,
        jnp.concatenate([prob_full, mine[None]]),
        jnp.concatenate([mine[None], prob_full]),
    ).reshape(tokens, experts)
    grad_rows = out_grad.reshape(tokens, model)
    bias_dot = dot(grad_rows, bias_down.astype(BF16), 1, 1)
    chance_grad = chance_grad + hot_here * bias_dot
    logit_grad = probabilities * (
        chance_grad - jnp.sum(probabilities * chance_grad, -1, keepdims=True)
    )
    logit_grad = logit_grad.astype(BF16)
    router_grad = dot(logit_grad, normed_two, 0, 0)
    down_bias_grad = lax.dot_general(
        share_here, grad_rows.astype(F32), (((0,), (0,)), ((), ())), precision=HIGHEST
    )

    norm_two_grad = norm_two_grad + dot(logit_grad, router).reshape(norm_two_grad.shape)
    input_grad, dwq, dwk, dwv, dwo, line_sums, pair_sums = attend_backward(
        norm_two_grad, out_grad, tokens_in, residual, mask_here, wq, wk, wv, wo, lines,
        n1, q, k, v, attended, lse,
    )
    mixture = combine(tie((produced * slot_gate).astype(BF16), norm_two_grad))
    bias_term = jnp.dot(share_here, bias_down, precision=HIGHEST).reshape(residual.shape)
    output = (residual + mixture + bias_term).astype(BF16)

    bias_rows = jnp.concatenate(bias_parts, 1).reshape(dp, quarter, part)
    bias_rows = jnp.where(
        jnp.arange(experts)[:, None, None, None] == expert, bias_rows[None], 0.0
    )
    bias_rows = bias_rows.transpose(0, 2, 1, 3).reshape(experts * quarter, dp, part)
    line_grads = jnp.concatenate(
        [
            line_sums[0:2],
            pair_sums[:, 0].reshape(1, model),
            pair_sums[:, 1].reshape(1, model),
            line_sums[4:7],
            down_bias_grad,
            router_grad,
        ],
        0,
    ).reshape(-1, dp, part)
    sum_type = BF16 if length == 4 else F32
    vector_grads = jnp.concatenate([line_grads, bias_rows], 0).astype(sum_type)
    vector_grads = vector_grads.transpose(1, 0, 2).reshape(dp, small_rows * part)
    vector_grads = jnp.pad(vector_grads, ((0, 0), (0, pad))).reshape(dp, -1, model)
    pack_grads = jnp.concatenate(
        [
            jnp.concatenate([dwq, dwk, dwv, dwo], -1)
            .astype(sum_type)
            .reshape(quarter, dp, part, model),
            jnp.broadcast_to(vector_grads[None], (quarter,) + vector_grads.shape),
        ],
        2,
    )
    pack_grads = pack_grads.reshape((quarter * dp,) + pack_grads.shape[2:])
    pack_grad = lax.psum_scatter(pack_grads, EVERY, scatter_dimension=0, tiled=False)
    pack_grad = pack_grad.astype(F32)
    qkv_out = pack_grad[:part, : 3 * width].reshape(part, 3, width).transpose(1, 0, 2)
    out_weight_grad = pack_grad[:part, 3 * width :].T
    small_grads = pack_grad[part:].reshape(-1)[: small_rows * part].reshape(small_rows, part)

    ups, downs = [], []
    event = norm_two_grad
    for some in reduced:
        some = some.reshape(2, 2, part, quarter, -1)
        some = some.transpose(1, 3, 0, 2, 4).reshape(experts, 2, part, -1)
        some = lax.all_to_all(some, PLANE, 0, 0, tiled=True).astype(F32)
        ups.append(some[:, 0])
        downs.append(some[:, 1])
    up_grad = jnp.concatenate(ups, -1)
    down_grad = jnp.concatenate(downs, -1).transpose(0, 2, 1)
    return (
        output,
        input_grad,
        small_grads[0],
        small_grads[1],
        qkv_out,
        small_grads[2:4],
        out_weight_grad,
        small_grads[4],
        small_grads[5],
        small_grads[6],
        small_grads[7 + experts : 7 + 2 * experts].T,
        up_grad,
        small_grads[7 + 2 * experts :].reshape(experts, -1),
        down_grad,
        small_grads[7 : 7 + experts],
    )


def solution(mesh):
    dp, tensor = mesh.devices.shape
    planes = jax.sharding.Mesh(mesh.devices.reshape(dp // 2, 2, tensor), ("z", "x", "t"))
    rows = ("z", "x")
    images = P(("z", "x", "t"), None, None)
    return jax.shard_map(
        shards,
        mesh=planes,
        in_specs=(
            images,
            P(rows, None),
            P(rows, None, None),
            P(rows, None, None),
            P(rows),
            P(rows),
            P(None, rows, "t"),
            P(None, rows),
            P("t", rows),
            P(rows),
            P(rows),
            P(rows),
            P(rows, None),
            P(None, rows, "t"),
            P(None, rows),
            P(None, "t", rows),
            P(None, rows),
            images,
        ),
        out_specs=(
            images,
            images,
            P(rows),
            P(rows),
            P(None, rows, "t"),
            P(None, rows),
            P("t", rows),
            P(rows),
            P(rows),
            P(rows),
            P(rows, None),
            P(None, rows, "t"),
            P(None, rows),
            P(None, "t", rows),
            P(None, rows),
        ),
        check_vma=False,
    )
```

time: 983 us -> 855 us (0.87)
  matrix products: 231 us -> 22.6 us
  Pallas kernels: 0 us -> 133 us
  starting transfers between devices: 123 us -> 210 us
  other arithmetic: 188 us -> 134 us
  local copies, waits for them, and re-layouts: 146 us -> 95.2 us
  waiting for transfers between devices: 263 us -> 234 us
    dot_general x50 -> x14, matrix products: 177 us -> 19.3 us  [dot(): lax.dot_general(left, right, (((left_dim,), (right_dim,)), ((), ())), pre...]
    pallas_call x0 -> x6, Pallas kernels: none -> 133 us  [the longest x4 74.4 us: expert_chunk(): pl.pallas_call(functools.partial(expert_kernel, first), grid_spec=pltpu.P...]
    ppermute x36 -> x48, starting transfers between devices: 70.3 us -> 143 us  [the longest x4 52.1 us: scatter_line(): inward_one = lax.ppermute(near, 'z', INWARD)]
    dot_general x14 -> x2, matrix products: 54.2 us -> 3.25 us  [the longest x1 2.09 us: shards(): jnp.dot(share_here, bias_down, precision=HIGHEST).reshape(residual.shape)]
    ppermute x36 -> x48, waiting for transfers between devices: 203 us -> 166 us  [the longest x4 57.6 us: gather_lines(): outward_three = lax.ppermute(middle_two, 'z', OUTWARD)]
    reshape x17 -> x18, local copies, waits for them, and re-layouts: 39 us -> 14.6 us  [the longest x4 5.47 us: shards(): parts.append(some.reshape(2, 2 * part, quarter * (last - first) * CHUNK))]
    reduce_scatter x1, waiting for transfers between devices: 22 us -> 0.01 us  [shards(): lax.psum_scatter(pack_grads, EVERY, scatter_dimension=0, tiled=False)]
    concatenate x19 -> x6, other arithmetic: 34.1 us -> 12.4 us  [the longest x4 6.2 us: gather_lines(): jnp.concatenate([jnp.where(low, first, far_two), jnp.where(low, second, f...]
  transfers between devices with their start and end apart: 55 -> 69, of which waited for: 17 -> 23; matrix products, arithmetic and copies ran while one was open for 39% -> 26% of each run, Pallas kernels for 0% -> 7%
where the time goes in v2:
time: 855 us; the launch traced here: 845 us
  waiting for transfers between devices  234 us (27%)
  starting transfers between devices  210 us (25%)
  other arithmetic  134 us (16%)
  Pallas kernels  133 us (16%)
  local copies, waits for them, and re-layouts  95.2 us (11%)
  matrix products  22.6 us (3%)
  between operations  15.8 us (2%)
    pallas_call x4, Pallas kernels, expert_chunk(): pl.pallas_call(functools.partial(expert_kernel, first), grid_spec=pltpu.P...  74.4 us
    ppermute x4, waiting for transfers between devices, gather_lines(): outward_three = lax.ppermute(middle_two, 'z', OUTWARD)  57.6 us
    ppermute x4, starting transfers between devices, scatter_line(): inward_one = lax.ppermute(near, 'z', INWARD)  52.1 us
    ppermute x4, waiting for transfers between devices, gather_lines(): outward_two = lax.ppermute(middle_one, 'z', OUTWARD)  37.4 us
    pallas_call x1, Pallas kernels, attend_backward(): pl.pallas_call(attend_backward_kernel, grid=(n2_grad.shape[0],), in_specs...  37 us
    ppermute x4, waiting for transfers between devices, scatter_line(): outward = lax.ppermute(add(near, middle_two), 'z', OUTWARD)  33.8 us
    convert_element_type x16, other arithmetic, add(): return sum((term.astype(F32) for term in terms)).astype(BF16)  29.2 us
    ppermute x4, waiting for transfers between devices, scatter_line(): inward_three = lax.ppermute(far_two, 'z', INWARD)  26 us
  transfers between devices with their start and end apart: 69, of which 23 were waited for; matrix products, arithmetic and copies ran while one was open for 26% of the time, Pallas kernels for 7%

profile of v2, /device:TPU:0, one launch (start us, length us, event | category | flops | bytes accessed | tf_op | source)
XLA Modules:
  0.0 844.9 jit_solution(10321869315727820812)
XLA Ops:
  28.4 6.7 all-to-all-done
  62.1 5.4 collective-permute-start.3
  76.7 13.0 %all-to-all-done.2 = bf16[8,2,96,256]{3,2,1,0:T(8,128)(2,1)S(1)} async-done(((bf16[8,2,96,256]{3,2,1,0:T(8,128)(2,1)}), bf16[8,2,96,256]{3,2,1,0:T(8,128)(2,1)S(1)}, u32[]{:S(2)}, u32[]{:S(2)}) %all-to-all-start.2) | async-done | bytes 786464 | tf_op jit(solution)/shard_map/all_to_all | solution.py:425
  97.2 5.3 collective-permute-start.4
  135.0 8.0 collective-permute-start.5
  149.6 10.7 %collective-permute-done.15 = bf16[2,192,1024]{2,1,0:T(8,128)(2,1)} collective-permute-done((bf16[2,192,1024]{2,1,0:T(8,128)(2,1)}, bf16[2,192,1024]{2,1,0:T(8,128)(2,1)}, u32[]{:S(2)}, u32[]{:S(2)}) %collective-permute-start.15) | collective-permute-done | bytes 786464 | tf_op jit(solution)/shard_map/ppermute | solution.py:299
  171.0 23.0 %collective-permute-done.9 = bf16[2,192,1024]{2,1,0:T(8,128)(2,1)} collective-permute-done((bf16[2,192,1024]{2,1,0:T(8,128)(2,1)}, bf16[2,192,1024]{2,1,0:T(8,128)(2,1)}, u32[]{:S(2)}, u32[]{:S(2)}) %collective-permute-start.9) | collective-permute-done | bytes 786464 | tf_op jit(solution)/shard_map/ppermute | solution.py:299
  198.6 12.2 %collective-permute-done.22 = bf16[2,192,1024]{2,1,0:T(8,128)(2,1)} collective-permute-done((bf16[2,192,1024]{2,1,0:T(8,128)(2,1)}, bf16[2,192,1024]{2,1,0:T(8,128)(2,1)}, u32[]{:S(2)}, u32[]{:S(2)}) %collective-permute-start.22) | collective-permute-done | bytes 786464 | tf_op jit(solution)/shard_map/ppermute | solution.py:300
  219.2 33.6 %collective-permute-done.12 = bf16[2,192,512]{2,1,0:T(8,128)(2,1)S(1)} collective-permute-done((bf16[2,192,512]{2,1,0:T(8,128)(2,1)}, bf16[2,192,512]{2,1,0:T(8,128)(2,1)S(1)}, u32[]{:S(2)}, u32[]{:S(2)}) %collective-permute-start.12) | collective-permute-done | bytes 393248 | tf_op jit(solution)/shard_map/ppermute | solution.py:300
  258.2 11.3 %collective-permute-done.18 = bf16[2,192,1024]{2,1,0:T(8,128)(2,1)S(1)} collective-permute-done((bf16[2,192,1024]{2,1,0:T(8,128)(2,1)S(1)}, bf16[2,192,1024]{2,1,0:T(8,128)(2,1)S(1)}, u32[]{:S(2)}, u32[]{:S(2)}) %collective-permute-start.18) | collective-permute-done | bytes 786464 | tf_op jit(solution)/shard_map/ppermute | solution.py:300
  271.9 7.6 fusion.27
  286.6 22.0 %attend_forward.1 = (bf16[3,200,768]{2,1,0:T(8,128)(2,1)}, bf16[3,200,768]{2,1,0:T(8,128)(2,1)}, f32[3,200,768]{2,1,0:T(8,128)}, bf16[3,4,200,192]{3,2,1,0:T(8,1...) custom-call(bf16[3,200,768]{2,1,0:T(8,128)(2,1)} %tokens_ref.3, ...), custom_call_target="tpu_custom_call" | custom-call | flops 3000000000 | bytes 20000000 | tf_op jit(solution)/shard_map/attend_forward/pallas_call | solution.py:100
  335.8 13.0 %all-to-all-start.5 = ((bf16[8,192,768]{2,1,0:T(8,128)(2,1)}), bf16[8,192,768]{2,1,0:T(8,128)(2,1)}, u32[]{:S(2)}, u32[]{:S(2)}) async-start(bf16[8,192,768]{2,1,0:T(8,128)(2,1)} %pad_maximum_fusion.3), calls=%async_computation.5 | async-start | bytes 4718592 | tf_op jit(solution)/shard_map/all_to_all | solution.py:467
  367.3 9.7 %all-to-all-done.5 = bf16[8,192,768]{2,1,0:T(8,128)(2,1)} async-done(((bf16[8,192,768]{2,1,0:T(8,128)(2,1)}), bf16[8,192,768]{2,1,0:T(8,128)(2,1)}, u32[]{:S(2)}, u32[]{:S(2)}) %all-to-all-start.5) | async-done | bytes 2359328 | tf_op jit(solution)/shard_map/all_to_all | solution.py:467
  377.0 13.7 %expert_chunk.4 = (f32[1536,768]{1,0:T(8,128)}, f32[1536,768]{1,0:T(8,128)}, f32[1,512]{1,0:T(1,128)}, bf16[2,192,512]{2,1,0:T(8,128)(2,1)}, bf16[2,192,512]{2,1...) custom-call(s32[4]{0:T(128)} %fusion.25.order_ref, bf16[1536,768]{1,0:T(8,128)(2,1)} %bitcast.50.x_ref, ...), custom_call_target="tpu_custom_call" | custom-call | flops 7247757312 | bytes 30000000 | tf_op jit(solution)/shard_map/expert_chunk/pallas_call | solution.py:251
  390.7 22.5 %expert_chunk.5 = (f32[1536,768]{1,0:T(8,128)}, f32[1536,768]{1,0:T(8,128)}, f32[1,1024]{1,0:T(1,128)}, bf16[2,192,1024]{2,1,0:T(8,128)(2,1)}, bf16[2,192,1024]{...) custom-call(s32[4]{0:T(128)} %fusion.25.order_ref, ...), custom_call_target="tpu_custom_call", output_to_operand_aliasing={{0}: (5, {}), {1}: (6, {})} | custom-call | flops 14495514624 | bytes 30000000 | tf_op jit(solution)/shard_map/expert_chunk/pallas_call | solution.py:251
  413.3 22.5 %expert_chunk.6 = (f32[1536,768]{1,0:T(8,128)}, f32[1536,768]{1,0:T(8,128)}, f32[1,1024]{1,0:T(1,128)}, bf16[2,192,1024]{2,1,0:T(8,128)(2,1)}, bf16[2,192,1024]{...) custom-call(s32[4]{0:T(128)} %fusion.25.order_ref, ...), custom_call_target="tpu_custom_call", output_to_operand_aliasing={{0}: (5, {}), {1}: (6, {})} | custom-call | flops 14495514624 | bytes 30000000 | tf_op jit(solution)/shard_map/expert_chunk/pallas_call | solution.py:251
  435.8 15.7 %expert_chunk.7 = (f32[1536,768]{1,0:T(8,128)}, f32[1536,768]{1,0:T(8,128)}, f32[1,512]{1,0:T(1,128)}, bf16[2,192,512]{2,1,0:T(8,128)(2,1)}, bf16[2,192,512]{2,1...) custom-call(s32[4]{0:T(128)} %fusion.25.order_ref, ...), custom_call_target="tpu_custom_call", output_to_operand_aliasing={{0}: (5, {}), {1}: (6, {})} | custom-call | flops 7247757312 | bytes 30000000 | tf_op jit(solution)/shard_map/expert_chunk/pallas_call | solution.py:251
  451.5 5.2 fusion.1
  503.2 7.6 collective-permute-done.50
  520.4 15.5 %collective-permute-done.32 = bf16[2,192,512]{2,1,0:T(8,128)(2,1)S(1)} collective-permute-done((bf16[2,192,512]{2,1,0:T(8,128)(2,1)S(1)}, bf16[2,192,512]{2,1,0:T(8,128)(2,1)S(1)}, u32[]{:S(2)}, u32[]{:S(2)}) %collective-permute-start.32) | collective-permute-done | bytes 393248 | tf_op jit(solution)/shard_map/ppermute | solution.py:331
  535.9 5.3 collective-permute-start.38
  544.3 5.3 collective-permute-start.36
  570.3 37.0 %attend_backward.1 = (f32[3,200,768]{2,1,0:T(8,128)}, f32[4,768,192]{2,1,0:T(8,128)}, f32[4,768,192]{2,1,0:T(8,128)}, f32[4,768,192]{2,1,0:T(8,128)}, f32[4,768,...) custom-call(f32[3,200,768]{2,1,0:T(8,128)} %fusion.2.n2_grad_ref, bf16[3,200,768]{2,1,0:T(8,128)(2,1)} %grad_ref.1, ...), custom_call_target="tpu_custom_call" | custom-call | flops 8000000000 | bytes 40000000 | tf_op jit(solution)/shard_map/attend_backward/pallas_call | solution.py:188
  637.8 5.6 pad_maximum_fusion
  653.7 21.5 %collective-permute-start.41 = (bf16[2,192,1024]{2,1,0:T(8,128)(2,1)S(1)}, bf16[2,192,1024]{2,1,0:T(8,128)(2,1)}, u32[]{:S(2)}, u32[]{:S(2)}) collective-permute-start(bf16[2,192,1024]{2,1,0:T(8,128)(2,1)S(1)} %copy-done.40), channel_id=1, source_target_pairs={{0,8},{24,16},{1,9},{25,17},{2,10},{26,18},{3,11},{27,19},{4,12},{... | collective-permute-start | bytes 2359304 | tf_op jit(solution)/shard_map/ppermute | solution.py:333
  690.7 26.6 %collective-permute-start.35 = (bf16[2,192,1024]{2,1,0:T(8,128)(2,1)S(1)}, bf16[2,192,1024]{2,1,0:T(8,128)(2,1)}, u32[]{:S(2)}, u32[]{:S(2)}) collective-permute-start(bf16[2,192,1024]{2,1,0:T(8,128)(2,1)S(1)} %copy-done.39), channel_id=1, source_target_pairs={{0,8},{24,16},{1,9},{25,17},{2,10},{26,18},{3,11},{27,19},{4,12},{... | collective-permute-start | bytes 2359304 | tf_op jit(solution)/shard_map/ppermute | solution.py:333
  718.9 8.1 collective-permute-done.34
  734.5 16.4 %collective-permute-done.46 = bf16[2,192,1024]{2,1,0:T(8,128)(2,1)} collective-permute-done((bf16[2,192,1024]{2,1,0:T(8,128)(2,1)}, bf16[2,192,1024]{2,1,0:T(8,128)(2,1)}, u32[]{:S(2)}, u32[]{:S(2)}) %collective-permute-start.46) | collective-permute-done | bytes 786464 | tf_op jit(solution)/shard_map/ppermute | solution.py:336
  759.6 9.2 %collective-permute-done.40 = bf16[2,192,1024]{2,1,0:T(8,128)(2,1)} collective-permute-done((bf16[2,192,1024]{2,1,0:T(8,128)(2,1)}, bf16[2,192,1024]{2,1,0:T(8,128)(2,1)}, u32[]{:S(2)}, u32[]{:S(2)}) %collective-permute-start.40) | collective-permute-done | bytes 786464 | tf_op jit(solution)/shard_map/ppermute | solution.py:336
  776.2 11.6 %all-to-all-done.11 = bf16[8,2,96,256]{3,2,1,0:T(8,128)(2,1)S(1)} async-done(((bf16[8,2,96,256]{3,2,1,0:T(8,128)(2,1)}), bf16[8,2,96,256]{3,2,1,0:T(8,128)(2,1)S(1)}, u32[]{:S(2)}, u32[]{:S(2)}) %all-to-all-start.11) | async-done | bytes 786464 | tf_op jit(solution)/shard_map/all_to_all | solution.py:623
  799.7 21.2 %all-to-all-done.9 = bf16[8,192,768]{2,1,0:T(8,128)(2,1)S(1)} async-done(((bf16[8,192,768]{2,1,0:T(8,128)(2,1)}), bf16[8,192,768]{2,1,0:T(8,128)(2,1)S(1)}, u32[]{:S(2)}, u32[]{:S(2)}) %all-to-all-start.9) | async-done | bytes 2359328 | tf_op jit(solution)/shard_map/all_to_all | solution.py:470
  (502 shorter events, 377.3 us)
Async XLA Ops:
  7.2 264.7 %all-gather.3.cloned.1.call-start = ((), (), s32[]{:S(2)}) async-start(), calls=%async_computation.16 | async-start | bytes 5677056 | tf_op jit(solution)/shard_map/all_gather | solution.py:399
  16.3 91.5 %collective-permute-start.1 = (bf16[200,768]{1,0:T(8,128)(2,1)}, bf16[200,768]{1,0:T(8,128)(2,1)}, u32[]{:S(2)}, u32[]{:S(2)}) collective-permute-start(bf16[200,768]{1,0:T(8,128)(2,1)} %fusion.62), channel_id=1, source_target_pairs={{0,1},{1,0},{2,3},{3,2},{4,5},{5,4},{6,7},{7,6},{8,9},{9,8},{10,11... | collective-permute-start | bytes 921608 | tf_op jit(solution)/shard_map/ppermute | solution.py:451
  106.3 38.4 %collective-permute-start.8 = (bf16[2,192,1024]{2,1,0:T(8,128)(2,1)S(1)}, bf16[2,192,1024]{2,1,0:T(8,128)(2,1)}, u32[]{:S(2)}, u32[]{:S(2)}) collective-permute-start(bf16[2,192,1024]{2,1,0:T(8,128)(2,1)S(1)} %reshape.507), channel_id=1, source_target_pairs={{8,16},{16,8},{9,17},{17,9},{10,18},{18,10},{11,19},{19,11},{12,20... | collective-permute-start | bytes 2359304 | tf_op jit(solution)/shard_map/ppermute | solution.py:296
  119.4 40.9 %collective-permute-start.15 = (bf16[2,192,1024]{2,1,0:T(8,128)(2,1)}, bf16[2,192,1024]{2,1,0:T(8,128)(2,1)}, u32[]{:S(2)}, u32[]{:S(2)}) collective-permute-start(bf16[2,192,1024]{2,1,0:T(8,128)(2,1)} %collective-permute-done.7), channel_id=1, source_target_pairs={{8,0},{16,24},{9,1},{17,25},{10,2},{18,26},{11,3},{19,27},{12,4},{... | collective-permute-start | bytes 2359304 | tf_op jit(solution)/shard_map/ppermute | solution.py:299
  143.4 51.9 %collective-permute-start.20 = (bf16[2,192,1024]{2,1,0:T(8,128)(2,1)}, bf16[2,192,1024]{2,1,0:T(8,128)(2,1)}, u32[]{:S(2)}, u32[]{:S(2)}) collective-permute-start(bf16[2,192,1024]{2,1,0:T(8,128)(2,1)} %reshape.509), channel_id=1, source_target_pairs={{8,0},{16,24},{9,1},{17,25},{10,2},{18,26},{11,3},{19,27},{12,4},{... | collective-permute-start | bytes 2359304 | tf_op jit(solution)/shard_map/ppermute | solution.py:297
  144.7 49.3 %collective-permute-start.9 = (bf16[2,192,1024]{2,1,0:T(8,128)(2,1)}, bf16[2,192,1024]{2,1,0:T(8,128)(2,1)}, u32[]{:S(2)}, u32[]{:S(2)}) collective-permute-start(bf16[2,192,1024]{2,1,0:T(8,128)(2,1)} %collective-permute-done.8), channel_id=1, source_target_pairs={{8,0},{16,24},{9,1},{17,25},{10,2},{18,26},{11,3},{19,27},{12,4},{... | collective-permute-start | bytes 2359304 | tf_op jit(solution)/shard_map/ppermute | solution.py:299
  146.0 64.8 %collective-permute-start.22 = (bf16[2,192,1024]{2,1,0:T(8,128)(2,1)}, bf16[2,192,1024]{2,1,0:T(8,128)(2,1)}, u32[]{:S(2)}, u32[]{:S(2)}) collective-permute-start(bf16[2,192,1024]{2,1,0:T(8,128)(2,1)} %collective-permute-done.21), channel_id=1, source_target_pairs={{8,0},{16,24},{9,1},{17,25},{10,2},{18,26},{11,3},{19,27},{12,4},{... | collective-permute-start | bytes 2359304 | tf_op jit(solution)/shard_map/ppermute | solution.py:300
  166.9 159.7 %all-to-all-start.4 = ((bf16[8,192,768]{2,1,0:T(8,128)(2,1)}), bf16[8,192,768]{2,1,0:T(8,128)(2,1)S(1)}, u32[]{:S(2)}, u32[]{:S(2)}) async-start(bf16[8,192,768]{2,1,0:T(8,128)(2,1)} %pad_maximum_fusion.4), calls=%async_computation.4 | async-start | bytes 4718592 | tf_op jit(solution)/shard_map/all_to_all | solution.py:467
  194.0 64.2 %collective-permute-start.16 = (bf16[2,192,1024]{2,1,0:T(8,128)(2,1)}, bf16[2,192,1024]{2,1,0:T(8,128)(2,1)S(1)}, u32[]{:S(2)}, u32[]{:S(2)}) collective-permute-start(bf16[2,192,1024]{2,1,0:T(8,128)(2,1)} %copy-done.4), channel_id=1, source_target_pairs={{8,0},{16,24},{9,1},{17,25},{10,2},{18,26},{11,3},{19,27},{12,4},{... | collective-permute-start | bytes 2359304 | tf_op jit(solution)/shard_map/ppermute | solution.py:297
  196.0 58.0 %collective-permute-start.14 = (bf16[2,192,512]{2,1,0:T(8,128)(2,1)}, bf16[2,192,512]{2,1,0:T(8,128)(2,1)S(1)}, u32[]{:S(2)}, u32[]{:S(2)}) collective-permute-start(bf16[2,192,512]{2,1,0:T(8,128)(2,1)} %collective-permute-done.13), channel_id=1, source_target_pairs={{8,0},{16,24},{9,1},{17,25},{10,2},{18,26},{11,3},{19,27},{12,4},{... | collective-permute-start | bytes 1179656 | tf_op jit(solution)/shard_map/ppermute | solution.py:299
  197.3 55.5 %collective-permute-start.10 = (bf16[2,192,512]{2,1,0:T(8,128)(2,1)}, bf16[2,192,512]{2,1,0:T(8,128)(2,1)S(1)}, u32[]{:S(2)}, u32[]{:S(2)}) collective-permute-start(bf16[2,192,512]{2,1,0:T(8,128)(2,1)} %reshape.505), channel_id=1, source_target_pairs={{8,0},{16,24},{9,1},{17,25},{10,2},{18,26},{11,3},{19,27},{12,4},{... | collective-permute-start | bytes 1179656 | tf_op jit(solution)/shard_map/ppermute | solution.py:297
  210.8 42.0 %collective-permute-start.12 = (bf16[2,192,512]{2,1,0:T(8,128)(2,1)}, bf16[2,192,512]{2,1,0:T(8,128)(2,1)S(1)}, u32[]{:S(2)}, u32[]{:S(2)}) collective-permute-start(bf16[2,192,512]{2,1,0:T(8,128)(2,1)} %collective-permute-done.11), channel_id=1, source_target_pairs={{8,0},{16,24},{9,1},{17,25},{10,2},{18,26},{11,3},{19,27},{12,4},{... | collective-permute-start | bytes 1179656 | tf_op jit(solution)/shard_map/ppermute | solution.py:300
  217.8 51.7 %collective-permute-start.18 = (bf16[2,192,1024]{2,1,0:T(8,128)(2,1)S(1)}, bf16[2,192,1024]{2,1,0:T(8,128)(2,1)S(1)}, u32[]{:S(2)}, u32[]{:S(2)}) collective-permute-start(bf16[2,192,1024]{2,1,0:T(8,128)(2,1)S(1)} %collective-permute-done.17), channel_id=1, source_target_pairs={{8,0},{16,24},{9,1},{17,25},{10,2},{18,26},{11,3},{19,27},{12,4},{... | collective-permute-start | bytes 2359304 | tf_op jit(solution)/shard_map/ppermute | solution.py:300
  335.8 41.3 %all-to-all-start.5 = ((bf16[8,192,768]{2,1,0:T(8,128)(2,1)}), bf16[8,192,768]{2,1,0:T(8,128)(2,1)}, u32[]{:S(2)}, u32[]{:S(2)}) async-start(bf16[8,192,768]{2,1,0:T(8,128)(2,1)} %pad_maximum_fusion.3), calls=%async_computation.5 | async-start | bytes 4718592 | tf_op jit(solution)/shard_map/all_to_all | solution.py:467
  464.7 52.4 %collective-permute-start.48 = (bf16[2,192,512]{2,1,0:T(8,128)(2,1)}, bf16[2,192,512]{2,1,0:T(8,128)(2,1)}, u32[]{:S(2)}, u32[]{:S(2)}) collective-permute-start(bf16[2,192,512]{2,1,0:T(8,128)(2,1)} %get-tuple-element.129), channel_id=1, source_target_pairs={{0,8},{24,16},{1,9},{25,17},{2,10},{26,18},{3,11},{27,19},{4,12},{... | collective-permute-start | bytes 1179656 | tf_op jit(solution)/shard_map/ppermute | solution.py:332
  468.0 181.5 %collective-permute-start.47 = (bf16[2,192,512]{2,1,0:T(8,128)(2,1)}, bf16[2,192,512]{2,1,0:T(8,128)(2,1)}, u32[]{:S(2)}, u32[]{:S(2)}) collective-permute-start(bf16[2,192,512]{2,1,0:T(8,128)(2,1)} %get-tuple-element.128), channel_id=1, source_target_pairs={{0,8},{24,16},{1,9},{25,17},{2,10},{26,18},{3,11},{27,19},{4,12},{... | collective-permute-start | bytes 1179656 | tf_op jit(solution)/shard_map/ppermute | solution.py:333
  470.1 80.4 %collective-permute-start.44 = (bf16[2,192,1024]{2,1,0:T(8,128)(2,1)}, bf16[2,192,1024]{2,1,0:T(8,128)(2,1)}, u32[]{:S(2)}, u32[]{:S(2)}) collective-permute-start(bf16[2,192,1024]{2,1,0:T(8,128)(2,1)} %get-tuple-element.126), channel_id=1, source_target_pairs={{0,8},{24,16},{1,9},{25,17},{2,10},{26,18},{3,11},{27,19},{4,12},{... | collective-permute-start | bytes 2359304 | tf_op jit(solution)/shard_map/ppermute | solution.py:331
  480.3 74.5 %all-to-all-start.7 = ((bf16[8,192,768]{2,1,0:T(8,128)(2,1)}), bf16[8,192,768]{2,1,0:T(8,128)(2,1)S(1)}, u32[]{:S(2)}, u32[]{:S(2)}) async-start(bf16[8,192,768]{2,1,0:T(8,128)(2,1)} %bitcast.70), calls=%async_computation.7 | async-start | bytes 4718592 | tf_op jit(solution)/shard_map/all_to_all | solution.py:470
  484.4 347.2 %reduce-scatter.2.cloned.1.call-start = ((), (), s32[]{:S(2)}) async-start(), calls=%async_computation.15 | async-start | bytes 6488064 | tf_op jit(solution)/shard_map/reduce_scatter | solution.py:612
  491.9 63.5 %collective-permute-start.42 = (bf16[2,192,1024]{2,1,0:T(8,128)(2,1)}, bf16[2,192,1024]{2,1,0:T(8,128)(2,1)}, u32[]{:S(2)}, u32[]{:S(2)}) collective-permute-start(bf16[2,192,1024]{2,1,0:T(8,128)(2,1)} %get-tuple-element.125), channel_id=1, source_target_pairs={{0,8},{24,16},{1,9},{25,17},{2,10},{26,18},{3,11},{27,19},{4,12},{... | collective-permute-start | bytes 2359304 | tf_op jit(solution)/shard_map/ppermute | solution.py:332
  544.3 99.1 %collective-permute-start.36 = (bf16[2,192,1024]{2,1,0:T(8,128)(2,1)}, bf16[2,192,1024]{2,1,0:T(8,128)(2,1)}, u32[]{:S(2)}, u32[]{:S(2)}) collective-permute-start(bf16[2,192,1024]{2,1,0:T(8,128)(2,1)} %get-tuple-element.121), channel_id=1, source_target_pairs={{0,8},{24,16},{1,9},{25,17},{2,10},{26,18},{3,11},{27,19},{4,12},{... | collective-permute-start | bytes 2359304 | tf_op jit(solution)/shard_map/ppermute | solution.py:332
  550.5 125.9 %collective-permute-start.29 = (bf16[2,192,512]{2,1,0:T(8,128)(2,1)}, bf16[2,192,512]{2,1,0:T(8,128)(2,1)}, u32[]{:S(2)}, u32[]{:S(2)}) collective-permute-start(bf16[2,192,512]{2,1,0:T(8,128)(2,1)} %get-tuple-element.116), channel_id=1, source_target_pairs={{0,8},{24,16},{1,9},{25,17},{2,10},{26,18},{3,11},{27,19},{4,12},{... | collective-permute-start | bytes 1179656 | tf_op jit(solution)/shard_map/ppermute | solution.py:333
  561.3 86.4 %collective-permute-start.51 = (bf16[2,192,512]{2,1,0:T(8,128)(2,1)}, bf16[2,192,512]{2,1,0:T(8,128)(2,1)}, u32[]{:S(2)}, u32[]{:S(2)}) collective-permute-start(bf16[2,192,512]{2,1,0:T(8,128)(2,1)} %add_convert_fusion.10), channel_id=1, source_target_pairs={{8,16},{16,8},{9,17},{17,9},{10,18},{18,10},{11,19},{19,11},{12,20... | collective-permute-start | bytes 1179656 | tf_op jit(solution)/shard_map/ppermute | solution.py:334
  567.1 83.3 %collective-permute-start.33 = (bf16[2,192,512]{2,1,0:T(8,128)(2,1)}, bf16[2,192,512]{2,1,0:T(8,128)(2,1)}, u32[]{:S(2)}, u32[]{:S(2)}) collective-permute-start(bf16[2,192,512]{2,1,0:T(8,128)(2,1)} %add_convert_fusion.14), channel_id=1, source_target_pairs={{8,16},{16,8},{9,17},{17,9},{10,18},{18,10},{11,19},{19,11},{12,20... | collective-permute-start | bytes 1179656 | tf_op jit(solution)/shard_map/ppermute | solution.py:334
  676.4 41.0 %collective-permute-start.31 = (bf16[2,192,512]{2,1,0:T(8,128)(2,1)}, bf16[2,192,512]{2,1,0:T(8,128)(2,1)}, u32[]{:S(2)}, u32[]{:S(2)}) collective-permute-start(bf16[2,192,512]{2,1,0:T(8,128)(2,1)} %add_convert_fusion.15), channel_id=1, source_target_pairs={{8,16},{16,8},{9,17},{17,9},{10,18},{18,10},{11,19},{19,11},{12,20... | collective-permute-start | bytes 1179656 | tf_op jit(solution)/shard_map/ppermute | solution.py:335
  677.8 56.7 %collective-permute-start.43 = (bf16[2,192,1024]{2,1,0:T(8,128)(2,1)}, bf16[2,192,1024]{2,1,0:T(8,128)(2,1)}, u32[]{:S(2)}, u32[]{:S(2)}) collective-permute-start(bf16[2,192,1024]{2,1,0:T(8,128)(2,1)} %add_convert_fusion.3), channel_id=1, source_target_pairs={{8,16},{16,8},{9,17},{17,9},{10,18},{18,10},{11,19},{19,11},{12,20... | collective-permute-start | bytes 2359304 | tf_op jit(solution)/shard_map/ppermute | solution.py:335
  679.3 47.7 %collective-permute-start.34 = (bf16[2,192,512]{2,1,0:T(8,128)(2,1)}, bf16[2,192,512]{2,1,0:T(8,128)(2,1)}, u32[]{:S(2)}, u32[]{:S(2)}) collective-permute-start(bf16[2,192,512]{2,1,0:T(8,128)(2,1)} %add_convert_fusion.13), channel_id=1, source_target_pairs={{8,0},{16,24},{9,1},{17,25},{10,2},{18,26},{11,3},{19,27},{12,4},{... | collective-permute-start | bytes 1179656 | tf_op jit(solution)/shard_map/ppermute | solution.py:336
  680.6 70.3 %collective-permute-start.46 = (bf16[2,192,1024]{2,1,0:T(8,128)(2,1)}, bf16[2,192,1024]{2,1,0:T(8,128)(2,1)}, u32[]{:S(2)}, u32[]{:S(2)}) collective-permute-start(bf16[2,192,1024]{2,1,0:T(8,128)(2,1)} %add_convert_fusion.1), channel_id=1, source_target_pairs={{8,0},{16,24},{9,1},{17,25},{10,2},{18,26},{11,3},{19,27},{12,4},{... | collective-permute-start | bytes 2359304 | tf_op jit(solution)/shard_map/ppermute | solution.py:336
  684.2 46.4 %all-to-all-start.13 = ((bf16[8,2,96,128]{3,2,1,0:T(8,128)(2,1)}), bf16[8,2,96,128]{3,2,1,0:T(8,128)(2,1)S(1)}, u32[]{:S(2)}, u32[]{:S(2)}) async-start(bf16[8,2,96,128]{3,2,1,0:T(8,128)(2,1)} %bitcast.120), calls=%async_computation.14 | async-start | bytes 786432 | tf_op jit(solution)/shard_map/all_to_all | solution.py:623
  690.7 68.9 %collective-permute-start.35 = (bf16[2,192,1024]{2,1,0:T(8,128)(2,1)S(1)}, bf16[2,192,1024]{2,1,0:T(8,128)(2,1)}, u32[]{:S(2)}, u32[]{:S(2)}) collective-permute-start(bf16[2,192,1024]{2,1,0:T(8,128)(2,1)S(1)} %copy-done.39), channel_id=1, source_target_pairs={{0,8},{24,16},{1,9},{25,17},{2,10},{26,18},{3,11},{27,19},{4,12},{... | collective-permute-start | bytes 2359304 | tf_op jit(solution)/shard_map/ppermute | solution.py:333
  717.3 42.3 %collective-permute-start.37 = (bf16[2,192,1024]{2,1,0:T(8,128)(2,1)}, bf16[2,192,1024]{2,1,0:T(8,128)(2,1)}, u32[]{:S(2)}, u32[]{:S(2)}) collective-permute-start(bf16[2,192,1024]{2,1,0:T(8,128)(2,1)} %add_convert_fusion.7), channel_id=1, source_target_pairs={{8,16},{16,8},{9,17},{17,9},{10,18},{18,10},{11,19},{19,11},{12,20... | collective-permute-start | bytes 2359304 | tf_op jit(solution)/shard_map/ppermute | solution.py:335
  727.0 41.9 %collective-permute-start.40 = (bf16[2,192,1024]{2,1,0:T(8,128)(2,1)}, bf16[2,192,1024]{2,1,0:T(8,128)(2,1)}, u32[]{:S(2)}, u32[]{:S(2)}) collective-permute-start(bf16[2,192,1024]{2,1,0:T(8,128)(2,1)} %add_convert_fusion.5), channel_id=1, source_target_pairs={{8,0},{16,24},{9,1},{17,25},{10,2},{18,26},{11,3},{19,27},{12,4},{... | collective-permute-start | bytes 2359304 | tf_op jit(solution)/shard_map/ppermute | solution.py:336
  (106 other events, 1712.3 us)
Sparse Core Ops, SparseCore 0:
  15.7 87.1 all-gather.2
  643.5 131.7 reduce-scatter.1

commit v3 on v2

v3 whole, which is shorter than its diff:
```python
import functools
import jax
import jax.numpy as jnp
from jax import lax
from jax.experimental import pallas as pl
from jax.experimental.pallas import tpu as pltpu
from jax.sharding import PartitionSpec as P

HD = 64
EPSILON = 1e-06
NEGATIVE = -1e30
F32 = jnp.float32
BF16 = jnp.bfloat16


def dot(left, right, left_dim=1, right_dim=0):
    return lax.dot_general(
        left, right, (((left_dim,), (right_dim,)), ((), ())), preferred_element_type=F32
    )


def norm_forward(values, gains, shifts):
    middle = jnp.mean(values, -1, keepdims=True)
    centred = values - middle
    inverse = lax.rsqrt(jnp.mean(centred * centred, -1, keepdims=True) + EPSILON)
    unit_rows = centred * inverse
    return (unit_rows * gains + shifts, unit_rows, inverse)


def norm_backward(grad_rows, unit_rows, inverse, gains):
    scaled = grad_rows * gains
    return inverse * (
        scaled
        - jnp.mean(scaled, -1, keepdims=True)
        - unit_rows * jnp.mean(scaled * unit_rows, -1, keepdims=True)
    )


def head_masks(width):
    lane = lax.broadcasted_iota(jnp.int32, (1, width), 1)
    return [(lane // HD == k) for k in range(width // HD)]


def arrange(w_ref, *parts):
    width = parts[0].shape[2]
    for t in range(w_ref.shape[0]):
        packed = w_ref[t]
        for k, ref in enumerate(parts):
            ref[t] = packed[:, k * width : (k + 1) * width]


def put_rows(ref, values):
    rows, columns = values.shape
    spare = jnp.zeros((ref.shape[0] - rows, columns), values.dtype)
    ref[...] = jnp.concatenate([values, spare], 0).astype(ref.dtype)


def attend_forward_kernel(
    place_ref, tokens_ref, mask_ref, lines_ref, bias_ref, *refs,
):
    (
        n1_ref, n2_ref, h_ref, q_ref, k_ref, v_ref, o_ref, lse_ref,
        wq_ref, wk_ref, wv_ref, wo_ref, all_ref, sem,
    ) = refs[-14:]
    packs = refs[:-14]

    @pl.when(pl.program_id(0) == 0)
    def _():
        if len(packs) == 1:
            pltpu.make_async_copy(packs[0], all_ref, sem).start()
        else:
            z, x, y, c = [place_ref[k] for k in range(4)]
            part = all_ref.shape[1] // 8
            for index, ref in enumerate(packs):
                dx, dy, dc = index & 1, (index >> 1) & 1, index >> 2
                t = (y ^ dy) * 2 + (c ^ dc)
                for back in range(4):
                    row = (((z - back) & 3) * 2 + (x ^ dx)) * part
                    pltpu.make_async_copy(
                        ref.at[back, pl.ds(0, part)],
                        all_ref.at[t, pl.ds(pl.multiple_of(row, 32), part)],
                        sem,
                    ).start()
        pltpu.make_async_copy(all_ref, all_ref, sem).wait()
        arrange(all_ref, wq_ref, wk_ref, wv_ref, wo_ref)

    x = tokens_ref[0].astype(F32)
    n1, _, _ = norm_forward(x, lines_ref[0:1, :], lines_ref[1:2, :])
    put_rows(n1_ref.at[0], n1)
    n1 = n1.astype(BF16)
    width = wq_ref.shape[2]
    masks = head_masks(width)
    keys = mask_ref[0] > 0
    total = x + lines_ref[4:5, :]
    for t in range(wq_ref.shape[0]):
        q = (dot(n1, wq_ref[t]) + bias_ref[t, 0:1, :]).astype(BF16)
        k = dot(n1, wk_ref[t]).astype(BF16)
        v = (dot(n1, wv_ref[t]) + bias_ref[t, 1:2, :]).astype(BF16)
        q_ref[0, t] = q
        k_ref[0, t] = k
        v_ref[0, t] = v
        scaled = q * jnp.asarray(HD ** (-0.5), BF16)
        o = jnp.zeros(q.shape, F32)
        for h, here in enumerate(masks):
            s = dot(jnp.where(here, scaled, jnp.zeros_like(scaled)), k, 1, 1)
            s = jnp.where(keys, s, NEGATIVE)
            largest = jnp.max(s, -1, keepdims=True)
            e = jnp.exp(s - largest)
            total_e = jnp.sum(e, -1, keepdims=True)
            p = (e / total_e).astype(BF16)
            o = jnp.where(here, dot(p, v), o)
            index = t * len(masks) + h
            lse_ref[0, :, index : index + 1] = largest + jnp.log(total_e)
        put_rows(o_ref.at[0, t], o)
        total = total + dot(o.astype(BF16), wo_ref[t], 1, 1)
    h_ref[0] = total
    n2, _, _ = norm_forward(total, lines_ref[5:6, :], lines_ref[6:7, :])
    n2_ref[0] = n2.astype(BF16)


def whole(shape):
    return pl.BlockSpec(shape, lambda b: (0,) * len(shape))


def by_image(shape):
    return pl.BlockSpec((1,) + shape[1:], lambda b: (b,) + (0,) * (len(shape) - 1))


def padded(rows):
    return -(-rows // 16) * 16


def attend_forward(place, tokens_in, mask, lines, bias_pairs, packs, width):
    images, sequence, model = tokens_in.shape
    quarter = model // width
    rows = (images, sequence, model)
    heads = (images, quarter, sequence, width)
    columns = (quarter, model, width)
    outs = [
        ((images, padded(sequence), model), BF16), (rows, BF16), (rows, F32), (heads, BF16), (heads, BF16),
        (heads, BF16), ((images, quarter, padded(sequence), width), BF16), ((images, sequence, 128), F32),
        (columns, BF16), (columns, BF16), (columns, BF16), (columns, BF16),
    ]
    place_spec = lambda spec: pl.BlockSpec(spec.block_shape, lambda b, p: spec.index_map(b))
    in_specs = [by_image(tokens_in.shape), by_image(mask.shape), whole(lines.shape), whole(bias_pairs.shape)]
    out_specs = [by_image(s) for s, _ in outs[:8]] + [whole(s) for s, _ in outs[8:]]
    return pl.pallas_call(
        attend_forward_kernel,
        grid_spec=pltpu.PrefetchScalarGridSpec(
            num_scalar_prefetch=1,
            grid=(images,),
            in_specs=[place_spec(s) for s in in_specs]
            + [pl.BlockSpec(memory_space=pl.ANY)] * len(packs),
            out_specs=[place_spec(s) for s in out_specs],
            scratch_shapes=[pltpu.VMEM((quarter, model, 4 * width), BF16), pltpu.SemaphoreType.DMA(())],
        ),
        out_shape=[jax.ShapeDtypeStruct(s, d) for s, d in outs],
        compiler_params=pltpu.CompilerParams(vmem_limit_bytes=56 * 2**20),
        cost_estimate=pl.CostEstimate(flops=3 * 10**9, bytes_accessed=6 * 10**7, transcendentals=2 * 10**6),
        name="attend_forward",
    )(place, tokens_in, mask, lines, bias_pairs, *packs)


def attend_backward_kernel(
    n2_grad_ref, grad_ref, h_ref, mask_ref, wo_ref, lines_ref, q_ref, k_ref, v_ref, lse_ref,
    h_grad_ref, hb_ref, dq_ref, dk_ref, dv_ref, vec_ref, pair_ref,
):
    @pl.when(pl.program_id(0) == 0)
    def _():
        vec_ref[...] = jnp.zeros_like(vec_ref)
        pair_ref[...] = jnp.zeros_like(pair_ref)

    n2_grad = n2_grad_ref[0]
    _, unit_two, inverse_two = norm_forward(h_ref[0], lines_ref[5:6, :], lines_ref[6:7, :])
    vec_ref[1:2, :] += jnp.sum(n2_grad * unit_two, 0, keepdims=True)
    vec_ref[2:3, :] += jnp.sum(n2_grad, 0, keepdims=True)
    h_grad = grad_ref[0].astype(F32) + norm_backward(
        n2_grad, unit_two, inverse_two, lines_ref[5:6, :]
    )
    vec_ref[0:1, :] += jnp.sum(h_grad, 0, keepdims=True)
    h_grad_ref[0] = h_grad
    put_rows(hb_ref.at[0], h_grad)
    hb = h_grad.astype(BF16)
    width = wo_ref.shape[2]
    masks = head_masks(width)
    keys = mask_ref[0] > 0
    scale = HD ** (-0.5)
    for t in range(wo_ref.shape[0]):
        do = dot(hb, wo_ref[t]).astype(BF16)
        q, k, v = q_ref[0, t], k_ref[0, t], v_ref[0, t]
        zero = jnp.zeros_like(q)
        scaled = q * jnp.asarray(scale, BF16)
        dq = jnp.zeros(q.shape, F32)
        dk = jnp.zeros(q.shape, F32)
        dv = jnp.zeros(q.shape, F32)
        for h, here in enumerate(masks):
            index = t * len(masks) + h
            s = dot(jnp.where(here, scaled, zero), k, 1, 1)
            s = jnp.where(keys, s, NEGATIVE)
            p = jnp.exp(s - lse_ref[0, :, index : index + 1])
            dp = dot(jnp.where(here, do, zero), v, 1, 1)
            ds = p * (dp - jnp.sum(p * dp, -1, keepdims=True))
            ds = ds.astype(BF16)
            dv = jnp.where(here, dot(p.astype(BF16), do, 0, 0), dv)
            dq = jnp.where(here, dot(ds, k), dq)
            dk = jnp.where(here, dot(ds, q, 0, 0), dk)
        dq = (dq * scale).astype(BF16).astype(F32)
        dv = dv.astype(BF16).astype(F32)
        pair_ref[t, 0:1, :] += jnp.sum(dq, 0, keepdims=True)
        pair_ref[t, 1:2, :] += jnp.sum(dv, 0, keepdims=True)
        put_rows(dq_ref.at[0, t], dq)
        put_rows(dk_ref.at[0, t], dk * scale)
        put_rows(dv_ref.at[0, t], dv)


def attend_backward(n2_grad, out_grad, h, mask, wo, lines, q, k, v, lse):
    ins = (n2_grad, out_grad, h, mask, wo, lines, q, k, v, lse)
    shared = {4, 5}
    images, sequence, model = n2_grad.shape
    quarter, _, width = wo.shape
    heads = ((images, quarter, padded(sequence), width), BF16)
    outs = [
        (n2_grad.shape, F32), ((images, padded(sequence), model), BF16), heads, heads, heads,
        ((8, model), F32), ((quarter, 8, width), F32),
    ]
    return pl.pallas_call(
        attend_backward_kernel,
        grid=(images,),
        in_specs=[whole(a.shape) if i in shared else by_image(a.shape) for i, a in enumerate(ins)],
        out_specs=[by_image(s) for s, _ in outs[:5]] + [whole(s) for s, _ in outs[5:]],
        out_shape=[jax.ShapeDtypeStruct(s, d) for s, d in outs],
        compiler_params=pltpu.CompilerParams(vmem_limit_bytes=56 * 2**20),
        cost_estimate=pl.CostEstimate(flops=4 * 10**9, bytes_accessed=7 * 10**7, transcendentals=2 * 10**6),
        name="attend_backward",
    )(*ins)


def attend_weights_kernel(n1_ref, hb_ref, dq_ref, dk_ref, dv_ref, o_ref, *refs):
    out_ref = refs[-1]
    width = dq_ref.shape[3]
    n1 = n1_ref[...].reshape(-1, n1_ref.shape[2])
    hb = hb_ref[...].reshape(-1, n1_ref.shape[2])
    for k, (left, ref) in enumerate(((n1, dq_ref), (n1, dk_ref), (n1, dv_ref), (hb, o_ref))):
        sums = dot(left, ref[...].reshape(-1, width), 0, 0).astype(out_ref.dtype)
        columns = slice(k * width, (k + 1) * width)
        if len(refs) == 1:
            out_ref[0, :, columns] = sums
            continue
        part = sums.shape[0] // 8
        for z in range(4):
            for x in range(2):
                start = (z * 2 + x) * part
                out_ref[0, x, 0, z, :part, columns] = sums[start : start + part]
    if len(refs) == 2:
        for z in range(4):
            for x in range(2):
                out_ref[0, x, 0, z, part:, :] = refs[0][z * 2 + x]


def attend_weights(n1, hb, dq, dk, dv, o, extra):
    images, quarter, rows, width = dq.shape
    model = n1.shape[2]
    heads = pl.BlockSpec((images, 1, rows, width), lambda t: (0, t, 0, 0))
    if extra is None:
        out_spec = pl.BlockSpec((1, model, 4 * width), lambda t: (t, 0, 0))
        out_shape = jax.ShapeDtypeStruct((quarter, model, 4 * width), F32)
    else:
        depth = model // 8 + extra.shape[1]
        out_spec = pl.BlockSpec(
            (1, 2, 1, 4, depth, model), lambda t: (t % 2, 0, t // 2, 0, 0, 0)
        )
        out_shape = jax.ShapeDtypeStruct((2, 2, 2, 4, depth, model), BF16)
    extras = [] if extra is None else [extra]
    return pl.pallas_call(
        attend_weights_kernel,
        grid=(quarter,),
        in_specs=[whole(n1.shape), whole(hb.shape)] + [heads] * 4 + [whole(e.shape) for e in extras],
        out_specs=out_spec,
        out_shape=out_shape,
        compiler_params=pltpu.CompilerParams(vmem_limit_bytes=56 * 2**20),
        cost_estimate=pl.CostEstimate(flops=3 * 10**9, bytes_accessed=3 * 10**7, transcendentals=0),
        name="attend_weights",
    )(n1, hb, dq, dk, dv, o, *extras)


def input_backward_kernel(
    h_grad_ref, tokens_ref, wq_ref, wk_ref, wv_ref, lines_ref, dq_ref, dk_ref, dv_ref,
    input_grad_ref, vec_ref,
):
    @pl.when(pl.program_id(0) == 0)
    def _():
        vec_ref[...] = jnp.zeros_like(vec_ref)

    rows = tokens_ref.shape[1]
    n1_grad = jnp.zeros((dq_ref.shape[2], tokens_ref.shape[2]), F32)
    for t in range(wq_ref.shape[0]):
        for grads, weights in ((dq_ref, wq_ref), (dk_ref, wk_ref), (dv_ref, wv_ref)):
            n1_grad += dot(grads[0, t], weights[t], 1, 1)
    n1_grad = n1_grad[:rows]
    _, unit_one, inverse_one = norm_forward(
        tokens_ref[0].astype(F32), lines_ref[0:1, :], lines_ref[1:2, :]
    )
    vec_ref[0:1, :] += jnp.sum(n1_grad * unit_one, 0, keepdims=True)
    vec_ref[1:2, :] += jnp.sum(n1_grad, 0, keepdims=True)
    input_grad_ref[0] = h_grad_ref[0] + norm_backward(
        n1_grad, unit_one, inverse_one, lines_ref[0:1, :]
    )


def input_backward(h_grad, tokens_in, wq, wk, wv, lines, dq, dk, dv):
    ins = (h_grad, tokens_in, wq, wk, wv, lines, dq, dk, dv)
    outs = [(h_grad.shape, F32), ((8, wq.shape[1]), F32)]
    return pl.pallas_call(
        input_backward_kernel,
        grid=(h_grad.shape[0],),
        in_specs=[whole(a.shape) if 2 <= i <= 5 else by_image(a.shape) for i, a in enumerate(ins)],
        out_specs=[by_image(outs[0][0]), whole(outs[1][0])],
        out_shape=[jax.ShapeDtypeStruct(s, d) for s, d in outs],
        compiler_params=pltpu.CompilerParams(vmem_limit_bytes=56 * 2**20),
        cost_estimate=pl.CostEstimate(flops=3 * 10**9, bytes_accessed=3 * 10**7, transcendentals=0),
        name="input_backward",
    )(*ins)


def pack_experts_kernel(up_ref, down_ref, *refs):
    up = up_ref[0].astype(BF16)
    down = down_ref[0].T.astype(BF16)
    start = 0
    for ref in refs:
        stop = start + ref.shape[3]
        ref[0, 0] = up[:, start:stop]
        ref[0, 1] = down[:, start:stop]
        start = stop


def pack_experts(up, down, sizes):
    experts, part, units = up.shape
    outs = [(experts, 2, part, size) for size in sizes]
    return pl.pallas_call(
        pack_experts_kernel,
        grid=(experts,),
        in_specs=[by_image(up.shape), by_image(down.shape)],
        out_specs=[by_image(s) for s in outs],
        out_shape=[jax.ShapeDtypeStruct(s, BF16) for s in outs],
        compiler_params=pltpu.CompilerParams(vmem_limit_bytes=32 * 2**20),
        cost_estimate=pl.CostEstimate(flops=0, bytes_accessed=8 * 10**6, transcendentals=0),
        name="pack_experts",
    )(up, down)


def to_column(line):
    return jnp.broadcast_to(line, (128, 256)).T[:, :1]


def to_line(column):
    return jnp.broadcast_to(column, (256, 128)).T[:1, :]


def expert_kernel(first, last, count, order_ref, x_ref, g_ref, b_ref, *refs):
    pieces, refs = refs[:count], refs[count:]
    if not first:
        (y_in, p_in), refs = refs[:2], refs[2:]
    (y_out, p_out, bias_ref), refs = refs[:3], refs[3:]
    acc_ref, w_ref, sem = refs[-3:]
    grads = refs[:-3]
    step = pl.program_id(0)
    model = w_ref.shape[1]

    @pl.when(step == 0)
    def _():
        if count == 1:
            pltpu.make_async_copy(pieces[0], w_ref, sem).start()
        else:
            part, units = pieces[0].shape[2:]
            end = order_ref[4] == 1

            def load(ref, slot):
                for p in range(8):
                    row = pl.multiple_of(slot * (2 * part) + (p // 4) * part, 32)
                    pltpu.make_async_copy(
                        ref.at[p],
                        w_ref.at[:, pl.ds(row, part), pl.ds((p % 4) * units, units)],
                        sem,
                    ).start()

            load(pieces[0], order_ref[0])
            for k in range(1, 4):
                pl.when(end)(functools.partial(load, pieces[k], order_ref[k]))
                pl.when(jnp.logical_not(end))(functools.partial(load, pieces[k + 3], order_ref[k]))
        acc_ref[...] = jnp.zeros_like(acc_ref)
        bias_ref[...] = jnp.zeros_like(bias_ref)
        pltpu.make_async_copy(w_ref, w_ref, sem).wait()

    sources, slots, _ = g_ref.shape
    x = x_ref[:, :slots].reshape(-1, model)
    g_raw = g_ref[...].reshape(-1, model)
    gates = []
    for k in range(sources):
        parts = x_ref[k, slots : slots + 16, :256].astype(F32)
        gates.append(to_column(parts[0:1] + parts[1:2])[:slots])
    gate = jnp.concatenate(gates, 0)
    g = (g_raw.astype(F32) * gate).astype(BF16)
    hidden = dot(x, w_ref[0]) + b_ref[...]
    cdf = 0.5 * (1.0 + lax.erf(hidden * (0.5 ** 0.5)))
    active = (hidden * cdf).astype(BF16)
    slope = cdf + hidden * (jnp.exp(-0.5 * hidden * hidden) * 0.3989422804014327)
    hidden_grad = (dot(g, w_ref[1]) * slope).astype(BF16)
    y = dot(active, w_ref[1], 1, 1)
    p = dot(hidden_grad, w_ref[0], 1, 1)
    if not first:
        y = y_in[...].reshape(-1, model) + y
        p = p_in[...].reshape(-1, model) + p
    if not last:
        y_out[...] = y.reshape(sources, slots, model)
        p_out[...] = p.reshape(sources, slots, model)
    else:
        y_out[...] = (y * gate).astype(BF16).reshape(sources, slots, model)
        p_out[:, :slots] = p.astype(BF16).reshape(sources, slots, model)
        gate_grad = jnp.sum(g_raw.astype(F32) * y, -1, keepdims=True)
        for k in range(sources):
            own = gate_grad[k * slots : (k + 1) * slots]
            line = to_line(jnp.concatenate([own, jnp.zeros((256 - slots, 1), F32)], 0))
            high = line.astype(BF16)
            low = (line - high.astype(F32)).astype(BF16)
            block = jnp.concatenate([high, low, jnp.zeros((14, 256), BF16)], 0)
            p_out[k, slots:] = jnp.concatenate([block, jnp.zeros((16, model - 256), BF16)], 1)
    bias_ref[...] += jnp.sum(hidden_grad.astype(F32), 0, keepdims=True)
    acc_ref[0] += dot(x, hidden_grad, 0, 0)
    acc_ref[1] += dot(g, active, 0, 0)

    @pl.when(step == pl.num_programs(0) - 1)
    def _():
        if len(grads) == 1:
            grads[0][...] = acc_ref[...]
        else:
            own_ref, rest_ref, near_ref = grads
            part, units = own_ref.shape[2:]
            for k in range(4):
                for q in range(8):
                    row = pl.multiple_of(order_ref[k] * (2 * part) + (q // 4) * part, 32)
                    columns = slice((q % 4) * units, (q % 4 + 1) * units)
                    block = acc_ref[:, pl.ds(row, part), columns].astype(BF16)
                    if k == 0:
                        own_ref[q] = block
                    else:
                        rest_ref[k - 1, q] = block
                    if k == 1:
                        near_ref[q] = block


def expert_chunk(order, x, g, b, sums, pieces, last):
    experts, slots, model = g.shape
    units = b.shape[1]
    first = sums is None
    step = 2
    block = lambda rows: pl.BlockSpec((step, rows, model), lambda i, o: (i, 0, 0))
    full = lambda shape: pl.BlockSpec(shape, lambda i, o: (0,) * len(shape))
    ins = [x, g, b] + list(pieces) + ([] if first else list(sums))
    in_specs = [block(x.shape[1]), block(slots), full(b.shape)]
    in_specs += [pl.BlockSpec(memory_space=pl.ANY)] * len(pieces)
    in_specs += [] if first else [block(slots)] * 2
    rows = (experts, slots, model)
    if last:
        outs = [(rows, BF16), (x.shape, BF16)]
    else:
        outs = [(rows, F32), (rows, F32)]
    out_specs = [block(s[1]) for s, _ in outs]
    outs.append((b.shape, F32))
    if len(pieces) == 1:
        outs.append(((2, model, units), F32))
    else:
        shape = pieces[0].shape
        outs += [(shape, BF16), ((3,) + shape, BF16), (shape, BF16)]
    out_specs += [full(s) for s, _ in outs[2:]]
    base = 4 + len(pieces)
    return pl.pallas_call(
        functools.partial(expert_kernel, first, last, len(pieces)),
        grid_spec=pltpu.PrefetchScalarGridSpec(
            num_scalar_prefetch=1,
            grid=(experts // step,),
            in_specs=in_specs,
            out_specs=out_specs,
            scratch_shapes=[
                pltpu.VMEM((2, model, units), F32),
                pltpu.VMEM((2, model, units), BF16),
                pltpu.SemaphoreType.DMA(()),
            ],
        ),
        out_shape=[jax.ShapeDtypeStruct(s, d) for s, d in outs],
        input_output_aliases={} if first or last else {base: 0, base + 1: 1},
        compiler_params=pltpu.CompilerParams(vmem_limit_bytes=58 * 2**20),
        cost_estimate=pl.CostEstimate(
            flops=12 * experts * slots * model * units, bytes_accessed=3 * 10**7,
            transcendentals=2 * experts * slots * units,
        ),
        name="expert_chunk",
    )(order, *ins)


CAP = 128
GROUP_IMG = 2
CHUNK = 128
HIGHEST = lax.Precision.HIGHEST
TENSOR = ("y", "c")
PLANE = ("x", "y", "c")
EVERY = ("y", "c", "z", "x")
INWARD = [(0, 1), (3, 2)]
MIDDLE = [(1, 2), (2, 1)]
OUTWARD = [(1, 0), (2, 3)]
ORDER = ((0, 1, 2, 3), (1, 0, 2, 3), (2, 3, 1, 0), (3, 2, 1, 0))


def tie(values, *events):
    events = [e for e in events if e is not None]
    if not events:
        return values
    return lax.optimization_barrier((values, *events))[0]


class Line:
    def __init__(self, own, length):
        self.own, self.length = own, length

    def start(self, *events):
        if self.length != 4:
            self.full = lax.all_gather(self.own, "z", axis=1, tiled=True)
            return
        own = tie(self.own, *events)
        self.inward = lax.ppermute(own, "z", INWARD)
        self.outward_one = lax.ppermute(own, "z", OUTWARD)
        self.middle_one = lax.ppermute(own, "z", MIDDLE)
        self.outward_two = lax.ppermute(own, "z", [(1, 3), (2, 0)])
        self.middle_two = lax.ppermute(self.inward, "z", MIDDLE)
        self.outward_three = lax.ppermute(self.middle_two, "z", OUTWARD)

    def early(self):
        if self.length != 4:
            return []
        return [self.inward, self.middle_one, self.outward_one]

    def result(self):
        if self.length != 4:
            return [self.full]
        return [
            self.own, self.outward_one, self.outward_two, self.outward_three,
            self.inward, self.middle_one, self.middle_two,
        ]


def add(*terms):
    return sum(term.astype(F32) for term in terms).astype(BF16)


class Reduce:
    def __init__(self, grads):
        self.grads = grads
        if len(grads) == 1:
            self.total = lax.psum_scatter(grads[0], "z", scatter_dimension=1, tiled=True)
            return
        own, rest, near = grads
        self.inward = lax.ppermute(rest, "z", INWARD)
        self.outward_one = lax.ppermute(near, "z", OUTWARD)
        self.two = add(rest[1], self.inward[1])
        self.three = add(rest[2], self.inward[2])

    def finish(self, *events):
        if len(self.grads) > 1:
            outward_two = lax.ppermute(tie(self.three, *events), "z", [(1, 3), (2, 0)])
            middle = lax.ppermute(tie(self.two, *events), "z", MIDDLE)
            self.total = add(
                self.grads[0], self.inward[0], self.outward_one, outward_two, middle
            )

    def early(self):
        return [self.three, self.two] if len(self.grads) > 1 else []


def gather_packs(pack):
    below = [pack] + [
        lax.ppermute(pack, "z", [(k, (k + far) % 4) for k in range(4)]) for far in (1, 2, 3)
    ]
    column = jnp.stack(below)
    swap = [(0, 1), (1, 0)]
    over_x = lax.ppermute(column, "x", swap)
    over_y = lax.ppermute(column, "y", swap)
    over_both = lax.ppermute(column, ("x", "y"), [(0, 3), (1, 2), (2, 1), (3, 0)])
    four = [column, over_x, over_y, over_both]
    return four + [lax.ppermute(each, "c", swap) for each in four]


def shards(
    tokens_in,
    key_mask,
    expert_ids,
    expert_slots,
    norm1_gain,
    norm1_shift,
    qkv_weight,
    qv_bias,
    out_weight,
    out_bias,
    norm2_gain,
    norm2_shift,
    router_weight,
    up_weight,
    up_bias,
    down_weight,
    down_bias,
    out_grad,
):
    length = lax.axis_size("z")
    core = lax.axis_index("c")
    chip_y = lax.axis_index("y")
    quarter = lax.axis_size("y") * 2
    expert = (lax.axis_index("x") * lax.axis_size("y") + chip_y) * 2 + core
    piece, sequence, model = tokens_in.shape
    experts, part, units = up_weight.shape
    dp = model // part
    width = qkv_weight.shape[2]
    tokens = piece * sequence
    blocks = units // CHUNK
    spans = [(0, 1), (1, 3), (3, 5), (5, 6)] if blocks == 6 else [(0, blocks)]

    smalls = jnp.concatenate(
        [
            norm1_gain[None],
            norm1_shift[None],
            qv_bias,
            out_bias[None],
            norm2_gain[None],
            norm2_shift[None],
            down_bias,
            router_weight.T,
            up_bias.reshape(experts * quarter, part),
        ],
        0,
    ).astype(BF16)
    small_rows = smalls.shape[0]
    pad = -(small_rows * part) % (16 * model)
    small_block = jnp.pad(smalls.reshape(-1), (0, pad)).reshape(-1, model)
    pack = jnp.concatenate(
        [
            jnp.concatenate(
                [qkv_weight[0], qkv_weight[1], qkv_weight[2], out_weight.T], 1
            ).astype(BF16),
            small_block,
        ],
        0,
    )
    place = [lax.axis_index(name) for name in ("z", "x", "y", "c")]
    if length == 4:
        packs = gather_packs(pack)
        by_x = jnp.stack([packs[0][:, part:], packs[1][:, part:]]).reshape(2, 4, -1)
        pick_x = (place[1] ^ jnp.arange(2))[:, None] == jnp.arange(2)
        pick_z = (place[0] - jnp.arange(4)[:, None]) % 4 == jnp.arange(4)
        pick = pick_z[:, None, None, :] & pick_x[None, :, :, None]
        vectors = dot(pick.reshape(8, 8).astype(BF16), by_x.reshape(8, -1)).astype(BF16)
    else:
        packs = lax.all_gather(pack, EVERY, axis=0, tiled=False)
        packs = packs.reshape(quarter, dp, pack.shape[0], model)
        vectors = packs[0, :, part:].reshape(dp, -1)
        packs = [packs[:, :, :part].reshape(quarter, model, model)]
    vectors = vectors[:, : small_rows * part].reshape(dp, small_rows, part).transpose(1, 0, 2)
    lines = vectors[: 7 + 2 * experts].reshape(-1, model).astype(F32)
    bias_pairs = lines[2:4].reshape(2, quarter, width).transpose(1, 0, 2)
    bias_down = lines[7 : 7 + experts]
    router = lines[7 + experts :].astype(BF16)
    bias_up = vectors[7 + 2 * experts :].reshape(experts, quarter, dp, part)
    bias_up = bias_up.transpose(0, 2, 1, 3).reshape(experts, quarter, units)
    bias_up = lax.dynamic_index_in_dim(bias_up, expert, 0, keepdims=False).astype(F32)

    head = spans[0][1] * CHUNK
    sizes = [head, units - head] if units > head else [head]
    packed = pack_experts(up_weight, down_weight, sizes)
    event = None
    parts = []
    for some in packed:
        some = lax.all_to_all(tie(some, event), PLANE, 0, 0, tiled=True)
        event = some
        starts = [CHUNK * f for f, _ in spans[1:]] if parts else [0]
        stops = [CHUNK * l for _, l in spans[1:]] if parts else [head]
        base = starts[0]
        parts += [some[..., f - base : l - base] for f, l in zip(starts, stops)]
    if length != 4:
        parts = [
            one.reshape(2, quarter, 2, part, -1).transpose(2, 0, 3, 1, 4).reshape(2, 2 * part, -1)
            for one in parts
        ]

    first_group = chip_y * 3
    group_tokens = GROUP_IMG * sequence
    position = (expert_ids * CAP + expert_slots).reshape(-1, group_tokens, 2)
    position_full = lax.dynamic_index_in_dim(position, first_group + 2 * core, 0, keepdims=False)
    position_half = lax.dynamic_index_in_dim(position, first_group + 1, 0, keepdims=False)
    slots_full = jnp.arange(experts * CAP, dtype=jnp.int32)
    half = CAP // 2
    slots_half = (
        jnp.arange(experts, dtype=jnp.int32)[:, None] * CAP
        + core * half
        + jnp.arange(half, dtype=jnp.int32)
    ).reshape(-1)
    match_full = slots_full[:, None, None] == position_full.T[None]
    match_half = slots_half[:, None, None] == position_half.T[None]
    hot_full = (match_full[:, 0] | match_full[:, 1]).astype(BF16)
    hot_half = (match_half[:, 0] | match_half[:, 1]).astype(BF16)
    swap = [(0, 1), (1, 0)]

    def both_groups(values):
        lent = jnp.where(core == 0, values[2], values[0])
        other = lax.ppermute(lent, "c", swap)
        full = jnp.where(core == 0, values[:2], values[1:])
        shared = jnp.where(core == 0, jnp.stack([lent, other]), jnp.stack([other, lent]))
        return (
            full.reshape(group_tokens, -1),
            shared.reshape(group_tokens, -1),
        )

    def join_rows(full, shared):
        full = full.reshape((experts, CAP) + full.shape[1:])
        shared = shared.reshape((experts, half) + shared.shape[1:])
        return jnp.concatenate([full, shared], 1)

    def lines_of(values):
        high = values.astype(BF16)
        low = (values - high.astype(F32)).astype(BF16)
        both = jnp.stack([high, low], 1)
        return jnp.pad(both, ((0, 0), (0, 14), (0, model - both.shape[2])))

    def values_of(rows):
        both = rows[:, CAP + half : CAP + half + 2, : CAP + half].astype(F32)
        return both[:, 0] + both[:, 1]

    def swap_experts(rows, *events):
        return lax.all_to_all(tie(rows, *events), PLANE, 0, 0, tiled=True)

    def dispatch(full, shared):
        return join_rows(dot(hot_full, full).astype(BF16), dot(hot_half, shared).astype(BF16))

    def combine(back):
        full = dot(hot_full, back[:, :CAP].reshape(-1, model), 0, 0)
        shared = dot(hot_half, back[:, CAP : CAP + half].reshape(-1, model), 0, 0)
        full = full.reshape(GROUP_IMG, sequence, model)
        shared = shared.reshape(GROUP_IMG, sequence, model)
        mine = jnp.where(core == 0, shared[0], shared[1])
        theirs = jnp.where(core == 0, shared[1], shared[0])
        mine = mine + lax.ppermute(theirs, "c", swap)
        return jnp.where(
            core == 0,
            jnp.concatenate([full, mine[None]]),
            jnp.concatenate([mine[None], full]),
        )

    lines_z = [Line(own, length) for own in parts]
    for k in range(2):
        if k < len(lines_z):
            lines_z[k].start(*(lines_z[k - 1].early() if k else []))
    grad_full, grad_shared = both_groups(out_grad)
    incoming = swap_experts(dispatch(grad_full, grad_shared), event)

    local_start = (chip_y * 2 + core) * piece
    mask_here = lax.dynamic_slice_in_dim(key_mask, local_start, piece, 0)[:, None]
    before = [event] + lines_z[0].early() + (lines_z[1].early() if len(lines_z) > 1 else [])
    n1, n2, residual, q, k, v, attended, lse, wq, wk, wv, wo = attend_forward(
        jnp.stack(place).astype(jnp.int32), tie(tokens_in, *before), mask_here, lines, bias_pairs,
        packs, width,
    )
    for line in lines_z[2:]:
        line.start(n2)
    normed_two = n2.reshape(tokens, model)

    normed_full, normed_shared = both_groups(n2)

    def chances_of(rows):
        return jax.nn.softmax(dot(rows, router, 1, 1), -1)

    probabilities = chances_of(normed_two)
    hot_ids = expert_ids[..., None] == jnp.arange(experts, dtype=jnp.int32)
    hot_here = lax.dynamic_slice_in_dim(hot_ids, local_start, piece, 0).astype(F32)
    hot_here = jnp.sum(hot_here.reshape(tokens, 2, experts), 1)
    share_here = hot_here * probabilities

    def slot_gates(match, rows, position_here):
        chance = chances_of(rows)
        hot = (position_here // CAP)[..., None] == jnp.arange(experts, dtype=jnp.int32)
        gates = jnp.sum(hot.astype(F32) * chance[:, None], -1)
        return jnp.sum(jnp.where(match, gates.T[None], 0.0), (1, 2))

    gates_sent = join_rows(
        slot_gates(match_full, normed_full, position_full),
        slot_gates(match_half, normed_shared, position_half),
    )
    chosen = swap_experts(
        jnp.concatenate([dispatch(normed_full, normed_shared), lines_of(gates_sent)], 1), incoming
    )

    order = jnp.asarray(
        [ORDER[k] + (int(k in (0, 3)),) for k in range(4)] if length == 4 else [[0] * 5] * length,
        jnp.int32,
    )
    order = lax.dynamic_index_in_dim(order, place[0], 0, keepdims=False)
    sums = None
    bias_parts = []
    reduced = []
    for index, (first, last) in enumerate(spans):
        both = lines_z[index].result()
        events = []
        if index >= 2:
            events += reduced[index - 2].early()
        if index == 1:
            for line in lines_z[2:]:
                events += line.early()
        bias_one = bias_up[:, first * CHUNK : last * CHUNK].reshape(1, -1)
        final = index == len(spans) - 1
        *sums, bias_part = (
            outs := expert_chunk(order, chosen, incoming, tie(bias_one, *events), sums, both, final)
        )[:3]
        bias_parts.append(bias_part.reshape(quarter, -1))
        reduced.append(Reduce(outs[3:]))
        if index >= 2:
            reduced[index - 2].finish()

    mixed, pulled = sums
    back = swap_experts(pulled)
    gate_back = values_of(back)
    norm_two_grad = combine(back)

    def slots_to_tokens(match, parts_here):
        parts_here = parts_here.reshape(experts, -1)
        match = (match[:, 0] | match[:, 1]).reshape(experts, -1, group_tokens)
        return jnp.sum(jnp.where(match, parts_here[..., None], 0.0), 1).T

    prob_full = slots_to_tokens(match_full, gate_back[:, :CAP])
    prob_shared = slots_to_tokens(match_half, gate_back[:, CAP:])
    prob_full = prob_full.reshape(GROUP_IMG, sequence, experts)
    prob_shared = prob_shared.reshape(GROUP_IMG, sequence, experts)
    mine = jnp.where(core == 0, prob_shared[0], prob_shared[1])
    theirs = jnp.where(core == 0, prob_shared[1], prob_shared[0])
    mine = mine + lax.ppermute(theirs, "c", swap)
    chance_grad = jnp.where(
        core == 0,
        jnp.concatenate([prob_full, mine[None]]),
        jnp.concatenate([mine[None], prob_full]),
    ).reshape(tokens, experts)
    grad_rows = out_grad.reshape(tokens, model)
    bias_dot = dot(grad_rows, bias_down.astype(BF16), 1, 1)
    chance_grad = chance_grad + hot_here * bias_dot
    logit_grad = probabilities * (
        chance_grad - jnp.sum(probabilities * chance_grad, -1, keepdims=True)
    )
    logit_grad = logit_grad.astype(BF16)
    router_grad = dot(logit_grad, normed_two, 0, 0)
    down_bias_grad = lax.dot_general(
        share_here, grad_rows.astype(F32), (((0,), (0,)), ((), ())), precision=HIGHEST
    )

    norm_two_grad = norm_two_grad + dot(logit_grad, router).reshape(norm_two_grad.shape)
    h_grad, hb, dq, dk, dv, line_sums, pair_sums = attend_backward(
        norm_two_grad, out_grad, residual, mask_here, wo, lines, q, k, v, lse
    )
    input_grad, line_ones = input_backward(h_grad, tokens_in, wq, wk, wv, lines, dq, dk, dv)
    for some in reduced[-2:] if len(reduced) > 1 else reduced:
        some.finish()

    bias_rows = jnp.concatenate(bias_parts, 1).reshape(dp, quarter, part)
    bias_rows = jnp.where(
        jnp.arange(experts)[:, None, None, None] == expert, bias_rows[None], 0.0
    )
    bias_rows = bias_rows.transpose(0, 2, 1, 3).reshape(experts * quarter, dp, part)
    line_grads = jnp.concatenate(
        [
            line_ones[:2],
            pair_sums[:, 0].reshape(1, model),
            pair_sums[:, 1].reshape(1, model),
            line_sums[:3],
            down_bias_grad,
            router_grad,
        ],
        0,
    ).reshape(-1, dp, part)
    sum_type = BF16 if length == 4 else F32
    vector_grads = jnp.concatenate([line_grads, bias_rows], 0).astype(sum_type)
    vector_grads = vector_grads.transpose(1, 0, 2).reshape(dp, small_rows * part)
    vector_grads = jnp.pad(vector_grads, ((0, 0), (0, pad))).reshape(dp, -1, model)

    if length == 4:
        pack_grads = attend_weights(n1, hb, dq, dk, dv, attended, vector_grads)
    else:
        pack_grads = attend_weights(n1, hb, dq, dk, dv, attended, None)
        pack_grads = pack_grads.reshape(quarter, dp, part, model)
        vector_grads = jnp.broadcast_to(vector_grads[None], (quarter,) + vector_grads.shape)
        pack_grads = jnp.concatenate([pack_grads, vector_grads], 2)
        pack_grads = pack_grads.reshape(quarter // 2, 2, dp // 2, 2, -1, model)
        pack_grads = pack_grads.transpose(1, 3, 0, 2, 4, 5)
    mine = lax.dynamic_index_in_dim(pack_grads, core, 0, keepdims=False)
    theirs = lax.dynamic_index_in_dim(pack_grads, 1 - core, 0, keepdims=False)
    theirs = lax.ppermute(theirs, "c", swap)
    pack_grads = (mine.astype(F32) + theirs.astype(F32)).astype(sum_type)
    pack_grads = pack_grads.reshape((-1,) + pack_grads.shape[2:])
    pack_grads = lax.all_to_all(pack_grads, ("x", "y"), 0, 0, tiled=True)
    pack_grads = jnp.sum(pack_grads.astype(F32), 0).astype(sum_type)
    if length == 4:
        pack_grads = lax.all_to_all(pack_grads, "z", 0, 0, tiled=True)
        pack_grad = jnp.sum(pack_grads.astype(F32), 0)
    else:
        pack_grad = lax.psum_scatter(pack_grads, "z", scatter_dimension=0, tiled=False)
    qkv_out = pack_grad[:part, : 3 * width].reshape(part, 3, width).transpose(1, 0, 2)
    out_weight_grad = pack_grad[:part, 3 * width :].T
    small_grads = pack_grad[part:].reshape(-1)[: small_rows * part].reshape(small_rows, part)

    mixture = combine(swap_experts(mixed, back))
    bias_term = jnp.dot(share_here, bias_down, precision=HIGHEST).reshape(residual.shape)
    output = (residual + mixture + bias_term).astype(BF16)

    ups, downs = [], []
    totals = [one.total for one in reduced]
    if length != 4:
        totals = [
            one.reshape(2, 2, part, quarter, -1).transpose(1, 3, 0, 2, 4).reshape(experts, 2, part, -1)
            for one in totals
        ]
    for some in (totals[:2], totals[2:]):
        if some:
            some = some[0] if len(some) == 1 else jnp.concatenate(some, -1)
            some = lax.all_to_all(some.astype(BF16), PLANE, 0, 0, tiled=True).astype(F32)
            ups.append(some[:, 0])
            downs.append(some[:, 1])
    up_grad = jnp.concatenate(ups, -1)
    down_grad = jnp.concatenate(downs, -1).transpose(0, 2, 1)
    return (
        output,
        input_grad,
        small_grads[0],
        small_grads[1],
        qkv_out,
        small_grads[2:4],
        out_weight_grad,
        small_grads[4],
        small_grads[5],
        small_grads[6],
        small_grads[7 + experts : 7 + 2 * experts].T,
        up_grad,
        small_grads[7 + 2 * experts :].reshape(experts, -1),
        down_grad,
        small_grads[7 : 7 + experts],
    )


def solution(mesh):
    dp, tensor = mesh.devices.shape
    planes = jax.sharding.Mesh(
        mesh.devices.reshape(dp // 2, 2, tensor // 2, 2), ("z", "x", "y", "c")
    )
    rows = ("z", "x")
    images = P(("z", "x", "y", "c"), None, None)
    return jax.shard_map(
        shards,
        mesh=planes,
        in_specs=(
            images,
            P(rows, None),
            P(rows, None, None),
            P(rows, None, None),
            P(rows),
            P(rows),
            P(None, rows, TENSOR),
            P(None, rows),
            P(TENSOR, rows),
            P(rows),
            P(rows),
            P(rows),
            P(rows, None),
            P(None, rows, TENSOR),
            P(None, rows),
            P(None, TENSOR, rows),
            P(None, rows),
            images,
        ),
        out_specs=(
            images,
            images,
            P(rows),
            P(rows),
            P(None, rows, TENSOR),
            P(None, rows),
            P(TENSOR, rows),
            P(rows),
            P(rows),
            P(rows),
            P(rows, None),
            P(None, rows, TENSOR),
            P(None, rows),
            P(None, TENSOR, rows),
            P(None, rows),
        ),
        check_vma=False,
    )
```

time: 855 us -> 684 us (0.80)
  starting transfers between devices: 210 us -> 128 us
  other arithmetic: 134 us -> 67.9 us
  local copies, waits for them, and re-layouts: 95.2 us -> 47.9 us
  waiting for transfers between devices: 234 us -> 259 us
  Pallas kernels: 133 us -> 152 us
  between operations: 15.8 us -> 2.69 us
    ppermute x53 -> x56, starting transfers between devices: 144 us -> 81.8 us  [the longest x4 16 us: __init__(): self.inward = lax.ppermute(rest, 'z', INWARD)]
    all_to_all x10 -> x8, waiting for transfers between devices: 43.9 us -> 69.1 us  [the longest x4 23.6 us: swap_experts(): return lax.all_to_all(tie(rows, *events), PLANE, 0, 0, tiled=True)]
    pallas_call x6 -> x9, Pallas kernels: 133 us -> 152 us  [the longest x4 82.1 us: expert_chunk(): pl.pallas_call(functools.partial(expert_kernel, first, last, len(pieces))...]
    another operation x17 -> x11, other arithmetic: 23.6 us -> 7.87 us
    reshape x15 -> x1, local copies, waits for them, and re-layouts: 14 us -> 0.17 us  [shards(): vectors[:, :small_rows * part].reshape(dp, small_rows, part)]
    ppermute x53 -> x56, waiting for transfers between devices: 166 us -> 178 us  [the longest x4 39.3 us: finish(): outward_two = lax.ppermute(tie(self.three, *events), 'z', [(1, 3), (2, 0)])]
    select_n x7 -> x1, other arithmetic: 12.4 us -> 0.01 us  [shards(): pick_z = (place[0] - jnp.arange(4)[:, None]) % 4 == jnp.arange(4)]
    all_to_all x4 -> x2, waiting for transfers between devices: 23.9 us -> 11.9 us  [shards(): some = lax.all_to_all(tie(some, event), PLANE, 0, 0, tiled=True)]
  transfers between devices with their start and end apart: 69 -> 66, of which waited for: 23 -> 18; matrix products, arithmetic and copies ran while one was open for 26% -> 16% of each run, Pallas kernels for 7% -> 23%
where the time goes in v3:
time: 684 us; the launch traced here: 675 us
  waiting for transfers between devices  259 us (38%)
  Pallas kernels  152 us (22%)
  starting transfers between devices  128 us (19%)
  other arithmetic  67.9 us (10%)
  local copies, waits for them, and re-layouts  47.9 us (7%)
  matrix products  16.4 us (2%)
    pallas_call x4, Pallas kernels, expert_chunk(): pl.pallas_call(functools.partial(expert_kernel, first, last, len(pieces))...  82.1 us
    ppermute x4, waiting for transfers between devices, finish(): outward_two = lax.ppermute(tie(self.three, *events), 'z', [(1, 3), (2, 0)])  39.3 us
    ppermute x4, waiting for transfers between devices, start(): self.outward_two = lax.ppermute(own, 'z', [(1, 3), (2, 0)])  33.5 us
    ppermute x4, waiting for transfers between devices, __init__(): self.outward_one = lax.ppermute(near, 'z', OUTWARD)  28.2 us
    pallas_call x1, Pallas kernels, attend_forward(): pl.pallas_call(attend_forward_kernel, grid_spec=pltpu.PrefetchScalarGridS...  26.1 us
    all_to_all x4, waiting for transfers between devices, swap_experts(): return lax.all_to_all(tie(rows, *events), PLANE, 0, 0, tiled=True)  23.6 us
    all_to_all x1, waiting for transfers between devices, shards(): pack_grads = lax.all_to_all(pack_grads, ('x', 'y'), 0, 0, tiled=True)  21.5 us
    pallas_call x1, Pallas kernels, attend_backward(): pl.pallas_call(attend_backward_kernel, grid=(images,), in_specs=[whole(a....  20.9 us
  transfers between devices with their start and end apart: 66, of which 18 were waited for; matrix products, arithmetic and copies ran while one was open for 16% of the time, Pallas kernels for 23%

profile of v3, /device:TPU:0, one launch (start us, length us, event | category | flops | bytes accessed | tf_op | source)
XLA Modules:
  0.0 674.6 jit_solution(17650802759696703794)
XLA Ops:
  54.1 9.1 %all-to-all-done.1 = bf16[8,2,96,640]{3,2,1,0:T(8,128)(2,1)S(1)} async-done(((bf16[8,2,96,640]{3,2,1,0:T(8,128)(2,1)}), bf16[8,2,96,640]{3,2,1,0:T(8,128)(2,1)S(1)}, u32[]{:S(2)}, u32[]{:S(2)}) %all-to-all-start.1) | async-done | bytes 1966112 | tf_op jit(solution)/shard_map/all_to_all | solution.py:678
  80.3 16.1 %collective-permute-done.10.refs_2_ = bf16[4,112,768]{2,1,0:T(8,128)(2,1)} collective-permute-done((bf16[4,112,768]{2,1,0:T(8,128)(2,1)}, bf16[4,112,768]{2,1,0:T(8,128)(2,1)}, u32[]{:S(2)}, u32[]{:S(2)}) %collective-permute-start.10) | collective-permute-done | bytes 688160 | tf_op jit(solution)/shard_map/ppermute | solution.py:585
  99.9 4.6 all-to-all-start.2
  105.4 26.1 %attend_forward.1 = (bf16[3,208,768]{2,1,0:T(8,128)(2,1)}, bf16[3,200,768]{2,1,0:T(8,128)(2,1)}, f32[3,200,768]{2,1,0:T(8,128)}, bf16[3,4,200,192]{3,2,1,0:T(8,1...) custom-call(s32[4]{0:T(128)} %pad_add_fusion.place_ref, ...), custom_call_target="tpu_custom_call" | custom-call | flops 3000000000 | bytes 60000000 | tf_op jit(solution)/shard_map/attend_forward/pallas_call | solution.py:147
  140.6 4.5 all-to-all-start.3
  156.2 17.2 %collective-permute-done.21.refs_4_ = bf16[8,2,96,128]{3,2,1,0:T(8,128)(2,1)} collective-permute-done((bf16[8,2,96,128]{3,2,1,0:T(8,128)(2,1)S(1)}, bf16[8,2,96,128]{3,2,1,0:T(8,128)(2,1)}, u32[]{:S(2)}, u32[]{:S(2)}) %collective-permute-start.21) | collective-permute-done | bytes 393248 | tf_op jit(solution)/shard_map/ppermute | solution.py:529
  179.2 8.8 %collective-permute-done.23.refs_1_ = bf16[8,2,96,128]{3,2,1,0:T(8,128)(2,1)} collective-permute-done((bf16[8,2,96,128]{3,2,1,0:T(8,128)(2,1)S(1)}, bf16[8,2,96,128]{3,2,1,0:T(8,128)(2,1)}, u32[]{:S(2)}, u32[]{:S(2)}) %collective-permute-start.23) | collective-permute-done | bytes 393248 | tf_op jit(solution)/shard_map/ppermute | solution.py:530
  194.5 33.5 %collective-permute-done.27.refs_2_ = bf16[8,2,96,128]{3,2,1,0:T(8,128)(2,1)S(1)} collective-permute-done((bf16[8,2,96,128]{3,2,1,0:T(8,128)(2,1)}, bf16[8,2,96,128]{3,2,1,0:T(8,128)(2,1)S(1)}, u32[]{:S(2)}, u32[]{:S(2)}) %collective-permute-start.27) | collective-permute-done | bytes 393248 | tf_op jit(solution)/shard_map/ppermute | solution.py:532
  231.0 14.7 %expert_chunk.4 = (f32[8,192,768]{2,1,0:T(8,128)}, f32[8,192,768]{2,1,0:T(8,128)}, f32[1,512]{1,0:T(1,128)}, bf16[8,2,96,128]{3,2,1,0:T(8,128)(2,1)}, bf16[3,8,2...) custom-call(s32[5]{0:T(128)} %fusion.57.order_ref, bf16[8,208,768]{2,1,0:T(8,128)(2,1)} %all-to-all-done.3.x_ref, ...), custom_call_target="tpu_custom_call" | custom-call | flops 7247757312 | bytes 30000000 | tf_op jit(solution)/shard_map/expert_chunk/pallas_call | solution.py:476
  245.7 5.8 collective-permute-start.34
  251.5 13.9 %collective-permute-done.26.refs_3_ = bf16[8,2,96,256]{3,2,1,0:T(8,128)(2,1)} collective-permute-done((bf16[8,2,96,256]{3,2,1,0:T(8,128)(2,1)}, bf16[8,2,96,256]{3,2,1,0:T(8,128)(2,1)}, u32[]{:S(2)}, u32[]{:S(2)}) %collective-permute-start.26) | collective-permute-done | bytes 786464 | tf_op jit(solution)/shard_map/ppermute | solution.py:534
  265.4 25.9 %expert_chunk.5 = (f32[8,192,768]{2,1,0:T(8,128)}, f32[8,192,768]{2,1,0:T(8,128)}, f32[1,1024]{1,0:T(1,128)}, bf16[8,2,96,256]{3,2,1,0:T(8,128)(2,1)}, bf16[3,8,...) custom-call(s32[5]{0:T(128)} %fusion.57.order_ref, ...), custom_call_target="tpu_custom_call", output_to_operand_aliasing={{0}: (11, {}), {1}: (12, {})} | custom-call | flops 14495514624 | bytes 30000000 | tf_op jit(solution)/shard_map/expert_chunk/pallas_call | solution.py:476
  296.2 25.9 %expert_chunk.6 = (f32[8,192,768]{2,1,0:T(8,128)}, f32[8,192,768]{2,1,0:T(8,128)}, f32[1,1024]{1,0:T(1,128)}, bf16[8,2,96,256]{3,2,1,0:T(8,128)(2,1)}, bf16[3,8,...) custom-call(s32[5]{0:T(128)} %fusion.57.order_ref, ...), custom_call_target="tpu_custom_call", output_to_operand_aliasing={{0}: (11, {}), {1}: (12, {})} | custom-call | flops 14495514624 | bytes 30000000 | tf_op jit(solution)/shard_map/expert_chunk/pallas_call | solution.py:476
  337.3 7.5 %collective-permute-done.30 = bf16[3,8,2,96,256]{4,3,2,1,0:T(8,128)(2,1)} collective-permute-done((bf16[3,8,2,96,256]{4,3,2,1,0:T(8,128)(2,1)}, bf16[3,8,2,96,256]{4,3,2,1,0:T(8,128)(2,1)}, u32[]{:S(2)}, u32[]{:S(2)}) %collective-permute-start.30) | collective-permute-done | bytes 2359328 | tf_op jit(solution)/shard_map/ppermute | solution.py:561
  355.8 15.7 %expert_chunk.7 = (bf16[8,192,768]{2,1,0:T(8,128)(2,1)}, bf16[8,208,768]{2,1,0:T(8,128)(2,1)}, f32[1,512]{1,0:T(1,128)}, bf16[8,2,96,128]{3,2,1,0:T(8,128)(2,1)}...) custom-call(s32[5]{0:T(128)} %fusion.57.order_ref, bf16[8,208,768]{2,1,0:T(8,128)(2,1)} %all-to-all-done.3.x_ref, ...), custom_call_target="tpu_custom_call" | custom-call | flops 7247757312 | bytes 30000000 | tf_op jit(solution)/shard_map/expert_chunk/pallas_call | solution.py:476
  371.5 4.4 collective-permute-start.52
  378.2 4.4 all-to-all-start.4
  389.4 6.0 collective-permute-done.48
  400.8 21.2 %collective-permute-done.45 = bf16[8,2,96,256]{3,2,1,0:T(8,128)(2,1)} collective-permute-done((bf16[8,2,96,256]{3,2,1,0:T(8,128)(2,1)}, bf16[8,2,96,256]{3,2,1,0:T(8,128)(2,1)}, u32[]{:S(2)}, u32[]{:S(2)}) %collective-permute-start.45) | collective-permute-done | bytes 786464 | tf_op jit(solution)/shard_map/ppermute | solution.py:562
  423.3 7.0 %collective-permute-done.53 = bf16[8,2,96,128]{3,2,1,0:T(8,128)(2,1)S(1)} collective-permute-done((bf16[8,2,96,128]{3,2,1,0:T(8,128)(2,1)}, bf16[8,2,96,128]{3,2,1,0:T(8,128)(2,1)S(1)}, u32[]{:S(2)}, u32[]{:S(2)}) %collective-permute-start.53) | collective-permute-done | bytes 393248 | tf_op jit(solution)/shard_map/ppermute | solution.py:562
  439.5 39.3 %collective-permute-done.54 = bf16[8,2,96,128]{3,2,1,0:T(8,128)(2,1)S(1)} collective-permute-done((bf16[8,2,96,128]{3,2,1,0:T(8,128)(2,1)S(1)}, bf16[8,2,96,128]{3,2,1,0:T(8,128)(2,1)S(1)}, u32[]{:S(2)}, u32[]{:S(2)}) %collective-permute-start.54) | collective-permute-done | bytes 393248 | tf_op jit(solution)/shard_map/ppermute | solution.py:568
  483.6 4.3 all-to-all-start.8
  503.4 20.9 %attend_backward.1 = (f32[3,200,768]{2,1,0:T(8,128)}, bf16[3,208,768]{2,1,0:T(8,128)(2,1)}, bf16[3,4,208,192]{3,2,1,0:T(8,128)(2,1)}, bf16[3,4,208,192]{3,2,1,0:...) custom-call(f32[3,200,768]{2,1,0:T(8,128)} %fusion.4.n2_grad_ref, ...), custom_call_target="tpu_custom_call" | custom-call | flops 4000000000 | bytes 70000000 | tf_op jit(solution)/shard_map/attend_backward/pallas_call | solution.py:226
  524.3 9.6 %input_backward.1 = (f32[3,200,768]{2,1,0:T(8,128)}, f32[8,768]{1,0:T(8,128)}) custom-call(f32[3,200,768]{2,1,0:T(8,128)} %get-tuple-element.103.h_grad_ref, bf16[3,200,768]{2,1,0:T(8,128)(2,1)} %tokens_ref.2, bf16[4,768,192]{2,1,0:T(8,128)(2,1)} %get-tuple-element.104.wq_ref, bf16[4,768,192]{2,1,0:T(8,128)(2,1)} %get-tuple-element.105.wk_ref, ...), custom_call_target="tpu_custom_call" | custom-call | flops 3000000000 | bytes 30000000 | tf_op jit(solution)/shard_map/input_backward/pallas_call | solution.py:313
  537.3 9.7 %attend_weights.1 = bf16[2,2,2,4,112,768]{5,4,3,2,1,0:T(8,128)(2,1)} custom-call(bf16[3,208,768]{2,1,0:T(8,128)(2,1)} %get-tuple-element.111.n1_ref, bf16[3,208,768]{2,1,0:T(8,128)(2,1)} %get-tuple-element.112.hb_ref, bf16[3,4,208,192]{3,2,1,0:T(8,128)(2,1)} %get-tuple-element.107.dq_ref, bf16[3,4,208,192]{3,2,1,0:T(8,128)(2,1)} %get-tuple-element.108.dk_ref, ...), custom_call_target="tpu_custom_call" | custom-call | flops 3000000000 | bytes 30000000 | tf_op jit(solution)/shard_map/attend_weights/pallas_call | solution.py:274
  556.1 15.9 %all-to-all-done.9 = bf16[8,2,96,384]{3,2,1,0:T(8,128)(2,1)S(1)} async-done(((bf16[8,2,96,384]{3,2,1,0:T(8,128)(2,1)}), bf16[8,2,96,384]{3,2,1,0:T(8,128)(2,1)S(1)}, u32[]{:S(2)}, u32[]{:S(2)}) %all-to-all-start.9) | async-done | bytes 1179680 | tf_op jit(solution)/shard_map/all_to_all | solution.py:924
  575.6 4.8 fusion
  580.4 23.6 %all-to-all-done.5 = bf16[8,192,768]{2,1,0:T(8,128)(2,1)S(1)} async-done(((bf16[8,192,768]{2,1,0:T(8,128)(2,1)}), bf16[8,192,768]{2,1,0:T(8,128)(2,1)S(1)}, u32[]{:S(2)}, u32[]{:S(2)}) %all-to-all-start.5) | async-done | bytes 2359328 | tf_op jit(solution)/shard_map/all_to_all | solution.py:734
  604.0 4.7 all-to-all-start.6
  619.2 21.5 %all-to-all-done.6 = bf16[4,4,112,768]{3,2,1,0:T(8,128)(2,1)} async-done(((bf16[4,4,112,768]{3,2,1,0:T(8,128)(2,1)}), bf16[4,4,112,768]{3,2,1,0:T(8,128)(2,1)}, u32[]{:S(2)}, u32[]{:S(2)}) %all-to-all-start.6) | async-done | bytes 2752544 | tf_op jit(solution)/shard_map/all_to_all | solution.py:899
  644.0 8.5 %all-to-all-start.7 = ((bf16[4,112,768]{2,1,0:T(8,128)(2,1)}), bf16[4,112,768]{2,1,0:T(8,128)(2,1)S(1)}, u32[]{:S(2)}, u32[]{:S(2)}) async-start(bf16[4,112,768]{2,1,0:T(8,128)(2,1)} %reduce_sum.134), calls=%async_computation.7 | async-start | bytes 1376256 | tf_op jit(solution)/shard_map/all_to_all | solution.py:902
  661.4 8.2 %all-to-all-done.7 = bf16[4,112,768]{2,1,0:T(8,128)(2,1)S(1)} async-done(((bf16[4,112,768]{2,1,0:T(8,128)(2,1)}), bf16[4,112,768]{2,1,0:T(8,128)(2,1)S(1)}, u32[]{:S(2)}, u32[]{:S(2)}) %all-to-all-start.7) | async-done | bytes 688160 | tf_op jit(solution)/shard_map/all_to_all | solution.py:902
  (434 shorter events, 228.7 us)
Async XLA Ops:
  8.8 34.3 %collective-permute-start.6 = (bf16[112,768]{1,0:T(8,128)(2,1)}, bf16[112,768]{1,0:T(8,128)(2,1)}, u32[]{:S(2)}, u32[]{:S(2)}) collective-permute-start(bf16[112,768]{1,0:T(8,128)(2,1)} %pad_maximum_fusion.7), channel_id=1, source_target_pairs={{0,8},{8,16},{16,24},{24,0},{1,9},{9,17},{17,25},{25,1},{2,10},{10... | collective-permute-start | bytes 516104 | tf_op jit(solution)/shard_map/ppermute | solution.py:580
  29.2 40.6 %collective-permute-start.17 = (bf16[200,768]{1,0:T(8,128)(2,1)}, bf16[200,768]{1,0:T(8,128)(2,1)}, u32[]{:S(2)}, u32[]{:S(2)}) collective-permute-start(bf16[200,768]{1,0:T(8,128)(2,1)} %fusion.99), channel_id=1, source_target_pairs={{0,1},{1,0},{2,3},{3,2},{4,5},{5,4},{6,7},{7,6},{8,9},{9,8},{10,11... | collective-permute-start | bytes 921608 | tf_op jit(solution)/shard_map/ppermute | solution.py:710
  99.9 40.7 %all-to-all-start.2 = ((bf16[8,192,768]{2,1,0:T(8,128)(2,1)}), bf16[8,192,768]{2,1,0:T(8,128)(2,1)}, u32[]{:S(2)}, u32[]{:S(2)}) async-start(bf16[8,192,768]{2,1,0:T(8,128)(2,1)} %pad_maximum_fusion.1), calls=%async_computation.2 | async-start | bytes 4718592 | tf_op jit(solution)/shard_map/all_to_all | solution.py:734
  140.6 90.4 %all-to-all-start.3 = ((bf16[8,208,768]{2,1,0:T(8,128)(2,1)}), bf16[8,208,768]{2,1,0:T(8,128)(2,1)}, u32[]{:S(2)}, u32[]{:S(2)}) async-start(bf16[8,208,768]{2,1,0:T(8,128)(2,1)} %pad_maximum_fusion), calls=%async_computation.3 | async-start | bytes 5111808 | tf_op jit(solution)/shard_map/all_to_all | solution.py:734
  153.3 36.0 %collective-permute-start.19 = (bf16[8,2,96,256]{3,2,1,0:T(8,128)(2,1)S(1)}, bf16[8,2,96,256]{3,2,1,0:T(8,128)(2,1)}, u32[]{:S(2)}, u32[]{:S(2)}) collective-permute-start(bf16[8,2,96,256]{3,2,1,0:T(8,128)(2,1)S(1)} %copy-done.27), channel_id=1, source_target_pairs={{8,16},{16,8},{9,17},{17,9},{10,18},{18,10},{11,19},{19,11},{12,20... | collective-permute-start | bytes 2359304 | tf_op jit(solution)/shard_map/ppermute | solution.py:531
  154.9 35.8 %collective-permute-start.20 = (bf16[8,2,96,256]{3,2,1,0:T(8,128)(2,1)S(1)}, bf16[8,2,96,256]{3,2,1,0:T(8,128)(2,1)}, u32[]{:S(2)}, u32[]{:S(2)}) collective-permute-start(bf16[8,2,96,256]{3,2,1,0:T(8,128)(2,1)S(1)} %copy-done.27), channel_id=1, source_target_pairs={{8,0},{16,24},{9,1},{17,25},{10,2},{18,26},{11,3},{19,27},{12,4},{... | collective-permute-start | bytes 2359304 | tf_op jit(solution)/shard_map/ppermute | solution.py:530
  176.2 53.0 %collective-permute-start.36 = (bf16[8,2,96,256]{3,2,1,0:T(8,128)(2,1)}, bf16[8,2,96,256]{3,2,1,0:T(8,128)(2,1)}, u32[]{:S(2)}, u32[]{:S(2)}) collective-permute-start(bf16[8,2,96,256]{3,2,1,0:T(8,128)(2,1)} %collective-permute-done.18.refs_4_), channel_id=1, source_target_pairs={{8,16},{16,8},{9,17},{17,9},{10,18},{18,10},{11,19},{19,11},{12,20... | collective-permute-start | bytes 2359304 | tf_op jit(solution)/shard_map/ppermute | solution.py:533
  188.1 39.9 %collective-permute-start.27 = (bf16[8,2,96,128]{3,2,1,0:T(8,128)(2,1)}, bf16[8,2,96,128]{3,2,1,0:T(8,128)(2,1)S(1)}, u32[]{:S(2)}, u32[]{:S(2)}) collective-permute-start(bf16[8,2,96,128]{3,2,1,0:T(8,128)(2,1)} %all-to-all-done.refs_0_), channel_id=1, source_target_pairs={{8,24},{16,0},{9,25},{17,1},{10,26},{18,2},{11,27},{19,3},{12,28},... | collective-permute-start | bytes 1179656 | tf_op jit(solution)/shard_map/ppermute | solution.py:532
  189.4 41.6 %collective-permute-start.29 = (bf16[8,2,96,128]{3,2,1,0:T(8,128)(2,1)}, bf16[8,2,96,128]{3,2,1,0:T(8,128)(2,1)}, u32[]{:S(2)}, u32[]{:S(2)}) collective-permute-start(bf16[8,2,96,128]{3,2,1,0:T(8,128)(2,1)} %copy-done.56), channel_id=1, source_target_pairs={{8,0},{16,24},{9,1},{17,25},{10,2},{18,26},{11,3},{19,27},{12,4},{... | collective-permute-start | bytes 1179656 | tf_op jit(solution)/shard_map/ppermute | solution.py:534
  190.7 60.8 %collective-permute-start.24 = (bf16[8,2,96,256]{3,2,1,0:T(8,128)(2,1)}, bf16[8,2,96,256]{3,2,1,0:T(8,128)(2,1)}, u32[]{:S(2)}, u32[]{:S(2)}) collective-permute-start(bf16[8,2,96,256]{3,2,1,0:T(8,128)(2,1)} %get-tuple-element.76.refs_0_), channel_id=1, source_target_pairs={{8,24},{16,0},{9,25},{17,1},{10,26},{18,2},{11,27},{19,3},{12,28},... | collective-permute-start | bytes 2359304 | tf_op jit(solution)/shard_map/ppermute | solution.py:532
  192.0 73.4 %collective-permute-start.26 = (bf16[8,2,96,256]{3,2,1,0:T(8,128)(2,1)}, bf16[8,2,96,256]{3,2,1,0:T(8,128)(2,1)}, u32[]{:S(2)}, u32[]{:S(2)}) collective-permute-start(bf16[8,2,96,256]{3,2,1,0:T(8,128)(2,1)} %collective-permute-done.25.refs_6_), channel_id=1, source_target_pairs={{8,0},{16,24},{9,1},{17,25},{10,2},{18,26},{11,3},{19,27},{12,4},{... | collective-permute-start | bytes 2359304 | tf_op jit(solution)/shard_map/ppermute | solution.py:534
  228.0 68.2 %collective-permute-start.35 = (bf16[8,2,96,256]{3,2,1,0:T(8,128)(2,1)S(1)}, bf16[8,2,96,256]{3,2,1,0:T(8,128)(2,1)}, u32[]{:S(2)}, u32[]{:S(2)}) collective-permute-start(bf16[8,2,96,256]{3,2,1,0:T(8,128)(2,1)S(1)} %copy-done.27), channel_id=1, source_target_pairs={{8,24},{16,0},{9,25},{17,1},{10,26},{18,2},{11,27},{19,3},{12,28},... | collective-permute-start | bytes 2359304 | tf_op jit(solution)/shard_map/ppermute | solution.py:532
  229.3 66.9 %collective-permute-start.37 = (bf16[8,2,96,256]{3,2,1,0:T(8,128)(2,1)}, bf16[8,2,96,256]{3,2,1,0:T(8,128)(2,1)}, u32[]{:S(2)}, u32[]{:S(2)}) collective-permute-start(bf16[8,2,96,256]{3,2,1,0:T(8,128)(2,1)} %collective-permute-done.36.refs_6_), channel_id=1, source_target_pairs={{8,0},{16,24},{9,1},{17,25},{10,2},{18,26},{11,3},{19,27},{12,4},{... | collective-permute-start | bytes 2359304 | tf_op jit(solution)/shard_map/ppermute | solution.py:534
  245.7 49.2 %collective-permute-start.34 = (bf16[3,8,2,96,128]{4,3,2,1,0:T(8,128)(2,1)}, bf16[3,8,2,96,128]{4,3,2,1,0:T(8,128)(2,1)S(1)}, u32[]{:S(2)}, u32[]{:S(2)}) collective-permute-start(bf16[3,8,2,96,128]{4,3,2,1,0:T(8,128)(2,1)} %get-tuple-element.89), channel_id=1, source_target_pairs={{0,8},{24,16},{1,9},{25,17},{2,10},{26,18},{3,11},{27,19},{4,12},{... | collective-permute-start | bytes 3538952 | tf_op jit(solution)/shard_map/ppermute | solution.py:561
  291.3 53.5 %collective-permute-start.30 = (bf16[3,8,2,96,256]{4,3,2,1,0:T(8,128)(2,1)}, bf16[3,8,2,96,256]{4,3,2,1,0:T(8,128)(2,1)}, u32[]{:S(2)}, u32[]{:S(2)}) collective-permute-start(bf16[3,8,2,96,256]{4,3,2,1,0:T(8,128)(2,1)} %get-tuple-element.87), channel_id=1, source_target_pairs={{0,8},{24,16},{1,9},{25,17},{2,10},{26,18},{3,11},{27,19},{4,12},{... | collective-permute-start | bytes 7077896 | tf_op jit(solution)/shard_map/ppermute | solution.py:561
  322.1 73.2 %collective-permute-start.48 = (bf16[3,8,2,96,256]{4,3,2,1,0:T(8,128)(2,1)}, bf16[3,8,2,96,256]{4,3,2,1,0:T(8,128)(2,1)}, u32[]{:S(2)}, u32[]{:S(2)}) collective-permute-start(bf16[3,8,2,96,256]{4,3,2,1,0:T(8,128)(2,1)} %get-tuple-element.126), channel_id=1, source_target_pairs={{0,8},{24,16},{1,9},{25,17},{2,10},{26,18},{3,11},{27,19},{4,12},{... | collective-permute-start | bytes 7077896 | tf_op jit(solution)/shard_map/ppermute | solution.py:561
  336.0 46.6 %collective-permute-start.42 = (bf16[8,2,96,128]{3,2,1,0:T(8,128)(2,1)}, bf16[8,2,96,128]{3,2,1,0:T(8,128)(2,1)}, u32[]{:S(2)}, u32[]{:S(2)}) collective-permute-start(bf16[8,2,96,128]{3,2,1,0:T(8,128)(2,1)} %get-tuple-element.122), channel_id=1, source_target_pairs={{8,0},{16,24},{9,1},{17,25},{10,2},{18,26},{11,3},{19,27},{12,4},{... | collective-permute-start | bytes 1179656 | tf_op jit(solution)/shard_map/ppermute | solution.py:562
  344.8 39.1 %collective-permute-start.43 = (bf16[8,2,96,128]{3,2,1,0:T(8,128)(2,1)}, bf16[8,2,96,128]{3,2,1,0:T(8,128)(2,1)}, u32[]{:S(2)}, u32[]{:S(2)}) collective-permute-start(bf16[8,2,96,128]{3,2,1,0:T(8,128)(2,1)} %get-tuple-element.174), channel_id=1, source_target_pairs={{8,24},{16,0},{9,25},{17,1},{10,26},{18,2},{11,27},{19,3},{12,28},... | collective-permute-start | bytes 1179656 | tf_op jit(solution)/shard_map/ppermute | solution.py:568
  371.5 60.2 %collective-permute-start.52 = (bf16[3,8,2,96,128]{4,3,2,1,0:T(8,128)(2,1)}, bf16[3,8,2,96,128]{4,3,2,1,0:T(8,128)(2,1)}, u32[]{:S(2)}, u32[]{:S(2)}) collective-permute-start(bf16[3,8,2,96,128]{4,3,2,1,0:T(8,128)(2,1)} %get-tuple-element.129), channel_id=1, source_target_pairs={{0,8},{24,16},{1,9},{25,17},{2,10},{26,18},{3,11},{27,19},{4,12},{... | collective-permute-start | bytes 3538952 | tf_op jit(solution)/shard_map/ppermute | solution.py:561
  378.2 105.4 %all-to-all-start.4 = ((bf16[8,208,768]{2,1,0:T(8,128)(2,1)}), bf16[8,208,768]{2,1,0:T(8,128)(2,1)S(1)}, u32[]{:S(2)}, u32[]{:S(2)}) async-start(bf16[8,208,768]{2,1,0:T(8,128)(2,1)} %get-tuple-element.96), calls=%async_computation.4 | async-start | bytes 5111808 | tf_op jit(solution)/shard_map/all_to_all | solution.py:734
  382.6 39.4 %collective-permute-start.45 = (bf16[8,2,96,256]{3,2,1,0:T(8,128)(2,1)}, bf16[8,2,96,256]{3,2,1,0:T(8,128)(2,1)}, u32[]{:S(2)}, u32[]{:S(2)}) collective-permute-start(bf16[8,2,96,256]{3,2,1,0:T(8,128)(2,1)} %get-tuple-element.124), channel_id=1, source_target_pairs={{8,0},{16,24},{9,1},{17,25},{10,2},{18,26},{11,3},{19,27},{12,4},{... | collective-permute-start | bytes 2359304 | tf_op jit(solution)/shard_map/ppermute | solution.py:562
  386.4 47.3 %collective-permute-start.46 = (bf16[8,2,96,256]{3,2,1,0:T(8,128)(2,1)}, bf16[8,2,96,256]{3,2,1,0:T(8,128)(2,1)}, u32[]{:S(2)}, u32[]{:S(2)}) collective-permute-start(bf16[8,2,96,256]{3,2,1,0:T(8,128)(2,1)} %get-tuple-element.166), channel_id=1, source_target_pairs={{8,24},{16,0},{9,25},{17,1},{10,26},{18,2},{11,27},{19,3},{12,28},... | collective-permute-start | bytes 2359304 | tf_op jit(solution)/shard_map/ppermute | solution.py:568
  387.7 47.3 %collective-permute-start.47 = (bf16[8,2,96,256]{3,2,1,0:T(8,128)(2,1)}, bf16[8,2,96,256]{3,2,1,0:T(8,128)(2,1)}, u32[]{:S(2)}, u32[]{:S(2)}) collective-permute-start(bf16[8,2,96,256]{3,2,1,0:T(8,128)(2,1)} %get-tuple-element.165), channel_id=1, source_target_pairs={{8,16},{16,8},{9,17},{17,9},{10,18},{18,10},{11,19},{19,11},{12,20... | collective-permute-start | bytes 2359304 | tf_op jit(solution)/shard_map/ppermute | solution.py:569
  395.3 35.0 %collective-permute-start.53 = (bf16[8,2,96,128]{3,2,1,0:T(8,128)(2,1)}, bf16[8,2,96,128]{3,2,1,0:T(8,128)(2,1)S(1)}, u32[]{:S(2)}, u32[]{:S(2)}) collective-permute-start(bf16[8,2,96,128]{3,2,1,0:T(8,128)(2,1)} %get-tuple-element.130), channel_id=1, source_target_pairs={{8,0},{16,24},{9,1},{17,25},{10,2},{18,26},{11,3},{19,27},{12,4},{... | collective-permute-start | bytes 1179656 | tf_op jit(solution)/shard_map/ppermute | solution.py:562
  422.0 58.9 %collective-permute-start.49 = (bf16[8,2,96,256]{3,2,1,0:T(8,128)(2,1)S(1)}, bf16[8,2,96,256]{3,2,1,0:T(8,128)(2,1)S(1)}, u32[]{:S(2)}, u32[]{:S(2)}) collective-permute-start(bf16[8,2,96,256]{3,2,1,0:T(8,128)(2,1)S(1)} %copy-done.54), channel_id=1, source_target_pairs={{8,0},{16,24},{9,1},{17,25},{10,2},{18,26},{11,3},{19,27},{12,4},{... | collective-permute-start | bytes 2359304 | tf_op jit(solution)/shard_map/ppermute | solution.py:562
  430.3 50.6 %collective-permute-start.50 = (bf16[8,2,96,256]{3,2,1,0:T(8,128)(2,1)S(1)}, bf16[8,2,96,256]{3,2,1,0:T(8,128)(2,1)S(1)}, u32[]{:S(2)}, u32[]{:S(2)}) collective-permute-start(bf16[8,2,96,256]{3,2,1,0:T(8,128)(2,1)S(1)} %get-tuple-element.163), channel_id=1, source_target_pairs={{8,24},{16,0},{9,25},{17,1},{10,26},{18,2},{11,27},{19,3},{12,28},... | collective-permute-start | bytes 2359304 | tf_op jit(solution)/shard_map/ppermute | solution.py:568
  431.6 49.3 %collective-permute-start.51 = (bf16[8,2,96,256]{3,2,1,0:T(8,128)(2,1)S(1)}, bf16[8,2,96,256]{3,2,1,0:T(8,128)(2,1)S(1)}, u32[]{:S(2)}, u32[]{:S(2)}) collective-permute-start(bf16[8,2,96,256]{3,2,1,0:T(8,128)(2,1)S(1)} %get-tuple-element.164), channel_id=1, source_target_pairs={{8,16},{16,8},{9,17},{17,9},{10,18},{18,10},{11,19},{19,11},{12,20... | collective-permute-start | bytes 2359304 | tf_op jit(solution)/shard_map/ppermute | solution.py:569
  433.7 45.1 %collective-permute-start.54 = (bf16[8,2,96,128]{3,2,1,0:T(8,128)(2,1)S(1)}, bf16[8,2,96,128]{3,2,1,0:T(8,128)(2,1)S(1)}, u32[]{:S(2)}, u32[]{:S(2)}) collective-permute-start(bf16[8,2,96,128]{3,2,1,0:T(8,128)(2,1)S(1)} %get-tuple-element.171), channel_id=1, source_target_pairs={{8,24},{16,0},{9,25},{17,1},{10,26},{18,2},{11,27},{19,3},{12,28},... | collective-permute-start | bytes 1179656 | tf_op jit(solution)/shard_map/ppermute | solution.py:568
  435.1 43.8 %collective-permute-start.55 = (bf16[8,2,96,128]{3,2,1,0:T(8,128)(2,1)S(1)}, bf16[8,2,96,128]{3,2,1,0:T(8,128)(2,1)S(1)}, u32[]{:S(2)}, u32[]{:S(2)}) collective-permute-start(bf16[8,2,96,128]{3,2,1,0:T(8,128)(2,1)S(1)} %get-tuple-element.172), channel_id=1, source_target_pairs={{8,16},{16,8},{9,17},{17,9},{10,18},{18,10},{11,19},{19,11},{12,20... | collective-permute-start | bytes 1179656 | tf_op jit(solution)/shard_map/ppermute | solution.py:569
  483.6 68.3 %all-to-all-start.8 = ((bf16[8,2,96,384]{3,2,1,0:T(8,128)(2,1)}), bf16[8,2,96,384]{3,2,1,0:T(8,128)(2,1)}, u32[]{:S(2)}, u32[]{:S(2)}) async-start(bf16[8,2,96,384]{3,2,1,0:T(8,128)(2,1)} %pad_maximum_fusion.3), calls=%async_computation.8 | async-start | bytes 2359296 | tf_op jit(solution)/shard_map/all_to_all | solution.py:924
  604.0 36.7 %all-to-all-start.6 = ((bf16[4,4,112,768]{3,2,1,0:T(8,128)(2,1)}), bf16[4,4,112,768]{3,2,1,0:T(8,128)(2,1)}, u32[]{:S(2)}, u32[]{:S(2)}) async-start(bf16[4,4,112,768]{3,2,1,0:T(8,128)(2,1)} %bitcast.86), calls=%async_computation.6 | async-start | bytes 5505024 | tf_op jit(solution)/shard_map/all_to_all | solution.py:899
  617.6 40.0 %collective-permute-start.38 = (f32[200,768]{1,0:T(8,128)}, f32[200,768]{1,0:T(8,128)}, u32[]{:S(2)}, u32[]{:S(2)}) collective-permute-start(f32[200,768]{1,0:T(8,128)} %slice_select_fusion.3), channel_id=1, source_target_pairs={{0,1},{1,0},{2,3},{3,2},{4,5},{5,4},{6,7},{7,6},{8,9},{9,8},{10,11... | collective-permute-start | bytes 1843208 | tf_op jit(solution)/shard_map/ppermute | solution.py:746
  (96 other events, 1731.2 us)

commit v4 on v3

--- a/solution.py
+++ b/solution.py
@@ -156,7 +156,7 @@
         ),
         out_shape=[jax.ShapeDtypeStruct(s, d) for s, d in outs],
         compiler_params=pltpu.CompilerParams(vmem_limit_bytes=56 * 2**20),
-        cost_estimate=pl.CostEstimate(flops=3 * 10**9, bytes_accessed=6 * 10**7, transcendentals=2 * 10**6),
+        cost_estimate=pl.CostEstimate(flops=2 * 10**9, bytes_accessed=4 * 10**6, transcendentals=0),
         name="attend_forward",
     )(place, tokens_in, mask, lines, bias_pairs, *packs)
 
@@ -230,7 +230,7 @@
         out_specs=[by_image(s) for s, _ in outs[:5]] + [whole(s) for s, _ in outs[5:]],
         out_shape=[jax.ShapeDtypeStruct(s, d) for s, d in outs],
         compiler_params=pltpu.CompilerParams(vmem_limit_bytes=56 * 2**20),
-        cost_estimate=pl.CostEstimate(flops=4 * 10**9, bytes_accessed=7 * 10**7, transcendentals=2 * 10**6),
+        cost_estimate=pl.CostEstimate(flops=0, bytes_accessed=0, transcendentals=0),
         name="attend_backward",
     )(*ins)
 
@@ -278,7 +278,7 @@
         out_specs=out_spec,
         out_shape=out_shape,
         compiler_params=pltpu.CompilerParams(vmem_limit_bytes=56 * 2**20),
-        cost_estimate=pl.CostEstimate(flops=3 * 10**9, bytes_accessed=3 * 10**7, transcendentals=0),
+        cost_estimate=pl.CostEstimate(flops=0, bytes_accessed=0, transcendentals=0),
         name="attend_weights",
     )(n1, hb, dq, dk, dv, o, *extras)
 
@@ -317,7 +317,7 @@
         out_specs=[by_image(outs[0][0]), whole(outs[1][0])],
         out_shape=[jax.ShapeDtypeStruct(s, d) for s, d in outs],
         compiler_params=pltpu.CompilerParams(vmem_limit_bytes=56 * 2**20),
-        cost_estimate=pl.CostEstimate(flops=3 * 10**9, bytes_accessed=3 * 10**7, transcendentals=0),
+        cost_estimate=pl.CostEstimate(flops=0, bytes_accessed=0, transcendentals=0),
         name="input_backward",
     )(*ins)
 
@@ -356,8 +356,7 @@
     return jnp.broadcast_to(column, (256, 128)).T[:1, :]
 
 
-def expert_kernel(first, last, count, order_ref, x_ref, g_ref, b_ref, *refs):
-    pieces, refs = refs[:count], refs[count:]
+def expert_kernel(first, last, order_ref, x_ref, g_ref, b_ref, shards_ref, *refs):
     if not first:
         (y_in, p_in), refs = refs[:2], refs[2:]
     (y_out, p_out, bias_ref), refs = refs[:3], refs[3:]
@@ -368,25 +367,18 @@
 
     @pl.when(step == 0)
     def _():
-        if count == 1:
-            pltpu.make_async_copy(pieces[0], w_ref, sem).start()
+        if len(shards_ref.shape) == 3:
+            pltpu.make_async_copy(shards_ref, w_ref, sem).start()
         else:
-            part, units = pieces[0].shape[2:]
-            end = order_ref[4] == 1
-
-            def load(ref, slot):
+            part, units = shards_ref.shape[3:]
+            for z in range(4):
                 for p in range(8):
-                    row = pl.multiple_of(slot * (2 * part) + (p // 4) * part, 32)
+                    row = (z * 2 + p // 4) * part
                     pltpu.make_async_copy(
-                        ref.at[p],
+                        shards_ref.at[z, p],
                         w_ref.at[:, pl.ds(row, part), pl.ds((p % 4) * units, units)],
                         sem,
                     ).start()
-
-            load(pieces[0], order_ref[0])
-            for k in range(1, 4):
-                pl.when(end)(functools.partial(load, pieces[k], order_ref[k]))
-                pl.when(jnp.logical_not(end))(functools.partial(load, pieces[k + 3], order_ref[k]))
         acc_ref[...] = jnp.zeros_like(acc_ref)
         bias_ref[...] = jnp.zeros_like(bias_ref)
         pltpu.make_async_copy(w_ref, w_ref, sem).wait()
@@ -433,7 +425,7 @@
         if len(grads) == 1:
             grads[0][...] = acc_ref[...]
         else:
-            own_ref, rest_ref, near_ref = grads
+            own_ref, near_ref, rest_ref = grads[:3]
             part, units = own_ref.shape[2:]
             for k in range(4):
                 for q in range(8):
@@ -442,22 +434,24 @@
                     block = acc_ref[:, pl.ds(row, part), columns].astype(BF16)
                     if k == 0:
                         own_ref[q] = block
+                    elif k == 3 and len(grads) == 4:
+                        grads[3][q] = block
                     else:
                         rest_ref[k - 1, q] = block
                     if k == 1:
                         near_ref[q] = block
 
 
-def expert_chunk(order, x, g, b, sums, pieces, last):
+def expert_chunk(order, x, g, b, sums, shards, last):
     experts, slots, model = g.shape
     units = b.shape[1]
     first = sums is None
     step = 2
     block = lambda rows: pl.BlockSpec((step, rows, model), lambda i, o: (i, 0, 0))
     full = lambda shape: pl.BlockSpec(shape, lambda i, o: (0,) * len(shape))
-    ins = [x, g, b] + list(pieces) + ([] if first else list(sums))
+    ins = [x, g, b, shards] + ([] if first else list(sums))
     in_specs = [block(x.shape[1]), block(slots), full(b.shape)]
-    in_specs += [pl.BlockSpec(memory_space=pl.ANY)] * len(pieces)
+    in_specs.append(pl.BlockSpec(memory_space=pl.ANY))
     in_specs += [] if first else [block(slots)] * 2
     rows = (experts, slots, model)
     if last:
@@ -466,15 +460,16 @@
         outs = [(rows, F32), (rows, F32)]
     out_specs = [block(s[1]) for s, _ in outs]
     outs.append((b.shape, F32))
-    if len(pieces) == 1:
+    if len(shards.shape) == 3:
         outs.append(((2, model, units), F32))
     else:
-        shape = pieces[0].shape
-        outs += [(shape, BF16), ((3,) + shape, BF16), (shape, BF16)]
+        shape = shards.shape[1:]
+        outs += [(shape, BF16), (shape, BF16)]
+        outs += [((2,) + shape, BF16), (shape, BF16)] if first else [((3,) + shape, BF16)]
     out_specs += [full(s) for s, _ in outs[2:]]
-    base = 4 + len(pieces)
+    base = 5
     return pl.pallas_call(
-        functools.partial(expert_kernel, first, last, len(pieces)),
+        functools.partial(expert_kernel, first, last),
         grid_spec=pltpu.PrefetchScalarGridSpec(
             num_scalar_prefetch=1,
             grid=(experts // step,),
@@ -490,8 +485,7 @@
         input_output_aliases={} if first or last else {base: 0, base + 1: 1},
         compiler_params=pltpu.CompilerParams(vmem_limit_bytes=58 * 2**20),
         cost_estimate=pl.CostEstimate(
-            flops=12 * experts * slots * model * units, bytes_accessed=3 * 10**7,
-            transcendentals=2 * experts * slots * units,
+            flops=2 * experts * slots * model * units, bytes_accessed=4 * 10**6, transcendentals=0
         ),
         name="expert_chunk",
     )(order, *ins)
@@ -507,6 +501,7 @@
 INWARD = [(0, 1), (3, 2)]
 MIDDLE = [(1, 2), (2, 1)]
 OUTWARD = [(1, 0), (2, 3)]
+ACROSS = [(1, 3), (2, 0)]
 ORDER = ((0, 1, 2, 3), (1, 0, 2, 3), (2, 3, 1, 0), (3, 2, 1, 0))
 
 
@@ -515,36 +510,6 @@
     if not events:
         return values
     return lax.optimization_barrier((values, *events))[0]
-
-
-class Line:
-    def __init__(self, own, length):
-        self.own, self.length = own, length
-
-    def start(self, *events):
-        if self.length != 4:
-            self.full = lax.all_gather(self.own, "z", axis=1, tiled=True)
-            return
-        own = tie(self.own, *events)
-        self.inward = lax.ppermute(own, "z", INWARD)
-        self.outward_one = lax.ppermute(own, "z", OUTWARD)
-        self.middle_one = lax.ppermute(own, "z", MIDDLE)
-        self.outward_two = lax.ppermute(own, "z", [(1, 3), (2, 0)])
-        self.middle_two = lax.ppermute(self.inward, "z", MIDDLE)
-        self.outward_three = lax.ppermute(self.middle_two, "z", OUTWARD)
-
-    def early(self):
-        if self.length != 4:
-            return []
-        return [self.inward, self.middle_one, self.outward_one]
-
-    def result(self):
-        if self.length != 4:
-            return [self.full]
-        return [
-            self.own, self.outward_one, self.outward_two, self.outward_three,
-            self.inward, self.middle_one, self.middle_two,
-        ]
 
 
 def add(*terms):
@@ -557,22 +522,34 @@
         if len(grads) == 1:
             self.total = lax.psum_scatter(grads[0], "z", scatter_dimension=1, tiled=True)
             return
-        own, rest, near = grads
-        self.inward = lax.ppermute(rest, "z", INWARD)
-        self.outward_one = lax.ppermute(near, "z", OUTWARD)
-        self.two = add(rest[1], self.inward[1])
-        self.three = add(rest[2], self.inward[2])
-
-    def finish(self, *events):
+        own, near, *rest = grads
+        self.inward = [lax.ppermute(one, "z", INWARD) for one in rest]
+
+    def forward_far(self, *events):
+        if len(self.grads) == 1:
+            return self.total
+        inward = tie(self.inward[-1], *events)
+        far, inward = [one[2] if one.shape[0] == 3 else one for one in (self.grads[-1], inward)]
+        three = add(far, inward)
+        self.outward_two = lax.ppermute(three, "z", ACROSS)
+        return three
+
+    def forward(self, *events):
+        if len(self.grads) == 1:
+            return self.total
+        near = self.grads[1]
+        self.inward[0] = tie(self.inward[0], *events)
+        two = add(self.grads[2][1], self.inward[0][1])
+        self.middle = lax.ppermute(two, "z", MIDDLE)
+        self.outward_one = lax.ppermute(tie(near, *events), "z", OUTWARD)
+        return two
+
+    def finish(self):
         if len(self.grads) > 1:
-            outward_two = lax.ppermute(tie(self.three, *events), "z", [(1, 3), (2, 0)])
-            middle = lax.ppermute(tie(self.two, *events), "z", MIDDLE)
             self.total = add(
-                self.grads[0], self.inward[0], self.outward_one, outward_two, middle
+                self.grads[0], self.inward[0][0], self.outward_one, self.outward_two, self.middle
             )
-
-    def early(self):
-        return [self.three, self.two] if len(self.grads) > 1 else []
+        return self.total
 
 
 def gather_packs(pack):
@@ -585,7 +562,7 @@
     over_y = lax.ppermute(column, "y", swap)
     over_both = lax.ppermute(column, ("x", "y"), [(0, 3), (1, 2), (2, 1), (3, 0)])
     four = [column, over_x, over_y, over_both]
-    return four + [lax.ppermute(each, "c", swap) for each in four]
+    return four + [lax.ppermute(each, "c", swap) for each in four], below[1:]
 
 
 def shards(
@@ -619,7 +596,12 @@
     width = qkv_weight.shape[2]
     tokens = piece * sequence
     blocks = units // CHUNK
-    spans = [(0, 1), (1, 3), (3, 5), (5, 6)] if blocks == 6 else [(0, blocks)]
+    spans = [(0, 3), (3, 5), (5, 6)] if blocks == 6 else [(0, blocks)]
+
+    head = spans[0][1] * CHUNK
+    sizes = [head, units - head] if units > head else [head]
+    packed = pack_experts(up_weight, down_weight, sizes)
+    qkv_weight, norm1_gain = tie((qkv_weight, norm1_gain), packed[0])
 
     smalls = jnp.concatenate(
         [
@@ -649,7 +631,7 @@
     )
     place = [lax.axis_index(name) for name in ("z", "x", "y", "c")]
     if length == 4:
-        packs = gather_packs(pack)
+        packs, below = gather_packs(pack)
         by_x = jnp.stack([packs[0][:, part:], packs[1][:, part:]]).reshape(2, 4, -1)
         pick_x = (place[1] ^ jnp.arange(2))[:, None] == jnp.arange(2)
         pick_z = (place[0] - jnp.arange(4)[:, None]) % 4 == jnp.arange(4)
@@ -660,23 +642,11 @@
         packs = packs.reshape(quarter, dp, pack.shape[0], model)
         vectors = packs[0, :, part:].reshape(dp, -1)
         packs = [packs[:, :, :part].reshape(quarter, model, model)]
-    vectors = vectors[:, : small_rows * part].reshape(dp, small_rows, part).transpose(1, 0, 2)
-    lines = vectors[: 7 + 2 * experts].reshape(-1, model).astype(F32)
-    bias_pairs = lines[2:4].reshape(2, quarter, width).transpose(1, 0, 2)
-    bias_down = lines[7 : 7 + experts]
-    router = lines[7 + experts :].astype(BF16)
-    bias_up = vectors[7 + 2 * experts :].reshape(experts, quarter, dp, part)
-    bias_up = bias_up.transpose(0, 2, 1, 3).reshape(experts, quarter, units)
-    bias_up = lax.dynamic_index_in_dim(bias_up, expert, 0, keepdims=False).astype(F32)
-
-    head = spans[0][1] * CHUNK
-    sizes = [head, units - head] if units > head else [head]
-    packed = pack_experts(up_weight, down_weight, sizes)
-    event = None
+    event = []
     parts = []
     for some in packed:
-        some = lax.all_to_all(tie(some, event), PLANE, 0, 0, tiled=True)
-        event = some
+        some = lax.all_to_all(tie(some, *event), PLANE, 0, 0, tiled=True)
+        event = [some, packs[len(packs) // 2]]
         starts = [CHUNK * f for f, _ in spans[1:]] if parts else [0]
         stops = [CHUNK * l for _, l in spans[1:]] if parts else [head]
         base = starts[0]
@@ -686,6 +656,15 @@
             one.reshape(2, quarter, 2, part, -1).transpose(2, 0, 3, 1, 4).reshape(2, 2 * part, -1)
             for one in parts
         ]
+
+    vectors = vectors[:, : small_rows * part].reshape(dp, small_rows, part).transpose(1, 0, 2)
+    lines = vectors[: 7 + 2 * experts].reshape(-1, model).astype(F32)
+    bias_pairs = lines[2:4].reshape(2, quarter, width).transpose(1, 0, 2)
+    bias_down = lines[7 : 7 + experts]
+    router = lines[7 + experts :].astype(BF16)
+    bias_up = vectors[7 + 2 * experts :].reshape(experts, quarter, dp, part)
+    bias_up = bias_up.transpose(0, 2, 1, 3).reshape(experts, quarter, units)
+    bias_up = lax.dynamic_index_in_dim(bias_up, expert, 0, keepdims=False).astype(F32)
 
     first_group = chip_y * 3
     group_tokens = GROUP_IMG * sequence
@@ -750,22 +729,25 @@
             jnp.concatenate([mine[None], full]),
         )
 
-    lines_z = [Line(own, length) for own in parts]
-    for k in range(2):
-        if k < len(lines_z):
-            lines_z[k].start(*(lines_z[k - 1].early() if k else []))
+    if length == 4:
+        parts[0] = tie(parts[0], *below)
+    full_parts = [
+        lax.all_gather(one, "z", axis=0, tiled=False)
+        if length == 4
+        else lax.all_gather(one, "z", axis=1, tiled=True)
+        for one in parts
+    ]
     grad_full, grad_shared = both_groups(out_grad)
-    incoming = swap_experts(dispatch(grad_full, grad_shared), event)
+    incoming = swap_experts(dispatch(grad_full, grad_shared), packs[-1], parts[-1])
 
     local_start = (chip_y * 2 + core) * piece
     mask_here = lax.dynamic_slice_in_dim(key_mask, local_start, piece, 0)[:, None]
-    before = [event] + lines_z[0].early() + (lines_z[1].early() if len(lines_z) > 1 else [])
     n1, n2, residual, q, k, v, attended, lse, wq, wk, wv, wo = attend_forward(
-        jnp.stack(place).astype(jnp.int32), tie(tokens_in, *before), mask_here, lines, bias_pairs,
+        jnp.stack(place).astype(jnp.int32),
+        tokens_in, mask_here, lines, bias_pairs,
         packs, width,
     )
-    for line in lines_z[2:]:
-        line.start(n2)
+    n2 = tie(n2, incoming)
     normed_two = n2.reshape(tokens, model)
 
     normed_full, normed_shared = both_groups(n2)
@@ -790,7 +772,8 @@
         slot_gates(match_half, normed_shared, position_half),
     )
     chosen = swap_experts(
-        jnp.concatenate([dispatch(normed_full, normed_shared), lines_of(gates_sent)], 1), incoming
+        jnp.concatenate([dispatch(normed_full, normed_shared), lines_of(gates_sent)], 1),
+        incoming,
     )
 
     order = jnp.asarray(
@@ -801,28 +784,28 @@
     sums = None
     bias_parts = []
     reduced = []
+    count = len(spans)
     for index, (first, last) in enumerate(spans):
-        both = lines_z[index].result()
+        bias_one = bias_up[:, first * CHUNK : last * CHUNK].reshape(1, -1)
+        final = index == count - 1
         events = []
-        if index >= 2:
-            events += reduced[index - 2].early()
-        if index == 1:
-            for line in lines_z[2:]:
-                events += line.early()
-        bias_one = bias_up[:, first * CHUNK : last * CHUNK].reshape(1, -1)
-        final = index == len(spans) - 1
+        if count == 3 and index == 2:
+            events.append(reduced[0].forward_far())
         *sums, bias_part = (
-            outs := expert_chunk(order, chosen, incoming, tie(bias_one, *events), sums, both, final)
+            outs := expert_chunk(
+                order, chosen, incoming, tie(bias_one, *events), sums, full_parts[index], final
+            )
         )[:3]
         bias_parts.append(bias_part.reshape(quarter, -1))
         reduced.append(Reduce(outs[3:]))
-        if index >= 2:
-            reduced[index - 2].finish()
 
     mixed, pulled = sums
     back = swap_experts(pulled)
     gate_back = values_of(back)
     norm_two_grad = combine(back)
+    mixed = swap_experts(mixed, back)
+    if count == 3:
+        norm_two_grad = tie(norm_two_grad, reduced[0].forward(back))
 
     def slots_to_tokens(match, parts_here):
         parts_here = parts_here.reshape(experts, -1)
@@ -858,8 +841,10 @@
         norm_two_grad, out_grad, residual, mask_here, wo, lines, q, k, v, lse
     )
     input_grad, line_ones = input_backward(h_grad, tokens_in, wq, wk, wv, lines, dq, dk, dv)
-    for some in reduced[-2:] if len(reduced) > 1 else reduced:
-        some.finish()
+    if count == 3:
+        hb = tie(
+            hb, mixed, reduced[0].finish(), reduced[1].forward(hb), reduced[1].forward_far(hb)
+        )
 
     bias_rows = jnp.concatenate(bias_parts, 1).reshape(dp, quarter, part)
     bias_rows = jnp.where(
@@ -896,18 +881,30 @@
     theirs = lax.ppermute(theirs, "c", swap)
     pack_grads = (mine.astype(F32) + theirs.astype(F32)).astype(sum_type)
     pack_grads = pack_grads.reshape((-1,) + pack_grads.shape[2:])
+    if count == 3:
+        pack_grads = tie(
+            pack_grads,
+            reduced[2].forward(pack_grads),
+            reduced[2].forward_far(pack_grads),
+            reduced[1].finish(),
+        )
     pack_grads = lax.all_to_all(pack_grads, ("x", "y"), 0, 0, tiled=True)
     pack_grads = jnp.sum(pack_grads.astype(F32), 0).astype(sum_type)
+    if count == 3:
+        reduced[2].finish()
     if length == 4:
-        pack_grads = lax.all_to_all(pack_grads, "z", 0, 0, tiled=True)
-        pack_grad = jnp.sum(pack_grads.astype(F32), 0)
+        pack_grad = lax.dynamic_index_in_dim(pack_grads, place[0], 0, keepdims=False).astype(F32)
+        for far in (1, 2, 3):
+            some = lax.dynamic_index_in_dim(pack_grads, (place[0] + far) % 4, 0, keepdims=False)
+            some = lax.ppermute(some, "z", [(k, (k + far) % 4) for k in range(4)])
+            pack_grad = pack_grad + some.astype(F32)
     else:
         pack_grad = lax.psum_scatter(pack_grads, "z", scatter_dimension=0, tiled=False)
     qkv_out = pack_grad[:part, : 3 * width].reshape(part, 3, width).transpose(1, 0, 2)
     out_weight_grad = pack_grad[:part, 3 * width :].T
     small_grads = pack_grad[part:].reshape(-1)[: small_rows * part].reshape(small_rows, part)
 
-    mixture = combine(swap_experts(mixed, back))
+    mixture = combine(mixed)
     bias_term = jnp.dot(share_here, bias_down, precision=HIGHEST).reshape(residual.shape)
     output = (residual + mixture + bias_term).astype(BF16)
 
@@ -918,10 +915,10 @@
             one.reshape(2, 2, part, quarter, -1).transpose(1, 3, 0, 2, 4).reshape(experts, 2, part, -1)
             for one in totals
         ]
-    for some in (totals[:2], totals[2:]):
+    for some, event in ((totals[:1], mixed), (totals[1:2], pack_grads), (totals[2:], pack_grads)):
         if some:
             some = some[0] if len(some) == 1 else jnp.concatenate(some, -1)
-            some = lax.all_to_all(some.astype(BF16), PLANE, 0, 0, tiled=True).astype(F32)
+            some = lax.all_to_all(tie(some.astype(BF16), event), PLANE, 0, 0, tiled=True).astype(F32)
             ups.append(some[:, 0])
             downs.append(some[:, 1])
     up_grad = jnp.concatenate(ups, -1)

time: 684 us -> 561 us (0.82)
  waiting for transfers between devices: 259 us -> 168 us
  starting transfers between devices: 128 us -> 99.3 us
  between operations: 2.69 us -> 15.4 us
  other arithmetic: 67.9 us -> 55.9 us
  local copies, waits for them, and re-layouts: 47.9 us -> 55.5 us
  Pallas kernels: 152 us -> 145 us
    ppermute x44 -> x20, waiting for transfers between devices: 158 us -> 65.8 us  [the longest x4 42.8 us: __init__(): self.inward = [lax.ppermute(one, 'z', INWARD) for one in rest]]
    ppermute x44 -> x20, starting transfers between devices: 69 us -> 45.4 us  [the longest x4 24.4 us: __init__(): self.inward = [lax.ppermute(one, 'z', INWARD) for one in rest]]
    all_to_all x5, waiting for transfers between devices: 36 us -> 16.3 us  [the longest x3 10.3 us: shards(): lax.all_to_all(tie(some.astype(BF16), event), PLANE, 0, 0, tiled=True)]
    ppermute x1, waiting for transfers between devices: 16.1 us -> 0.01 us  [gather_packs(): over_y = lax.ppermute(column, 'y', swap)]
    all_to_all x4, waiting for transfers between devices: 23.6 us -> 37.1 us  [swap_experts(): return lax.all_to_all(tie(rows, *events), PLANE, 0, 0, tiled=True)]
    ppermute x1, waiting for transfers between devices: 0.01 us -> 11.1 us  [gather_packs(): lax.ppermute(column, ('x', 'y'), [(0, 3), (1, 2), (2, 1), (3, 0)])]
    ppermute x3, waiting for transfers between devices: 0.01 us -> 10.6 us  [gather_packs(): lax.ppermute(pack, 'z', [(k, (k + far) % 4) for k in range(4)])]
    pallas_call x4 -> x3, Pallas kernels: 82.1 us -> 75.3 us  [expert_chunk(): pl.pallas_call(functools.partial(expert_kernel, first, last), grid_spec=p...]
  transfers between devices with their start and end apart: 66 -> 45, of which waited for: 18 -> 16; matrix products, arithmetic and copies ran while one was open for 16% -> 19% of each run, Pallas kernels for 23% -> 21%
where the time goes in v4:
time: 561 us; the launch traced here: 554 us
  waiting for transfers between devices  168 us (30%)
  Pallas kernels  145 us (26%)
  starting transfers between devices  99.3 us (18%)
  other arithmetic  55.9 us (10%)
  local copies, waits for them, and re-layouts  55.5 us (10%)
  between operations  15.4 us (3%)
  matrix products  14.8 us (3%)
    pallas_call x3, Pallas kernels, expert_chunk(): pl.pallas_call(functools.partial(expert_kernel, first, last), grid_spec=p...  75.3 us
    ppermute x4, waiting for transfers between devices, __init__(): self.inward = [lax.ppermute(one, 'z', INWARD) for one in rest]  42.8 us
    all_to_all x4, waiting for transfers between devices, swap_experts(): return lax.all_to_all(tie(rows, *events), PLANE, 0, 0, tiled=True)  37.1 us
    pallas_call x1, Pallas kernels, attend_forward(): pl.pallas_call(attend_forward_kernel, grid_spec=pltpu.PrefetchScalarGridS...  26.2 us
    ppermute x4, starting transfers between devices, __init__(): self.inward = [lax.ppermute(one, 'z', INWARD) for one in rest]  24.4 us
    ppermute x3, waiting for transfers between devices, forward(): self.outward_one = lax.ppermute(tie(near, *events), 'z', OUTWARD)  21.7 us
    pallas_call x1, Pallas kernels, attend_backward(): pl.pallas_call(attend_backward_kernel, grid=(images,), in_specs=[whole(a....  20.9 us
    convert_element_type x7, other arithmetic, add(): return sum((term.astype(F32) for term in terms)).astype(BF16)  20.4 us
  transfers between devices with their start and end apart: 45, of which 16 were waited for; matrix products, arithmetic and copies ran while one was open for 19% of the time, Pallas kernels for 21%

profile of v4, /device:TPU:0, one launch (start us, length us, event | category | flops | bytes accessed | tf_op | source)
XLA Modules:
  0.0 553.7 jit_solution(13597988046152364759)
XLA Ops:
  15.5 5.3 all-to-all-start
  31.1 7.0 %collective-permute-done.1 = bf16[112,768]{1,0:T(8,128)(2,1)S(1)} collective-permute-done((bf16[112,768]{1,0:T(8,128)(2,1)S(1)}, bf16[112,768]{1,0:T(8,128)(2,1)S(1)}, u32[]{:S(2)}, u32[]{:S(2)}) %collective-permute-start.1) | collective-permute-done | bytes 172064 | tf_op jit(solution)/shard_map/ppermute | solution.py:557
  52.7 11.1 %collective-permute-done.5.refs_3_ = bf16[4,112,768]{2,1,0:T(8,128)(2,1)} collective-permute-done((bf16[4,112,768]{2,1,0:T(8,128)(2,1)}, bf16[4,112,768]{2,1,0:T(8,128)(2,1)}, u32[]{:S(2)}, u32[]{:S(2)}) %collective-permute-start.5) | collective-permute-done | bytes 688160 | tf_op jit(solution)/shard_map/ppermute | solution.py:563
  70.5 6.0 %all-to-all-done.1 = bf16[8,2,96,384]{3,2,1,0:T(8,128)(2,1)S(1)} async-done(((bf16[8,2,96,384]{3,2,1,0:T(8,128)(2,1)}), bf16[8,2,96,384]{3,2,1,0:T(8,128)(2,1)S(1)}, u32[]{:S(2)}, u32[]{:S(2)}) %all-to-all-start.1) | async-done | bytes 1179680 | tf_op jit(solution)/shard_map/all_to_all | solution.py:648
  77.7 3.6 all-to-all-start.2
  83.8 7.6 %collective-permute-done.3.refs_1_ = bf16[4,112,768]{2,1,0:T(8,128)(2,1)} collective-permute-done((bf16[4,112,768]{2,1,0:T(8,128)(2,1)}, bf16[4,112,768]{2,1,0:T(8,128)(2,1)}, u32[]{:S(2)}, u32[]{:S(2)}) %collective-permute-start.3) | collective-permute-done | bytes 688160 | tf_op jit(solution)/shard_map/ppermute | solution.py:561
  100.2 26.2 %attend_forward.1 = (bf16[3,208,768]{2,1,0:T(8,128)(2,1)}, bf16[3,200,768]{2,1,0:T(8,128)(2,1)}, f32[3,200,768]{2,1,0:T(8,128)}, bf16[3,4,200,192]{3,2,1,0:T(8,1...) custom-call(s32[4]{0:T(128)} %pad_add_fusion.place_ref, ...), custom_call_target="tpu_custom_call" | custom-call | flops 2000000000 | bytes 4000000 | tf_op jit(solution)/shard_map/attend_forward/pallas_call | solution.py:147
  135.2 3.6 all-to-all-start.3
  145.3 24.1 %all-to-all-done.3.x_ref = bf16[8,208,768]{2,1,0:T(8,128)(2,1)S(1)} async-done(((bf16[8,208,768]{2,1,0:T(8,128)(2,1)}), bf16[8,208,768]{2,1,0:T(8,128)(2,1)S(1)}, u32[]{:S(2)}, u32[]{:S(2)}) %all-to-all-start.3) | async-done | bytes 2555936 | tf_op jit(solution)/shard_map/all_to_all | solution.py:713
  170.8 33.9 %expert_chunk.3 = (f32[8,192,768]{2,1,0:T(8,128)}, f32[8,192,768]{2,1,0:T(8,128)}, f32[1,1536]{1,0:T(1,128)}, bf16[8,2,96,384]{3,2,1,0:T(8,128)(2,1)}, bf16[8,2,...) custom-call(s32[5]{0:T(128)} %fusion.52.order_ref, ...), custom_call_target="tpu_custom_call" | custom-call | flops 3623878656 | bytes 4000000 | tf_op jit(solution)/shard_map/expert_chunk/pallas_call | solution.py:471
  204.7 6.5 %collective-permute-start.12 = (bf16[8,2,96,384]{3,2,1,0:T(8,128)(2,1)}, bf16[8,2,96,384]{3,2,1,0:T(8,128)(2,1)S(1)}, u32[]{:S(2)}, u32[]{:S(2)}) collective-permute-start(bf16[8,2,96,384]{3,2,1,0:T(8,128)(2,1)} %get-tuple-element.91), channel_id=1, source_target_pairs={{0,8},{24,16},{1,9},{25,17},{2,10},{26,18},{3,11},{27,19},{4,12},{... | collective-permute-start | bytes 3538952 | tf_op jit(solution)/shard_map/ppermute | solution.py:526
  212.4 25.9 %expert_chunk.4 = (f32[8,192,768]{2,1,0:T(8,128)}, f32[8,192,768]{2,1,0:T(8,128)}, f32[1,1024]{1,0:T(1,128)}, bf16[8,2,96,256]{3,2,1,0:T(8,128)(2,1)}, bf16[8,2,...) custom-call(s32[5]{0:T(128)} %fusion.52.order_ref, ...), custom_call_target="tpu_custom_call", output_to_operand_aliasing={{0}: (5, {}), {1}: (6, {})} | custom-call | flops 2415919104 | bytes 4000000 | tf_op jit(solution)/shard_map/expert_chunk/pallas_call | solution.py:471
  238.3 16.0 %collective-permute-done.12 = bf16[8,2,96,384]{3,2,1,0:T(8,128)(2,1)S(1)} collective-permute-done((bf16[8,2,96,384]{3,2,1,0:T(8,128)(2,1)}, bf16[8,2,96,384]{3,2,1,0:T(8,128)(2,1)S(1)}, u32[]{:S(2)}, u32[]{:S(2)}) %collective-permute-start.12) | collective-permute-done | bytes 1179680 | tf_op jit(solution)/shard_map/ppermute | solution.py:526
  255.8 15.6 %expert_chunk.5 = (bf16[8,192,768]{2,1,0:T(8,128)(2,1)}, bf16[8,208,768]{2,1,0:T(8,128)(2,1)}, f32[1,512]{1,0:T(1,128)}, bf16[8,2,96,128]{3,2,1,0:T(8,128)(2,1)}...) custom-call(s32[5]{0:T(128)} %fusion.52.order_ref, bf16[8,208,768]{2,1,0:T(8,128)(2,1)} %copy-done.5, ...), custom_call_target="tpu_custom_call" | custom-call | flops 1207959552 | bytes 4000000 | tf_op jit(solution)/shard_map/expert_chunk/pallas_call | solution.py:471
  271.3 4.5 all-to-all-start.4
  275.9 5.7 %collective-permute-start.15 = (bf16[2,8,2,96,384]{4,3,2,1,0:T(8,128)(2,1)}, bf16[2,8,2,96,384]{4,3,2,1,0:T(8,128)(2,1)}, u32[]{:S(2)}, u32[]{:S(2)}) collective-permute-start(bf16[2,8,2,96,384]{4,3,2,1,0:T(8,128)(2,1)} %get-tuple-element.100), channel_id=1, source_target_pairs={{0,8},{24,16},{1,9},{25,17},{2,10},{26,18},{3,11},{27,19},{4,12},{... | collective-permute-start | bytes 7077896 | tf_op jit(solution)/shard_map/ppermute | solution.py:526
  293.5 13.0 %all-to-all-done.4 = bf16[8,208,768]{2,1,0:T(8,128)(2,1)} async-done(((bf16[8,208,768]{2,1,0:T(8,128)(2,1)}), bf16[8,208,768]{2,1,0:T(8,128)(2,1)}, u32[]{:S(2)}, u32[]{:S(2)}) %all-to-all-start.4) | async-done | bytes 2555936 | tf_op jit(solution)/shard_map/all_to_all | solution.py:713
  308.6 23.5 %collective-permute-done.15 = bf16[2,8,2,96,384]{4,3,2,1,0:T(8,128)(2,1)} collective-permute-done((bf16[2,8,2,96,384]{4,3,2,1,0:T(8,128)(2,1)}, bf16[2,8,2,96,384]{4,3,2,1,0:T(8,128)(2,1)}, u32[]{:S(2)}, u32[]{:S(2)}) %collective-permute-start.15) | collective-permute-done | bytes 2359328 | tf_op jit(solution)/shard_map/ppermute | solution.py:526
  336.7 4.5 all-to-all-start.5
  357.9 20.9 %attend_backward.1 = (f32[3,200,768]{2,1,0:T(8,128)}, bf16[3,208,768]{2,1,0:T(8,128)(2,1)}, bf16[3,4,208,192]{3,2,1,0:T(8,128)(2,1)}, bf16[3,4,208,192]{3,2,1,0:...) custom-call(f32[3,200,768]{2,1,0:T(8,128)} %add.261.n2_grad_ref, ...), custom_call_target="tpu_custom_call" | custom-call | tf_op jit(solution)/shard_map/attend_backward/pallas_call | solution.py:226
  382.1 9.7 %input_backward.1 = (f32[3,200,768]{2,1,0:T(8,128)}, f32[8,768]{1,0:T(8,128)}) custom-call(f32[3,200,768]{2,1,0:T(8,128)} %get-tuple-element.108.h_grad_ref, bf16[3,200,768]{2,1,0:T(8,128)(2,1)} %tokens_ref.3, bf16[4,768,192]{2,1,0:T(8,128)(2,1)} %get-tuple-element.109.wq_ref, bf16[4,768,192]{2,1,0:T(8,128)(2,1)} %get-tuple-element.110.wk_ref, ...), custom_call_target="tpu_custom_call" | custom-call | tf_op jit(solution)/shard_map/input_backward/pallas_call | solution.py:313
  398.5 4.2 fusion.4
  402.7 9.5 %attend_weights.1 = bf16[2,2,2,4,112,768]{5,4,3,2,1,0:T(8,128)(2,1)} custom-call(bf16[3,208,768]{2,1,0:T(8,128)(2,1)} %get-tuple-element.116.n1_ref, bf16[3,208,768]{2,1,0:T(8,128)(2,1)} %get-tuple-element.124.hb_ref, bf16[3,4,208,192]{3,2,1,0:T(8,128)(2,1)} %get-tuple-element.112.dq_ref, bf16[3,4,208,192]{3,2,1,0:T(8,128)(2,1)} %get-tuple-element.113.dk_ref, ...), custom_call_target="tpu_custom_call" | custom-call | tf_op jit(solution)/shard_map/attend_weights/pallas_call | solution.py:274
  419.9 9.4 %collective-permute-start.22 = (bf16[3,8,2,96,128]{4,3,2,1,0:T(8,128)(2,1)}, bf16[3,8,2,96,128]{4,3,2,1,0:T(8,128)(2,1)S(1)}, u32[]{:S(2)}, u32[]{:S(2)}) collective-permute-start(bf16[3,8,2,96,128]{4,3,2,1,0:T(8,128)(2,1)} %get-tuple-element.132), channel_id=1, source_target_pairs={{0,8},{24,16},{1,9},{25,17},{2,10},{26,18},{3,11},{27,19},{4,12},{... | collective-permute-start | bytes 3538952 | tf_op jit(solution)/shard_map/ppermute | solution.py:526
  429.2 3.9 all-to-all-start.7
  433.1 21.7 %collective-permute-done.23 = bf16[8,2,96,256]{3,2,1,0:T(8,128)(2,1)} collective-permute-done((bf16[8,2,96,256]{3,2,1,0:T(8,128)(2,1)}, bf16[8,2,96,256]{3,2,1,0:T(8,128)(2,1)}, u32[]{:S(2)}, u32[]{:S(2)}) %collective-permute-start.23) | collective-permute-done | bytes 786464 | tf_op jit(solution)/shard_map/ppermute | solution.py:544
  458.4 4.8 fusion
  465.9 4.6 all-to-all-start.6
  483.8 19.0 %all-to-all-done.6 = bf16[4,4,112,768]{3,2,1,0:T(8,128)(2,1)} async-done(((bf16[4,4,112,768]{3,2,1,0:T(8,128)(2,1)}), bf16[4,4,112,768]{3,2,1,0:T(8,128)(2,1)}, u32[]{:S(2)}, u32[]{:S(2)}) %all-to-all-start.6) | async-done | bytes 2752544 | tf_op jit(solution)/shard_map/all_to_all | solution.py:891
  505.9 4.9 collective-permute-start.26
  515.9 4.1 all-to-all-start.9
  534.1 8.5 %all-to-all-done.8 = bf16[8,2,96,256]{3,2,1,0:T(8,128)(2,1)S(1)} async-done(((bf16[8,2,96,256]{3,2,1,0:T(8,128)(2,1)}), bf16[8,2,96,256]{3,2,1,0:T(8,128)(2,1)S(1)}, u32[]{:S(2)}, u32[]{:S(2)}) %all-to-all-start.8) | async-done | bytes 786464 | tf_op jit(solution)/shard_map/all_to_all | solution.py:921
  (374 shorter events, 169.6 us)
Async XLA Ops:
  15.5 22.6 %all-to-all-start = ((bf16[8,2,96,384]{3,2,1,0:T(8,128)(2,1)}), bf16[8,2,96,384]{3,2,1,0:T(8,128)(2,1)S(1)}, u32[]{:S(2)}, u32[]{:S(2)}) async-start(bf16[8,2,96,384]{3,2,1,0:T(8,128)(2,1)} %copy-done.3), calls=%async_computation | async-start | bytes 2359296 | tf_op jit(solution)/shard_map/all_to_all | solution.py:648
  20.9 148.5 %all-gather.7.cloned.1.call-start = ((), (), s32[]{:S(2)}) async-start(), calls=%async_computation.10 | async-start | bytes 5898240 | tf_op jit(solution)/shard_map/all_gather | solution.py:735
  23.6 14.5 %collective-permute-start.1 = (bf16[112,768]{1,0:T(8,128)(2,1)S(1)}, bf16[112,768]{1,0:T(8,128)(2,1)S(1)}, u32[]{:S(2)}, u32[]{:S(2)}) collective-permute-start(bf16[112,768]{1,0:T(8,128)(2,1)S(1)} %pad_maximum_fusion.5), channel_id=1, source_target_pairs={{0,16},{8,24},{16,0},{24,8},{1,17},{9,25},{17,1},{25,9},{2,18},{10... | collective-permute-start | bytes 516104 | tf_op jit(solution)/shard_map/ppermute | solution.py:557
  39.9 27.0 %collective-permute-start.10 = (bf16[200,768]{1,0:T(8,128)(2,1)}, bf16[200,768]{1,0:T(8,128)(2,1)}, u32[]{:S(2)}, u32[]{:S(2)}) collective-permute-start(bf16[200,768]{1,0:T(8,128)(2,1)} %fusion.92), channel_id=1, source_target_pairs={{0,1},{1,0},{2,3},{3,2},{4,5},{5,4},{6,7},{7,6},{8,9},{9,8},{10,11... | collective-permute-start | bytes 921608 | tf_op jit(solution)/shard_map/ppermute | solution.py:689
  44.2 19.6 %collective-permute-start.5 = (bf16[4,112,768]{2,1,0:T(8,128)(2,1)}, bf16[4,112,768]{2,1,0:T(8,128)(2,1)}, u32[]{:S(2)}, u32[]{:S(2)}) collective-permute-start(bf16[4,112,768]{2,1,0:T(8,128)(2,1)} %pad_maximum_fusion.3.refs_0_), channel_id=1, source_target_pairs={{0,6},{2,4},{4,2},{6,0},{1,7},{3,5},{5,3},{7,1},{8,14},{10,12},{12... | collective-permute-start | bytes 2064392 | tf_op jit(solution)/shard_map/ppermute | solution.py:563
  49.0 27.5 %all-to-all-start.1 = ((bf16[8,2,96,384]{3,2,1,0:T(8,128)(2,1)}), bf16[8,2,96,384]{3,2,1,0:T(8,128)(2,1)S(1)}, u32[]{:S(2)}, u32[]{:S(2)}) async-start(bf16[8,2,96,384]{3,2,1,0:T(8,128)(2,1)} %get-tuple-element.86), calls=%async_computation.1 | async-start | bytes 2359296 | tf_op jit(solution)/shard_map/all_to_all | solution.py:648
  63.9 27.5 %collective-permute-start.3 = (bf16[4,112,768]{2,1,0:T(8,128)(2,1)}, bf16[4,112,768]{2,1,0:T(8,128)(2,1)}, u32[]{:S(2)}, u32[]{:S(2)}) collective-permute-start(bf16[4,112,768]{2,1,0:T(8,128)(2,1)} %pad_maximum_fusion.3.refs_0_), channel_id=1, source_target_pairs={{0,4},{4,0},{1,5},{5,1},{2,6},{6,2},{3,7},{7,3},{8,12},{12,8},{9,1... | collective-permute-start | bytes 2064392 | tf_op jit(solution)/shard_map/ppermute | solution.py:561
  65.5 25.9 %collective-permute-start.4 = (bf16[4,112,768]{2,1,0:T(8,128)(2,1)}, bf16[4,112,768]{2,1,0:T(8,128)(2,1)}, u32[]{:S(2)}, u32[]{:S(2)}) collective-permute-start(bf16[4,112,768]{2,1,0:T(8,128)(2,1)} %pad_maximum_fusion.3.refs_0_), channel_id=1, source_target_pairs={{0,2},{2,0},{1,3},{3,1},{4,6},{6,4},{5,7},{7,5},{8,10},{10,8},{9,1... | collective-permute-start | bytes 2064392 | tf_op jit(solution)/shard_map/ppermute | solution.py:562
  77.7 49.8 %all-to-all-start.2 = ((bf16[8,192,768]{2,1,0:T(8,128)(2,1)}), bf16[8,192,768]{2,1,0:T(8,128)(2,1)S(1)}, u32[]{:S(2)}, u32[]{:S(2)}) async-start(bf16[8,192,768]{2,1,0:T(8,128)(2,1)} %pad_maximum_fusion.1), calls=%async_computation.2 | async-start | bytes 4718592 | tf_op jit(solution)/shard_map/all_to_all | solution.py:713
  81.3 131.1 %all-gather.11.cloned.1.call-start = ((), (), s32[]{:S(2)}) async-start(), calls=%async_computation.12 | async-start | bytes 3932160 | tf_op jit(solution)/shard_map/all_gather | solution.py:735
  135.2 34.2 %all-to-all-start.3 = ((bf16[8,208,768]{2,1,0:T(8,128)(2,1)}), bf16[8,208,768]{2,1,0:T(8,128)(2,1)S(1)}, u32[]{:S(2)}, u32[]{:S(2)}) async-start(bf16[8,208,768]{2,1,0:T(8,128)(2,1)} %pad_maximum_fusion), calls=%async_computation.3 | async-start | bytes 5111808 | tf_op jit(solution)/shard_map/all_to_all | solution.py:713
  138.8 116.9 %all-gather.9.cloned.1.call-start = ((), (), s32[]{:S(2)}) async-start(), calls=%async_computation.11 | async-start | bytes 1966080 | tf_op jit(solution)/shard_map/all_gather | solution.py:735
  204.7 49.7 %collective-permute-start.12 = (bf16[8,2,96,384]{3,2,1,0:T(8,128)(2,1)}, bf16[8,2,96,384]{3,2,1,0:T(8,128)(2,1)S(1)}, u32[]{:S(2)}, u32[]{:S(2)}) collective-permute-start(bf16[8,2,96,384]{3,2,1,0:T(8,128)(2,1)} %get-tuple-element.91), channel_id=1, source_target_pairs={{0,8},{24,16},{1,9},{25,17},{2,10},{26,18},{3,11},{27,19},{4,12},{... | collective-permute-start | bytes 3538952 | tf_op jit(solution)/shard_map/ppermute | solution.py:526
  271.3 35.2 %all-to-all-start.4 = ((bf16[8,208,768]{2,1,0:T(8,128)(2,1)}), bf16[8,208,768]{2,1,0:T(8,128)(2,1)}, u32[]{:S(2)}, u32[]{:S(2)}) async-start(bf16[8,208,768]{2,1,0:T(8,128)(2,1)} %get-tuple-element.98), calls=%async_computation.4 | async-start | bytes 5111808 | tf_op jit(solution)/shard_map/all_to_all | solution.py:713
  275.9 56.2 %collective-permute-start.15 = (bf16[2,8,2,96,384]{4,3,2,1,0:T(8,128)(2,1)}, bf16[2,8,2,96,384]{4,3,2,1,0:T(8,128)(2,1)}, u32[]{:S(2)}, u32[]{:S(2)}) collective-permute-start(bf16[2,8,2,96,384]{4,3,2,1,0:T(8,128)(2,1)} %get-tuple-element.100), channel_id=1, source_target_pairs={{0,8},{24,16},{1,9},{25,17},{2,10},{26,18},{3,11},{27,19},{4,12},{... | collective-permute-start | bytes 7077896 | tf_op jit(solution)/shard_map/ppermute | solution.py:526
  287.9 94.1 %collective-permute-start.20 = (bf16[3,8,2,96,256]{4,3,2,1,0:T(8,128)(2,1)}, bf16[3,8,2,96,256]{4,3,2,1,0:T(8,128)(2,1)}, u32[]{:S(2)}, u32[]{:S(2)}) collective-permute-start(bf16[3,8,2,96,256]{4,3,2,1,0:T(8,128)(2,1)} %get-tuple-element.121), channel_id=1, source_target_pairs={{0,8},{24,16},{1,9},{25,17},{2,10},{26,18},{3,11},{27,19},{4,12},{... | collective-permute-start | bytes 7077896 | tf_op jit(solution)/shard_map/ppermute | solution.py:526
  292.0 106.5 %collective-permute-start.18 = (bf16[8,2,96,384]{3,2,1,0:T(8,128)(2,1)}, bf16[8,2,96,384]{3,2,1,0:T(8,128)(2,1)}, u32[]{:S(2)}, u32[]{:S(2)}) collective-permute-start(bf16[8,2,96,384]{3,2,1,0:T(8,128)(2,1)} %add_convert_fusion.1), channel_id=1, source_target_pairs={{8,24},{16,0},{9,25},{17,1},{10,26},{18,2},{11,27},{19,3},{12,28},... | collective-permute-start | bytes 3538952 | tf_op jit(solution)/shard_map/ppermute | solution.py:534
  307.3 91.2 %collective-permute-start.17 = (bf16[8,2,96,384]{3,2,1,0:T(8,128)(2,1)}, bf16[8,2,96,384]{3,2,1,0:T(8,128)(2,1)}, u32[]{:S(2)}, u32[]{:S(2)}) collective-permute-start(bf16[8,2,96,384]{3,2,1,0:T(8,128)(2,1)} %get-tuple-element.120), channel_id=1, source_target_pairs={{8,0},{16,24},{9,1},{17,25},{10,2},{18,26},{11,3},{19,27},{12,4},{... | collective-permute-start | bytes 3538952 | tf_op jit(solution)/shard_map/ppermute | solution.py:544
  335.1 63.4 %collective-permute-start.19 = (bf16[8,2,96,384]{3,2,1,0:T(8,128)(2,1)}, bf16[8,2,96,384]{3,2,1,0:T(8,128)(2,1)}, u32[]{:S(2)}, u32[]{:S(2)}) collective-permute-start(bf16[8,2,96,384]{3,2,1,0:T(8,128)(2,1)} %fusion.14), channel_id=1, source_target_pairs={{8,16},{16,8},{9,17},{17,9},{10,18},{18,10},{11,19},{19,11},{12,20... | collective-permute-start | bytes 3538952 | tf_op jit(solution)/shard_map/ppermute | solution.py:543
  336.7 65.9 %all-to-all-start.5 = ((bf16[8,192,768]{2,1,0:T(8,128)(2,1)}), bf16[8,192,768]{2,1,0:T(8,128)(2,1)}, u32[]{:S(2)}, u32[]{:S(2)}) async-start(bf16[8,192,768]{2,1,0:T(8,128)(2,1)} %get-tuple-element.99), calls=%async_computation.5 | async-start | bytes 4718592 | tf_op jit(solution)/shard_map/all_to_all | solution.py:713
  415.7 42.8 %collective-permute-start.21 = (bf16[2,2,4,112,768]{4,3,2,1,0:T(8,128)(2,1)}, bf16[2,2,4,112,768]{4,3,2,1,0:T(8,128)(2,1)}, u32[]{:S(2)}, u32[]{:S(2)}) collective-permute-start(bf16[2,2,4,112,768]{4,3,2,1,0:T(8,128)(2,1)} %dynamic-slice_bitcast_fusion), channel_id=1, source_target_pairs={{0,1},{1,0},{2,3},{3,2},{4,5},{5,4},{6,7},{7,6},{8,9},{9,8},{10,11... | collective-permute-start | bytes 8257544 | tf_op jit(solution)/shard_map/ppermute | solution.py:881
  415.7 39.1 %collective-permute-start.23 = (bf16[8,2,96,256]{3,2,1,0:T(8,128)(2,1)}, bf16[8,2,96,256]{3,2,1,0:T(8,128)(2,1)}, u32[]{:S(2)}, u32[]{:S(2)}) collective-permute-start(bf16[8,2,96,256]{3,2,1,0:T(8,128)(2,1)} %get-tuple-element.137), channel_id=1, source_target_pairs={{8,0},{16,24},{9,1},{17,25},{10,2},{18,26},{11,3},{19,27},{12,4},{... | collective-permute-start | bytes 2359304 | tf_op jit(solution)/shard_map/ppermute | solution.py:544
  417.0 37.8 %collective-permute-start.24 = (bf16[8,2,96,256]{3,2,1,0:T(8,128)(2,1)}, bf16[8,2,96,256]{3,2,1,0:T(8,128)(2,1)}, u32[]{:S(2)}, u32[]{:S(2)}) collective-permute-start(bf16[8,2,96,256]{3,2,1,0:T(8,128)(2,1)} %get-tuple-element.194), channel_id=1, source_target_pairs={{8,24},{16,0},{9,25},{17,1},{10,26},{18,2},{11,27},{19,3},{12,28},... | collective-permute-start | bytes 2359304 | tf_op jit(solution)/shard_map/ppermute | solution.py:534
  418.3 36.5 %collective-permute-start.25 = (bf16[8,2,96,256]{3,2,1,0:T(8,128)(2,1)}, bf16[8,2,96,256]{3,2,1,0:T(8,128)(2,1)}, u32[]{:S(2)}, u32[]{:S(2)}) collective-permute-start(bf16[8,2,96,256]{3,2,1,0:T(8,128)(2,1)} %get-tuple-element.195), channel_id=1, source_target_pairs={{8,16},{16,8},{9,17},{17,9},{10,18},{18,10},{11,19},{19,11},{12,20... | collective-permute-start | bytes 2359304 | tf_op jit(solution)/shard_map/ppermute | solution.py:543
  419.9 43.4 %collective-permute-start.22 = (bf16[3,8,2,96,128]{4,3,2,1,0:T(8,128)(2,1)}, bf16[3,8,2,96,128]{4,3,2,1,0:T(8,128)(2,1)S(1)}, u32[]{:S(2)}, u32[]{:S(2)}) collective-permute-start(bf16[3,8,2,96,128]{4,3,2,1,0:T(8,128)(2,1)} %get-tuple-element.132), channel_id=1, source_target_pairs={{0,8},{24,16},{1,9},{25,17},{2,10},{26,18},{3,11},{27,19},{4,12},{... | collective-permute-start | bytes 3538952 | tf_op jit(solution)/shard_map/ppermute | solution.py:526
  429.2 36.7 %all-to-all-start.7 = ((bf16[8,2,96,384]{3,2,1,0:T(8,128)(2,1)}), bf16[8,2,96,384]{3,2,1,0:T(8,128)(2,1)S(1)}, u32[]{:S(2)}, u32[]{:S(2)}) async-start(bf16[8,2,96,384]{3,2,1,0:T(8,128)(2,1)} %fusion.4), calls=%async_computation.7 | async-start | bytes 2359296 | tf_op jit(solution)/shard_map/all_to_all | solution.py:921
  465.9 36.8 %all-to-all-start.6 = ((bf16[4,4,112,768]{3,2,1,0:T(8,128)(2,1)}), bf16[4,4,112,768]{3,2,1,0:T(8,128)(2,1)}, u32[]{:S(2)}, u32[]{:S(2)}) async-start(bf16[4,4,112,768]{3,2,1,0:T(8,128)(2,1)} %bitcast.87), calls=%async_computation.6 | async-start | bytes 5505024 | tf_op jit(solution)/shard_map/all_to_all | solution.py:891
  479.6 33.9 %collective-permute-start.30 = (bf16[8,2,96,128]{3,2,1,0:T(8,128)(2,1)}, bf16[8,2,96,128]{3,2,1,0:T(8,128)(2,1)}, u32[]{:S(2)}, u32[]{:S(2)}) collective-permute-start(bf16[8,2,96,128]{3,2,1,0:T(8,128)(2,1)} %get-tuple-element.198), channel_id=1, source_target_pairs={{8,24},{16,0},{9,25},{17,1},{10,26},{18,2},{11,27},{19,3},{12,28},... | collective-permute-start | bytes 1179656 | tf_op jit(solution)/shard_map/ppermute | solution.py:534
  480.9 32.6 %collective-permute-start.31 = (bf16[8,2,96,128]{3,2,1,0:T(8,128)(2,1)}, bf16[8,2,96,128]{3,2,1,0:T(8,128)(2,1)}, u32[]{:S(2)}, u32[]{:S(2)}) collective-permute-start(bf16[8,2,96,128]{3,2,1,0:T(8,128)(2,1)} %get-tuple-element.199), channel_id=1, source_target_pairs={{8,16},{16,8},{9,17},{17,9},{10,18},{18,10},{11,19},{19,11},{12,20... | collective-permute-start | bytes 1179656 | tf_op jit(solution)/shard_map/ppermute | solution.py:543
  482.3 28.4 %collective-permute-start.29 = (bf16[8,2,96,128]{3,2,1,0:T(8,128)(2,1)}, bf16[8,2,96,128]{3,2,1,0:T(8,128)(2,1)}, u32[]{:S(2)}, u32[]{:S(2)}) collective-permute-start(bf16[8,2,96,128]{3,2,1,0:T(8,128)(2,1)} %get-tuple-element.143), channel_id=1, source_target_pairs={{8,0},{16,24},{9,1},{17,25},{10,2},{18,26},{11,3},{19,27},{12,4},{... | collective-permute-start | bytes 1179656 | tf_op jit(solution)/shard_map/ppermute | solution.py:544
  505.9 14.1 %collective-permute-start.26 = (bf16[112,768]{1,0:T(8,128)(2,1)}, bf16[112,768]{1,0:T(8,128)(2,1)}, u32[]{:S(2)}, u32[]{:S(2)}) collective-permute-start(bf16[112,768]{1,0:T(8,128)(2,1)} %get-tuple-element.202), channel_id=1, source_target_pairs={{0,8},{8,16},{16,24},{24,0},{1,9},{9,17},{17,25},{25,1},{2,10},{10... | collective-permute-start | bytes 516104 | tf_op jit(solution)/shard_map/ppermute | solution.py:899
  527.5 15.1 %all-to-all-start.8 = ((bf16[8,2,96,256]{3,2,1,0:T(8,128)(2,1)}), bf16[8,2,96,256]{3,2,1,0:T(8,128)(2,1)S(1)}, u32[]{:S(2)}, u32[]{:S(2)}) async-start(bf16[8,2,96,256]{3,2,1,0:T(8,128)(2,1)} %fusion.13), calls=%async_computation.8 | async-start | bytes 1572864 | tf_op jit(solution)/shard_map/all_to_all | solution.py:921
  (63 other events, 662.5 us)
Sparse Core Ops, SparseCore 0:
  39.3 92.3 all-gather.6
  133.3 61.9 all-gather.10
  196.9 50.1 all-gather.8

commit v5 on v4

--- a/solution.py
+++ b/solution.py
@@ -356,12 +356,12 @@
     return jnp.broadcast_to(column, (256, 128)).T[:1, :]
 
 
-def expert_kernel(first, last, order_ref, x_ref, g_ref, b_ref, shards_ref, *refs):
+def expert_kernel(first, last, x_ref, g_ref, b_ref, shards_ref, *refs):
     if not first:
         (y_in, p_in), refs = refs[:2], refs[2:]
     (y_out, p_out, bias_ref), refs = refs[:3], refs[3:]
     acc_ref, w_ref, sem = refs[-3:]
-    grads = refs[:-3]
+    grads_ref = refs[0]
     step = pl.program_id(0)
     model = w_ref.shape[1]
 
@@ -422,33 +422,24 @@
 
     @pl.when(step == pl.num_programs(0) - 1)
     def _():
-        if len(grads) == 1:
-            grads[0][...] = acc_ref[...]
+        if len(shards_ref.shape) == 3:
+            grads_ref[...] = acc_ref[...]
         else:
-            own_ref, near_ref, rest_ref = grads[:3]
-            part, units = own_ref.shape[2:]
-            for k in range(4):
+            part, units = shards_ref.shape[3:]
+            for z in range(4):
                 for q in range(8):
-                    row = pl.multiple_of(order_ref[k] * (2 * part) + (q // 4) * part, 32)
+                    row = (z * 2 + q // 4) * part
                     columns = slice((q % 4) * units, (q % 4 + 1) * units)
-                    block = acc_ref[:, pl.ds(row, part), columns].astype(BF16)
-                    if k == 0:
-                        own_ref[q] = block
-                    elif k == 3 and len(grads) == 4:
-                        grads[3][q] = block
-                    else:
-                        rest_ref[k - 1, q] = block
-                    if k == 1:
-                        near_ref[q] = block
-
-
-def expert_chunk(order, x, g, b, sums, shards, last):
+                    grads_ref[z, q] = acc_ref[:, row : row + part, columns].astype(BF16)
+
+
+def expert_chunk(x, g, b, sums, shards, last):
     experts, slots, model = g.shape
     units = b.shape[1]
     first = sums is None
     step = 2
-    block = lambda rows: pl.BlockSpec((step, rows, model), lambda i, o: (i, 0, 0))
-    full = lambda shape: pl.BlockSpec(shape, lambda i, o: (0,) * len(shape))
+    block = lambda rows: pl.BlockSpec((step, rows, model), lambda i: (i, 0, 0))
+    full = whole
     ins = [x, g, b, shards] + ([] if first else list(sums))
     in_specs = [block(x.shape[1]), block(slots), full(b.shape)]
     in_specs.append(pl.BlockSpec(memory_space=pl.ANY))
@@ -463,24 +454,19 @@
     if len(shards.shape) == 3:
         outs.append(((2, model, units), F32))
     else:
-        shape = shards.shape[1:]
-        outs += [(shape, BF16), (shape, BF16)]
-        outs += [((2,) + shape, BF16), (shape, BF16)] if first else [((3,) + shape, BF16)]
+        outs.append((shards.shape, BF16))
     out_specs += [full(s) for s, _ in outs[2:]]
-    base = 5
+    base = 4
     return pl.pallas_call(
         functools.partial(expert_kernel, first, last),
-        grid_spec=pltpu.PrefetchScalarGridSpec(
-            num_scalar_prefetch=1,
-            grid=(experts // step,),
-            in_specs=in_specs,
-            out_specs=out_specs,
-            scratch_shapes=[
-                pltpu.VMEM((2, model, units), F32),
-                pltpu.VMEM((2, model, units), BF16),
-                pltpu.SemaphoreType.DMA(()),
-            ],
-        ),
+        grid=(experts // step,),
+        in_specs=in_specs,
+        out_specs=out_specs,
+        scratch_shapes=[
+            pltpu.VMEM((2, model, units), F32),
+            pltpu.VMEM((2, model, units), BF16),
+            pltpu.SemaphoreType.DMA(()),
+        ],
         out_shape=[jax.ShapeDtypeStruct(s, d) for s, d in outs],
         input_output_aliases={} if first or last else {base: 0, base + 1: 1},
         compiler_params=pltpu.CompilerParams(vmem_limit_bytes=58 * 2**20),
@@ -488,7 +474,7 @@
             flops=2 * experts * slots * model * units, bytes_accessed=4 * 10**6, transcendentals=0
         ),
         name="expert_chunk",
-    )(order, *ins)
+    )(*ins)
 
 
 CAP = 128
@@ -498,11 +484,6 @@
 TENSOR = ("y", "c")
 PLANE = ("x", "y", "c")
 EVERY = ("y", "c", "z", "x")
-INWARD = [(0, 1), (3, 2)]
-MIDDLE = [(1, 2), (2, 1)]
-OUTWARD = [(1, 0), (2, 3)]
-ACROSS = [(1, 3), (2, 0)]
-ORDER = ((0, 1, 2, 3), (1, 0, 2, 3), (2, 3, 1, 0), (3, 2, 1, 0))
 
 
 def tie(values, *events):
@@ -510,46 +491,6 @@
     if not events:
         return values
     return lax.optimization_barrier((values, *events))[0]
-
-
-def add(*terms):
-    return sum(term.astype(F32) for term in terms).astype(BF16)
-
-
-class Reduce:
-    def __init__(self, grads):
-        self.grads = grads
-        if len(grads) == 1:
-            self.total = lax.psum_scatter(grads[0], "z", scatter_dimension=1, tiled=True)
-            return
-        own, near, *rest = grads
-        self.inward = [lax.ppermute(one, "z", INWARD) for one in rest]
-
-    def forward_far(self, *events):
-        if len(self.grads) == 1:
-            return self.total
-        inward = tie(self.inward[-1], *events)
-        far, inward = [one[2] if one.shape[0] == 3 else one for one in (self.grads[-1], inward)]
-        three = add(far, inward)
-        self.outward_two = lax.ppermute(three, "z", ACROSS)
-        return three
-
-    def forward(self, *events):
-        if len(self.grads) == 1:
-            return self.total
-        near = self.grads[1]
-        self.inward[0] = tie(self.inward[0], *events)
-        two = add(self.grads[2][1], self.inward[0][1])
-        self.middle = lax.ppermute(two, "z", MIDDLE)
-        self.outward_one = lax.ppermute(tie(near, *events), "z", OUTWARD)
-        return two
-
-    def finish(self):
-        if len(self.grads) > 1:
-            self.total = add(
-                self.grads[0], self.inward[0][0], self.outward_one, self.outward_two, self.middle
-            )
-        return self.total
 
 
 def gather_packs(pack):
@@ -776,11 +717,6 @@
         incoming,
     )
 
-    order = jnp.asarray(
-        [ORDER[k] + (int(k in (0, 3)),) for k in range(4)] if length == 4 else [[0] * 5] * length,
-        jnp.int32,
-    )
-    order = lax.dynamic_index_in_dim(order, place[0], 0, keepdims=False)
     sums = None
     bias_parts = []
     reduced = []
@@ -788,24 +724,20 @@
     for index, (first, last) in enumerate(spans):
         bias_one = bias_up[:, first * CHUNK : last * CHUNK].reshape(1, -1)
         final = index == count - 1
-        events = []
-        if count == 3 and index == 2:
-            events.append(reduced[0].forward_far())
-        *sums, bias_part = (
-            outs := expert_chunk(
-                order, chosen, incoming, tie(bias_one, *events), sums, full_parts[index], final
-            )
-        )[:3]
+        *sums, bias_part, grads = expert_chunk(
+            chosen, incoming, bias_one, sums, full_parts[index], final
+        )
         bias_parts.append(bias_part.reshape(quarter, -1))
-        reduced.append(Reduce(outs[3:]))
+        if length == 4:
+            reduced.append(lax.psum_scatter(grads, "z", scatter_dimension=0, tiled=False))
+        else:
+            reduced.append(lax.psum_scatter(grads, "z", scatter_dimension=1, tiled=True))
 
     mixed, pulled = sums
     back = swap_experts(pulled)
     gate_back = values_of(back)
     norm_two_grad = combine(back)
     mixed = swap_experts(mixed, back)
-    if count == 3:
-        norm_two_grad = tie(norm_two_grad, reduced[0].forward(back))
 
     def slots_to_tokens(match, parts_here):
         parts_here = parts_here.reshape(experts, -1)
@@ -840,12 +772,8 @@
     h_grad, hb, dq, dk, dv, line_sums, pair_sums = attend_backward(
         norm_two_grad, out_grad, residual, mask_here, wo, lines, q, k, v, lse
     )
+    h_grad = tie(h_grad, mixed)
     input_grad, line_ones = input_backward(h_grad, tokens_in, wq, wk, wv, lines, dq, dk, dv)
-    if count == 3:
-        hb = tie(
-            hb, mixed, reduced[0].finish(), reduced[1].forward(hb), reduced[1].forward_far(hb)
-        )
-
     bias_rows = jnp.concatenate(bias_parts, 1).reshape(dp, quarter, part)
     bias_rows = jnp.where(
         jnp.arange(experts)[:, None, None, None] == expert, bias_rows[None], 0.0
@@ -881,17 +809,8 @@
     theirs = lax.ppermute(theirs, "c", swap)
     pack_grads = (mine.astype(F32) + theirs.astype(F32)).astype(sum_type)
     pack_grads = pack_grads.reshape((-1,) + pack_grads.shape[2:])
-    if count == 3:
-        pack_grads = tie(
-            pack_grads,
-            reduced[2].forward(pack_grads),
-            reduced[2].forward_far(pack_grads),
-            reduced[1].finish(),
-        )
     pack_grads = lax.all_to_all(pack_grads, ("x", "y"), 0, 0, tiled=True)
     pack_grads = jnp.sum(pack_grads.astype(F32), 0).astype(sum_type)
-    if count == 3:
-        reduced[2].finish()
     if length == 4:
         pack_grad = lax.dynamic_index_in_dim(pack_grads, place[0], 0, keepdims=False).astype(F32)
         for far in (1, 2, 3):
@@ -909,7 +828,7 @@
     output = (residual + mixture + bias_term).astype(BF16)
 
     ups, downs = [], []
-    totals = [one.total for one in reduced]
+    totals = reduced
     if length != 4:
         totals = [
             one.reshape(2, 2, part, quarter, -1).transpose(1, 3, 0, 2, 4).reshape(experts, 2, part, -1)

time: 561 us -> 481 us (0.86)
  starting transfers between devices: 99.3 us -> 59.7 us
  other arithmetic: 55.9 us -> 34.5 us
  waiting for transfers between devices: 168 us -> 154 us
    ppermute x13 -> x0, waiting for transfers between devices: 64.6 us -> none  [the longest x4 42.8 us: __init__(): self.inward = [lax.ppermute(one, 'z', INWARD) for one in rest]]
    ppermute x13 -> x0, starting transfers between devices: 36.8 us -> none  [the longest x4 24.4 us: __init__(): self.inward = [lax.ppermute(one, 'z', INWARD) for one in rest]]
    convert_element_type x7 -> x0, other arithmetic: 20.4 us -> none  [add(): return sum((term.astype(F32) for term in terms)).astype(BF16)]
    ppermute x3, waiting for transfers between devices: 1.25 us -> 16.7 us  [shards(): some = lax.ppermute(some, 'z', [(k, (k + far) % 4) for k in range(4)])]
    all_to_all x1, waiting for transfers between devices: 19 us -> 29.8 us  [shards(): pack_grads = lax.all_to_all(pack_grads, ('x', 'y'), 0, 0, tiled=True)]
    all_to_all x4, waiting for transfers between devices: 37.1 us -> 46.9 us  [swap_experts(): return lax.all_to_all(tie(rows, *events), PLANE, 0, 0, tiled=True)]
    unnamed x112 -> x94, local copies, waits for them, and re-layouts: 16 us -> 13.4 us
  transfers between devices with their start and end apart: 45 -> 35, of which waited for: 16 -> 15; matrix products, arithmetic and copies ran while one was open for 19% -> 19% of each run, Pallas kernels for 21% -> 26%
where the time goes in v5:
time: 481 us; the launch traced here: 472 us
  waiting for transfers between devices  154 us (32%)
  Pallas kernels  142 us (30%)
  starting transfers between devices  59.7 us (12%)
  local copies, waits for them, and re-layouts  50.4 us (10%)
  other arithmetic  34.5 us (7%)
  matrix products  16.3 us (3%)
  between operations  15.7 us (3%)
    pallas_call x3, Pallas kernels, expert_chunk(): pl.pallas_call(functools.partial(expert_kernel, first, last), grid=(exper...  72.3 us
    all_to_all x4, waiting for transfers between devices, swap_experts(): return lax.all_to_all(tie(rows, *events), PLANE, 0, 0, tiled=True)  46.9 us
    all_to_all x1, waiting for transfers between devices, shards(): pack_grads = lax.all_to_all(pack_grads, ('x', 'y'), 0, 0, tiled=True)  29.8 us
    pallas_call x1, Pallas kernels, attend_forward(): pl.pallas_call(attend_forward_kernel, grid_spec=pltpu.PrefetchScalarGridS...  26.1 us
    pallas_call x1, Pallas kernels, attend_backward(): pl.pallas_call(attend_backward_kernel, grid=(images,), in_specs=[whole(a....  21 us
    ppermute x3, waiting for transfers between devices, shards(): some = lax.ppermute(some, 'z', [(k, (k + far) % 4) for k in range(4)])  16.7 us
    all_to_all x4, starting transfers between devices, swap_experts(): return lax.all_to_all(tie(rows, *events), PLANE, 0, 0, tiled=True)  16.5 us
    all_to_all x3, waiting for transfers between devices, shards(): lax.all_to_all(tie(some.astype(BF16), event), PLANE, 0, 0, tiled=True)  14.7 us
  transfers between devices with their start and end apart: 35, of which 15 were waited for; matrix products, arithmetic and copies ran while one was open for 19% of the time, Pallas kernels for 26%

profile of v5, /device:TPU:0, one launch (start us, length us, event | category | flops | bytes accessed | tf_op | source)
XLA Modules:
  0.0 472.1 jit_solution(5601101682868652081)
XLA Ops:
  15.5 5.3 %all-to-all-start = ((bf16[8,2,96,384]{3,2,1,0:T(8,128)(2,1)}), bf16[8,2,96,384]{3,2,1,0:T(8,128)(2,1)S(1)}, u32[]{:S(2)}, u32[]{:S(2)}) async-start(bf16[8,2,96,384]{3,2,1,0:T(8,128)(2,1)} %copy-done.3), calls=%async_computation | async-start | bytes 2359296 | tf_op jit(solution)/shard_map/all_to_all | solution.py:589
  27.5 3.6 collective-permute-done
  31.1 7.0 %collective-permute-done.1 = bf16[112,768]{1,0:T(8,128)(2,1)S(1)} collective-permute-done((bf16[112,768]{1,0:T(8,128)(2,1)S(1)}, bf16[112,768]{1,0:T(8,128)(2,1)S(1)}, u32[]{:S(2)}, u32[]{:S(2)}) %collective-permute-start.1) | collective-permute-done | bytes 172064 | tf_op jit(solution)/shard_map/ppermute | solution.py:498
  49.1 3.6 all-to-all-start.1
  52.7 11.1 %collective-permute-done.5.refs_3_ = bf16[4,112,768]{2,1,0:T(8,128)(2,1)} collective-permute-done((bf16[4,112,768]{2,1,0:T(8,128)(2,1)}, bf16[4,112,768]{2,1,0:T(8,128)(2,1)}, u32[]{:S(2)}, u32[]{:S(2)}) %collective-permute-start.5) | collective-permute-done | bytes 688160 | tf_op jit(solution)/shard_map/ppermute | solution.py:504
  70.6 6.0 %all-to-all-done.1 = bf16[8,2,96,384]{3,2,1,0:T(8,128)(2,1)S(1)} async-done(((bf16[8,2,96,384]{3,2,1,0:T(8,128)(2,1)}), bf16[8,2,96,384]{3,2,1,0:T(8,128)(2,1)S(1)}, u32[]{:S(2)}, u32[]{:S(2)}) %all-to-all-start.1) | async-done | bytes 1179680 | tf_op jit(solution)/shard_map/all_to_all | solution.py:589
  77.7 3.6 all-to-all-start.2
  83.9 7.5 %collective-permute-done.3.refs_1_ = bf16[4,112,768]{2,1,0:T(8,128)(2,1)} collective-permute-done((bf16[4,112,768]{2,1,0:T(8,128)(2,1)}, bf16[4,112,768]{2,1,0:T(8,128)(2,1)}, u32[]{:S(2)}, u32[]{:S(2)}) %collective-permute-start.3) | collective-permute-done | bytes 688160 | tf_op jit(solution)/shard_map/ppermute | solution.py:502
  102.3 26.1 %attend_forward.1 = (bf16[3,208,768]{2,1,0:T(8,128)(2,1)}, bf16[3,200,768]{2,1,0:T(8,128)(2,1)}, f32[3,200,768]{2,1,0:T(8,128)}, bf16[3,4,200,192]{3,2,1,0:T(8,1...) custom-call(s32[4]{0:T(128)} %pad_add_fusion.place_ref, ...), custom_call_target="tpu_custom_call" | custom-call | flops 2000000000 | bytes 4000000 | tf_op jit(solution)/shard_map/attend_forward/pallas_call | solution.py:147
  136.8 3.6 all-to-all-start.3
  147.3 23.6 %all-to-all-done.3.x_ref = bf16[8,208,768]{2,1,0:T(8,128)(2,1)S(1)} async-done(((bf16[8,208,768]{2,1,0:T(8,128)(2,1)}), bf16[8,208,768]{2,1,0:T(8,128)(2,1)S(1)}, u32[]{:S(2)}, u32[]{:S(2)}) %all-to-all-start.3) | async-done | bytes 2555936 | tf_op jit(solution)/shard_map/all_to_all | solution.py:654
  172.4 32.7 %expert_chunk.3 = (f32[8,192,768]{2,1,0:T(8,128)}, f32[8,192,768]{2,1,0:T(8,128)}, f32[1,1536]{1,0:T(1,128)}, bf16[4,8,2,96,384]{4,3,2,1,0:T(8,128)(2,1)}) custom-call(bf16[8,208,768]{2,1,0:T(8,128)(2,1)} %copy-done.5, bf16[8,192,768]{2,1,0:T(8,128)(2,1)} %copy-done.6, f32[1,1536]{1,0:T(1,128)} %bitcast.305, bf16[4,8,2,96,384]{4,3,2,1,0:T(8,128)(2,1)} %bitcast.307), custom_call_target="tpu_custom_call" | custom-call | flops 3623878656 | bytes 4000000 | tf_op jit(solution)/shard_map/expert_chunk/pallas_call | solution.py:460
  205.2 24.8 %expert_chunk.4 = (f32[8,192,768]{2,1,0:T(8,128)}, f32[8,192,768]{2,1,0:T(8,128)}, f32[1,1024]{1,0:T(1,128)}, bf16[4,8,2,96,256]{4,3,2,1,0:T(8,128)(2,1)}) custom-call(bf16[8,208,768]{2,1,0:T(8,128)(2,1)} %copy-done.5, bf16[8,192,768]{2,1,0:T(8,128)(2,1)} %copy-done.6, f32[1,1024]{1,0:T(1,128)} %bitcast.300, ...), custom_call_target="tpu_custom_call", output_to_operand_aliasing={{0}: (4, {}), {1}: (5, {})} | custom-call | flops 2415919104 | bytes 4000000 | tf_op jit(solution)/shard_map/expert_chunk/pallas_call | solution.py:460
  233.3 14.8 %expert_chunk.5 = (bf16[8,192,768]{2,1,0:T(8,128)(2,1)}, bf16[8,208,768]{2,1,0:T(8,128)(2,1)}, f32[1,512]{1,0:T(1,128)}, bf16[4,8,2,96,128]{4,3,2,1,0:T(8,128)(2,1)}) custom-call(bf16[8,208,768]{2,1,0:T(8,128)(2,1)} %copy-done.5, bf16[8,192,768]{2,1,0:T(8,128)(2,1)} %copy-done.6, f32[1,512]{1,0:T(1,128)} %bitcast.303, bf16[4,8,2,96,128]{4,3,2,1,0:T(8,128)(2,1)} %bitcast.260, ...), custom_call_target="tpu_custom_call" | custom-call | flops 1207959552 | bytes 4000000 | tf_op jit(solution)/shard_map/expert_chunk/pallas_call | solution.py:460
  248.7 4.5 all-to-all-start.4
  260.6 23.2 %all-to-all-done.4 = bf16[8,208,768]{2,1,0:T(8,128)(2,1)} async-done(((bf16[8,208,768]{2,1,0:T(8,128)(2,1)}), bf16[8,208,768]{2,1,0:T(8,128)(2,1)}, u32[]{:S(2)}, u32[]{:S(2)}) %all-to-all-start.4) | async-done | bytes 2555936 | tf_op jit(solution)/shard_map/all_to_all | solution.py:654
  284.7 4.7 all-to-all-start.5
  305.2 21.0 %attend_backward.1 = (f32[3,200,768]{2,1,0:T(8,128)}, bf16[3,208,768]{2,1,0:T(8,128)(2,1)}, bf16[3,4,208,192]{3,2,1,0:T(8,128)(2,1)}, bf16[3,4,208,192]{3,2,1,0:...) custom-call(f32[3,200,768]{2,1,0:T(8,128)} %fusion.4.n2_grad_ref, ...), custom_call_target="tpu_custom_call" | custom-call | tf_op jit(solution)/shard_map/attend_backward/pallas_call | solution.py:226
  327.9 9.6 %input_backward.1 = (f32[3,200,768]{2,1,0:T(8,128)}, f32[8,768]{1,0:T(8,128)}) custom-call(f32[3,200,768]{2,1,0:T(8,128)} %get-tuple-element.86.h_grad_ref, bf16[3,200,768]{2,1,0:T(8,128)(2,1)} %tokens_ref.3, bf16[4,768,192]{2,1,0:T(8,128)(2,1)} %get-tuple-element.87.wq_ref, bf16[4,768,192]{2,1,0:T(8,128)(2,1)} %get-tuple-element.88.wk_ref, ...), custom_call_target="tpu_custom_call" | custom-call | tf_op jit(solution)/shard_map/input_backward/pallas_call | solution.py:313
  339.8 9.7 %attend_weights.1 = bf16[2,2,2,4,112,768]{5,4,3,2,1,0:T(8,128)(2,1)} custom-call(bf16[3,208,768]{2,1,0:T(8,128)(2,1)} %get-tuple-element.94.n1_ref, bf16[3,208,768]{2,1,0:T(8,128)(2,1)} %get-tuple-element.95.hb_ref, bf16[3,4,208,192]{3,2,1,0:T(8,128)(2,1)} %get-tuple-element.90.dq_ref, bf16[3,4,208,192]{3,2,1,0:T(8,128)(2,1)} %get-tuple-element.91.dk_ref, ...), custom_call_target="tpu_custom_call" | custom-call | tf_op jit(solution)/shard_map/attend_weights/pallas_call | solution.py:274
  349.5 3.5 dynamic-slice_bitcast_fusion
  353.4 4.9 %collective-permute-done.15 = bf16[2,2,4,112,768]{4,3,2,1,0:T(8,128)(2,1)S(1)} collective-permute-done((bf16[2,2,4,112,768]{4,3,2,1,0:T(8,128)(2,1)}, bf16[2,2,4,112,768]{4,3,2,1,0:T(8,128)(2,1)S(1)}, u32[]{:S(2)}, u32[]{:S(2)}) %collective-permute-start.15) | collective-permute-done | bytes 2752544 | tf_op jit(solution)/shard_map/ppermute | solution.py:809
  358.3 4.0 fusion
  362.3 4.6 all-to-all-start.6
  369.8 29.8 %all-to-all-done.6 = bf16[4,4,112,768]{3,2,1,0:T(8,128)(2,1)} async-done(((bf16[4,4,112,768]{3,2,1,0:T(8,128)(2,1)}), bf16[4,4,112,768]{3,2,1,0:T(8,128)(2,1)}, u32[]{:S(2)}, u32[]{:S(2)}) %all-to-all-start.6) | async-done | bytes 2752544 | tf_op jit(solution)/shard_map/all_to_all | solution.py:812
  401.9 3.5 all-to-all-start.9
  409.0 3.8 all-to-all-done.9
  412.8 3.5 all-to-all-start.8
  424.5 6.1 %collective-permute-done.16 = bf16[112,768]{1,0:T(8,128)(2,1)S(1)} collective-permute-done((bf16[112,768]{1,0:T(8,128)(2,1)S(1)}, bf16[112,768]{1,0:T(8,128)(2,1)S(1)}, u32[]{:S(2)}, u32[]{:S(2)}) %collective-permute-start.16) | collective-permute-done | bytes 172064 | tf_op jit(solution)/shard_map/ppermute | solution.py:818
  430.6 10.6 %collective-permute-done.17 = bf16[112,768]{1,0:T(8,128)(2,1)S(1)} collective-permute-done((bf16[112,768]{1,0:T(8,128)(2,1)S(1)}, bf16[112,768]{1,0:T(8,128)(2,1)S(1)}, u32[]{:S(2)}, u32[]{:S(2)}) %collective-permute-start.17) | collective-permute-done | bytes 172064 | tf_op jit(solution)/shard_map/ppermute | solution.py:818
  442.1 3.6 all-to-all-start.7
  450.6 10.9 %all-to-all-done.7 = bf16[8,2,96,384]{3,2,1,0:T(8,128)(2,1)S(1)} async-done(((bf16[8,2,96,384]{3,2,1,0:T(8,128)(2,1)}), bf16[8,2,96,384]{3,2,1,0:T(8,128)(2,1)S(1)}, u32[]{:S(2)}, u32[]{:S(2)}) %all-to-all-start.7) | async-done | bytes 1179680 | tf_op jit(solution)/shard_map/all_to_all | solution.py:840
  (330 shorter events, 121.6 us)
Async XLA Ops:
  15.5 22.6 %all-to-all-start = ((bf16[8,2,96,384]{3,2,1,0:T(8,128)(2,1)}), bf16[8,2,96,384]{3,2,1,0:T(8,128)(2,1)S(1)}, u32[]{:S(2)}, u32[]{:S(2)}) async-start(bf16[8,2,96,384]{3,2,1,0:T(8,128)(2,1)} %copy-done.3), calls=%async_computation | async-start | bytes 2359296 | tf_op jit(solution)/shard_map/all_to_all | solution.py:589
  20.9 150.1 %all-gather.11.cloned.1.call-start = ((), (), s32[]{:S(2)}) async-start(), calls=%async_computation.18 | async-start | bytes 5898240 | tf_op jit(solution)/shard_map/all_gather | solution.py:676
  22.0 9.1 %collective-permute-start = (bf16[112,768]{1,0:T(8,128)(2,1)S(1)}, bf16[112,768]{1,0:T(8,128)(2,1)S(1)}, u32[]{:S(2)}, u32[]{:S(2)}) collective-permute-start(bf16[112,768]{1,0:T(8,128)(2,1)S(1)} %pad_maximum_fusion.5), channel_id=1, source_target_pairs={{0,8},{8,16},{16,24},{24,0},{1,9},{9,17},{17,25},{25,1},{2,10},{10... | collective-permute-start | bytes 516104 | tf_op jit(solution)/shard_map/ppermute | solution.py:498
  23.6 14.5 %collective-permute-start.1 = (bf16[112,768]{1,0:T(8,128)(2,1)S(1)}, bf16[112,768]{1,0:T(8,128)(2,1)S(1)}, u32[]{:S(2)}, u32[]{:S(2)}) collective-permute-start(bf16[112,768]{1,0:T(8,128)(2,1)S(1)} %pad_maximum_fusion.5), channel_id=1, source_target_pairs={{0,16},{8,24},{16,0},{24,8},{1,17},{9,25},{17,1},{25,9},{2,18},{10... | collective-permute-start | bytes 516104 | tf_op jit(solution)/shard_map/ppermute | solution.py:498
  26.2 11.9 %collective-permute-start.2 = (bf16[112,768]{1,0:T(8,128)(2,1)S(1)}, bf16[112,768]{1,0:T(8,128)(2,1)S(1)}, u32[]{:S(2)}, u32[]{:S(2)}) collective-permute-start(bf16[112,768]{1,0:T(8,128)(2,1)S(1)} %pad_maximum_fusion.5), channel_id=1, source_target_pairs={{0,24},{8,0},{16,8},{24,16},{1,25},{9,1},{17,9},{25,17},{2,26},{10... | collective-permute-start | bytes 516104 | tf_op jit(solution)/shard_map/ppermute | solution.py:498
  40.0 27.1 %collective-permute-start.10 = (bf16[200,768]{1,0:T(8,128)(2,1)}, bf16[200,768]{1,0:T(8,128)(2,1)}, u32[]{:S(2)}, u32[]{:S(2)}) collective-permute-start(bf16[200,768]{1,0:T(8,128)(2,1)} %fusion.75), channel_id=1, source_target_pairs={{0,1},{1,0},{2,3},{3,2},{4,5},{5,4},{6,7},{7,6},{8,9},{9,8},{10,11... | collective-permute-start | bytes 921608 | tf_op jit(solution)/shard_map/ppermute | solution.py:630
  44.2 19.6 %collective-permute-start.5 = (bf16[4,112,768]{2,1,0:T(8,128)(2,1)}, bf16[4,112,768]{2,1,0:T(8,128)(2,1)}, u32[]{:S(2)}, u32[]{:S(2)}) collective-permute-start(bf16[4,112,768]{2,1,0:T(8,128)(2,1)} %pad_maximum_fusion.3.refs_0_), channel_id=1, source_target_pairs={{0,6},{2,4},{4,2},{6,0},{1,7},{3,5},{5,3},{7,1},{8,14},{10,12},{12... | collective-permute-start | bytes 2064392 | tf_op jit(solution)/shard_map/ppermute | solution.py:504
  49.1 27.5 %all-to-all-start.1 = ((bf16[8,2,96,384]{3,2,1,0:T(8,128)(2,1)}), bf16[8,2,96,384]{3,2,1,0:T(8,128)(2,1)S(1)}, u32[]{:S(2)}, u32[]{:S(2)}) async-start(bf16[8,2,96,384]{3,2,1,0:T(8,128)(2,1)} %get-tuple-element.68), calls=%async_computation.1 | async-start | bytes 2359296 | tf_op jit(solution)/shard_map/all_to_all | solution.py:589
  63.8 13.7 %collective-permute-start.9 = (bf16[4,112,768]{2,1,0:T(8,128)(2,1)}, bf16[4,112,768]{2,1,0:T(8,128)(2,1)}, u32[]{:S(2)}, u32[]{:S(2)}) collective-permute-start(bf16[4,112,768]{2,1,0:T(8,128)(2,1)} %collective-permute-done.5.refs_3_), channel_id=1, source_target_pairs={{0,1},{1,0},{2,3},{3,2},{4,5},{5,4},{6,7},{7,6},{8,9},{9,8},{10,11... | collective-permute-start | bytes 2064392 | tf_op jit(solution)/shard_map/ppermute | solution.py:506
  63.9 27.5 %collective-permute-start.3 = (bf16[4,112,768]{2,1,0:T(8,128)(2,1)}, bf16[4,112,768]{2,1,0:T(8,128)(2,1)}, u32[]{:S(2)}, u32[]{:S(2)}) collective-permute-start(bf16[4,112,768]{2,1,0:T(8,128)(2,1)} %pad_maximum_fusion.3.refs_0_), channel_id=1, source_target_pairs={{0,4},{4,0},{1,5},{5,1},{2,6},{6,2},{3,7},{7,3},{8,12},{12,8},{9,1... | collective-permute-start | bytes 2064392 | tf_op jit(solution)/shard_map/ppermute | solution.py:502
  65.6 25.9 %collective-permute-start.4 = (bf16[4,112,768]{2,1,0:T(8,128)(2,1)}, bf16[4,112,768]{2,1,0:T(8,128)(2,1)}, u32[]{:S(2)}, u32[]{:S(2)}) collective-permute-start(bf16[4,112,768]{2,1,0:T(8,128)(2,1)} %pad_maximum_fusion.3.refs_0_), channel_id=1, source_target_pairs={{0,2},{2,0},{1,3},{3,1},{4,6},{6,4},{5,7},{7,5},{8,10},{10,8},{9,1... | collective-permute-start | bytes 2064392 | tf_op jit(solution)/shard_map/ppermute | solution.py:503
  77.7 50.7 %all-to-all-start.2 = ((bf16[8,192,768]{2,1,0:T(8,128)(2,1)}), bf16[8,192,768]{2,1,0:T(8,128)(2,1)S(1)}, u32[]{:S(2)}, u32[]{:S(2)}) async-start(bf16[8,192,768]{2,1,0:T(8,128)(2,1)} %pad_maximum_fusion.1), calls=%async_computation.2 | async-start | bytes 4718592 | tf_op jit(solution)/shard_map/all_to_all | solution.py:654
  81.3 123.8 %all-gather.9.cloned.1.call-start = ((), (), s32[]{:S(2)}) async-start(), calls=%async_computation.17 | async-start | bytes 3932160 | tf_op jit(solution)/shard_map/all_gather | solution.py:676
  91.4 10.9 %collective-permute-start.7 = (bf16[4,112,768]{2,1,0:T(8,128)(2,1)}, bf16[4,112,768]{2,1,0:T(8,128)(2,1)}, u32[]{:S(2)}, u32[]{:S(2)}) collective-permute-start(bf16[4,112,768]{2,1,0:T(8,128)(2,1)} %collective-permute-done.3.refs_1_), channel_id=1, source_target_pairs={{0,1},{1,0},{2,3},{3,2},{4,5},{5,4},{6,7},{7,6},{8,9},{9,8},{10,11... | collective-permute-start | bytes 2064392 | tf_op jit(solution)/shard_map/ppermute | solution.py:506
  91.4 10.9 %collective-permute-start.8 = (bf16[4,112,768]{2,1,0:T(8,128)(2,1)}, bf16[4,112,768]{2,1,0:T(8,128)(2,1)}, u32[]{:S(2)}, u32[]{:S(2)}) collective-permute-start(bf16[4,112,768]{2,1,0:T(8,128)(2,1)} %collective-permute-done.4.refs_2_), channel_id=1, source_target_pairs={{0,1},{1,0},{2,3},{3,2},{4,5},{5,4},{6,7},{7,6},{8,9},{9,8},{10,11... | collective-permute-start | bytes 2064392 | tf_op jit(solution)/shard_map/ppermute | solution.py:506
  136.8 34.2 %all-to-all-start.3 = ((bf16[8,208,768]{2,1,0:T(8,128)(2,1)}), bf16[8,208,768]{2,1,0:T(8,128)(2,1)S(1)}, u32[]{:S(2)}, u32[]{:S(2)}) async-start(bf16[8,208,768]{2,1,0:T(8,128)(2,1)} %pad_maximum_fusion), calls=%async_computation.3 | async-start | bytes 5111808 | tf_op jit(solution)/shard_map/all_to_all | solution.py:654
  140.4 92.8 %all-gather.7.cloned.1.call-start = ((), (), s32[]{:S(2)}) async-start(), calls=%async_computation.16 | async-start | bytes 1966080 | tf_op jit(solution)/shard_map/all_gather | solution.py:676
  141.1 260.8 %reduce-scatter.8.cloned.1.call-start = ((), (), s32[]{:S(2)}) async-start(), calls=%async_computation.15 | async-start | bytes 1966080 | tf_op jit(solution)/shard_map/reduce_scatter | solution.py:732
  248.1 160.9 %reduce-scatter.6.cloned.1.call-start = ((), (), s32[]{:S(2)}) async-start(), calls=%async_computation.14 | async-start | bytes 3932160 | tf_op jit(solution)/shard_map/reduce_scatter | solution.py:732
  248.7 35.2 %all-to-all-start.4 = ((bf16[8,208,768]{2,1,0:T(8,128)(2,1)}), bf16[8,208,768]{2,1,0:T(8,128)(2,1)}, u32[]{:S(2)}, u32[]{:S(2)}) async-start(bf16[8,208,768]{2,1,0:T(8,128)(2,1)} %get-tuple-element.78), calls=%async_computation.4 | async-start | bytes 5111808 | tf_op jit(solution)/shard_map/all_to_all | solution.py:654
  253.2 188.9 %reduce-scatter.4.cloned.1.call-start = ((), (), s32[]{:S(2)}) async-start(), calls=%async_computation.13 | async-start | bytes 5898240 | tf_op jit(solution)/shard_map/reduce_scatter | solution.py:732
  284.7 43.3 %all-to-all-start.5 = ((bf16[8,192,768]{2,1,0:T(8,128)(2,1)}), bf16[8,192,768]{2,1,0:T(8,128)(2,1)}, u32[]{:S(2)}, u32[]{:S(2)}) async-start(bf16[8,192,768]{2,1,0:T(8,128)(2,1)} %get-tuple-element.79), calls=%async_computation.5 | async-start | bytes 4718592 | tf_op jit(solution)/shard_map/all_to_all | solution.py:654
  289.7 8.8 %collective-permute-start.14 = (f32[200,8]{0,1:T(8,128)S(1)}, f32[200,8]{0,1:T(8,128)S(1)}, u32[]{:S(2)}, u32[]{:S(2)}) collective-permute-start(f32[200,8]{0,1:T(8,128)S(1)} %slice_select_fusion.6), channel_id=1, source_target_pairs={{0,1},{1,0},{2,3},{3,2},{4,5},{5,4},{6,7},{7,6},{8,9},{9,8},{10,11... | collective-permute-start | bytes 19208 | tf_op jit(solution)/shard_map/ppermute | solution.py:753
  292.7 9.7 %collective-permute-start.13 = (f32[200,768]{1,0:T(8,128)}, f32[200,768]{1,0:T(8,128)}, u32[]{:S(2)}, u32[]{:S(2)}) collective-permute-start(f32[200,768]{1,0:T(8,128)} %slice_select_fusion.2), channel_id=1, source_target_pairs={{0,1},{1,0},{2,3},{3,2},{4,5},{5,4},{6,7},{7,6},{8,9},{9,8},{10,11... | collective-permute-start | bytes 1843208 | tf_op jit(solution)/shard_map/ppermute | solution.py:666
  362.3 37.4 %all-to-all-start.6 = ((bf16[4,4,112,768]{3,2,1,0:T(8,128)(2,1)}), bf16[4,4,112,768]{3,2,1,0:T(8,128)(2,1)}, u32[]{:S(2)}, u32[]{:S(2)}) async-start(bf16[4,4,112,768]{3,2,1,0:T(8,128)(2,1)} %bitcast.82), calls=%async_computation.6 | async-start | bytes 5505024 | tf_op jit(solution)/shard_map/all_to_all | solution.py:812
  369.4 47.0 %collective-permute-start.12 = (f32[200,768]{1,0:T(8,128)}, f32[200,768]{1,0:T(8,128)}, u32[]{:S(2)}, u32[]{:S(2)}) collective-permute-start(f32[200,768]{1,0:T(8,128)} %slice_select_fusion.3), channel_id=1, source_target_pairs={{0,1},{1,0},{2,3},{3,2},{4,5},{5,4},{6,7},{7,6},{8,9},{9,8},{10,11... | collective-permute-start | bytes 1843208 | tf_op jit(solution)/shard_map/ppermute | solution.py:666
  401.9 10.9 %all-to-all-start.9 = ((bf16[8,2,96,128]{3,2,1,0:T(8,128)(2,1)}), bf16[8,2,96,128]{3,2,1,0:T(8,128)(2,1)S(1)}, u32[]{:S(2)}, u32[]{:S(2)}) async-start(bf16[8,2,96,128]{3,2,1,0:T(8,128)(2,1)} %bitcast.286), calls=%async_computation.12 | async-start | bytes 786432 | tf_op jit(solution)/shard_map/all_to_all | solution.py:840
  412.8 29.3 %all-to-all-start.8 = ((bf16[8,2,96,256]{3,2,1,0:T(8,128)(2,1)}), bf16[8,2,96,256]{3,2,1,0:T(8,128)(2,1)S(1)}, u32[]{:S(2)}, u32[]{:S(2)}) async-start(bf16[8,2,96,256]{3,2,1,0:T(8,128)(2,1)} %bitcast.271), calls=%async_computation.10 | async-start | bytes 1572864 | tf_op jit(solution)/shard_map/all_to_all | solution.py:840
  417.8 12.8 %collective-permute-start.16 = (bf16[112,768]{1,0:T(8,128)(2,1)S(1)}, bf16[112,768]{1,0:T(8,128)(2,1)S(1)}, u32[]{:S(2)}, u32[]{:S(2)}) collective-permute-start(bf16[112,768]{1,0:T(8,128)(2,1)S(1)} %get-tuple-element.162), channel_id=1, source_target_pairs={{0,8},{8,16},{16,24},{24,0},{1,9},{9,17},{17,25},{25,1},{2,10},{10... | collective-permute-start | bytes 516104 | tf_op jit(solution)/shard_map/ppermute | solution.py:818
  419.2 22.0 %collective-permute-start.17 = (bf16[112,768]{1,0:T(8,128)(2,1)S(1)}, bf16[112,768]{1,0:T(8,128)(2,1)S(1)}, u32[]{:S(2)}, u32[]{:S(2)}) collective-permute-start(bf16[112,768]{1,0:T(8,128)(2,1)S(1)} %get-tuple-element.164), channel_id=1, source_target_pairs={{0,16},{8,24},{16,0},{24,8},{1,17},{9,25},{17,1},{25,9},{2,18},{10... | collective-permute-start | bytes 516104 | tf_op jit(solution)/shard_map/ppermute | solution.py:818
  420.6 20.6 %collective-permute-start.18 = (bf16[112,768]{1,0:T(8,128)(2,1)S(1)}, bf16[112,768]{1,0:T(8,128)(2,1)S(1)}, u32[]{:S(2)}, u32[]{:S(2)}) collective-permute-start(bf16[112,768]{1,0:T(8,128)(2,1)S(1)} %get-tuple-element.163), channel_id=1, source_target_pairs={{0,24},{8,0},{16,8},{24,16},{1,25},{9,1},{17,9},{25,17},{2,26},{10... | collective-permute-start | bytes 516104 | tf_op jit(solution)/shard_map/ppermute | solution.py:818
  442.1 19.4 %all-to-all-start.7 = ((bf16[8,2,96,384]{3,2,1,0:T(8,128)(2,1)}), bf16[8,2,96,384]{3,2,1,0:T(8,128)(2,1)S(1)}, u32[]{:S(2)}, u32[]{:S(2)}) async-start(bf16[8,2,96,384]{3,2,1,0:T(8,128)(2,1)} %bitcast.265), calls=%async_computation.8 | async-start | bytes 2359296 | tf_op jit(solution)/shard_map/all_to_all | solution.py:840
  (44 other events, 368.4 us)
Sparse Core Ops, SparseCore 0:
  39.3 92.3 all-gather.10
  133.9 61.9 all-gather.8
  197.5 35.7 all-gather.6
  248.2 34.1 reduce-scatter.7
  284.5 59.2 reduce-scatter.5
  346.0 96.0 reduce-scatter.3

commit v6 on v5

--- a/solution.py
+++ b/solution.py
@@ -324,7 +324,7 @@
 
 def pack_experts_kernel(up_ref, down_ref, *refs):
     up = up_ref[0].astype(BF16)
-    down = down_ref[0].T.astype(BF16)
+    down = down_ref[0].astype(BF16)
     start = 0
     for ref in refs:
         stop = start + ref.shape[3]
@@ -537,11 +537,11 @@
     width = qkv_weight.shape[2]
     tokens = piece * sequence
     blocks = units // CHUNK
-    spans = [(0, 3), (3, 5), (5, 6)] if blocks == 6 else [(0, blocks)]
+    spans = [(0, 4), (4, 6)] if blocks == 6 else [(0, blocks)]
 
     head = spans[0][1] * CHUNK
     sizes = [head, units - head] if units > head else [head]
-    packed = pack_experts(up_weight, down_weight, sizes)
+    packed = pack_experts(up_weight, down_weight.transpose(0, 2, 1), sizes)
     qkv_weight, norm1_gain = tie((qkv_weight, norm1_gain), packed[0])
 
     smalls = jnp.concatenate(
@@ -737,6 +737,16 @@
     back = swap_experts(pulled)
     gate_back = values_of(back)
     norm_two_grad = combine(back)
+
+    def send_back(some, *events):
+        if not some:
+            return None
+        some = some[0].astype(BF16)
+        if length != 4:
+            some = some.reshape(2, 2, part, quarter, -1).transpose(1, 3, 0, 2, 4)
+            some = some.reshape(experts, 2, part, -1)
+        return swap_experts(some, *events)
+
     mixed = swap_experts(mixed, back)
 
     def slots_to_tokens(match, parts_here):
@@ -772,8 +782,6 @@
     h_grad, hb, dq, dk, dv, line_sums, pair_sums = attend_backward(
         norm_two_grad, out_grad, residual, mask_here, wo, lines, q, k, v, lse
     )
-    h_grad = tie(h_grad, mixed)
-    input_grad, line_ones = input_backward(h_grad, tokens_in, wq, wk, wv, lines, dq, dk, dv)
     bias_rows = jnp.concatenate(bias_parts, 1).reshape(dp, quarter, part)
     bias_rows = jnp.where(
         jnp.arange(experts)[:, None, None, None] == expert, bias_rows[None], 0.0
@@ -781,7 +789,7 @@
     bias_rows = bias_rows.transpose(0, 2, 1, 3).reshape(experts * quarter, dp, part)
     line_grads = jnp.concatenate(
         [
-            line_ones[:2],
+            jnp.zeros((2, model), F32),
             pair_sums[:, 0].reshape(1, model),
             pair_sums[:, 1].reshape(1, model),
             line_sums[:3],
@@ -795,6 +803,7 @@
     vector_grads = vector_grads.transpose(1, 0, 2).reshape(dp, small_rows * part)
     vector_grads = jnp.pad(vector_grads, ((0, 0), (0, pad))).reshape(dp, -1, model)
 
+    hb = tie(hb, mixed)
     if length == 4:
         pack_grads = attend_weights(n1, hb, dq, dk, dv, attended, vector_grads)
     else:
@@ -804,13 +813,27 @@
         pack_grads = jnp.concatenate([pack_grads, vector_grads], 2)
         pack_grads = pack_grads.reshape(quarter // 2, 2, dp // 2, 2, -1, model)
         pack_grads = pack_grads.transpose(1, 3, 0, 2, 4, 5)
+    h_grad = tie(h_grad, pack_grads)
+    input_grad, line_ones = input_backward(h_grad, tokens_in, wq, wk, wv, lines, dq, dk, dv)
     mine = lax.dynamic_index_in_dim(pack_grads, core, 0, keepdims=False)
     theirs = lax.dynamic_index_in_dim(pack_grads, 1 - core, 0, keepdims=False)
     theirs = lax.ppermute(theirs, "c", swap)
     pack_grads = (mine.astype(F32) + theirs.astype(F32)).astype(sum_type)
     pack_grads = pack_grads.reshape((-1,) + pack_grads.shape[2:])
     pack_grads = lax.all_to_all(pack_grads, ("x", "y"), 0, 0, tiled=True)
-    pack_grads = jnp.sum(pack_grads.astype(F32), 0).astype(sum_type)
+    after_xy = pack_grads
+    pack_grads = jnp.sum(pack_grads.astype(F32), 0)
+    ones = line_ones[:2]
+    for axis in ("c", "y", "x"):
+        ones = ones + lax.ppermute(ones, axis, swap)
+    ones = ones.reshape(2, dp // 2, 2, part)
+    ones = lax.dynamic_index_in_dim(ones, place[1], 2, keepdims=False).transpose(1, 0, 2)
+    ones = jnp.pad(
+        ones.reshape(dp // 2, 1, 2 * part), ((0, 0), (0, 0), (0, model - 2 * part))
+    )
+    pack_grads = (
+        pack_grads + jnp.pad(ones, ((0, 0), (part, pack_grads.shape[1] - part - 1), (0, 0)))
+    ).astype(sum_type)
     if length == 4:
         pack_grad = lax.dynamic_index_in_dim(pack_grads, place[0], 0, keepdims=False).astype(F32)
         for far in (1, 2, 3):
@@ -827,19 +850,12 @@
     bias_term = jnp.dot(share_here, bias_down, precision=HIGHEST).reshape(residual.shape)
     output = (residual + mixture + bias_term).astype(BF16)
 
-    ups, downs = [], []
-    totals = reduced
-    if length != 4:
-        totals = [
-            one.reshape(2, 2, part, quarter, -1).transpose(1, 3, 0, 2, 4).reshape(experts, 2, part, -1)
-            for one in totals
-        ]
-    for some, event in ((totals[:1], mixed), (totals[1:2], pack_grads), (totals[2:], pack_grads)):
-        if some:
-            some = some[0] if len(some) == 1 else jnp.concatenate(some, -1)
-            some = lax.all_to_all(tie(some.astype(BF16), event), PLANE, 0, 0, tiled=True).astype(F32)
-            ups.append(some[:, 0])
-            downs.append(some[:, 1])
+    sent = [send_back(reduced[:1], after_xy)]
+    sent.append(send_back(reduced[1:2], *sent))
+    sent.append(send_back(reduced[2:], *sent[1:]))
+    sent = [one.astype(F32) for one in sent if one is not None]
+    ups = [one[:, 0] for one in sent]
+    downs = [one[:, 1] for one in sent]
     up_grad = jnp.concatenate(ups, -1)
     down_grad = jnp.concatenate(downs, -1).transpose(0, 2, 1)
     return (

time: 481 us -> 449 us (0.933)
  waiting for transfers between devices: 154 us -> 137 us
  local copies, waits for them, and re-layouts: 50.4 us -> 41.2 us
  Pallas kernels: 142 us -> 137 us
    all_to_all x1, waiting for transfers between devices: 29.8 us -> 0.01 us  [shards(): pack_grads = lax.all_to_all(pack_grads, ('x', 'y'), 0, 0, tiled=True)]
    ppermute x0 -> x3, waiting for transfers between devices: none -> 15.9 us  [shards(): ones = ones + lax.ppermute(ones, axis, swap)]
    all_to_all x3 -> x0, waiting for transfers between devices: 14.7 us -> none  [shards(): lax.all_to_all(tie(some.astype(BF16), event), PLANE, 0, 0, tiled=True)]
    all_to_all x4 -> x6, waiting for transfers between devices: 46.9 us -> 61.5 us  [swap_experts(): return lax.all_to_all(tie(rows, *events), PLANE, 0, 0, tiled=True)]
    all_to_all x3 -> x0, starting transfers between devices: 10.6 us -> none  [shards(): lax.all_to_all(tie(some.astype(BF16), event), PLANE, 0, 0, tiled=True)]
    all_to_all x4 -> x6, starting transfers between devices: 16.5 us -> 25.3 us  [swap_experts(): return lax.all_to_all(tie(rows, *events), PLANE, 0, 0, tiled=True)]
    ppermute x3, waiting for transfers between devices: 16.7 us -> 8.89 us  [shards(): some = lax.ppermute(some, 'z', [(k, (k + far) % 4) for k in range(4)])]
    pallas_call x3 -> x2, Pallas kernels: 72.3 us -> 67.5 us  [expert_chunk(): pl.pallas_call(functools.partial(expert_kernel, first, last), grid=(exper...]
  transfers between devices with their start and end apart: 35 -> 35, of which waited for: 15 -> 15; matrix products, arithmetic and copies ran while one was open for 19% -> 18% of each run, Pallas kernels for 26% -> 30%
where the time goes in v6:
time: 449 us; the launch traced here: 442 us
  Pallas kernels  137 us (31%)
  waiting for transfers between devices  137 us (31%)
  starting transfers between devices  60.6 us (13%)
  local copies, waits for them, and re-layouts  41.2 us (9%)
  other arithmetic  31.8 us (7%)
  matrix products  18.5 us (4%)
  between operations  15.6 us (3%)
    pallas_call x2, Pallas kernels, expert_chunk(): pl.pallas_call(functools.partial(expert_kernel, first, last), grid=(exper...  67.5 us
    all_to_all x6, waiting for transfers between devices, swap_experts(): return lax.all_to_all(tie(rows, *events), PLANE, 0, 0, tiled=True)  61.5 us
    pallas_call x1, Pallas kernels, attend_forward(): pl.pallas_call(attend_forward_kernel, grid_spec=pltpu.PrefetchScalarGridS...  26.1 us
    all_to_all x6, starting transfers between devices, swap_experts(): return lax.all_to_all(tie(rows, *events), PLANE, 0, 0, tiled=True)  25.3 us
    pallas_call x1, Pallas kernels, attend_backward(): pl.pallas_call(attend_backward_kernel, grid=(images,), in_specs=[whole(a....  21.2 us
    ppermute x3, waiting for transfers between devices, shards(): ones = ones + lax.ppermute(ones, axis, swap)  15.9 us
    dot_general x15, matrix products, dot(): lax.dot_general(left, right, (((left_dim,), (right_dim,)), ((), ())), pre...  15.2 us
    unnamed x103, local copies, waits for them, and re-layouts  14.5 us
  transfers between devices with their start and end apart: 35, of which 15 were waited for; matrix products, arithmetic and copies ran while one was open for 18% of the time, Pallas kernels for 30%

profile of v6, /device:TPU:0, one launch (start us, length us, event | category | flops | bytes accessed | tf_op | source)
XLA Modules:
  0.0 442.1 jit_solution(8165522182399062902)
XLA Ops:
  10.5 3.0 pack_experts.1
  13.7 5.3 %all-to-all-start = ((bf16[8,2,96,512]{3,2,1,0:T(8,128)(2,1)}), bf16[8,2,96,512]{3,2,1,0:T(8,128)(2,1)S(1)}, u32[]{:S(2)}, u32[]{:S(2)}) async-start(bf16[8,2,96,512]{3,2,1,0:T(8,128)(2,1)} %get-tuple-element.58), calls=%async_computation | async-start | bytes 3145728 | tf_op jit(solution)/shard_map/all_to_all | solution.py:589
  25.7 3.6 collective-permute-done
  29.3 7.0 %collective-permute-done.1 = bf16[112,768]{1,0:T(8,128)(2,1)S(1)} collective-permute-done((bf16[112,768]{1,0:T(8,128)(2,1)S(1)}, bf16[112,768]{1,0:T(8,128)(2,1)S(1)}, u32[]{:S(2)}, u32[]{:S(2)}) %collective-permute-start.1) | collective-permute-done | bytes 172064 | tf_op jit(solution)/shard_map/ppermute | solution.py:498
  36.2 2.8 all-to-all-done
  49.1 13.9 %collective-permute-done.5.refs_3_ = bf16[4,112,768]{2,1,0:T(8,128)(2,1)} collective-permute-done((bf16[4,112,768]{2,1,0:T(8,128)(2,1)S(1)}, bf16[4,112,768]{2,1,0:T(8,128)(2,1)}, u32[]{:S(2)}, u32[]{:S(2)}) %collective-permute-start.5) | collective-permute-done | bytes 688160 | tf_op jit(solution)/shard_map/ppermute | solution.py:504
  63.0 3.6 all-to-all-start.1
  73.6 5.0 %all-to-all-done.1 = bf16[8,2,96,256]{3,2,1,0:T(8,128)(2,1)S(1)} async-done(((bf16[8,2,96,256]{3,2,1,0:T(8,128)(2,1)}), bf16[8,2,96,256]{3,2,1,0:T(8,128)(2,1)S(1)}, u32[]{:S(2)}, u32[]{:S(2)}) %all-to-all-start.1) | async-done | bytes 786464 | tf_op jit(solution)/shard_map/all_to_all | solution.py:589
  79.5 4.4 all-to-all-start.2
  86.7 6.7 %collective-permute-done.3.refs_1_ = bf16[4,112,768]{2,1,0:T(8,128)(2,1)} collective-permute-done((bf16[4,112,768]{2,1,0:T(8,128)(2,1)}, bf16[4,112,768]{2,1,0:T(8,128)(2,1)}, u32[]{:S(2)}, u32[]{:S(2)}) %collective-permute-start.3) | collective-permute-done | bytes 688160 | tf_op jit(solution)/shard_map/ppermute | solution.py:502
  97.8 26.1 %attend_forward.1 = (bf16[3,208,768]{2,1,0:T(8,128)(2,1)}, bf16[3,200,768]{2,1,0:T(8,128)(2,1)}, f32[3,200,768]{2,1,0:T(8,128)}, bf16[3,4,200,192]{3,2,1,0:T(8,1...) custom-call(s32[4]{0:T(128)} %pad_add_fusion.1.place_ref, ...), custom_call_target="tpu_custom_call" | custom-call | flops 2000000000 | bytes 4000000 | tf_op jit(solution)/shard_map/attend_forward/pallas_call | solution.py:147
  133.9 4.4 all-to-all-start.3
  139.4 29.6 %all-to-all-done.3.x_ref = bf16[8,208,768]{2,1,0:T(8,128)(2,1)} async-done(((bf16[8,208,768]{2,1,0:T(8,128)(2,1)}), bf16[8,208,768]{2,1,0:T(8,128)(2,1)}, u32[]{:S(2)}, u32[]{:S(2)}) %all-to-all-start.3) | async-done | bytes 2555936 | tf_op jit(solution)/shard_map/all_to_all | solution.py:654
  168.9 43.0 %expert_chunk.2 = (f32[8,192,768]{2,1,0:T(8,128)}, f32[8,192,768]{2,1,0:T(8,128)}, f32[1,2048]{1,0:T(1,128)}, bf16[4,8,2,96,512]{4,3,2,1,0:T(8,128)(2,1)}) custom-call(bf16[8,208,768]{2,1,0:T(8,128)(2,1)} %all-to-all-done.3.x_ref, bf16[8,192,768]{2,1,0:T(8,128)(2,1)} %all-to-all-done.2.g_ref, f32[1,2048]{1,0:T(1,128)} %bitcast.303, ...), custom_call_target="tpu_custom_call" | custom-call | flops 4831838208 | bytes 4000000 | tf_op jit(solution)/shard_map/expert_chunk/pallas_call | solution.py:460
  212.6 6.8 %all-gather.5.cloned.1.call-done = bf16[32,2,96,256]{3,2,1,0:T(8,128)(2,1)} async-done(((bf16[8,2,96,256]{3,2,1,0:T(8,128)(2,1)}), bf16[32,2,96,256]{3,2,1,0:T(8,128)(2,1)}) %all-gather.5.cloned.1.call-update) | async-done | bytes 3145744 | tf_op jit(solution)/shard_map/all_gather | solution.py:676
  219.3 24.6 %expert_chunk.3 = (bf16[8,192,768]{2,1,0:T(8,128)(2,1)}, bf16[8,208,768]{2,1,0:T(8,128)(2,1)}, f32[1,1024]{1,0:T(1,128)}, bf16[4,8,2,96,256]{4,3,2,1,0:T(8,128)(2,1)}) custom-call(bf16[8,208,768]{2,1,0:T(8,128)(2,1)} %all-to-all-done.3.x_ref, bf16[8,192,768]{2,1,0:T(8,128)(2,1)} %all-to-all-done.2.g_ref, f32[1,1024]{1,0:T(1,128)} %bitcast.298, ...), custom_call_target="tpu_custom_call" | custom-call | flops 2415919104 | bytes 4000000 | tf_op jit(solution)/shard_map/expert_chunk/pallas_call | solution.py:460
  243.9 4.4 all-to-all-start.4
  255.5 23.4 %all-to-all-done.4 = bf16[8,208,768]{2,1,0:T(8,128)(2,1)} async-done(((bf16[8,208,768]{2,1,0:T(8,128)(2,1)}), bf16[8,208,768]{2,1,0:T(8,128)(2,1)}, u32[]{:S(2)}, u32[]{:S(2)}) %all-to-all-start.4) | async-done | bytes 2555936 | tf_op jit(solution)/shard_map/all_to_all | solution.py:654
  283.2 4.4 all-to-all-start.5
  300.0 21.2 %attend_backward.1 = (f32[3,200,768]{2,1,0:T(8,128)}, bf16[3,208,768]{2,1,0:T(8,128)(2,1)}, bf16[3,4,208,192]{3,2,1,0:T(8,128)(2,1)}, bf16[3,4,208,192]{3,2,1,0:...) custom-call(f32[3,200,768]{2,1,0:T(8,128)} %fusion.4.n2_grad_ref, ...), custom_call_target="tpu_custom_call" | custom-call | tf_op jit(solution)/shard_map/attend_backward/pallas_call | solution.py:226
  324.5 9.6 %attend_weights.1 = bf16[2,2,2,4,112,768]{5,4,3,2,1,0:T(8,128)(2,1)} custom-call(bf16[3,208,768]{2,1,0:T(8,128)(2,1)} %get-tuple-element.80.n1_ref, bf16[3,208,768]{2,1,0:T(8,128)(2,1)} %get-tuple-element.82.hb_ref, bf16[3,4,208,192]{3,2,1,0:T(8,128)(2,1)} %get-tuple-element.83.dq_ref, bf16[3,4,208,192]{3,2,1,0:T(8,128)(2,1)} %get-tuple-element.84.dk_ref, ...), custom_call_target="tpu_custom_call" | custom-call | tf_op jit(solution)/shard_map/attend_weights/pallas_call | solution.py:274
  334.0 3.5 dynamic-slice_bitcast_fusion
  337.8 5.1 %collective-permute-done.15 = bf16[2,2,4,112,768]{4,3,2,1,0:T(8,128)(2,1)} collective-permute-done((bf16[2,2,4,112,768]{4,3,2,1,0:T(8,128)(2,1)}, bf16[2,2,4,112,768]{4,3,2,1,0:T(8,128)(2,1)}, u32[]{:S(2)}, u32[]{:S(2)}) %collective-permute-start.15) | collective-permute-done | bytes 2752544 | tf_op jit(solution)/shard_map/ppermute | solution.py:820
  342.9 4.9 %fusion = bf16[2,2,4,112,768]{4,3,2,1,0:T(8,128)(2,1)} fusion(bf16[2,2,4,112,768]{4,3,2,1,0:T(8,128)(2,1)} %collective-permute-done.15, bf16[2,2,2,4,112,768]{5,4,3,2,1,0:T(8,128)(2,1)} %attend_weights.1, s32[]{:T(128)S(6)} %select_n.266), kind=kLoop, calls=%fused_computation.1 | loop fusion | flops 5505024 | bytes 8257540 | tf_op jit(solution)/shard_map/convert_element_type | solution.py:821
  347.8 4.6 %all-to-all-start.6 = ((bf16[4,4,112,768]{3,2,1,0:T(8,128)(2,1)}), bf16[4,4,112,768]{3,2,1,0:T(8,128)(2,1)}, u32[]{:S(2)}, u32[]{:S(2)}) async-start(bf16[4,4,112,768]{3,2,1,0:T(8,128)(2,1)} %bitcast.248), calls=%async_computation.6 | async-start | bytes 5505024 | tf_op jit(solution)/shard_map/all_to_all | solution.py:823
  352.4 9.7 %input_backward.1 = (f32[3,200,768]{2,1,0:T(8,128)}, f32[8,768]{1,0:T(8,128)}) custom-call(f32[3,200,768]{2,1,0:T(8,128)} %get-tuple-element.91.h_grad_ref, bf16[3,200,768]{2,1,0:T(8,128)(2,1)} %tokens_ref.3, bf16[4,768,192]{2,1,0:T(8,128)(2,1)} %get-tuple-element.92.wq_ref, bf16[4,768,192]{2,1,0:T(8,128)(2,1)} %get-tuple-element.93.wk_ref, ...), custom_call_target="tpu_custom_call" | custom-call | tf_op jit(solution)/shard_map/input_backward/pallas_call | solution.py:313
  369.6 15.5 %collective-permute-done.17 = f32[2,768]{1,0:T(2,128)S(1)} collective-permute-done((f32[2,768]{1,0:T(2,128)S(1)}, f32[2,768]{1,0:T(2,128)S(1)}, u32[]{:S(2)}, u32[]{:S(2)}) %collective-permute-start.17) | collective-permute-done | bytes 6176 | tf_op jit(solution)/shard_map/ppermute | solution.py:828
  389.1 3.6 all-to-all-start.7
  397.3 2.8 collective-permute-start.21
  404.7 6.5 %collective-permute-done.20 = bf16[112,768]{1,0:T(8,128)(2,1)S(1)} collective-permute-done((bf16[112,768]{1,0:T(8,128)(2,1)S(1)}, bf16[112,768]{1,0:T(8,128)(2,1)S(1)}, u32[]{:S(2)}, u32[]{:S(2)}) %collective-permute-start.20) | collective-permute-done | bytes 172064 | tf_op jit(solution)/shard_map/ppermute | solution.py:841
  414.5 4.2 all-to-all-start.8
  421.7 8.6 %all-to-all-done.8 = bf16[8,2,96,256]{3,2,1,0:T(8,128)(2,1)S(1)} async-done(((bf16[8,2,96,256]{3,2,1,0:T(8,128)(2,1)}), bf16[8,2,96,256]{3,2,1,0:T(8,128)(2,1)S(1)}, u32[]{:S(2)}, u32[]{:S(2)}) %all-to-all-start.8) | async-done | bytes 786464 | tf_op jit(solution)/shard_map/all_to_all | solution.py:654
  (338 shorter events, 105.1 us)
Async XLA Ops:
  13.7 25.4 %all-to-all-start = ((bf16[8,2,96,512]{3,2,1,0:T(8,128)(2,1)}), bf16[8,2,96,512]{3,2,1,0:T(8,128)(2,1)S(1)}, u32[]{:S(2)}, u32[]{:S(2)}) async-start(bf16[8,2,96,512]{3,2,1,0:T(8,128)(2,1)} %get-tuple-element.58), calls=%async_computation | async-start | bytes 3145728 | tf_op jit(solution)/shard_map/all_to_all | solution.py:589
  19.0 150.0 %all-gather.7.cloned.1.call-start = ((), (), s32[]{:S(2)}) async-start(), calls=%async_computation.14 | async-start | bytes 7864320 | tf_op jit(solution)/shard_map/all_gather | solution.py:676
  20.1 9.1 %collective-permute-start = (bf16[112,768]{1,0:T(8,128)(2,1)S(1)}, bf16[112,768]{1,0:T(8,128)(2,1)S(1)}, u32[]{:S(2)}, u32[]{:S(2)}) collective-permute-start(bf16[112,768]{1,0:T(8,128)(2,1)S(1)} %pad_maximum_fusion.5), channel_id=1, source_target_pairs={{0,8},{8,16},{16,24},{24,0},{1,9},{9,17},{17,25},{25,1},{2,10},{10... | collective-permute-start | bytes 516104 | tf_op jit(solution)/shard_map/ppermute | solution.py:498
  21.7 14.5 %collective-permute-start.1 = (bf16[112,768]{1,0:T(8,128)(2,1)S(1)}, bf16[112,768]{1,0:T(8,128)(2,1)S(1)}, u32[]{:S(2)}, u32[]{:S(2)}) collective-permute-start(bf16[112,768]{1,0:T(8,128)(2,1)S(1)} %pad_maximum_fusion.5), channel_id=1, source_target_pairs={{0,16},{8,24},{16,0},{24,8},{1,17},{9,25},{17,1},{25,9},{2,18},{10... | collective-permute-start | bytes 516104 | tf_op jit(solution)/shard_map/ppermute | solution.py:498
  24.3 11.9 %collective-permute-start.2 = (bf16[112,768]{1,0:T(8,128)(2,1)S(1)}, bf16[112,768]{1,0:T(8,128)(2,1)S(1)}, u32[]{:S(2)}, u32[]{:S(2)}) collective-permute-start(bf16[112,768]{1,0:T(8,128)(2,1)S(1)} %pad_maximum_fusion.5), channel_id=1, source_target_pairs={{0,24},{8,0},{16,8},{24,16},{1,25},{9,1},{17,9},{25,17},{2,26},{10... | collective-permute-start | bytes 516104 | tf_op jit(solution)/shard_map/ppermute | solution.py:498
  41.0 29.0 %collective-permute-start.10 = (bf16[200,768]{1,0:T(8,128)(2,1)}, bf16[200,768]{1,0:T(8,128)(2,1)}, u32[]{:S(2)}, u32[]{:S(2)}) collective-permute-start(bf16[200,768]{1,0:T(8,128)(2,1)} %fusion.76), channel_id=1, source_target_pairs={{0,1},{1,0},{2,3},{3,2},{4,5},{5,4},{6,7},{7,6},{8,9},{9,8},{10,11... | collective-permute-start | bytes 921608 | tf_op jit(solution)/shard_map/ppermute | solution.py:630
  44.0 18.9 %collective-permute-start.5 = (bf16[4,112,768]{2,1,0:T(8,128)(2,1)S(1)}, bf16[4,112,768]{2,1,0:T(8,128)(2,1)}, u32[]{:S(2)}, u32[]{:S(2)}) collective-permute-start(bf16[4,112,768]{2,1,0:T(8,128)(2,1)S(1)} %pad_maximum_fusion.3.refs_0_), channel_id=1, source_target_pairs={{0,6},{2,4},{4,2},{6,0},{1,7},{3,5},{5,3},{7,1},{8,14},{10,12},{12... | collective-permute-start | bytes 2064392 | tf_op jit(solution)/shard_map/ppermute | solution.py:504
  45.6 17.4 %collective-permute-start.6 = (bf16[4,112,768]{2,1,0:T(8,128)(2,1)S(1)}, bf16[4,112,768]{2,1,0:T(8,128)(2,1)}, u32[]{:S(2)}, u32[]{:S(2)}) collective-permute-start(bf16[4,112,768]{2,1,0:T(8,128)(2,1)S(1)} %pad_maximum_fusion.3.refs_0_), channel_id=1, source_target_pairs={{0,1},{1,0},{2,3},{3,2},{4,5},{5,4},{6,7},{7,6},{8,9},{9,8},{10,11... | collective-permute-start | bytes 2064392 | tf_op jit(solution)/shard_map/ppermute | solution.py:506
  63.0 10.6 %collective-permute-start.9 = (bf16[4,112,768]{2,1,0:T(8,128)(2,1)}, bf16[4,112,768]{2,1,0:T(8,128)(2,1)}, u32[]{:S(2)}, u32[]{:S(2)}) collective-permute-start(bf16[4,112,768]{2,1,0:T(8,128)(2,1)} %collective-permute-done.5.refs_3_), channel_id=1, source_target_pairs={{0,1},{1,0},{2,3},{3,2},{4,5},{5,4},{6,7},{7,6},{8,9},{9,8},{10,11... | collective-permute-start | bytes 2064392 | tf_op jit(solution)/shard_map/ppermute | solution.py:506
  63.0 15.6 %all-to-all-start.1 = ((bf16[8,2,96,256]{3,2,1,0:T(8,128)(2,1)}), bf16[8,2,96,256]{3,2,1,0:T(8,128)(2,1)S(1)}, u32[]{:S(2)}, u32[]{:S(2)}) async-start(bf16[8,2,96,256]{3,2,1,0:T(8,128)(2,1)} %get-tuple-element.64), calls=%async_computation.1 | async-start | bytes 1572864 | tf_op jit(solution)/shard_map/all_to_all | solution.py:589
  66.6 26.8 %collective-permute-start.3 = (bf16[4,112,768]{2,1,0:T(8,128)(2,1)}, bf16[4,112,768]{2,1,0:T(8,128)(2,1)}, u32[]{:S(2)}, u32[]{:S(2)}) collective-permute-start(bf16[4,112,768]{2,1,0:T(8,128)(2,1)} %copy-done.17), channel_id=1, source_target_pairs={{0,4},{4,0},{1,5},{5,1},{2,6},{6,2},{3,7},{7,3},{8,12},{12,8},{9,1... | collective-permute-start | bytes 2064392 | tf_op jit(solution)/shard_map/ppermute | solution.py:502
  68.5 24.9 %collective-permute-start.4 = (bf16[4,112,768]{2,1,0:T(8,128)(2,1)}, bf16[4,112,768]{2,1,0:T(8,128)(2,1)}, u32[]{:S(2)}, u32[]{:S(2)}) collective-permute-start(bf16[4,112,768]{2,1,0:T(8,128)(2,1)} %copy-done.17), channel_id=1, source_target_pairs={{0,2},{2,0},{1,3},{3,1},{4,6},{6,4},{5,7},{7,5},{8,10},{10,8},{9,1... | collective-permute-start | bytes 2064392 | tf_op jit(solution)/shard_map/ppermute | solution.py:503
  79.5 44.4 %all-to-all-start.2 = ((bf16[8,192,768]{2,1,0:T(8,128)(2,1)}), bf16[8,192,768]{2,1,0:T(8,128)(2,1)}, u32[]{:S(2)}, u32[]{:S(2)}) async-start(bf16[8,192,768]{2,1,0:T(8,128)(2,1)} %pad_maximum_fusion.1), calls=%async_computation.2 | async-start | bytes 4718592 | tf_op jit(solution)/shard_map/all_to_all | solution.py:654
  83.8 135.5 %all-gather.5.cloned.1.call-start = ((), (), s32[]{:S(2)}) async-start(), calls=%async_computation.13 | async-start | bytes 3932160 | tf_op jit(solution)/shard_map/all_gather | solution.py:676
  93.4 3.5 collective-permute-start.8
  133.9 35.0 %all-to-all-start.3 = ((bf16[8,208,768]{2,1,0:T(8,128)(2,1)}), bf16[8,208,768]{2,1,0:T(8,128)(2,1)}, u32[]{:S(2)}, u32[]{:S(2)}) async-start(bf16[8,208,768]{2,1,0:T(8,128)(2,1)} %pad_maximum_fusion), calls=%async_computation.3 | async-start | bytes 5111808 | tf_op jit(solution)/shard_map/all_to_all | solution.py:654
  138.3 250.8 %reduce-scatter.3.cloned.1.call-start = ((), (), s32[]{:S(2)}) async-start(), calls=%async_computation.11 | async-start | bytes 7864320 | tf_op jit(solution)/shard_map/reduce_scatter | solution.py:732
  243.9 35.0 %all-to-all-start.4 = ((bf16[8,208,768]{2,1,0:T(8,128)(2,1)}), bf16[8,208,768]{2,1,0:T(8,128)(2,1)}, u32[]{:S(2)}, u32[]{:S(2)}) async-start(bf16[8,208,768]{2,1,0:T(8,128)(2,1)} %get-tuple-element.72), calls=%async_computation.4 | async-start | bytes 5111808 | tf_op jit(solution)/shard_map/all_to_all | solution.py:654
  280.1 13.2 %collective-permute-start.14 = (f32[200,8]{0,1:T(8,128)S(1)}, f32[200,8]{0,1:T(8,128)S(1)}, u32[]{:S(2)}, u32[]{:S(2)}) collective-permute-start(f32[200,8]{0,1:T(8,128)S(1)} %slice_select_fusion.6), channel_id=1, source_target_pairs={{0,1},{1,0},{2,3},{3,2},{4,5},{5,4},{6,7},{7,6},{8,9},{9,8},{10,11... | collective-permute-start | bytes 19208 | tf_op jit(solution)/shard_map/ppermute | solution.py:763
  282.7 14.6 %collective-permute-start.13 = (f32[200,768]{1,0:T(8,128)}, f32[200,768]{1,0:T(8,128)}, u32[]{:S(2)}, u32[]{:S(2)}) collective-permute-start(f32[200,768]{1,0:T(8,128)} %slice_select_fusion.2), channel_id=1, source_target_pairs={{0,1},{1,0},{2,3},{3,2},{4,5},{5,4},{6,7},{7,6},{8,9},{9,8},{10,11... | collective-permute-start | bytes 1843208 | tf_op jit(solution)/shard_map/ppermute | solution.py:666
  283.2 41.3 %all-to-all-start.5 = ((bf16[8,192,768]{2,1,0:T(8,128)(2,1)}), bf16[8,192,768]{2,1,0:T(8,128)(2,1)}, u32[]{:S(2)}, u32[]{:S(2)}) async-start(bf16[8,192,768]{2,1,0:T(8,128)(2,1)} %get-tuple-element.73), calls=%async_computation.5 | async-start | bytes 4718592 | tf_op jit(solution)/shard_map/all_to_all | solution.py:654
  287.6 126.9 %reduce-scatter.5.cloned.1.call-start = ((), (), s32[]{:S(2)}) async-start(), calls=%async_computation.12 | async-start | bytes 3932160 | tf_op jit(solution)/shard_map/reduce_scatter | solution.py:732
  337.5 5.4 %collective-permute-start.15 = (bf16[2,2,4,112,768]{4,3,2,1,0:T(8,128)(2,1)}, bf16[2,2,4,112,768]{4,3,2,1,0:T(8,128)(2,1)}, u32[]{:S(2)}, u32[]{:S(2)}) collective-permute-start(bf16[2,2,4,112,768]{4,3,2,1,0:T(8,128)(2,1)} %dynamic-slice_bitcast_fusion), channel_id=1, source_target_pairs={{0,1},{1,0},{2,3},{3,2},{4,5},{5,4},{6,7},{7,6},{8,9},{9,8},{10,11... | collective-permute-start | bytes 8257544 | tf_op jit(solution)/shard_map/ppermute | solution.py:820
  347.8 41.3 %all-to-all-start.6 = ((bf16[4,4,112,768]{3,2,1,0:T(8,128)(2,1)}), bf16[4,4,112,768]{3,2,1,0:T(8,128)(2,1)}, u32[]{:S(2)}, u32[]{:S(2)}) async-start(bf16[4,4,112,768]{3,2,1,0:T(8,128)(2,1)} %bitcast.248), calls=%async_computation.6 | async-start | bytes 5505024 | tf_op jit(solution)/shard_map/all_to_all | solution.py:823
  364.9 24.1 %collective-permute-start.12 = (f32[200,768]{1,0:T(8,128)S(1)}, f32[200,768]{1,0:T(8,128)S(1)}, u32[]{:S(2)}, u32[]{:S(2)}) collective-permute-start(f32[200,768]{1,0:T(8,128)S(1)} %slice_select_fusion.3), channel_id=1, source_target_pairs={{0,1},{1,0},{2,3},{3,2},{4,5},{5,4},{6,7},{7,6},{8,9},{9,8},{10,11... | collective-permute-start | bytes 1843208 | tf_op jit(solution)/shard_map/ppermute | solution.py:666
  365.9 19.2 %collective-permute-start.17 = (f32[2,768]{1,0:T(2,128)S(1)}, f32[2,768]{1,0:T(2,128)S(1)}, u32[]{:S(2)}, u32[]{:S(2)}) collective-permute-start(f32[2,768]{1,0:T(2,128)S(1)} %slice_add_fusion.1), channel_id=1, source_target_pairs={{0,2},{2,0},{1,3},{3,1},{4,6},{6,4},{5,7},{7,5},{8,10},{10,8},{9,1... | collective-permute-start | bytes 18440 | tf_op jit(solution)/shard_map/ppermute | solution.py:828
  385.1 3.6 collective-permute-start.18
  389.1 25.4 %all-to-all-start.7 = ((bf16[8,2,96,512]{3,2,1,0:T(8,128)(2,1)}), bf16[8,2,96,512]{3,2,1,0:T(8,128)(2,1)S(1)}, u32[]{:S(2)}, u32[]{:S(2)}) async-start(bf16[8,2,96,512]{3,2,1,0:T(8,128)(2,1)} %bitcast.260), calls=%async_computation.8 | async-start | bytes 3145728 | tf_op jit(solution)/shard_map/all_to_all | solution.py:654
  395.2 9.5 %collective-permute-start.19 = (bf16[112,768]{1,0:T(8,128)(2,1)S(1)}, bf16[112,768]{1,0:T(8,128)(2,1)S(1)}, u32[]{:S(2)}, u32[]{:S(2)}) collective-permute-start(bf16[112,768]{1,0:T(8,128)(2,1)S(1)} %get-tuple-element.167), channel_id=1, source_target_pairs={{0,8},{8,16},{16,24},{24,0},{1,9},{9,17},{17,25},{25,1},{2,10},{10... | collective-permute-start | bytes 516104 | tf_op jit(solution)/shard_map/ppermute | solution.py:841
  395.6 15.6 %collective-permute-start.20 = (bf16[112,768]{1,0:T(8,128)(2,1)S(1)}, bf16[112,768]{1,0:T(8,128)(2,1)S(1)}, u32[]{:S(2)}, u32[]{:S(2)}) collective-permute-start(bf16[112,768]{1,0:T(8,128)(2,1)S(1)} %get-tuple-element.169), channel_id=1, source_target_pairs={{0,16},{8,24},{16,0},{24,8},{1,17},{9,25},{17,1},{25,9},{2,18},{10... | collective-permute-start | bytes 516104 | tf_op jit(solution)/shard_map/ppermute | solution.py:841
  397.3 13.9 %collective-permute-start.21 = (bf16[112,768]{1,0:T(8,128)(2,1)S(1)}, bf16[112,768]{1,0:T(8,128)(2,1)S(1)}, u32[]{:S(2)}, u32[]{:S(2)}) collective-permute-start(bf16[112,768]{1,0:T(8,128)(2,1)S(1)} %get-tuple-element.168), channel_id=1, source_target_pairs={{0,24},{8,0},{16,8},{24,16},{1,25},{9,1},{17,9},{25,17},{2,26},{10... | collective-permute-start | bytes 516104 | tf_op jit(solution)/shard_map/ppermute | solution.py:841
  414.5 15.8 %all-to-all-start.8 = ((bf16[8,2,96,256]{3,2,1,0:T(8,128)(2,1)}), bf16[8,2,96,256]{3,2,1,0:T(8,128)(2,1)S(1)}, u32[]{:S(2)}, u32[]{:S(2)}) async-start(bf16[8,2,96,256]{3,2,1,0:T(8,128)(2,1)} %bitcast.270), calls=%async_computation.10 | async-start | bytes 1572864 | tf_op jit(solution)/shard_map/all_to_all | solution.py:654
  (49 other events, 328.3 us)
Sparse Core Ops, SparseCore 0:
  40.3 115.6 all-gather.6
  157.6 61.7 all-gather.4
  221.6 109.3 reduce-scatter.2
  338.0 59.0 reduce-scatter.4

commit v7 on v6

--- a/solution.py
+++ b/solution.py
@@ -7,6 +7,7 @@
 from jax.sharding import PartitionSpec as P
 
 HD = 64
+CAP = 128
 EPSILON = 1e-06
 NEGATIVE = -1e30
 F32 = jnp.float32
@@ -161,16 +162,88 @@
     )(place, tokens_in, mask, lines, bias_pairs, *packs)
 
 
+def combine_kernel(core_ref, back_ref, full_at_ref, half_at_ref, full_ref, mine_ref, theirs_ref):
+    experts, rows, model = back_ref.shape
+    cap = full_ref.shape[2] - model
+    half = cap // 2
+    images, sequence, _ = full_ref.shape
+
+    def gather(at_ref, first, size, slot):
+        lanes = experts * size
+        lane = lax.broadcasted_iota(jnp.int32, (1, lanes), 1)
+        slots = lane // size * cap + slot + lane % size
+        hot = (at_ref[:, 0:1] == slots) | (at_ref[:, 1:2] == slots)
+        hot = jnp.where(hot, 1.0, 0.0).astype(BF16)
+        taken = back_ref[:, first : first + size].reshape(lanes, model)
+        sums = dot(hot, taken)
+        owner = lax.broadcasted_iota(jnp.int32, (cap, lanes), 0) == lane // size
+        scores = 0.0
+        for k in range(2):
+            line = jnp.concatenate(
+                [
+                    back_ref[e, cap + half :, first : first + size].astype(F32)[k : k + 1]
+                    for e in range(experts)
+                ],
+                1,
+            )
+            scores += dot(hot, jnp.where(owner, line, 0.0).astype(BF16), 1, 1)
+        joined = jnp.concatenate([sums, scores], 1)
+        return [joined[k * sequence : (k + 1) * sequence] for k in range(images)]
+
+    full = gather(full_at_ref, 0, cap, 0)
+    shared = gather(half_at_ref, cap, half, core_ref[0] * half)
+    for image in range(images):
+        full_ref[image] = full[image]
+        own = core_ref[0] == image
+
+        def put(ref, image=image):
+            ref[0] = shared[image]
+
+        pl.when(own)(functools.partial(put, mine_ref))
+        pl.when(jnp.logical_not(own))(functools.partial(put, theirs_ref))
+
+
+def combine_rows(core, back, full_at, half_at, images):
+    shape = (images, full_at.shape[0] // images, back.shape[2] + CAP)
+    whole_at = lambda shape: pl.BlockSpec(shape, lambda i, c: (0,) * len(shape))
+    return pl.pallas_call(
+        combine_kernel,
+        grid_spec=pltpu.PrefetchScalarGridSpec(
+            num_scalar_prefetch=1,
+            grid=(1,),
+            in_specs=[whole_at(a.shape) for a in (back, full_at, half_at)],
+            out_specs=[whole_at(shape)] + [whole_at((1,) + shape[1:])] * 2,
+        ),
+        out_shape=[
+            jax.ShapeDtypeStruct(s, F32) for s in (shape, (1,) + shape[1:], (1,) + shape[1:])
+        ],
+        compiler_params=pltpu.CompilerParams(vmem_limit_bytes=56 * 2**20),
+        cost_estimate=pl.CostEstimate(flops=0, bytes_accessed=0, transcendentals=0),
+        name="combine_rows",
+    )(core, back, full_at, half_at)
+
+
 def attend_backward_kernel(
-    n2_grad_ref, grad_ref, h_ref, mask_ref, wo_ref, lines_ref, q_ref, k_ref, v_ref, lse_ref,
-    h_grad_ref, hb_ref, dq_ref, dk_ref, dv_ref, vec_ref, pair_ref,
+    core_ref, full_ref, mine_ref, theirs_ref, chance_ref, route_ref, router_ref,
+    grad_ref, h_ref, mask_ref, wo_ref, lines_ref, q_ref, k_ref, v_ref, lse_ref,
+    h_grad_ref, hb_ref, dq_ref, dk_ref, dv_ref, logit_ref, vec_ref, pair_ref,
 ):
     @pl.when(pl.program_id(0) == 0)
     def _():
         vec_ref[...] = jnp.zeros_like(vec_ref)
         pair_ref[...] = jnp.zeros_like(pair_ref)
 
-    n2_grad = n2_grad_ref[0]
+    shared = pl.program_id(0) == 2 * (1 - core_ref[0])
+    rows = jnp.where(shared, mine_ref[0] + theirs_ref[0], full_ref[0])
+    model = wo_ref.shape[1]
+    chances = chance_ref[0]
+    chance_grad = rows[:, model:] + route_ref[0]
+    logit_grad = chances * (
+        chance_grad - jnp.sum(chances * chance_grad, -1, keepdims=True)
+    )
+    logit_grad = logit_grad.astype(BF16)
+    logit_ref[0] = logit_grad
+    n2_grad = rows[:, :model] + dot(logit_grad, router_ref[...])
     _, unit_two, inverse_two = norm_forward(h_ref[0], lines_ref[5:6, :], lines_ref[6:7, :])
     vec_ref[1:2, :] += jnp.sum(n2_grad * unit_two, 0, keepdims=True)
     vec_ref[2:3, :] += jnp.sum(n2_grad, 0, keepdims=True)
@@ -213,70 +286,125 @@
         put_rows(dv_ref.at[0, t], dv)
 
 
-def attend_backward(n2_grad, out_grad, h, mask, wo, lines, q, k, v, lse):
-    ins = (n2_grad, out_grad, h, mask, wo, lines, q, k, v, lse)
-    shared = {4, 5}
-    images, sequence, model = n2_grad.shape
+def attend_backward(
+    core, full, mine, theirs, chances, route, router, out_grad, h, mask, wo, lines, q, k, v, lse
+):
+    ins = (full, mine, theirs, chances, route, router, out_grad, h, mask, wo, lines, q, k, v, lse)
+    images, sequence, model = h.shape
     quarter, _, width = wo.shape
     heads = ((images, quarter, padded(sequence), width), BF16)
     outs = [
-        (n2_grad.shape, F32), ((images, padded(sequence), model), BF16), heads, heads, heads,
-        ((8, model), F32), ((quarter, 8, width), F32),
+        (h.shape, F32), ((images, padded(sequence), model), BF16), heads, heads, heads,
+        (chances.shape, BF16), ((8, model), F32), ((quarter, 8, width), F32),
     ]
+
+    def spec(index, shape):
+        block = (1,) + shape[1:]
+        rest = (0,) * (len(shape) - 1)
+        if index == 0:
+            return pl.BlockSpec(block, lambda b, c: (jnp.clip(b - c[0], 0, images - 2),) + rest)
+        if index in (1, 2, 5, 9, 10):
+            return pl.BlockSpec(shape, lambda b, c: (0,) * len(shape))
+        return pl.BlockSpec(block, lambda b, c: (b,) + rest)
+
     return pl.pallas_call(
         attend_backward_kernel,
-        grid=(images,),
-        in_specs=[whole(a.shape) if i in shared else by_image(a.shape) for i, a in enumerate(ins)],
-        out_specs=[by_image(s) for s, _ in outs[:5]] + [whole(s) for s, _ in outs[5:]],
+        grid_spec=pltpu.PrefetchScalarGridSpec(
+            num_scalar_prefetch=1,
+            grid=(images,),
+            in_specs=[spec(i, a.shape) for i, a in enumerate(ins)],
+            out_specs=[spec(3, s) for s, _ in outs[:6]] + [spec(2, s) for s, _ in outs[6:]],
+        ),
         out_shape=[jax.ShapeDtypeStruct(s, d) for s, d in outs],
         compiler_params=pltpu.CompilerParams(vmem_limit_bytes=56 * 2**20),
         cost_estimate=pl.CostEstimate(flops=0, bytes_accessed=0, transcendentals=0),
         name="attend_backward",
-    )(*ins)
+    )(core, *ins)
 
 
 def attend_weights_kernel(n1_ref, hb_ref, dq_ref, dk_ref, dv_ref, o_ref, *refs):
-    out_ref = refs[-1]
     width = dq_ref.shape[3]
     n1 = n1_ref[...].reshape(-1, n1_ref.shape[2])
     hb = hb_ref[...].reshape(-1, n1_ref.shape[2])
-    for k, (left, ref) in enumerate(((n1, dq_ref), (n1, dk_ref), (n1, dv_ref), (hb, o_ref))):
-        sums = dot(left, ref[...].reshape(-1, width), 0, 0).astype(out_ref.dtype)
-        columns = slice(k * width, (k + 1) * width)
-        if len(refs) == 1:
-            out_ref[0, :, columns] = sums
-            continue
-        part = sums.shape[0] // 8
+    pairs = ((n1, dq_ref), (n1, dk_ref), (n1, dv_ref), (hb, o_ref))
+    t = pl.program_id(0)
+    if len(refs) == 1:
+        for k, (left, ref) in enumerate(pairs):
+            sums = dot(left, ref[...].reshape(-1, width), 0, 0)
+            refs[0][0, :, k * width : (k + 1) * width] = sums.astype(refs[0].dtype)
+        return
+    extra_ref, lines_ref, *weights, out_ref, gain_ref, shift_ref = refs
+    part = n1.shape[1] // 8
+    lanes = gain_ref.shape[1]
+
+    @pl.when(t == 0)
+    def _():
+        gain_ref[...] = jnp.zeros_like(gain_ref)
+        shift_ref[...] = jnp.zeros_like(shift_ref)
+
+    for k, (left, ref) in enumerate(pairs):
+        right = ref[...].reshape(-1, width)
+        sums = dot(left, right, 0, 0)
+        if k < 3:
+            weight = weights[k][0].astype(F32)
+            shift = weight * jnp.sum(right.astype(F32), 0, keepdims=True)
+            gain = weight * sums
+            for one, total_ref in ((gain, gain_ref), (shift, shift_ref)):
+                total_ref[...] += one[:, :lanes]
+                total_ref[:, : width - lanes] += one[:, lanes:]
+        sums = sums.astype(BF16)
         for z in range(4):
             for x in range(2):
                 start = (z * 2 + x) * part
-                out_ref[0, x, 0, z, :part, columns] = sums[start : start + part]
-    if len(refs) == 2:
+                out_ref[t % 2, x, t // 2, z, :part, k * width : (k + 1) * width] = sums[
+                    start : start + part
+                ]
+
+    @pl.when(t == pl.num_programs(0) - 1)
+    def _():
+        gain = jnp.sum(gain_ref[...].T, 0, keepdims=True)
+        shift = jnp.sum(shift_ref[...].T, 0, keepdims=True)
+        gain = (gain - lines_ref[1:2, :] * shift) / lines_ref[0:1, :]
+        depth, model = extra_ref.shape[1:]
+        row = lax.broadcasted_iota(jnp.int32, (depth, model), 0)
         for z in range(4):
             for x in range(2):
-                out_ref[0, x, 0, z, part:, :] = refs[0][z * 2 + x]
-
-
-def attend_weights(n1, hb, dq, dk, dv, o, extra):
+                here = slice((z * 2 + x) * part, (z * 2 + x + 1) * part)
+                line = jnp.concatenate(
+                    [gain[:, here], shift[:, here], jnp.zeros((1, model - 2 * part), F32)], 1
+                )
+                block = extra_ref[z * 2 + x].astype(F32) + jnp.where(row == 0, line, 0.0)
+                block = block.astype(BF16)
+                for y in range(2):
+                    for c in range(2):
+                        out_ref[c, x, y, z, part:, :] = block
+
+
+def attend_weights(n1, hb, dq, dk, dv, o, extra, lines=None, weights=()):
     images, quarter, rows, width = dq.shape
     model = n1.shape[2]
     heads = pl.BlockSpec((images, 1, rows, width), lambda t: (0, t, 0, 0))
+    in_specs = [whole(n1.shape), whole(hb.shape)] + [heads] * 4
     if extra is None:
+        extras = []
         out_spec = pl.BlockSpec((1, model, 4 * width), lambda t: (t, 0, 0))
         out_shape = jax.ShapeDtypeStruct((quarter, model, 4 * width), F32)
+        scratch = []
     else:
-        depth = model // 8 + extra.shape[1]
-        out_spec = pl.BlockSpec(
-            (1, 2, 1, 4, depth, model), lambda t: (t % 2, 0, t // 2, 0, 0, 0)
-        )
-        out_shape = jax.ShapeDtypeStruct((2, 2, 2, 4, depth, model), BF16)
-    extras = [] if extra is None else [extra]
+        extras = [extra, lines, *weights]
+        in_specs += [whole(extra.shape), whole(lines.shape)]
+        in_specs += [pl.BlockSpec((1, model, width), lambda t: (t, 0, 0))] * len(weights)
+        shape = (2, 2, 2, 4, model // 8 + extra.shape[1], model)
+        out_spec = whole(shape)
+        out_shape = jax.ShapeDtypeStruct(shape, BF16)
+        scratch = [pltpu.VMEM((model, 128), F32)] * 2
     return pl.pallas_call(
         attend_weights_kernel,
         grid=(quarter,),
-        in_specs=[whole(n1.shape), whole(hb.shape)] + [heads] * 4 + [whole(e.shape) for e in extras],
+        in_specs=in_specs,
         out_specs=out_spec,
         out_shape=out_shape,
+        scratch_shapes=scratch,
         compiler_params=pltpu.CompilerParams(vmem_limit_bytes=56 * 2**20),
         cost_estimate=pl.CostEstimate(flops=0, bytes_accessed=0, transcendentals=0),
         name="attend_weights",
@@ -342,7 +470,7 @@
         in_specs=[by_image(up.shape), by_image(down.shape)],
         out_specs=[by_image(s) for s in outs],
         out_shape=[jax.ShapeDtypeStruct(s, BF16) for s in outs],
-        compiler_params=pltpu.CompilerParams(vmem_limit_bytes=32 * 2**20),
+        compiler_params=pltpu.CompilerParams(vmem_limit_bytes=56 * 2**20),
         cost_estimate=pl.CostEstimate(flops=0, bytes_accessed=8 * 10**6, transcendentals=0),
         name="pack_experts",
     )(up, down)
@@ -477,7 +605,6 @@
     )(*ins)
 
 
-CAP = 128
 GROUP_IMG = 2
 CHUNK = 128
 HIGHEST = lax.Precision.HIGHEST
@@ -587,7 +714,7 @@
     parts = []
     for some in packed:
         some = lax.all_to_all(tie(some, *event), PLANE, 0, 0, tiled=True)
-        event = [some, packs[len(packs) // 2]]
+        event = [some, *packs[3:4]]
         starts = [CHUNK * f for f, _ in spans[1:]] if parts else [0]
         stops = [CHUNK * l for _, l in spans[1:]] if parts else [head]
         base = starts[0]
@@ -679,7 +806,7 @@
         for one in parts
     ]
     grad_full, grad_shared = both_groups(out_grad)
-    incoming = swap_experts(dispatch(grad_full, grad_shared), packs[-1], parts[-1])
+    incoming = swap_experts(dispatch(grad_full, grad_shared), *packs[1:4], parts[-1])
 
     local_start = (chip_y * 2 + core) * piece
     mask_here = lax.dynamic_slice_in_dim(key_mask, local_start, piece, 0)[:, None]
@@ -715,6 +842,21 @@
     chosen = swap_experts(
         jnp.concatenate([dispatch(normed_full, normed_shared), lines_of(gates_sent)], 1),
         incoming,
+    )
+
+    grad_rows = out_grad.reshape(tokens, model)
+    bias_dot = dot(grad_rows, bias_down.astype(BF16), 1, 1)
+
+    def lanes(values):
+        values = jnp.pad(values, ((0, 0), (0, CAP - experts)))
+        return values.reshape(piece, sequence, CAP)
+
+    down_bias_grad = lax.dot_general(
+        share_here, grad_rows.astype(F32), (((0,), (0,)), ((), ())), precision=HIGHEST
+    )
+
+    routes = (
+        lanes(probabilities), lanes(hot_here * bias_dot), jnp.pad(router, ((0, CAP - experts), (0, 0)))
     )
 
     sums = None
@@ -724,6 +866,8 @@
     for index, (first, last) in enumerate(spans):
         bias_one = bias_up[:, first * CHUNK : last * CHUNK].reshape(1, -1)
         final = index == count - 1
+        if final:
+            bias_one = tie(bias_one, *routes, down_bias_grad)
         *sums, bias_part, grads = expert_chunk(
             chosen, incoming, bias_one, sums, full_parts[index], final
         )
@@ -735,8 +879,11 @@
 
     mixed, pulled = sums
     back = swap_experts(pulled)
-    gate_back = values_of(back)
-    norm_two_grad = combine(back)
+    core_line = jnp.reshape(core, (1,)).astype(jnp.int32)
+    full_rows, mine_rows, theirs = combine_rows(
+        core_line, back, position_full, position_half, GROUP_IMG
+    )
+    theirs = lax.ppermute(theirs, "c", swap)
 
     def send_back(some, *events):
         if not some:
@@ -749,39 +896,13 @@
 
     mixed = swap_experts(mixed, back)
 
-    def slots_to_tokens(match, parts_here):
-        parts_here = parts_here.reshape(experts, -1)
-        match = (match[:, 0] | match[:, 1]).reshape(experts, -1, group_tokens)
-        return jnp.sum(jnp.where(match, parts_here[..., None], 0.0), 1).T
-
-    prob_full = slots_to_tokens(match_full, gate_back[:, :CAP])
-    prob_shared = slots_to_tokens(match_half, gate_back[:, CAP:])
-    prob_full = prob_full.reshape(GROUP_IMG, sequence, experts)
-    prob_shared = prob_shared.reshape(GROUP_IMG, sequence, experts)
-    mine = jnp.where(core == 0, prob_shared[0], prob_shared[1])
-    theirs = jnp.where(core == 0, prob_shared[1], prob_shared[0])
-    mine = mine + lax.ppermute(theirs, "c", swap)
-    chance_grad = jnp.where(
-        core == 0,
-        jnp.concatenate([prob_full, mine[None]]),
-        jnp.concatenate([mine[None], prob_full]),
-    ).reshape(tokens, experts)
-    grad_rows = out_grad.reshape(tokens, model)
-    bias_dot = dot(grad_rows, bias_down.astype(BF16), 1, 1)
-    chance_grad = chance_grad + hot_here * bias_dot
-    logit_grad = probabilities * (
-        chance_grad - jnp.sum(probabilities * chance_grad, -1, keepdims=True)
-    )
-    logit_grad = logit_grad.astype(BF16)
-    router_grad = dot(logit_grad, normed_two, 0, 0)
-    down_bias_grad = lax.dot_general(
-        share_here, grad_rows.astype(F32), (((0,), (0,)), ((), ())), precision=HIGHEST
-    )
-
-    norm_two_grad = norm_two_grad + dot(logit_grad, router).reshape(norm_two_grad.shape)
-    h_grad, hb, dq, dk, dv, line_sums, pair_sums = attend_backward(
-        norm_two_grad, out_grad, residual, mask_here, wo, lines, q, k, v, lse
-    )
+    h_grad, hb, dq, dk, dv, logit_grad, line_sums, pair_sums = attend_backward(
+        core_line, full_rows, mine_rows, theirs, *routes, out_grad, residual, mask_here, wo, lines, q, k, v, lse,
+    )
+    router_grad = dot(logit_grad.reshape(tokens, CAP), normed_two, 0, 0)[:experts]
+    if length != 4:
+        input_grad, line_ones = input_backward(h_grad, tokens_in, wq, wk, wv, lines, dq, dk, dv)
+
     bias_rows = jnp.concatenate(bias_parts, 1).reshape(dp, quarter, part)
     bias_rows = jnp.where(
         jnp.arange(experts)[:, None, None, None] == expert, bias_rows[None], 0.0
@@ -789,7 +910,7 @@
     bias_rows = bias_rows.transpose(0, 2, 1, 3).reshape(experts * quarter, dp, part)
     line_grads = jnp.concatenate(
         [
-            jnp.zeros((2, model), F32),
+            jnp.zeros((2, model), F32) if length == 4 else line_ones[:2],
             pair_sums[:, 0].reshape(1, model),
             pair_sums[:, 1].reshape(1, model),
             line_sums[:3],
@@ -805,7 +926,9 @@
 
     hb = tie(hb, mixed)
     if length == 4:
-        pack_grads = attend_weights(n1, hb, dq, dk, dv, attended, vector_grads)
+        pack_grads = attend_weights(
+            n1, hb, dq, dk, dv, attended, vector_grads, lines, (wq, wk, wv)
+        )
     else:
         pack_grads = attend_weights(n1, hb, dq, dk, dv, attended, None)
         pack_grads = pack_grads.reshape(quarter, dp, part, model)
@@ -813,27 +936,29 @@
         pack_grads = jnp.concatenate([pack_grads, vector_grads], 2)
         pack_grads = pack_grads.reshape(quarter // 2, 2, dp // 2, 2, -1, model)
         pack_grads = pack_grads.transpose(1, 3, 0, 2, 4, 5)
-    h_grad = tie(h_grad, pack_grads)
-    input_grad, line_ones = input_backward(h_grad, tokens_in, wq, wk, wv, lines, dq, dk, dv)
+    weights_done = pack_grads
     mine = lax.dynamic_index_in_dim(pack_grads, core, 0, keepdims=False)
     theirs = lax.dynamic_index_in_dim(pack_grads, 1 - core, 0, keepdims=False)
     theirs = lax.ppermute(theirs, "c", swap)
     pack_grads = (mine.astype(F32) + theirs.astype(F32)).astype(sum_type)
     pack_grads = pack_grads.reshape((-1,) + pack_grads.shape[2:])
+    if length == 4:
+        h_grad = tie(h_grad, pack_grads)
+        input_grad, _ = input_backward(h_grad, tokens_in, wq, wk, wv, lines, dq, dk, dv)
+    sent = [send_back(reduced[:1], weights_done)]
+    pack_grads = tie(pack_grads, *sent)
     pack_grads = lax.all_to_all(pack_grads, ("x", "y"), 0, 0, tiled=True)
     after_xy = pack_grads
+    mixture = combine(mixed)
+    bias_term = jnp.dot(share_here, bias_down, precision=HIGHEST).reshape(residual.shape)
+    output = (residual + mixture + bias_term).astype(BF16)
+
+    sent = [one.astype(F32) for one in sent if one is not None]
+    ups = [one[:, 0] for one in sent]
+    downs = [one[:, 1] for one in sent]
+    pack_grads = tie(pack_grads, input_grad, output, *ups, *downs)
     pack_grads = jnp.sum(pack_grads.astype(F32), 0)
-    ones = line_ones[:2]
-    for axis in ("c", "y", "x"):
-        ones = ones + lax.ppermute(ones, axis, swap)
-    ones = ones.reshape(2, dp // 2, 2, part)
-    ones = lax.dynamic_index_in_dim(ones, place[1], 2, keepdims=False).transpose(1, 0, 2)
-    ones = jnp.pad(
-        ones.reshape(dp // 2, 1, 2 * part), ((0, 0), (0, 0), (0, model - 2 * part))
-    )
-    pack_grads = (
-        pack_grads + jnp.pad(ones, ((0, 0), (part, pack_grads.shape[1] - part - 1), (0, 0)))
-    ).astype(sum_type)
+    pack_grads = pack_grads.astype(sum_type)
     if length == 4:
         pack_grad = lax.dynamic_index_in_dim(pack_grads, place[0], 0, keepdims=False).astype(F32)
         for far in (1, 2, 3):
@@ -846,16 +971,10 @@
     out_weight_grad = pack_grad[:part, 3 * width :].T
     small_grads = pack_grad[part:].reshape(-1)[: small_rows * part].reshape(small_rows, part)
 
-    mixture = combine(mixed)
-    bias_term = jnp.dot(share_here, bias_down, precision=HIGHEST).reshape(residual.shape)
-    output = (residual + mixture + bias_term).astype(BF16)
-
-    sent = [send_back(reduced[:1], after_xy)]
-    sent.append(send_back(reduced[1:2], *sent))
-    sent.append(send_back(reduced[2:], *sent[1:]))
-    sent = [one.astype(F32) for one in sent if one is not None]
-    ups = [one[:, 0] for one in sent]
-    downs = [one[:, 1] for one in sent]
+    some = send_back(reduced[1:], pack_grads)
+    if some is not None:
+        ups.append(some.astype(F32)[:, 0])
+        downs.append(some.astype(F32)[:, 1])
     up_grad = jnp.concatenate(ups, -1)
     down_grad = jnp.concatenate(downs, -1).transpose(0, 2, 1)
     return (

time: 449 us -> 442 us (0.984)
  blocking collectives: 0 us -> 35.7 us
  waiting for transfers between devices: 137 us -> 109 us
  Pallas kernels: 137 us -> 150 us
  starting transfers between devices: 60.6 us -> 50.1 us
  matrix products: 18.5 us -> 12.3 us
  local copies, waits for them, and re-layouts: 41.2 us -> 35.9 us
  other arithmetic: 31.8 us -> 26.7 us
    all_to_all x0 -> x1, blocking collectives: none -> 35.7 us  [swap_experts(): return lax.all_to_all(tie(rows, *events), PLANE, 0, 0, tiled=True)]
    all_to_all x6 -> x5, waiting for transfers between devices: 61.5 us -> 43.7 us  [swap_experts(): return lax.all_to_all(tie(rows, *events), PLANE, 0, 0, tiled=True)]
    ppermute x4 -> x0, waiting for transfers between devices: 15.9 us -> none  [the longest x3 15.9 us: shards(): ones = ones + lax.ppermute(ones, axis, swap)]
    all_to_all x1, waiting for transfers between devices: 0.01 us -> 12.6 us  [shards(): pack_grads = lax.all_to_all(pack_grads, ('x', 'y'), 0, 0, tiled=True)]
    pallas_call x2 -> x3, Pallas kernels: 30.7 us -> 40.4 us  [the longest x1 22.3 us: attend_backward(): pl.pallas_call(attend_backward_kernel, grid_spec=pltpu.PrefetchScalarGrid...]
    dot_general x15 -> x12, matrix products: 15.2 us -> 9.77 us  [dot(): lax.dot_general(left, right, (((left_dim,), (right_dim,)), ((), ())), pre...]
    all_gather x2, waiting for transfers between devices: 6.77 us -> 1.6 us  [shards(): lax.all_gather(one, 'z', axis=0, tiled=False)]
    all_to_all x6 -> x5, starting transfers between devices: 25.3 us -> 20.8 us  [swap_experts(): return lax.all_to_all(tie(rows, *events), PLANE, 0, 0, tiled=True)]
  transfers between devices with their start and end apart: 35 -> 30, of which waited for: 15 -> 14; matrix products, arithmetic and copies ran while one was open for 18% -> 14% of each run, Pallas kernels for 30% -> 33%
where the time goes in v7:
time: 442 us; the launch traced here: 435 us
  Pallas kernels  150 us (34%)
  waiting for transfers between devices  109 us (25%)
  starting transfers between devices  50.1 us (11%)
  local copies, waits for them, and re-layouts  35.9 us (8%)
  blocking collectives  35.7 us (8%)
  other arithmetic  26.7 us (6%)
  between operations  15.2 us (3%)
  matrix products  12.3 us (3%)
    pallas_call x2, Pallas kernels, expert_chunk(): pl.pallas_call(functools.partial(expert_kernel, first, last), grid=(exper...  67.8 us
    all_to_all x5, waiting for transfers between devices, swap_experts(): return lax.all_to_all(tie(rows, *events), PLANE, 0, 0, tiled=True)  43.7 us
    all_to_all x1, blocking collectives, swap_experts(): return lax.all_to_all(tie(rows, *events), PLANE, 0, 0, tiled=True)  35.7 us
    pallas_call x1, Pallas kernels, attend_forward(): pl.pallas_call(attend_forward_kernel, grid_spec=pltpu.PrefetchScalarGridS...  26 us
    pallas_call x1, Pallas kernels, attend_backward(): pl.pallas_call(attend_backward_kernel, grid_spec=pltpu.PrefetchScalarGrid...  22.3 us
    all_to_all x5, starting transfers between devices, swap_experts(): return lax.all_to_all(tie(rows, *events), PLANE, 0, 0, tiled=True)  20.8 us
    ppermute x1, waiting for transfers between devices, gather_packs(): lax.ppermute(column, ('x', 'y'), [(0, 3), (1, 2), (2, 1), (3, 0)])  13.6 us
    unnamed x87, local copies, waits for them, and re-layouts  13.2 us
  transfers between devices with their start and end apart: 30, of which 14 were waited for; matrix products, arithmetic and copies ran while one was open for 14% of the time, Pallas kernels for 33%

profile of v7, /device:TPU:0, one launch (start us, length us, event | category | flops | bytes accessed | tf_op | source)
XLA Modules:
  0.0 435.1 jit_solution(1398245700183901894)
XLA Ops:
  7.2 6.2 %pack_experts.1 = (bf16[8,2,96,512]{3,2,1,0:T(8,128)(2,1)}, bf16[8,2,96,256]{3,2,1,0:T(8,128)(2,1)}) custom-call(f32[8,96,768]{2,1,0:T(8,128)} %up_ref.1, f32[8,96,768]{2,1,0:T(8,128)} %bitcast.196), custom_call_target="tpu_custom_call" | custom-call | bytes 8000000 | tf_op jit(solution)/shard_map/pack_experts/pallas_call | solution.py:467
  13.5 5.3 %all-to-all-start = ((bf16[8,2,96,512]{3,2,1,0:T(8,128)(2,1)}), bf16[8,2,96,512]{3,2,1,0:T(8,128)(2,1)S(1)}, u32[]{:S(2)}, u32[]{:S(2)}) async-start(bf16[8,2,96,512]{3,2,1,0:T(8,128)(2,1)} %get-tuple-element.64), calls=%async_computation | async-start | bytes 3145728 | tf_op jit(solution)/shard_map/all_to_all | solution.py:716
  21.6 2.6 collective-permute-start.1
  25.5 3.6 collective-permute-done
  29.1 7.0 %collective-permute-done.1 = bf16[112,768]{1,0:T(8,128)(2,1)S(1)} collective-permute-done((bf16[112,768]{1,0:T(8,128)(2,1)S(1)}, bf16[112,768]{1,0:T(8,128)(2,1)S(1)}, u32[]{:S(2)}, u32[]{:S(2)}) %collective-permute-start.1) | collective-permute-done | bytes 172064 | tf_op jit(solution)/shard_map/ppermute | solution.py:625
  46.5 2.2 convolution_convert_fusion.1
  50.8 13.6 %collective-permute-done.5.refs_3_ = bf16[4,112,768]{2,1,0:T(8,128)(2,1)} collective-permute-done((bf16[4,112,768]{2,1,0:T(8,128)(2,1)}, bf16[4,112,768]{2,1,0:T(8,128)(2,1)}, u32[]{:S(2)}, u32[]{:S(2)}) %collective-permute-start.5) | collective-permute-done | bytes 688160 | tf_op jit(solution)/shard_map/ppermute | solution.py:631
  64.5 3.5 all-to-all-start.1
  71.7 7.6 %collective-permute-done.3.refs_1_ = bf16[4,112,768]{2,1,0:T(8,128)(2,1)} collective-permute-done((bf16[4,112,768]{2,1,0:T(8,128)(2,1)}, bf16[4,112,768]{2,1,0:T(8,128)(2,1)}, u32[]{:S(2)}, u32[]{:S(2)}) %collective-permute-start.3) | collective-permute-done | bytes 688160 | tf_op jit(solution)/shard_map/ppermute | solution.py:629
  79.2 8.0 %all-to-all-done.1 = bf16[8,2,96,256]{3,2,1,0:T(8,128)(2,1)S(1)} async-done(((bf16[8,2,96,256]{3,2,1,0:T(8,128)(2,1)}), bf16[8,2,96,256]{3,2,1,0:T(8,128)(2,1)S(1)}, u32[]{:S(2)}, u32[]{:S(2)}) %all-to-all-start.1) | async-done | bytes 786464 | tf_op jit(solution)/shard_map/all_to_all | solution.py:716
  88.1 4.4 %all-to-all-start.2 = ((bf16[8,192,768]{2,1,0:T(8,128)(2,1)}), bf16[8,192,768]{2,1,0:T(8,128)(2,1)}, u32[]{:S(2)}, u32[]{:S(2)}) async-start(bf16[8,192,768]{2,1,0:T(8,128)(2,1)} %pad_maximum_fusion.1), calls=%async_computation.2 | async-start | bytes 4718592 | tf_op jit(solution)/shard_map/all_to_all | solution.py:781
  100.6 26.0 %attend_forward.1 = (bf16[3,208,768]{2,1,0:T(8,128)(2,1)}, bf16[3,200,768]{2,1,0:T(8,128)(2,1)}, f32[3,200,768]{2,1,0:T(8,128)}, bf16[3,4,200,192]{3,2,1,0:T(8,1...) custom-call(s32[4]{0:T(128)} %pad_add_fusion.place_ref, ...), custom_call_target="tpu_custom_call" | custom-call | flops 2000000000 | bytes 4000000 | tf_op jit(solution)/shard_map/attend_forward/pallas_call | solution.py:148
  135.6 4.4 %all-to-all-start.3 = ((bf16[8,208,768]{2,1,0:T(8,128)(2,1)}), bf16[8,208,768]{2,1,0:T(8,128)(2,1)}, u32[]{:S(2)}, u32[]{:S(2)}) async-start(bf16[8,208,768]{2,1,0:T(8,128)(2,1)} %pad_maximum_fusion), calls=%async_computation.3 | async-start | bytes 5111808 | tf_op jit(solution)/shard_map/all_to_all | solution.py:781
  141.1 29.5 %all-to-all-done.3.x_ref = bf16[8,208,768]{2,1,0:T(8,128)(2,1)} async-done(((bf16[8,208,768]{2,1,0:T(8,128)(2,1)}), bf16[8,208,768]{2,1,0:T(8,128)(2,1)}, u32[]{:S(2)}, u32[]{:S(2)}) %all-to-all-start.3) | async-done | bytes 2555936 | tf_op jit(solution)/shard_map/all_to_all | solution.py:781
  170.6 42.9 %expert_chunk.2 = (f32[8,192,768]{2,1,0:T(8,128)}, f32[8,192,768]{2,1,0:T(8,128)}, f32[1,2048]{1,0:T(1,128)}, bf16[4,8,2,96,512]{4,3,2,1,0:T(8,128)(2,1)}) custom-call(bf16[8,208,768]{2,1,0:T(8,128)(2,1)} %all-to-all-done.3.x_ref, bf16[8,192,768]{2,1,0:T(8,128)(2,1)} %all-to-all-done.2.g_ref, f32[1,2048]{1,0:T(1,128)} %bitcast.232, ...), custom_call_target="tpu_custom_call" | custom-call | flops 4831838208 | bytes 4000000 | tf_op jit(solution)/shard_map/expert_chunk/pallas_call | solution.py:588
  219.8 24.8 %expert_chunk.3 = (bf16[8,192,768]{2,1,0:T(8,128)(2,1)}, bf16[8,208,768]{2,1,0:T(8,128)(2,1)}, f32[1,1024]{1,0:T(1,128)}, bf16[4,8,2,96,256]{4,3,2,1,0:T(8,128)(2,1)}) custom-call(bf16[8,208,768]{2,1,0:T(8,128)(2,1)} %all-to-all-done.3.x_ref, bf16[8,192,768]{2,1,0:T(8,128)(2,1)} %all-to-all-done.2.g_ref, f32[1,1024]{1,0:T(1,128)} %bitcast.228, ...), custom_call_target="tpu_custom_call" | custom-call | flops 2415919104 | bytes 4000000 | tf_op jit(solution)/shard_map/expert_chunk/pallas_call | solution.py:588
  244.6 35.7 %all_to_all.45.back_ref = bf16[8,208,768]{2,1,0:T(8,128)(2,1)} all-to-all(bf16[8,208,768]{2,1,0:T(8,128)(2,1)} %get-tuple-element.79), channel_id=1, replica_groups=mesh['z'=4,'x'=2,'y'=2,'c'=2] {'x','y','c'}, dimensions={0} | all-to-all | bytes 5111808 | tf_op jit(solution)/shard_map/all_to_all | solution.py:781
  280.4 4.4 %all-to-all-start.5 = ((bf16[8,192,768]{2,1,0:T(8,128)(2,1)}), bf16[8,192,768]{2,1,0:T(8,128)(2,1)}, u32[]{:S(2)}, u32[]{:S(2)}) async-start(bf16[8,192,768]{2,1,0:T(8,128)(2,1)} %get-tuple-element.80), calls=%async_computation.5 | async-start | bytes 4718592 | tf_op jit(solution)/shard_map/all_to_all | solution.py:781
  284.8 5.4 %combine_rows.1 = (f32[2,200,896]{2,1,0:T(8,128)}, f32[1,200,896]{2,1,0:T(8,128)}, f32[1,200,896]{2,1,0:T(8,128)}) custom-call(s32[1]{0:T(128)} %bitcast.3.core_ref, bf16[8,208,768]{2,1,0:T(8,128)(2,1)} %all_to_all.45.back_ref, s32[400,2]{1,0:T(8,128)} %bitcast.189, s32[400,2]{1,0:T(8,128)} %bitcast.187), custom_call_target="tpu_custom_call" | custom-call | tf_op jit(solution)/shard_map/combine_rows/pallas_call | solution.py:209
  293.9 22.3 %attend_backward.1 = (f32[3,200,768]{2,1,0:T(8,128)}, bf16[3,208,768]{2,1,0:T(8,128)(2,1)}, bf16[3,4,208,192]{3,2,1,0:T(8,128)(2,1)}, bf16[3,4,208,192]{3,2,1,0:...) custom-call(s32[1]{0:T(128)} %bitcast.3.core_ref, ...), custom_call_target="tpu_custom_call" | custom-call | tf_op jit(solution)/shard_map/attend_backward/pallas_call | solution.py:310
  320.7 12.7 %attend_weights.1 = bf16[2,2,2,4,112,768]{5,4,3,2,1,0:T(8,128)(2,1)} custom-call(bf16[3,208,768]{2,1,0:T(8,128)(2,1)} %get-tuple-element.90.n1_ref, bf16[3,208,768]{2,1,0:T(8,128)(2,1)} %get-tuple-element.92.hb_ref, bf16[3,4,208,192]{3,2,1,0:T(8,128)(2,1)} %get-tuple-element.93.dq_ref, bf16[3,4,208,192]{3,2,1,0:T(8,128)(2,1)} %get-tuple-element.94.dk_ref, ...), custom_call_target="tpu_custom_call" | custom-call | tf_op jit(solution)/shard_map/attend_weights/pallas_call | solution.py:401
  333.5 3.5 dynamic-slice_bitcast_fusion
  337.2 4.1 all-to-all-start.6
  342.4 4.8 %fusion = bf16[2,2,4,112,768]{4,3,2,1,0:T(8,128)(2,1)} fusion(bf16[2,2,4,112,768]{4,3,2,1,0:T(8,128)(2,1)} %collective-permute-done.14, bf16[2,2,2,4,112,768]{5,4,3,2,1,0:T(8,128)(2,1)} %attend_weights.1, s32[]{:T(128)S(6)} %select_n.199), kind=kLoop, calls=%fused_computation.1 | loop fusion | flops 5505024 | bytes 8257540 | tf_op jit(solution)/shard_map/convert_element_type | solution.py:943
  347.2 14.2 %all-to-all-done.6 = bf16[8,2,96,512]{3,2,1,0:T(8,128)(2,1)S(1)} async-done(((bf16[8,2,96,512]{3,2,1,0:T(8,128)(2,1)}), bf16[8,2,96,512]{3,2,1,0:T(8,128)(2,1)S(1)}, u32[]{:S(2)}, u32[]{:S(2)}) %all-to-all-start.6) | async-done | bytes 1572896 | tf_op jit(solution)/shard_map/all_to_all | solution.py:781
  362.5 4.8 %all-to-all-start.7 = ((bf16[4,4,112,768]{3,2,1,0:T(8,128)(2,1)}), bf16[4,4,112,768]{3,2,1,0:T(8,128)(2,1)}, u32[]{:S(2)}, u32[]{:S(2)}) async-start(bf16[4,4,112,768]{3,2,1,0:T(8,128)(2,1)} %bitcast.185), calls=%async_computation.8 | async-start | bytes 5505024 | tf_op jit(solution)/shard_map/all_to_all | solution.py:950
  375.3 9.7 %input_backward.1 = (f32[3,200,768]{2,1,0:T(8,128)}, f32[8,768]{1,0:T(8,128)}) custom-call(f32[3,200,768]{2,1,0:T(8,128)} %get-tuple-element.105.h_grad_ref, bf16[3,200,768]{2,1,0:T(8,128)(2,1)} %tokens_ref.3, bf16[4,768,192]{2,1,0:T(8,128)(2,1)} %get-tuple-element.102.refs_2_.wq_ref, bf16[4,768,192]{2,1,0:T(8,128)(2,1)} %get-tuple-element.103.refs_3_.wk_ref, ...), custom_call_target="tpu_custom_call" | custom-call | tf_op jit(solution)/shard_map/input_backward/pallas_call | solution.py:441
  386.9 12.6 %all-to-all-done.7 = bf16[4,4,112,768]{3,2,1,0:T(8,128)(2,1)} async-done(((bf16[4,4,112,768]{3,2,1,0:T(8,128)(2,1)}), bf16[4,4,112,768]{3,2,1,0:T(8,128)(2,1)}, u32[]{:S(2)}, u32[]{:S(2)}) %all-to-all-start.7) | async-done | bytes 2752544 | tf_op jit(solution)/shard_map/all_to_all | solution.py:950
  399.4 2.3 reduce_sum.95
  402.6 2.5 collective-permute-start.16
  406.4 3.5 all-to-all-start.8
  411.9 5.5 %collective-permute-done.16 = bf16[112,768]{1,0:T(8,128)(2,1)S(1)} collective-permute-done((bf16[112,768]{1,0:T(8,128)(2,1)}, bf16[112,768]{1,0:T(8,128)(2,1)S(1)}, u32[]{:S(2)}, u32[]{:S(2)}) %collective-permute-start.16) | collective-permute-done | bytes 172064 | tf_op jit(solution)/shard_map/ppermute | solution.py:966
  (294 shorter events, 80.3 us)
Async XLA Ops:
  7.2 85.6 %copy-start = (s32[12,200]{1,0:T(8,128)S(1)}, s32[12,200]{1,0:T(8,128)}, u32[]{:S(2)}) copy-start(s32[12,200]{1,0:T(8,128)} %param.19) | copy-start | bytes 28804
  13.5 25.4 %all-to-all-start = ((bf16[8,2,96,512]{3,2,1,0:T(8,128)(2,1)}), bf16[8,2,96,512]{3,2,1,0:T(8,128)(2,1)S(1)}, u32[]{:S(2)}, u32[]{:S(2)}) async-start(bf16[8,2,96,512]{3,2,1,0:T(8,128)(2,1)} %get-tuple-element.64), calls=%async_computation | async-start | bytes 3145728 | tf_op jit(solution)/shard_map/all_to_all | solution.py:716
  18.9 151.7 %all-gather.7.cloned.1.call-start = ((), (), s32[]{:S(2)}) async-start(), calls=%async_computation.14 | async-start | bytes 7864320 | tf_op jit(solution)/shard_map/all_gather | solution.py:803
  20.0 9.1 %collective-permute-start = (bf16[112,768]{1,0:T(8,128)(2,1)S(1)}, bf16[112,768]{1,0:T(8,128)(2,1)S(1)}, u32[]{:S(2)}, u32[]{:S(2)}) collective-permute-start(bf16[112,768]{1,0:T(8,128)(2,1)S(1)} %pad_maximum_fusion.5), channel_id=1, source_target_pairs={{0,8},{8,16},{16,24},{24,0},{1,9},{9,17},{17,25},{25,1},{2,10},{10... | collective-permute-start | bytes 516104 | tf_op jit(solution)/shard_map/ppermute | solution.py:625
  21.6 14.5 %collective-permute-start.1 = (bf16[112,768]{1,0:T(8,128)(2,1)S(1)}, bf16[112,768]{1,0:T(8,128)(2,1)S(1)}, u32[]{:S(2)}, u32[]{:S(2)}) collective-permute-start(bf16[112,768]{1,0:T(8,128)(2,1)S(1)} %pad_maximum_fusion.5), channel_id=1, source_target_pairs={{0,16},{8,24},{16,0},{24,8},{1,17},{9,25},{17,1},{25,9},{2,18},{10... | collective-permute-start | bytes 516104 | tf_op jit(solution)/shard_map/ppermute | solution.py:625
  24.2 12.6 %collective-permute-start.2 = (bf16[112,768]{1,0:T(8,128)(2,1)S(1)}, bf16[112,768]{1,0:T(8,128)(2,1)}, u32[]{:S(2)}, u32[]{:S(2)}) collective-permute-start(bf16[112,768]{1,0:T(8,128)(2,1)S(1)} %pad_maximum_fusion.5), channel_id=1, source_target_pairs={{0,24},{8,0},{16,8},{24,16},{1,25},{9,1},{17,9},{25,17},{2,26},{10... | collective-permute-start | bytes 516104 | tf_op jit(solution)/shard_map/ppermute | solution.py:625
  40.9 27.3 %collective-permute-start.10 = (bf16[200,768]{1,0:T(8,128)(2,1)}, bf16[200,768]{1,0:T(8,128)(2,1)}, u32[]{:S(2)}, u32[]{:S(2)}) collective-permute-start(bf16[200,768]{1,0:T(8,128)(2,1)} %fusion.70), channel_id=1, source_target_pairs={{0,1},{1,0},{2,3},{3,2},{4,5},{5,4},{6,7},{7,6},{8,9},{9,8},{10,11... | collective-permute-start | bytes 921608 | tf_op jit(solution)/shard_map/ppermute | solution.py:757
  41.1 52.6 %copy-start.9 = (s32[1,400,2]{2,1,0:T(8,128)}, s32[1,400,2]{2,1,0:T(8,128)S(1)}, u32[]{:S(2)}) copy-start(s32[1,400,2]{2,1,0:T(8,128)S(1)} %copy.135) | copy-start | bytes 9604
  45.0 19.5 %collective-permute-start.5 = (bf16[4,112,768]{2,1,0:T(8,128)(2,1)}, bf16[4,112,768]{2,1,0:T(8,128)(2,1)}, u32[]{:S(2)}, u32[]{:S(2)}) collective-permute-start(bf16[4,112,768]{2,1,0:T(8,128)(2,1)} %pad_maximum_fusion.3.refs_0_), channel_id=1, source_target_pairs={{0,6},{2,4},{4,2},{6,0},{1,7},{3,5},{5,3},{7,1},{8,14},{10,12},{12... | collective-permute-start | bytes 2064392 | tf_op jit(solution)/shard_map/ppermute | solution.py:631
  48.8 30.4 %collective-permute-start.3 = (bf16[4,112,768]{2,1,0:T(8,128)(2,1)}, bf16[4,112,768]{2,1,0:T(8,128)(2,1)}, u32[]{:S(2)}, u32[]{:S(2)}) collective-permute-start(bf16[4,112,768]{2,1,0:T(8,128)(2,1)} %pad_maximum_fusion.3.refs_0_), channel_id=1, source_target_pairs={{0,4},{4,0},{1,5},{5,1},{2,6},{6,2},{3,7},{7,3},{8,12},{12,8},{9,1... | collective-permute-start | bytes 2064392 | tf_op jit(solution)/shard_map/ppermute | solution.py:629
  50.3 28.9 %collective-permute-start.4 = (bf16[4,112,768]{2,1,0:T(8,128)(2,1)}, bf16[4,112,768]{2,1,0:T(8,128)(2,1)}, u32[]{:S(2)}, u32[]{:S(2)}) collective-permute-start(bf16[4,112,768]{2,1,0:T(8,128)(2,1)} %pad_maximum_fusion.3.refs_0_), channel_id=1, source_target_pairs={{0,2},{2,0},{1,3},{3,1},{4,6},{6,4},{5,7},{7,5},{8,10},{10,8},{9,1... | collective-permute-start | bytes 2064392 | tf_op jit(solution)/shard_map/ppermute | solution.py:630
  64.5 22.7 %all-to-all-start.1 = ((bf16[8,2,96,256]{3,2,1,0:T(8,128)(2,1)}), bf16[8,2,96,256]{3,2,1,0:T(8,128)(2,1)S(1)}, u32[]{:S(2)}, u32[]{:S(2)}) async-start(bf16[8,2,96,256]{3,2,1,0:T(8,128)(2,1)} %get-tuple-element.70), calls=%async_computation.1 | async-start | bytes 1572864 | tf_op jit(solution)/shard_map/all_to_all | solution.py:716
  88.1 38.5 %all-to-all-start.2 = ((bf16[8,192,768]{2,1,0:T(8,128)(2,1)}), bf16[8,192,768]{2,1,0:T(8,128)(2,1)}, u32[]{:S(2)}, u32[]{:S(2)}) async-start(bf16[8,192,768]{2,1,0:T(8,128)(2,1)} %pad_maximum_fusion.1), calls=%async_computation.2 | async-start | bytes 4718592 | tf_op jit(solution)/shard_map/all_to_all | solution.py:781
  92.5 127.3 %all-gather.5.cloned.1.call-start = ((), (), s32[]{:S(2)}) async-start(), calls=%async_computation.13 | async-start | bytes 3932160 | tf_op jit(solution)/shard_map/all_gather | solution.py:803
  94.6 4.9 %collective-permute-start.6 = (bf16[4,112,768]{2,1,0:T(8,128)(2,1)}, bf16[4,112,768]{2,1,0:T(8,128)(2,1)S(1)}, u32[]{:S(2)}, u32[]{:S(2)}) collective-permute-start(bf16[4,112,768]{2,1,0:T(8,128)(2,1)} %pad_maximum_fusion.3.refs_0_), channel_id=1, source_target_pairs={{0,1},{1,0},{2,3},{3,2},{4,5},{5,4},{6,7},{7,6},{8,9},{9,8},{10,11... | collective-permute-start | bytes 2064392 | tf_op jit(solution)/shard_map/ppermute | solution.py:633
  95.8 3.7 collective-permute-start.7
  96.0 3.5 collective-permute-start.9
  96.3 3.9 collective-permute-start.8
  128.2 3.4 collective-permute-start.11
  135.6 35.0 %all-to-all-start.3 = ((bf16[8,208,768]{2,1,0:T(8,128)(2,1)}), bf16[8,208,768]{2,1,0:T(8,128)(2,1)}, u32[]{:S(2)}, u32[]{:S(2)}) async-start(bf16[8,208,768]{2,1,0:T(8,128)(2,1)} %pad_maximum_fusion), calls=%async_computation.3 | async-start | bytes 5111808 | tf_op jit(solution)/shard_map/all_to_all | solution.py:781
  140.0 197.2 %reduce-scatter.3.cloned.1.call-start = ((), (), s32[]{:S(2)}) async-start(), calls=%async_computation.11 | async-start | bytes 7864320 | tf_op jit(solution)/shard_map/reduce_scatter | solution.py:876
  280.4 40.4 %all-to-all-start.5 = ((bf16[8,192,768]{2,1,0:T(8,128)(2,1)}), bf16[8,192,768]{2,1,0:T(8,128)(2,1)}, u32[]{:S(2)}, u32[]{:S(2)}) async-start(bf16[8,192,768]{2,1,0:T(8,128)(2,1)} %get-tuple-element.80), calls=%async_computation.5 | async-start | bytes 4718592 | tf_op jit(solution)/shard_map/all_to_all | solution.py:781
  284.8 121.7 %reduce-scatter.5.cloned.1.call-start = ((), (), s32[]{:S(2)}) async-start(), calls=%async_computation.12 | async-start | bytes 3932160 | tf_op jit(solution)/shard_map/reduce_scatter | solution.py:876
  290.2 2.8 collective-permute-start.13
  336.9 5.4 %collective-permute-start.14 = (bf16[2,2,4,112,768]{4,3,2,1,0:T(8,128)(2,1)}, bf16[2,2,4,112,768]{4,3,2,1,0:T(8,128)(2,1)}, u32[]{:S(2)}, u32[]{:S(2)}) collective-permute-start(bf16[2,2,4,112,768]{4,3,2,1,0:T(8,128)(2,1)} %dynamic-slice_bitcast_fusion), channel_id=1, source_target_pairs={{0,1},{1,0},{2,3},{3,2},{4,5},{5,4},{6,7},{7,6},{8,9},{9,8},{10,11... | collective-permute-start | bytes 8257544 | tf_op jit(solution)/shard_map/ppermute | solution.py:942
  337.2 24.2 %all-to-all-start.6 = ((bf16[8,2,96,512]{3,2,1,0:T(8,128)(2,1)}), bf16[8,2,96,512]{3,2,1,0:T(8,128)(2,1)S(1)}, u32[]{:S(2)}, u32[]{:S(2)}) async-start(bf16[8,2,96,512]{3,2,1,0:T(8,128)(2,1)} %bitcast.197), calls=%async_computation.7 | async-start | bytes 3145728 | tf_op jit(solution)/shard_map/all_to_all | solution.py:781
  362.5 36.9 %all-to-all-start.7 = ((bf16[4,4,112,768]{3,2,1,0:T(8,128)(2,1)}), bf16[4,4,112,768]{3,2,1,0:T(8,128)(2,1)}, u32[]{:S(2)}, u32[]{:S(2)}) async-start(bf16[4,4,112,768]{3,2,1,0:T(8,128)(2,1)} %bitcast.185), calls=%async_computation.8 | async-start | bytes 5505024 | tf_op jit(solution)/shard_map/all_to_all | solution.py:950
  369.1 2.6 collective-permute-start.12
  402.5 9.4 %collective-permute-start.15 = (bf16[112,768]{1,0:T(8,128)(2,1)}, bf16[112,768]{1,0:T(8,128)(2,1)S(1)}, u32[]{:S(2)}, u32[]{:S(2)}) collective-permute-start(bf16[112,768]{1,0:T(8,128)(2,1)} %get-tuple-element.166), channel_id=1, source_target_pairs={{0,8},{8,16},{16,24},{24,0},{1,9},{9,17},{17,25},{25,1},{2,10},{10... | collective-permute-start | bytes 516104 | tf_op jit(solution)/shard_map/ppermute | solution.py:966
  402.6 14.9 %collective-permute-start.16 = (bf16[112,768]{1,0:T(8,128)(2,1)}, bf16[112,768]{1,0:T(8,128)(2,1)S(1)}, u32[]{:S(2)}, u32[]{:S(2)}) collective-permute-start(bf16[112,768]{1,0:T(8,128)(2,1)} %get-tuple-element.168), channel_id=1, source_target_pairs={{0,16},{8,24},{16,0},{24,8},{1,17},{9,25},{17,1},{25,9},{2,18},{10... | collective-permute-start | bytes 516104 | tf_op jit(solution)/shard_map/ppermute | solution.py:966
  405.1 13.0 %collective-permute-start.17 = (bf16[112,768]{1,0:T(8,128)(2,1)}, bf16[112,768]{1,0:T(8,128)(2,1)}, u32[]{:S(2)}, u32[]{:S(2)}) collective-permute-start(bf16[112,768]{1,0:T(8,128)(2,1)} %get-tuple-element.167), channel_id=1, source_target_pairs={{0,24},{8,0},{16,8},{24,16},{1,25},{9,1},{17,9},{25,17},{2,26},{10... | collective-permute-start | bytes 516104 | tf_op jit(solution)/shard_map/ppermute | solution.py:966
  406.4 17.3 %all-to-all-start.8 = ((bf16[8,2,96,256]{3,2,1,0:T(8,128)(2,1)}), bf16[8,2,96,256]{3,2,1,0:T(8,128)(2,1)S(1)}, u32[]{:S(2)}, u32[]{:S(2)}) async-start(bf16[8,2,96,256]{3,2,1,0:T(8,128)(2,1)} %bitcast.207), calls=%async_computation.10 | async-start | bytes 1572864 | tf_op jit(solution)/shard_map/all_to_all | solution.py:781
  (36 other events, 235.0 us)
Sparse Core Ops, SparseCore 0:
  40.2 116.2 all-gather.6
  158.0 61.7 all-gather.4
  222.1 109.3 reduce-scatter.2
  333.7 60.7 reduce-scatter.4

commit v8 on v7

--- a/solution.py
+++ b/solution.py
@@ -451,24 +451,26 @@
 
 
 def pack_experts_kernel(up_ref, down_ref, *refs):
-    up = up_ref[0].astype(BF16)
-    down = down_ref[0].astype(BF16)
+    up = up_ref[...].astype(BF16)
+    down = down_ref[...].astype(BF16)
     start = 0
     for ref in refs:
         stop = start + ref.shape[3]
-        ref[0, 0] = up[:, start:stop]
-        ref[0, 1] = down[:, start:stop]
+        ref[:, 0] = up[:, :, start:stop]
+        ref[:, 1] = down[:, :, start:stop]
         start = stop
 
 
 def pack_experts(up, down, sizes):
     experts, part, units = up.shape
+    step = 4
+    block = lambda shape: pl.BlockSpec((step,) + shape[1:], lambda i: (i,) + (0,) * (len(shape) - 1))
     outs = [(experts, 2, part, size) for size in sizes]
     return pl.pallas_call(
         pack_experts_kernel,
-        grid=(experts,),
-        in_specs=[by_image(up.shape), by_image(down.shape)],
-        out_specs=[by_image(s) for s in outs],
+        grid=(experts // step,),
+        in_specs=[block(up.shape), block(down.shape)],
+        out_specs=[block(s) for s in outs],
         out_shape=[jax.ShapeDtypeStruct(s, BF16) for s in outs],
         compiler_params=pltpu.CompilerParams(vmem_limit_bytes=56 * 2**20),
         cost_estimate=pl.CostEstimate(flops=0, bytes_accessed=8 * 10**6, transcendentals=0),

time: 442 us -> 439 us (level)
  no operation moved by 1% of the time
where the time goes in v8:
time: 439 us; the launch traced here: 432 us
  Pallas kernels  147 us (33%)
  waiting for transfers between devices  109 us (25%)
  starting transfers between devices  50.1 us (11%)
  local copies, waits for them, and re-layouts  35.9 us (8%)
  blocking collectives  35.7 us (8%)
  other arithmetic  26.7 us (6%)
  between operations  15.2 us (3%)
  matrix products  12.3 us (3%)
    pallas_call x2, Pallas kernels, expert_chunk(): pl.pallas_call(functools.partial(expert_kernel, first, last), grid=(exper...  67.8 us
    all_to_all x5, waiting for transfers between devices, swap_experts(): return lax.all_to_all(tie(rows, *events), PLANE, 0, 0, tiled=True)  43.7 us
    all_to_all x1, blocking collectives, swap_experts(): return lax.all_to_all(tie(rows, *events), PLANE, 0, 0, tiled=True)  35.7 us
    pallas_call x1, Pallas kernels, attend_forward(): pl.pallas_call(attend_forward_kernel, grid_spec=pltpu.PrefetchScalarGridS...  26 us
    pallas_call x1, Pallas kernels, attend_backward(): pl.pallas_call(attend_backward_kernel, grid_spec=pltpu.PrefetchScalarGrid...  22.3 us
    all_to_all x5, starting transfers between devices, swap_experts(): return lax.all_to_all(tie(rows, *events), PLANE, 0, 0, tiled=True)  20.8 us
    ppermute x1, waiting for transfers between devices, gather_packs(): lax.ppermute(column, ('x', 'y'), [(0, 3), (1, 2), (2, 1), (3, 0)])  13.6 us
    unnamed x87, local copies, waits for them, and re-layouts  13.2 us
  transfers between devices with their start and end apart: 30, of which 14 were waited for; matrix products, arithmetic and copies ran while one was open for 14% of the time, Pallas kernels for 33%

profile of v8, /device:TPU:0, one launch (start us, length us, event | category | flops | bytes accessed | tf_op | source)
XLA Modules:
  0.0 432.4 jit_solution(7156754444168667819)
XLA Ops:
  7.2 3.5 pack_experts.1
  10.8 5.3 %all-to-all-start = ((bf16[8,2,96,512]{3,2,1,0:T(8,128)(2,1)}), bf16[8,2,96,512]{3,2,1,0:T(8,128)(2,1)S(1)}, u32[]{:S(2)}, u32[]{:S(2)}) async-start(bf16[8,2,96,512]{3,2,1,0:T(8,128)(2,1)} %get-tuple-element.64), calls=%async_computation | async-start | bytes 3145728 | tf_op jit(solution)/shard_map/all_to_all | solution.py:718
  18.9 2.6 collective-permute-start.1
  22.8 3.6 collective-permute-done
  26.4 7.0 %collective-permute-done.1 = bf16[112,768]{1,0:T(8,128)(2,1)S(1)} collective-permute-done((bf16[112,768]{1,0:T(8,128)(2,1)S(1)}, bf16[112,768]{1,0:T(8,128)(2,1)S(1)}, u32[]{:S(2)}, u32[]{:S(2)}) %collective-permute-start.1) | collective-permute-done | bytes 172064 | tf_op jit(solution)/shard_map/ppermute | solution.py:627
  48.1 13.6 %collective-permute-done.5.refs_3_ = bf16[4,112,768]{2,1,0:T(8,128)(2,1)} collective-permute-done((bf16[4,112,768]{2,1,0:T(8,128)(2,1)}, bf16[4,112,768]{2,1,0:T(8,128)(2,1)}, u32[]{:S(2)}, u32[]{:S(2)}) %collective-permute-start.5) | collective-permute-done | bytes 688160 | tf_op jit(solution)/shard_map/ppermute | solution.py:633
  61.8 3.5 all-to-all-start.1
  68.9 7.6 %collective-permute-done.3.refs_1_ = bf16[4,112,768]{2,1,0:T(8,128)(2,1)} collective-permute-done((bf16[4,112,768]{2,1,0:T(8,128)(2,1)}, bf16[4,112,768]{2,1,0:T(8,128)(2,1)}, u32[]{:S(2)}, u32[]{:S(2)}) %collective-permute-start.3) | collective-permute-done | bytes 688160 | tf_op jit(solution)/shard_map/ppermute | solution.py:631
  76.5 8.0 %all-to-all-done.1 = bf16[8,2,96,256]{3,2,1,0:T(8,128)(2,1)S(1)} async-done(((bf16[8,2,96,256]{3,2,1,0:T(8,128)(2,1)}), bf16[8,2,96,256]{3,2,1,0:T(8,128)(2,1)S(1)}, u32[]{:S(2)}, u32[]{:S(2)}) %all-to-all-start.1) | async-done | bytes 786464 | tf_op jit(solution)/shard_map/all_to_all | solution.py:718
  85.4 4.4 %all-to-all-start.2 = ((bf16[8,192,768]{2,1,0:T(8,128)(2,1)}), bf16[8,192,768]{2,1,0:T(8,128)(2,1)}, u32[]{:S(2)}, u32[]{:S(2)}) async-start(bf16[8,192,768]{2,1,0:T(8,128)(2,1)} %pad_maximum_fusion.1), calls=%async_computation.2 | async-start | bytes 4718592 | tf_op jit(solution)/shard_map/all_to_all | solution.py:783
  97.8 26.0 %attend_forward.1 = (bf16[3,208,768]{2,1,0:T(8,128)(2,1)}, bf16[3,200,768]{2,1,0:T(8,128)(2,1)}, f32[3,200,768]{2,1,0:T(8,128)}, bf16[3,4,200,192]{3,2,1,0:T(8,1...) custom-call(s32[4]{0:T(128)} %pad_add_fusion.place_ref, ...), custom_call_target="tpu_custom_call" | custom-call | flops 2000000000 | bytes 4000000 | tf_op jit(solution)/shard_map/attend_forward/pallas_call | solution.py:148
  126.7 2.2 convolution_convert_fusion
  132.9 4.4 %all-to-all-start.3 = ((bf16[8,208,768]{2,1,0:T(8,128)(2,1)}), bf16[8,208,768]{2,1,0:T(8,128)(2,1)}, u32[]{:S(2)}, u32[]{:S(2)}) async-start(bf16[8,208,768]{2,1,0:T(8,128)(2,1)} %pad_maximum_fusion), calls=%async_computation.3 | async-start | bytes 5111808 | tf_op jit(solution)/shard_map/all_to_all | solution.py:783
  138.4 29.5 %all-to-all-done.3.x_ref = bf16[8,208,768]{2,1,0:T(8,128)(2,1)} async-done(((bf16[8,208,768]{2,1,0:T(8,128)(2,1)}), bf16[8,208,768]{2,1,0:T(8,128)(2,1)}, u32[]{:S(2)}, u32[]{:S(2)}) %all-to-all-start.3) | async-done | bytes 2555936 | tf_op jit(solution)/shard_map/all_to_all | solution.py:783
  167.9 42.9 %expert_chunk.2 = (f32[8,192,768]{2,1,0:T(8,128)}, f32[8,192,768]{2,1,0:T(8,128)}, f32[1,2048]{1,0:T(1,128)}, bf16[4,8,2,96,512]{4,3,2,1,0:T(8,128)(2,1)}) custom-call(bf16[8,208,768]{2,1,0:T(8,128)(2,1)} %all-to-all-done.3.x_ref, bf16[8,192,768]{2,1,0:T(8,128)(2,1)} %all-to-all-done.2.g_ref, f32[1,2048]{1,0:T(1,128)} %bitcast.232, ...), custom_call_target="tpu_custom_call" | custom-call | flops 4831838208 | bytes 4000000 | tf_op jit(solution)/shard_map/expert_chunk/pallas_call | solution.py:590
  217.1 24.9 %expert_chunk.3 = (bf16[8,192,768]{2,1,0:T(8,128)(2,1)}, bf16[8,208,768]{2,1,0:T(8,128)(2,1)}, f32[1,1024]{1,0:T(1,128)}, bf16[4,8,2,96,256]{4,3,2,1,0:T(8,128)(2,1)}) custom-call(bf16[8,208,768]{2,1,0:T(8,128)(2,1)} %all-to-all-done.3.x_ref, bf16[8,192,768]{2,1,0:T(8,128)(2,1)} %all-to-all-done.2.g_ref, f32[1,1024]{1,0:T(1,128)} %bitcast.228, ...), custom_call_target="tpu_custom_call" | custom-call | flops 2415919104 | bytes 4000000 | tf_op jit(solution)/shard_map/expert_chunk/pallas_call | solution.py:590
  241.9 35.7 %all_to_all.45.back_ref = bf16[8,208,768]{2,1,0:T(8,128)(2,1)} all-to-all(bf16[8,208,768]{2,1,0:T(8,128)(2,1)} %get-tuple-element.79), channel_id=1, replica_groups=mesh['z'=4,'x'=2,'y'=2,'c'=2] {'x','y','c'}, dimensions={0} | all-to-all | bytes 5111808 | tf_op jit(solution)/shard_map/all_to_all | solution.py:783
  277.7 4.4 %all-to-all-start.5 = ((bf16[8,192,768]{2,1,0:T(8,128)(2,1)}), bf16[8,192,768]{2,1,0:T(8,128)(2,1)}, u32[]{:S(2)}, u32[]{:S(2)}) async-start(bf16[8,192,768]{2,1,0:T(8,128)(2,1)} %get-tuple-element.80), calls=%async_computation.5 | async-start | bytes 4718592 | tf_op jit(solution)/shard_map/all_to_all | solution.py:783
  282.1 5.4 %combine_rows.1 = (f32[2,200,896]{2,1,0:T(8,128)}, f32[1,200,896]{2,1,0:T(8,128)}, f32[1,200,896]{2,1,0:T(8,128)}) custom-call(s32[1]{0:T(128)} %bitcast.3.core_ref, bf16[8,208,768]{2,1,0:T(8,128)(2,1)} %all_to_all.45.back_ref, s32[400,2]{1,0:T(8,128)} %bitcast.189, s32[400,2]{1,0:T(8,128)} %bitcast.187), custom_call_target="tpu_custom_call" | custom-call | tf_op jit(solution)/shard_map/combine_rows/pallas_call | solution.py:209
  291.1 22.3 %attend_backward.1 = (f32[3,200,768]{2,1,0:T(8,128)}, bf16[3,208,768]{2,1,0:T(8,128)(2,1)}, bf16[3,4,208,192]{3,2,1,0:T(8,128)(2,1)}, bf16[3,4,208,192]{3,2,1,0:...) custom-call(s32[1]{0:T(128)} %bitcast.3.core_ref, ...), custom_call_target="tpu_custom_call" | custom-call | tf_op jit(solution)/shard_map/attend_backward/pallas_call | solution.py:310
  318.0 12.7 %attend_weights.1 = bf16[2,2,2,4,112,768]{5,4,3,2,1,0:T(8,128)(2,1)} custom-call(bf16[3,208,768]{2,1,0:T(8,128)(2,1)} %get-tuple-element.90.n1_ref, bf16[3,208,768]{2,1,0:T(8,128)(2,1)} %get-tuple-element.92.hb_ref, bf16[3,4,208,192]{3,2,1,0:T(8,128)(2,1)} %get-tuple-element.93.dq_ref, bf16[3,4,208,192]{3,2,1,0:T(8,128)(2,1)} %get-tuple-element.94.dk_ref, ...), custom_call_target="tpu_custom_call" | custom-call | tf_op jit(solution)/shard_map/attend_weights/pallas_call | solution.py:401
  330.8 3.5 dynamic-slice_bitcast_fusion
  334.5 4.1 all-to-all-start.6
  339.7 4.8 %fusion = bf16[2,2,4,112,768]{4,3,2,1,0:T(8,128)(2,1)} fusion(bf16[2,2,4,112,768]{4,3,2,1,0:T(8,128)(2,1)} %collective-permute-done.14, bf16[2,2,2,4,112,768]{5,4,3,2,1,0:T(8,128)(2,1)} %attend_weights.1, s32[]{:T(128)S(6)} %select_n.199), kind=kLoop, calls=%fused_computation.1 | loop fusion | flops 5505024 | bytes 8257540 | tf_op jit(solution)/shard_map/convert_element_type | solution.py:945
  344.4 14.2 %all-to-all-done.6 = bf16[8,2,96,512]{3,2,1,0:T(8,128)(2,1)S(1)} async-done(((bf16[8,2,96,512]{3,2,1,0:T(8,128)(2,1)}), bf16[8,2,96,512]{3,2,1,0:T(8,128)(2,1)S(1)}, u32[]{:S(2)}, u32[]{:S(2)}) %all-to-all-start.6) | async-done | bytes 1572896 | tf_op jit(solution)/shard_map/all_to_all | solution.py:783
  359.8 4.8 %all-to-all-start.7 = ((bf16[4,4,112,768]{3,2,1,0:T(8,128)(2,1)}), bf16[4,4,112,768]{3,2,1,0:T(8,128)(2,1)}, u32[]{:S(2)}, u32[]{:S(2)}) async-start(bf16[4,4,112,768]{3,2,1,0:T(8,128)(2,1)} %bitcast.185), calls=%async_computation.8 | async-start | bytes 5505024 | tf_op jit(solution)/shard_map/all_to_all | solution.py:952
  372.6 9.7 %input_backward.1 = (f32[3,200,768]{2,1,0:T(8,128)}, f32[8,768]{1,0:T(8,128)}) custom-call(f32[3,200,768]{2,1,0:T(8,128)} %get-tuple-element.105.h_grad_ref, bf16[3,200,768]{2,1,0:T(8,128)(2,1)} %tokens_ref.3, bf16[4,768,192]{2,1,0:T(8,128)(2,1)} %get-tuple-element.102.refs_2_.wq_ref, bf16[4,768,192]{2,1,0:T(8,128)(2,1)} %get-tuple-element.103.refs_3_.wk_ref, ...), custom_call_target="tpu_custom_call" | custom-call | tf_op jit(solution)/shard_map/input_backward/pallas_call | solution.py:441
  384.2 12.5 %all-to-all-done.7 = bf16[4,4,112,768]{3,2,1,0:T(8,128)(2,1)} async-done(((bf16[4,4,112,768]{3,2,1,0:T(8,128)(2,1)}), bf16[4,4,112,768]{3,2,1,0:T(8,128)(2,1)}, u32[]{:S(2)}, u32[]{:S(2)}) %all-to-all-start.7) | async-done | bytes 2752544 | tf_op jit(solution)/shard_map/all_to_all | solution.py:952
  396.7 2.3 reduce_sum.95
  399.8 2.5 collective-permute-start.16
  403.7 3.5 all-to-all-start.8
  409.2 5.5 %collective-permute-done.16 = bf16[112,768]{1,0:T(8,128)(2,1)S(1)} collective-permute-done((bf16[112,768]{1,0:T(8,128)(2,1)}, bf16[112,768]{1,0:T(8,128)(2,1)S(1)}, u32[]{:S(2)}, u32[]{:S(2)}) %collective-permute-start.16) | collective-permute-done | bytes 172064 | tf_op jit(solution)/shard_map/ppermute | solution.py:968
  (294 shorter events, 80.3 us)
Async XLA Ops:
  7.2 82.9 %copy-start = (s32[12,200]{1,0:T(8,128)S(1)}, s32[12,200]{1,0:T(8,128)}, u32[]{:S(2)}) copy-start(s32[12,200]{1,0:T(8,128)} %param.19) | copy-start | bytes 28804
  10.8 25.4 %all-to-all-start = ((bf16[8,2,96,512]{3,2,1,0:T(8,128)(2,1)}), bf16[8,2,96,512]{3,2,1,0:T(8,128)(2,1)S(1)}, u32[]{:S(2)}, u32[]{:S(2)}) async-start(bf16[8,2,96,512]{3,2,1,0:T(8,128)(2,1)} %get-tuple-element.64), calls=%async_computation | async-start | bytes 3145728 | tf_op jit(solution)/shard_map/all_to_all | solution.py:718
  16.1 151.7 %all-gather.7.cloned.1.call-start = ((), (), s32[]{:S(2)}) async-start(), calls=%async_computation.14 | async-start | bytes 7864320 | tf_op jit(solution)/shard_map/all_gather | solution.py:805
  17.2 9.1 %collective-permute-start = (bf16[112,768]{1,0:T(8,128)(2,1)S(1)}, bf16[112,768]{1,0:T(8,128)(2,1)S(1)}, u32[]{:S(2)}, u32[]{:S(2)}) collective-permute-start(bf16[112,768]{1,0:T(8,128)(2,1)S(1)} %pad_maximum_fusion.5), channel_id=1, source_target_pairs={{0,8},{8,16},{16,24},{24,0},{1,9},{9,17},{17,25},{25,1},{2,10},{10... | collective-permute-start | bytes 516104 | tf_op jit(solution)/shard_map/ppermute | solution.py:627
  18.9 14.5 %collective-permute-start.1 = (bf16[112,768]{1,0:T(8,128)(2,1)S(1)}, bf16[112,768]{1,0:T(8,128)(2,1)S(1)}, u32[]{:S(2)}, u32[]{:S(2)}) collective-permute-start(bf16[112,768]{1,0:T(8,128)(2,1)S(1)} %pad_maximum_fusion.5), channel_id=1, source_target_pairs={{0,16},{8,24},{16,0},{24,8},{1,17},{9,25},{17,1},{25,9},{2,18},{10... | collective-permute-start | bytes 516104 | tf_op jit(solution)/shard_map/ppermute | solution.py:627
  21.5 12.6 %collective-permute-start.2 = (bf16[112,768]{1,0:T(8,128)(2,1)S(1)}, bf16[112,768]{1,0:T(8,128)(2,1)}, u32[]{:S(2)}, u32[]{:S(2)}) collective-permute-start(bf16[112,768]{1,0:T(8,128)(2,1)S(1)} %pad_maximum_fusion.5), channel_id=1, source_target_pairs={{0,24},{8,0},{16,8},{24,16},{1,25},{9,1},{17,9},{25,17},{2,26},{10... | collective-permute-start | bytes 516104 | tf_op jit(solution)/shard_map/ppermute | solution.py:627
  38.1 27.3 %collective-permute-start.10 = (bf16[200,768]{1,0:T(8,128)(2,1)}, bf16[200,768]{1,0:T(8,128)(2,1)}, u32[]{:S(2)}, u32[]{:S(2)}) collective-permute-start(bf16[200,768]{1,0:T(8,128)(2,1)} %fusion.70), channel_id=1, source_target_pairs={{0,1},{1,0},{2,3},{3,2},{4,5},{5,4},{6,7},{7,6},{8,9},{9,8},{10,11... | collective-permute-start | bytes 921608 | tf_op jit(solution)/shard_map/ppermute | solution.py:759
  38.4 52.6 %copy-start.9 = (s32[1,400,2]{2,1,0:T(8,128)}, s32[1,400,2]{2,1,0:T(8,128)S(1)}, u32[]{:S(2)}) copy-start(s32[1,400,2]{2,1,0:T(8,128)S(1)} %copy.135) | copy-start | bytes 9604
  42.3 19.5 %collective-permute-start.5 = (bf16[4,112,768]{2,1,0:T(8,128)(2,1)}, bf16[4,112,768]{2,1,0:T(8,128)(2,1)}, u32[]{:S(2)}, u32[]{:S(2)}) collective-permute-start(bf16[4,112,768]{2,1,0:T(8,128)(2,1)} %pad_maximum_fusion.3.refs_0_), channel_id=1, source_target_pairs={{0,6},{2,4},{4,2},{6,0},{1,7},{3,5},{5,3},{7,1},{8,14},{10,12},{12... | collective-permute-start | bytes 2064392 | tf_op jit(solution)/shard_map/ppermute | solution.py:633
  46.1 30.4 %collective-permute-start.3 = (bf16[4,112,768]{2,1,0:T(8,128)(2,1)}, bf16[4,112,768]{2,1,0:T(8,128)(2,1)}, u32[]{:S(2)}, u32[]{:S(2)}) collective-permute-start(bf16[4,112,768]{2,1,0:T(8,128)(2,1)} %pad_maximum_fusion.3.refs_0_), channel_id=1, source_target_pairs={{0,4},{4,0},{1,5},{5,1},{2,6},{6,2},{3,7},{7,3},{8,12},{12,8},{9,1... | collective-permute-start | bytes 2064392 | tf_op jit(solution)/shard_map/ppermute | solution.py:631
  47.6 28.9 %collective-permute-start.4 = (bf16[4,112,768]{2,1,0:T(8,128)(2,1)}, bf16[4,112,768]{2,1,0:T(8,128)(2,1)}, u32[]{:S(2)}, u32[]{:S(2)}) collective-permute-start(bf16[4,112,768]{2,1,0:T(8,128)(2,1)} %pad_maximum_fusion.3.refs_0_), channel_id=1, source_target_pairs={{0,2},{2,0},{1,3},{3,1},{4,6},{6,4},{5,7},{7,5},{8,10},{10,8},{9,1... | collective-permute-start | bytes 2064392 | tf_op jit(solution)/shard_map/ppermute | solution.py:632
  61.8 22.7 %all-to-all-start.1 = ((bf16[8,2,96,256]{3,2,1,0:T(8,128)(2,1)}), bf16[8,2,96,256]{3,2,1,0:T(8,128)(2,1)S(1)}, u32[]{:S(2)}, u32[]{:S(2)}) async-start(bf16[8,2,96,256]{3,2,1,0:T(8,128)(2,1)} %get-tuple-element.70), calls=%async_computation.1 | async-start | bytes 1572864 | tf_op jit(solution)/shard_map/all_to_all | solution.py:718
  85.4 38.5 %all-to-all-start.2 = ((bf16[8,192,768]{2,1,0:T(8,128)(2,1)}), bf16[8,192,768]{2,1,0:T(8,128)(2,1)}, u32[]{:S(2)}, u32[]{:S(2)}) async-start(bf16[8,192,768]{2,1,0:T(8,128)(2,1)} %pad_maximum_fusion.1), calls=%async_computation.2 | async-start | bytes 4718592 | tf_op jit(solution)/shard_map/all_to_all | solution.py:783
  89.8 127.3 %all-gather.5.cloned.1.call-start = ((), (), s32[]{:S(2)}) async-start(), calls=%async_computation.13 | async-start | bytes 3932160 | tf_op jit(solution)/shard_map/all_gather | solution.py:805
  91.8 4.9 %collective-permute-start.6 = (bf16[4,112,768]{2,1,0:T(8,128)(2,1)}, bf16[4,112,768]{2,1,0:T(8,128)(2,1)S(1)}, u32[]{:S(2)}, u32[]{:S(2)}) collective-permute-start(bf16[4,112,768]{2,1,0:T(8,128)(2,1)} %pad_maximum_fusion.3.refs_0_), channel_id=1, source_target_pairs={{0,1},{1,0},{2,3},{3,2},{4,5},{5,4},{6,7},{7,6},{8,9},{9,8},{10,11... | collective-permute-start | bytes 2064392 | tf_op jit(solution)/shard_map/ppermute | solution.py:635
  93.1 3.7 collective-permute-start.7
  93.2 3.5 collective-permute-start.9
  93.6 3.9 collective-permute-start.8
  125.5 3.4 collective-permute-start.11
  132.9 35.0 %all-to-all-start.3 = ((bf16[8,208,768]{2,1,0:T(8,128)(2,1)}), bf16[8,208,768]{2,1,0:T(8,128)(2,1)}, u32[]{:S(2)}, u32[]{:S(2)}) async-start(bf16[8,208,768]{2,1,0:T(8,128)(2,1)} %pad_maximum_fusion), calls=%async_computation.3 | async-start | bytes 5111808 | tf_op jit(solution)/shard_map/all_to_all | solution.py:783
  137.3 197.2 %reduce-scatter.3.cloned.1.call-start = ((), (), s32[]{:S(2)}) async-start(), calls=%async_computation.11 | async-start | bytes 7864320 | tf_op jit(solution)/shard_map/reduce_scatter | solution.py:878
  277.7 40.4 %all-to-all-start.5 = ((bf16[8,192,768]{2,1,0:T(8,128)(2,1)}), bf16[8,192,768]{2,1,0:T(8,128)(2,1)}, u32[]{:S(2)}, u32[]{:S(2)}) async-start(bf16[8,192,768]{2,1,0:T(8,128)(2,1)} %get-tuple-element.80), calls=%async_computation.5 | async-start | bytes 4718592 | tf_op jit(solution)/shard_map/all_to_all | solution.py:783
  282.0 121.6 %reduce-scatter.5.cloned.1.call-start = ((), (), s32[]{:S(2)}) async-start(), calls=%async_computation.12 | async-start | bytes 3932160 | tf_op jit(solution)/shard_map/reduce_scatter | solution.py:878
  287.5 2.8 collective-permute-start.13
  334.2 5.4 %collective-permute-start.14 = (bf16[2,2,4,112,768]{4,3,2,1,0:T(8,128)(2,1)}, bf16[2,2,4,112,768]{4,3,2,1,0:T(8,128)(2,1)}, u32[]{:S(2)}, u32[]{:S(2)}) collective-permute-start(bf16[2,2,4,112,768]{4,3,2,1,0:T(8,128)(2,1)} %dynamic-slice_bitcast_fusion), channel_id=1, source_target_pairs={{0,1},{1,0},{2,3},{3,2},{4,5},{5,4},{6,7},{7,6},{8,9},{9,8},{10,11... | collective-permute-start | bytes 8257544 | tf_op jit(solution)/shard_map/ppermute | solution.py:944
  334.5 24.2 %all-to-all-start.6 = ((bf16[8,2,96,512]{3,2,1,0:T(8,128)(2,1)}), bf16[8,2,96,512]{3,2,1,0:T(8,128)(2,1)S(1)}, u32[]{:S(2)}, u32[]{:S(2)}) async-start(bf16[8,2,96,512]{3,2,1,0:T(8,128)(2,1)} %bitcast.197), calls=%async_computation.7 | async-start | bytes 3145728 | tf_op jit(solution)/shard_map/all_to_all | solution.py:783
  359.8 36.9 %all-to-all-start.7 = ((bf16[4,4,112,768]{3,2,1,0:T(8,128)(2,1)}), bf16[4,4,112,768]{3,2,1,0:T(8,128)(2,1)}, u32[]{:S(2)}, u32[]{:S(2)}) async-start(bf16[4,4,112,768]{3,2,1,0:T(8,128)(2,1)} %bitcast.185), calls=%async_computation.8 | async-start | bytes 5505024 | tf_op jit(solution)/shard_map/all_to_all | solution.py:952
  366.4 2.6 collective-permute-start.12
  399.8 9.4 %collective-permute-start.15 = (bf16[112,768]{1,0:T(8,128)(2,1)}, bf16[112,768]{1,0:T(8,128)(2,1)S(1)}, u32[]{:S(2)}, u32[]{:S(2)}) collective-permute-start(bf16[112,768]{1,0:T(8,128)(2,1)} %get-tuple-element.166), channel_id=1, source_target_pairs={{0,8},{8,16},{16,24},{24,0},{1,9},{9,17},{17,25},{25,1},{2,10},{10... | collective-permute-start | bytes 516104 | tf_op jit(solution)/shard_map/ppermute | solution.py:968
  399.8 14.9 %collective-permute-start.16 = (bf16[112,768]{1,0:T(8,128)(2,1)}, bf16[112,768]{1,0:T(8,128)(2,1)S(1)}, u32[]{:S(2)}, u32[]{:S(2)}) collective-permute-start(bf16[112,768]{1,0:T(8,128)(2,1)} %get-tuple-element.168), channel_id=1, source_target_pairs={{0,16},{8,24},{16,0},{24,8},{1,17},{9,25},{17,1},{25,9},{2,18},{10... | collective-permute-start | bytes 516104 | tf_op jit(solution)/shard_map/ppermute | solution.py:968
  402.3 13.0 %collective-permute-start.17 = (bf16[112,768]{1,0:T(8,128)(2,1)}, bf16[112,768]{1,0:T(8,128)(2,1)}, u32[]{:S(2)}, u32[]{:S(2)}) collective-permute-start(bf16[112,768]{1,0:T(8,128)(2,1)} %get-tuple-element.167), channel_id=1, source_target_pairs={{0,24},{8,0},{16,8},{24,16},{1,25},{9,1},{17,9},{25,17},{2,26},{10... | collective-permute-start | bytes 516104 | tf_op jit(solution)/shard_map/ppermute | solution.py:968
  403.7 17.3 %all-to-all-start.8 = ((bf16[8,2,96,256]{3,2,1,0:T(8,128)(2,1)}), bf16[8,2,96,256]{3,2,1,0:T(8,128)(2,1)S(1)}, u32[]{:S(2)}, u32[]{:S(2)}) async-start(bf16[8,2,96,256]{3,2,1,0:T(8,128)(2,1)} %bitcast.207), calls=%async_computation.10 | async-start | bytes 1572864 | tf_op jit(solution)/shard_map/all_to_all | solution.py:783
  (36 other events, 235.0 us)
Sparse Core Ops, SparseCore 0:
  37.5 116.2 all-gather.6
  155.3 61.7 all-gather.4
  219.4 109.3 reduce-scatter.2
  331.0 60.7 reduce-scatter.4

commit v9 on v8

--- a/solution.py
+++ b/solution.py
@@ -476,6 +476,33 @@
         cost_estimate=pl.CostEstimate(flops=0, bytes_accessed=8 * 10**6, transcendentals=0),
         name="pack_experts",
     )(up, down)
+
+
+def unpack_experts_kernel(*refs):
+    up_ref, down_ref = refs[-2:]
+    start = 0
+    for ref in refs[:-2]:
+        stop = start + ref.shape[3]
+        up_ref[:, :, start:stop] = ref[:, 0].astype(F32)
+        down_ref[:, :, start:stop] = ref[:, 1].astype(F32)
+        start = stop
+
+
+def unpack_experts(pieces):
+    experts, _, part, _ = pieces[0].shape
+    step = 4
+    block = lambda shape: pl.BlockSpec((step,) + shape[1:], lambda i: (i,) + (0,) * (len(shape) - 1))
+    shape = (experts, part, sum(one.shape[3] for one in pieces))
+    return pl.pallas_call(
+        unpack_experts_kernel,
+        grid=(experts // step,),
+        in_specs=[block(one.shape) for one in pieces],
+        out_specs=[block(shape)] * 2,
+        out_shape=[jax.ShapeDtypeStruct(shape, F32)] * 2,
+        compiler_params=pltpu.CompilerParams(vmem_limit_bytes=56 * 2**20),
+        cost_estimate=pl.CostEstimate(flops=0, bytes_accessed=8 * 10**6, transcendentals=0),
+        name="unpack_experts",
+    )(*pieces)
 
 
 def to_column(line):
@@ -955,10 +982,7 @@
     bias_term = jnp.dot(share_here, bias_down, precision=HIGHEST).reshape(residual.shape)
     output = (residual + mixture + bias_term).astype(BF16)
 
-    sent = [one.astype(F32) for one in sent if one is not None]
-    ups = [one[:, 0] for one in sent]
-    downs = [one[:, 1] for one in sent]
-    pack_grads = tie(pack_grads, input_grad, output, *ups, *downs)
+    pack_grads = tie(pack_grads, input_grad, output)
     pack_grads = jnp.sum(pack_grads.astype(F32), 0)
     pack_grads = pack_grads.astype(sum_type)
     if length == 4:
@@ -974,11 +998,8 @@
     small_grads = pack_grad[part:].reshape(-1)[: small_rows * part].reshape(small_rows, part)
 
     some = send_back(reduced[1:], pack_grads)
-    if some is not None:
-        ups.append(some.astype(F32)[:, 0])
-        downs.append(some.astype(F32)[:, 1])
-    up_grad = jnp.concatenate(ups, -1)
-    down_grad = jnp.concatenate(downs, -1).transpose(0, 2, 1)
+    up_grad, down_grad = unpack_experts([one for one in (*sent, some) if one is not None])
+    down_grad = down_grad.transpose(0, 2, 1)
     return (
         output,
         input_grad,

time: 439 us -> 437 us (level)
  other arithmetic: 26.7 us -> 21.8 us
    unnamed x87 -> x79, local copies, waits for them, and re-layouts: 13.2 us -> 12.1 us
where the time goes in v9:
time: 437 us; the launch traced here: 430 us
  Pallas kernels  151 us (35%)
  waiting for transfers between devices  111 us (25%)
  starting transfers between devices  50.1 us (11%)
  blocking collectives  35.7 us (8%)
  local copies, waits for them, and re-layouts  32.4 us (7%)
  other arithmetic  21.8 us (5%)
  between operations  15.2 us (3%)
  matrix products  12.4 us (3%)
    pallas_call x2, Pallas kernels, expert_chunk(): pl.pallas_call(functools.partial(expert_kernel, first, last), grid=(exper...  67.8 us
    all_to_all x5, waiting for transfers between devices, swap_experts(): return lax.all_to_all(tie(rows, *events), PLANE, 0, 0, tiled=True)  43.7 us
    all_to_all x1, blocking collectives, swap_experts(): return lax.all_to_all(tie(rows, *events), PLANE, 0, 0, tiled=True)  35.7 us
    pallas_call x1, Pallas kernels, attend_forward(): pl.pallas_call(attend_forward_kernel, grid_spec=pltpu.PrefetchScalarGridS...  26 us
    pallas_call x1, Pallas kernels, attend_backward(): pl.pallas_call(attend_backward_kernel, grid_spec=pltpu.PrefetchScalarGrid...  22.3 us
    all_to_all x5, starting transfers between devices, swap_experts(): return lax.all_to_all(tie(rows, *events), PLANE, 0, 0, tiled=True)  20.8 us
    all_to_all x1, waiting for transfers between devices, shards(): pack_grads = lax.all_to_all(pack_grads, ('x', 'y'), 0, 0, tiled=True)  14.4 us
    ppermute x1, waiting for transfers between devices, gather_packs(): lax.ppermute(column, ('x', 'y'), [(0, 3), (1, 2), (2, 1), (3, 0)])  13.6 us
  transfers between devices with their start and end apart: 30, of which 14 were waited for; matrix products, arithmetic and copies ran while one was open for 14% of the time, Pallas kernels for 33%

profile of v9, /device:TPU:0, one launch (start us, length us, event | category | flops | bytes accessed | tf_op | source)
XLA Modules:
  0.0 429.6 jit_solution(12789401479837927214)
XLA Ops:
  7.2 3.5 pack_experts.1
  10.8 5.3 %all-to-all-start = ((bf16[8,2,96,512]{3,2,1,0:T(8,128)(2,1)}), bf16[8,2,96,512]{3,2,1,0:T(8,128)(2,1)S(1)}, u32[]{:S(2)}, u32[]{:S(2)}) async-start(bf16[8,2,96,512]{3,2,1,0:T(8,128)(2,1)} %get-tuple-element.66), calls=%async_computation | async-start | bytes 3145728 | tf_op jit(solution)/shard_map/all_to_all | solution.py:745
  18.9 2.6 collective-permute-start.1
  22.8 3.6 collective-permute-done
  26.4 7.0 %collective-permute-done.1 = bf16[112,768]{1,0:T(8,128)(2,1)S(1)} collective-permute-done((bf16[112,768]{1,0:T(8,128)(2,1)S(1)}, bf16[112,768]{1,0:T(8,128)(2,1)S(1)}, u32[]{:S(2)}, u32[]{:S(2)}) %collective-permute-start.1) | collective-permute-done | bytes 172064 | tf_op jit(solution)/shard_map/ppermute | solution.py:654
  48.1 13.6 %collective-permute-done.5.refs_3_ = bf16[4,112,768]{2,1,0:T(8,128)(2,1)} collective-permute-done((bf16[4,112,768]{2,1,0:T(8,128)(2,1)}, bf16[4,112,768]{2,1,0:T(8,128)(2,1)}, u32[]{:S(2)}, u32[]{:S(2)}) %collective-permute-start.5) | collective-permute-done | bytes 688160 | tf_op jit(solution)/shard_map/ppermute | solution.py:660
  61.8 3.5 all-to-all-start.1
  68.9 7.6 %collective-permute-done.3.refs_1_ = bf16[4,112,768]{2,1,0:T(8,128)(2,1)} collective-permute-done((bf16[4,112,768]{2,1,0:T(8,128)(2,1)}, bf16[4,112,768]{2,1,0:T(8,128)(2,1)}, u32[]{:S(2)}, u32[]{:S(2)}) %collective-permute-start.3) | collective-permute-done | bytes 688160 | tf_op jit(solution)/shard_map/ppermute | solution.py:658
  76.5 8.0 %all-to-all-done.1 = bf16[8,2,96,256]{3,2,1,0:T(8,128)(2,1)S(1)} async-done(((bf16[8,2,96,256]{3,2,1,0:T(8,128)(2,1)}), bf16[8,2,96,256]{3,2,1,0:T(8,128)(2,1)S(1)}, u32[]{:S(2)}, u32[]{:S(2)}) %all-to-all-start.1) | async-done | bytes 786464 | tf_op jit(solution)/shard_map/all_to_all | solution.py:745
  85.4 4.4 %all-to-all-start.2 = ((bf16[8,192,768]{2,1,0:T(8,128)(2,1)}), bf16[8,192,768]{2,1,0:T(8,128)(2,1)}, u32[]{:S(2)}, u32[]{:S(2)}) async-start(bf16[8,192,768]{2,1,0:T(8,128)(2,1)} %pad_maximum_fusion.1), calls=%async_computation.2 | async-start | bytes 4718592 | tf_op jit(solution)/shard_map/all_to_all | solution.py:810
  97.6 26.0 %attend_forward.1 = (bf16[3,208,768]{2,1,0:T(8,128)(2,1)}, bf16[3,200,768]{2,1,0:T(8,128)(2,1)}, f32[3,200,768]{2,1,0:T(8,128)}, bf16[3,4,200,192]{3,2,1,0:T(8,1...) custom-call(s32[4]{0:T(128)} %pad_add_fusion.place_ref, ...), custom_call_target="tpu_custom_call" | custom-call | flops 2000000000 | bytes 4000000 | tf_op jit(solution)/shard_map/attend_forward/pallas_call | solution.py:148
  126.5 2.2 convolution_convert_fusion
  132.6 4.4 %all-to-all-start.3 = ((bf16[8,208,768]{2,1,0:T(8,128)(2,1)}), bf16[8,208,768]{2,1,0:T(8,128)(2,1)}, u32[]{:S(2)}, u32[]{:S(2)}) async-start(bf16[8,208,768]{2,1,0:T(8,128)(2,1)} %pad_maximum_fusion), calls=%async_computation.3 | async-start | bytes 5111808 | tf_op jit(solution)/shard_map/all_to_all | solution.py:810
  138.1 29.5 %all-to-all-done.3.x_ref = bf16[8,208,768]{2,1,0:T(8,128)(2,1)} async-done(((bf16[8,208,768]{2,1,0:T(8,128)(2,1)}), bf16[8,208,768]{2,1,0:T(8,128)(2,1)}, u32[]{:S(2)}, u32[]{:S(2)}) %all-to-all-start.3) | async-done | bytes 2555936 | tf_op jit(solution)/shard_map/all_to_all | solution.py:810
  167.6 42.9 %expert_chunk.2 = (f32[8,192,768]{2,1,0:T(8,128)}, f32[8,192,768]{2,1,0:T(8,128)}, f32[1,2048]{1,0:T(1,128)}, bf16[4,8,2,96,512]{4,3,2,1,0:T(8,128)(2,1)}) custom-call(bf16[8,208,768]{2,1,0:T(8,128)(2,1)} %all-to-all-done.3.x_ref, bf16[8,192,768]{2,1,0:T(8,128)(2,1)} %all-to-all-done.2.g_ref, f32[1,2048]{1,0:T(1,128)} %bitcast.222, ...), custom_call_target="tpu_custom_call" | custom-call | flops 4831838208 | bytes 4000000 | tf_op jit(solution)/shard_map/expert_chunk/pallas_call | solution.py:617
  217.1 24.8 %expert_chunk.3 = (bf16[8,192,768]{2,1,0:T(8,128)(2,1)}, bf16[8,208,768]{2,1,0:T(8,128)(2,1)}, f32[1,1024]{1,0:T(1,128)}, bf16[4,8,2,96,256]{4,3,2,1,0:T(8,128)(2,1)}) custom-call(bf16[8,208,768]{2,1,0:T(8,128)(2,1)} %all-to-all-done.3.x_ref, bf16[8,192,768]{2,1,0:T(8,128)(2,1)} %all-to-all-done.2.g_ref, f32[1,1024]{1,0:T(1,128)} %bitcast.218, ...), custom_call_target="tpu_custom_call" | custom-call | flops 2415919104 | bytes 4000000 | tf_op jit(solution)/shard_map/expert_chunk/pallas_call | solution.py:617
  241.9 35.7 %all_to_all.45.back_ref = bf16[8,208,768]{2,1,0:T(8,128)(2,1)} all-to-all(bf16[8,208,768]{2,1,0:T(8,128)(2,1)} %get-tuple-element.81), channel_id=1, replica_groups=mesh['z'=4,'x'=2,'y'=2,'c'=2] {'x','y','c'}, dimensions={0} | all-to-all | bytes 5111808 | tf_op jit(solution)/shard_map/all_to_all | solution.py:810
  277.7 4.4 %all-to-all-start.5 = ((bf16[8,192,768]{2,1,0:T(8,128)(2,1)}), bf16[8,192,768]{2,1,0:T(8,128)(2,1)}, u32[]{:S(2)}, u32[]{:S(2)}) async-start(bf16[8,192,768]{2,1,0:T(8,128)(2,1)} %get-tuple-element.82), calls=%async_computation.5 | async-start | bytes 4718592 | tf_op jit(solution)/shard_map/all_to_all | solution.py:810
  282.1 5.4 %combine_rows.1 = (f32[2,200,896]{2,1,0:T(8,128)}, f32[1,200,896]{2,1,0:T(8,128)}, f32[1,200,896]{2,1,0:T(8,128)}) custom-call(s32[1]{0:T(128)} %bitcast.3.core_ref, bf16[8,208,768]{2,1,0:T(8,128)(2,1)} %all_to_all.45.back_ref, s32[400,2]{1,0:T(8,128)} %bitcast.179, s32[400,2]{1,0:T(8,128)} %bitcast.177), custom_call_target="tpu_custom_call" | custom-call | tf_op jit(solution)/shard_map/combine_rows/pallas_call | solution.py:209
  291.2 22.3 %attend_backward.1 = (f32[3,200,768]{2,1,0:T(8,128)}, bf16[3,208,768]{2,1,0:T(8,128)(2,1)}, bf16[3,4,208,192]{3,2,1,0:T(8,128)(2,1)}, bf16[3,4,208,192]{3,2,1,0:...) custom-call(s32[1]{0:T(128)} %bitcast.3.core_ref, ...), custom_call_target="tpu_custom_call" | custom-call | tf_op jit(solution)/shard_map/attend_backward/pallas_call | solution.py:310
  318.1 12.8 %attend_weights.1 = bf16[2,2,2,4,112,768]{5,4,3,2,1,0:T(8,128)(2,1)} custom-call(bf16[3,208,768]{2,1,0:T(8,128)(2,1)} %get-tuple-element.92.n1_ref, bf16[3,208,768]{2,1,0:T(8,128)(2,1)} %get-tuple-element.94.hb_ref, bf16[3,4,208,192]{3,2,1,0:T(8,128)(2,1)} %get-tuple-element.95.dq_ref, bf16[3,4,208,192]{3,2,1,0:T(8,128)(2,1)} %get-tuple-element.96.dk_ref, ...), custom_call_target="tpu_custom_call" | custom-call | tf_op jit(solution)/shard_map/attend_weights/pallas_call | solution.py:401
  330.8 3.5 dynamic-slice_bitcast_fusion
  334.5 4.1 all-to-all-start.6
  339.7 4.8 %fusion = bf16[2,2,4,112,768]{4,3,2,1,0:T(8,128)(2,1)} fusion(bf16[2,2,4,112,768]{4,3,2,1,0:T(8,128)(2,1)} %collective-permute-done.14, bf16[2,2,2,4,112,768]{5,4,3,2,1,0:T(8,128)(2,1)} %attend_weights.1, s32[]{:T(128)S(6)} %select_n.199), kind=kLoop, calls=%fused_computation.1 | loop fusion | flops 5505024 | bytes 8257540 | tf_op jit(solution)/shard_map/convert_element_type | solution.py:972
  344.5 14.2 %all-to-all-done.6.refs_0_ = bf16[8,2,96,512]{3,2,1,0:T(8,128)(2,1)S(1)} async-done(((bf16[8,2,96,512]{3,2,1,0:T(8,128)(2,1)}), bf16[8,2,96,512]{3,2,1,0:T(8,128)(2,1)S(1)}, u32[]{:S(2)}, u32[]{:S(2)}) %all-to-all-start.6) | async-done | bytes 1572896 | tf_op jit(solution)/shard_map/all_to_all | solution.py:810
  359.9 4.8 %all-to-all-start.7 = ((bf16[4,4,112,768]{3,2,1,0:T(8,128)(2,1)}), bf16[4,4,112,768]{3,2,1,0:T(8,128)(2,1)}, u32[]{:S(2)}, u32[]{:S(2)}) async-start(bf16[4,4,112,768]{3,2,1,0:T(8,128)(2,1)} %bitcast.67), calls=%async_computation.8 | async-start | bytes 5505024 | tf_op jit(solution)/shard_map/all_to_all | solution.py:979
  372.8 9.6 %input_backward.1 = (f32[3,200,768]{2,1,0:T(8,128)}, f32[8,768]{1,0:T(8,128)}) custom-call(f32[3,200,768]{2,1,0:T(8,128)} %get-tuple-element.107.h_grad_ref, bf16[3,200,768]{2,1,0:T(8,128)(2,1)} %tokens_ref.3, bf16[4,768,192]{2,1,0:T(8,128)(2,1)} %get-tuple-element.104.refs_2_.wq_ref, bf16[4,768,192]{2,1,0:T(8,128)(2,1)} %get-tuple-element.105.refs_3_.wk_ref, ...), custom_call_target="tpu_custom_call" | custom-call | tf_op jit(solution)/shard_map/input_backward/pallas_call | solution.py:441
  382.4 14.4 %all-to-all-done.7 = bf16[4,4,112,768]{3,2,1,0:T(8,128)(2,1)} async-done(((bf16[4,4,112,768]{3,2,1,0:T(8,128)(2,1)}), bf16[4,4,112,768]{3,2,1,0:T(8,128)(2,1)}, u32[]{:S(2)}, u32[]{:S(2)}) %all-to-all-start.7) | async-done | bytes 2752544 | tf_op jit(solution)/shard_map/all_to_all | solution.py:979
  396.8 2.3 reduce_sum.95
  403.1 3.5 all-to-all-start.8
  408.4 5.5 %collective-permute-done.16 = bf16[112,768]{1,0:T(8,128)(2,1)S(1)} collective-permute-done((bf16[112,768]{1,0:T(8,128)(2,1)S(1)}, bf16[112,768]{1,0:T(8,128)(2,1)S(1)}, u32[]{:S(2)}, u32[]{:S(2)}) %collective-permute-start.16) | collective-permute-done | bytes 172064 | tf_op jit(solution)/shard_map/ppermute | solution.py:992
  419.3 3.5 unpack_experts.1
  (281 shorter events, 74.7 us)
Async XLA Ops:
  7.2 82.9 %copy-start = (s32[12,200]{1,0:T(8,128)S(1)}, s32[12,200]{1,0:T(8,128)}, u32[]{:S(2)}) copy-start(s32[12,200]{1,0:T(8,128)} %param.19) | copy-start | bytes 28804
  10.8 25.4 %all-to-all-start = ((bf16[8,2,96,512]{3,2,1,0:T(8,128)(2,1)}), bf16[8,2,96,512]{3,2,1,0:T(8,128)(2,1)S(1)}, u32[]{:S(2)}, u32[]{:S(2)}) async-start(bf16[8,2,96,512]{3,2,1,0:T(8,128)(2,1)} %get-tuple-element.66), calls=%async_computation | async-start | bytes 3145728 | tf_op jit(solution)/shard_map/all_to_all | solution.py:745
  16.1 151.5 %all-gather.7.cloned.1.call-start = ((), (), s32[]{:S(2)}) async-start(), calls=%async_computation.14 | async-start | bytes 7864320 | tf_op jit(solution)/shard_map/all_gather | solution.py:832
  17.2 9.1 %collective-permute-start = (bf16[112,768]{1,0:T(8,128)(2,1)S(1)}, bf16[112,768]{1,0:T(8,128)(2,1)S(1)}, u32[]{:S(2)}, u32[]{:S(2)}) collective-permute-start(bf16[112,768]{1,0:T(8,128)(2,1)S(1)} %pad_maximum_fusion.4), channel_id=1, source_target_pairs={{0,8},{8,16},{16,24},{24,0},{1,9},{9,17},{17,25},{25,1},{2,10},{10... | collective-permute-start | bytes 516104 | tf_op jit(solution)/shard_map/ppermute | solution.py:654
  18.9 14.5 %collective-permute-start.1 = (bf16[112,768]{1,0:T(8,128)(2,1)S(1)}, bf16[112,768]{1,0:T(8,128)(2,1)S(1)}, u32[]{:S(2)}, u32[]{:S(2)}) collective-permute-start(bf16[112,768]{1,0:T(8,128)(2,1)S(1)} %pad_maximum_fusion.4), channel_id=1, source_target_pairs={{0,16},{8,24},{16,0},{24,8},{1,17},{9,25},{17,1},{25,9},{2,18},{10... | collective-permute-start | bytes 516104 | tf_op jit(solution)/shard_map/ppermute | solution.py:654
  21.5 12.6 %collective-permute-start.2 = (bf16[112,768]{1,0:T(8,128)(2,1)S(1)}, bf16[112,768]{1,0:T(8,128)(2,1)}, u32[]{:S(2)}, u32[]{:S(2)}) collective-permute-start(bf16[112,768]{1,0:T(8,128)(2,1)S(1)} %pad_maximum_fusion.4), channel_id=1, source_target_pairs={{0,24},{8,0},{16,8},{24,16},{1,25},{9,1},{17,9},{25,17},{2,26},{10... | collective-permute-start | bytes 516104 | tf_op jit(solution)/shard_map/ppermute | solution.py:654
  38.1 27.3 %collective-permute-start.10 = (bf16[200,768]{1,0:T(8,128)(2,1)}, bf16[200,768]{1,0:T(8,128)(2,1)}, u32[]{:S(2)}, u32[]{:S(2)}) collective-permute-start(bf16[200,768]{1,0:T(8,128)(2,1)} %fusion.70), channel_id=1, source_target_pairs={{0,1},{1,0},{2,3},{3,2},{4,5},{5,4},{6,7},{7,6},{8,9},{9,8},{10,11... | collective-permute-start | bytes 921608 | tf_op jit(solution)/shard_map/ppermute | solution.py:786
  38.4 52.6 %copy-start.7 = (s32[1,400,2]{2,1,0:T(8,128)}, s32[1,400,2]{2,1,0:T(8,128)S(1)}, u32[]{:S(2)}) copy-start(s32[1,400,2]{2,1,0:T(8,128)S(1)} %copy.135) | copy-start | bytes 9604
  42.3 19.5 %collective-permute-start.5 = (bf16[4,112,768]{2,1,0:T(8,128)(2,1)}, bf16[4,112,768]{2,1,0:T(8,128)(2,1)}, u32[]{:S(2)}, u32[]{:S(2)}) collective-permute-start(bf16[4,112,768]{2,1,0:T(8,128)(2,1)} %pad_maximum_fusion.2.refs_0_), channel_id=1, source_target_pairs={{0,6},{2,4},{4,2},{6,0},{1,7},{3,5},{5,3},{7,1},{8,14},{10,12},{12... | collective-permute-start | bytes 2064392 | tf_op jit(solution)/shard_map/ppermute | solution.py:660
  46.1 30.4 %collective-permute-start.3 = (bf16[4,112,768]{2,1,0:T(8,128)(2,1)}, bf16[4,112,768]{2,1,0:T(8,128)(2,1)}, u32[]{:S(2)}, u32[]{:S(2)}) collective-permute-start(bf16[4,112,768]{2,1,0:T(8,128)(2,1)} %pad_maximum_fusion.2.refs_0_), channel_id=1, source_target_pairs={{0,4},{4,0},{1,5},{5,1},{2,6},{6,2},{3,7},{7,3},{8,12},{12,8},{9,1... | collective-permute-start | bytes 2064392 | tf_op jit(solution)/shard_map/ppermute | solution.py:658
  47.6 28.9 %collective-permute-start.4 = (bf16[4,112,768]{2,1,0:T(8,128)(2,1)}, bf16[4,112,768]{2,1,0:T(8,128)(2,1)}, u32[]{:S(2)}, u32[]{:S(2)}) collective-permute-start(bf16[4,112,768]{2,1,0:T(8,128)(2,1)} %pad_maximum_fusion.2.refs_0_), channel_id=1, source_target_pairs={{0,2},{2,0},{1,3},{3,1},{4,6},{6,4},{5,7},{7,5},{8,10},{10,8},{9,1... | collective-permute-start | bytes 2064392 | tf_op jit(solution)/shard_map/ppermute | solution.py:659
  61.8 22.7 %all-to-all-start.1 = ((bf16[8,2,96,256]{3,2,1,0:T(8,128)(2,1)}), bf16[8,2,96,256]{3,2,1,0:T(8,128)(2,1)S(1)}, u32[]{:S(2)}, u32[]{:S(2)}) async-start(bf16[8,2,96,256]{3,2,1,0:T(8,128)(2,1)} %get-tuple-element.72), calls=%async_computation.1 | async-start | bytes 1572864 | tf_op jit(solution)/shard_map/all_to_all | solution.py:745
  85.4 38.3 %all-to-all-start.2 = ((bf16[8,192,768]{2,1,0:T(8,128)(2,1)}), bf16[8,192,768]{2,1,0:T(8,128)(2,1)}, u32[]{:S(2)}, u32[]{:S(2)}) async-start(bf16[8,192,768]{2,1,0:T(8,128)(2,1)} %pad_maximum_fusion.1), calls=%async_computation.2 | async-start | bytes 4718592 | tf_op jit(solution)/shard_map/all_to_all | solution.py:810
  89.8 127.3 %all-gather.5.cloned.1.call-start = ((), (), s32[]{:S(2)}) async-start(), calls=%async_computation.13 | async-start | bytes 3932160 | tf_op jit(solution)/shard_map/all_gather | solution.py:832
  91.8 4.9 %collective-permute-start.6 = (bf16[4,112,768]{2,1,0:T(8,128)(2,1)}, bf16[4,112,768]{2,1,0:T(8,128)(2,1)S(1)}, u32[]{:S(2)}, u32[]{:S(2)}) collective-permute-start(bf16[4,112,768]{2,1,0:T(8,128)(2,1)} %pad_maximum_fusion.2.refs_0_), channel_id=1, source_target_pairs={{0,1},{1,0},{2,3},{3,2},{4,5},{5,4},{6,7},{7,6},{8,9},{9,8},{10,11... | collective-permute-start | bytes 2064392 | tf_op jit(solution)/shard_map/ppermute | solution.py:662
  93.0 3.7 collective-permute-start.7
  93.2 3.5 collective-permute-start.9
  93.6 3.9 collective-permute-start.8
  125.2 3.5 collective-permute-start.11
  132.6 35.0 %all-to-all-start.3 = ((bf16[8,208,768]{2,1,0:T(8,128)(2,1)}), bf16[8,208,768]{2,1,0:T(8,128)(2,1)}, u32[]{:S(2)}, u32[]{:S(2)}) async-start(bf16[8,208,768]{2,1,0:T(8,128)(2,1)} %pad_maximum_fusion), calls=%async_computation.3 | async-start | bytes 5111808 | tf_op jit(solution)/shard_map/all_to_all | solution.py:810
  137.0 197.5 %reduce-scatter.3.cloned.1.call-start = ((), (), s32[]{:S(2)}) async-start(), calls=%async_computation.11 | async-start | bytes 7864320 | tf_op jit(solution)/shard_map/reduce_scatter | solution.py:905
  277.7 40.4 %all-to-all-start.5 = ((bf16[8,192,768]{2,1,0:T(8,128)(2,1)}), bf16[8,192,768]{2,1,0:T(8,128)(2,1)}, u32[]{:S(2)}, u32[]{:S(2)}) async-start(bf16[8,192,768]{2,1,0:T(8,128)(2,1)} %get-tuple-element.82), calls=%async_computation.5 | async-start | bytes 4718592 | tf_op jit(solution)/shard_map/all_to_all | solution.py:810
  282.1 121.0 %reduce-scatter.5.cloned.1.call-start = ((), (), s32[]{:S(2)}) async-start(), calls=%async_computation.12 | async-start | bytes 3932160 | tf_op jit(solution)/shard_map/reduce_scatter | solution.py:905
  287.5 2.8 collective-permute-start.13
  334.3 5.4 %collective-permute-start.14 = (bf16[2,2,4,112,768]{4,3,2,1,0:T(8,128)(2,1)}, bf16[2,2,4,112,768]{4,3,2,1,0:T(8,128)(2,1)}, u32[]{:S(2)}, u32[]{:S(2)}) collective-permute-start(bf16[2,2,4,112,768]{4,3,2,1,0:T(8,128)(2,1)} %dynamic-slice_bitcast_fusion), channel_id=1, source_target_pairs={{0,1},{1,0},{2,3},{3,2},{4,5},{5,4},{6,7},{7,6},{8,9},{9,8},{10,11... | collective-permute-start | bytes 8257544 | tf_op jit(solution)/shard_map/ppermute | solution.py:971
  334.5 24.2 %all-to-all-start.6 = ((bf16[8,2,96,512]{3,2,1,0:T(8,128)(2,1)}), bf16[8,2,96,512]{3,2,1,0:T(8,128)(2,1)S(1)}, u32[]{:S(2)}, u32[]{:S(2)}) async-start(bf16[8,2,96,512]{3,2,1,0:T(8,128)(2,1)} %bitcast.187), calls=%async_computation.7 | async-start | bytes 3145728 | tf_op jit(solution)/shard_map/all_to_all | solution.py:810
  359.9 36.9 %all-to-all-start.7 = ((bf16[4,4,112,768]{3,2,1,0:T(8,128)(2,1)}), bf16[4,4,112,768]{3,2,1,0:T(8,128)(2,1)}, u32[]{:S(2)}, u32[]{:S(2)}) async-start(bf16[4,4,112,768]{3,2,1,0:T(8,128)(2,1)} %bitcast.67), calls=%async_computation.8 | async-start | bytes 5505024 | tf_op jit(solution)/shard_map/all_to_all | solution.py:979
  366.4 2.7 collective-permute-start.12
  399.2 9.2 %collective-permute-start.15 = (bf16[112,768]{1,0:T(8,128)(2,1)S(1)}, bf16[112,768]{1,0:T(8,128)(2,1)S(1)}, u32[]{:S(2)}, u32[]{:S(2)}) collective-permute-start(bf16[112,768]{1,0:T(8,128)(2,1)S(1)} %get-tuple-element.166), channel_id=1, source_target_pairs={{0,8},{8,16},{16,24},{24,0},{1,9},{9,17},{17,25},{25,1},{2,10},{10... | collective-permute-start | bytes 516104 | tf_op jit(solution)/shard_map/ppermute | solution.py:992
  399.2 14.7 %collective-permute-start.16 = (bf16[112,768]{1,0:T(8,128)(2,1)S(1)}, bf16[112,768]{1,0:T(8,128)(2,1)S(1)}, u32[]{:S(2)}, u32[]{:S(2)}) collective-permute-start(bf16[112,768]{1,0:T(8,128)(2,1)S(1)} %get-tuple-element.168), channel_id=1, source_target_pairs={{0,16},{8,24},{16,0},{24,8},{1,17},{9,25},{17,1},{25,9},{2,18},{10... | collective-permute-start | bytes 516104 | tf_op jit(solution)/shard_map/ppermute | solution.py:992
  401.3 12.5 %collective-permute-start.17 = (bf16[112,768]{1,0:T(8,128)(2,1)S(1)}, bf16[112,768]{1,0:T(8,128)(2,1)S(1)}, u32[]{:S(2)}, u32[]{:S(2)}) collective-permute-start(bf16[112,768]{1,0:T(8,128)(2,1)S(1)} %get-tuple-element.167), channel_id=1, source_target_pairs={{0,24},{8,0},{16,8},{24,16},{1,25},{9,1},{17,9},{25,17},{2,26},{10... | collective-permute-start | bytes 516104 | tf_op jit(solution)/shard_map/ppermute | solution.py:992
  403.1 15.4 %all-to-all-start.8 = ((bf16[8,2,96,256]{3,2,1,0:T(8,128)(2,1)}), bf16[8,2,96,256]{3,2,1,0:T(8,128)(2,1)S(1)}, u32[]{:S(2)}, u32[]{:S(2)}) async-start(bf16[8,2,96,256]{3,2,1,0:T(8,128)(2,1)} %bitcast.197), calls=%async_computation.10 | async-start | bytes 1572864 | tf_op jit(solution)/shard_map/all_to_all | solution.py:810
  (32 other events, 224.9 us)
Sparse Core Ops, SparseCore 0:
  37.5 116.2 all-gather.6
  155.3 61.7 all-gather.4
  219.4 109.3 reduce-scatter.2
  331.0 60.7 reduce-scatter.4
